TPU v7x, 128 devices: a whole 4x4x4 slice. The times are simulated.
128 devices in a mesh: dt: 8 (over x, y_lo), tmpl: 16 (over y_hi, z, core).
Axes of the slice: x: 4, y: 4 (y_hi: 2, y_lo: 2; y = y_hi * 2 + y_lo), z: 4, core: 2. Of those that a mesh axis runs over, the one named last changes fastest.
Arguments:
- strain: bfloat16 [8, 3, 2, 96, 256], P('dt', None, None, 'tmpl'), may hold values from -6 to 6
- templates: bfloat16 [1536, 2, 96, 256], P(('dt', 'tmpl')), may hold values from -6 to 6
- live_count: int32 [8, 16], P('dt', 'tmpl'), may hold values from 0 to 12, as said below
- chi_edges: int32 [1536, 15], P(('dt', 'tmpl')), may hold values from 1 to 95, as said below
- shifts: int32 [8, 3], replicated, may hold values from -41 to 41
Outputs:
- best: float32 [8, 8, 8], P(None, 'dt')
Inputs may be any that keep to these rules, and one draw needn't show every extreme that they name: `live_count`: in each row the counts sum to 96; every row has a device with 12 templates and one with none. `chi_edges`: each row is strictly increasing.
All inputs are finite; a program needn't handle non-finite values.
Results may differ from a plain program's by a relative error of at most 0.00081.
Values may be sent and summed in bfloat16 or wider, within the bound.
No kernel may reach another device: no remote copies, remote signals or barrier semaphores. Data moves between devices by JAX's collectives and lax.ppermute only.
A program may use at most 64 MiB of HBM per device.

v0:
```python
import math

import jax
import jax.numpy as jnp
from jax import lax
from jax.sharding import PartitionSpec as P

FB = 256
NBLK = 96
NFFT = 1048576
FLOW = 5120
NBIN = 16
TW = 128
TX = 256
WIN = 16


TWO_PI = 2.0 * math.pi
EPSILON = 1e-05


def from_root(shard, axis, root):
    mine = lax.axis_index(axis) == root
    return lax.psum(jnp.where(mine, shard, jnp.zeros_like(shard)), axis)


def stride_turns(values):
    spacing = NFFT // FB
    return (values % FB * spacing + values % NFFT) % NFFT


def local_table():
    bins = jnp.arange(FB, dtype=jnp.int32)
    times = jnp.arange(TX, dtype=jnp.int32)
    turns = stride_turns(bins[:, None] * times[None, :])
    angle = turns.astype(jnp.float32) * jnp.float32(TWO_PI / NFFT)
    cosine = jnp.cos(angle)
    sine = jnp.sin(angle)
    upper = jnp.concatenate([cosine, sine], axis=1)
    lower = jnp.concatenate([-sine, cosine], axis=1)
    return jnp.concatenate([upper, lower], axis=0).astype(jnp.bfloat16)


def twiddle(blocks):
    times = jnp.arange(TX, dtype=jnp.int32)
    base = FLOW + blocks * FB
    turns = stride_turns(base[:, None] * times[None, :])
    angle = turns.astype(jnp.float32) * jnp.float32(TWO_PI / NFFT)
    return (jnp.cos(angle), jnp.sin(angle))


def edge_onehot(edges):
    blocks = jnp.arange(NBLK, dtype=jnp.int32)
    bin_of = jnp.sum((edges[:, :, None] <= blocks[None, None, :]).astype(jnp.int32), axis=1)
    labels = jnp.arange(NBIN, dtype=jnp.int32)
    return (bin_of[:, None, :] == labels[None, :, None]).astype(jnp.float32)


def prepare(template_set, onehot):
    wide = template_set.astype(jnp.float32)
    block_power = jnp.sum(wide * wide, axis=(1, 3))
    sigma2 = jnp.sum(block_power, axis=1) + EPSILON
    in_bins = jnp.einsum("kbj,kj->kb", onehot, block_power, precision=lax.Precision.HIGHEST)
    return (sigma2, (in_bins + EPSILON) / sigma2[:, None])


def correlate(strain_blocks, template_blocks, blocks, phase_table):
    strain_real = strain_blocks[:, 0].astype(jnp.float32)[:, None]
    strain_imag = strain_blocks[:, 1].astype(jnp.float32)[:, None]
    templ_real = template_blocks[:, 0].astype(jnp.float32)[None]
    templ_imag = template_blocks[:, 1].astype(jnp.float32)[None]
    prod_real = strain_real * templ_real + strain_imag * templ_imag
    prod_imag = strain_imag * templ_real - strain_real * templ_imag
    stacked = jnp.concatenate([prod_real, prod_imag], axis=-1).astype(jnp.bfloat16)
    detectors, count, nblocks = (stacked.shape[0], stacked.shape[1], stacked.shape[2])
    flat = stacked.reshape(-1, 2 * FB)
    raw = jnp.dot(flat, phase_table, preferred_element_type=jnp.float32)
    raw = raw.reshape(detectors, count, nblocks, 2, TX)
    cos_turn, sin_turn = twiddle(blocks)
    raw_real = raw[:, :, :, 0, :]
    raw_imag = raw[:, :, :, 1, :]
    out_real = cos_turn * raw_real - sin_turn * raw_imag
    out_imag = cos_turn * raw_imag + sin_turn * raw_real
    return jnp.concatenate([out_real, out_imag], axis=-1)


def statistic(partial_value, onehot, fraction, sigma2, shift_row, live):
    binned = jnp.einsum("kbj,dkjt->dkbt", onehot, partial_value, precision=lax.Precision.HIGHEST)
    series = jnp.sum(binned, axis=2)
    series_real = series[..., :TX]
    series_imag = series[..., TX:]
    snr = (
        jnp.sqrt(series_real * series_real + series_imag * series_imag)
        / jnp.sqrt(2.0 * sigma2)[None, :, None]
    )
    frac_full = fraction[None, :, :, None]
    gap_real = binned[..., :TX] - frac_full * series_real[:, :, None, :]
    gap_imag = binned[..., TX:] - frac_full * series_imag[:, :, None, :]
    chi_square = jnp.sum(
        (gap_real * gap_real + gap_imag * gap_imag)
        / (fraction * sigma2[:, None])[None, :, :, None],
        axis=2,
    )
    reduced = chi_square / (2.0 * NBIN - 2.0)
    factor = jnp.where(
        reduced > 1.0, ((1.0 + reduced * reduced * reduced) * 0.5) ** (-1.0 / 6.0), 1.0
    )
    newsnr = snr * factor
    margin = (TX - TW) // 2
    squares = jnp.zeros((newsnr.shape[1], TW), jnp.float32)
    for detector in range(newsnr.shape[0]):
        moved = lax.dynamic_slice_in_dim(newsnr[detector], margin + shift_row[detector], TW, 1)
        squares = squares + moved * moved
    network = jnp.sqrt(squares) * live[:, None]
    windows = jnp.max(network.reshape(network.shape[0], TW // WIN, WIN), axis=2)
    return jnp.max(windows, axis=0)


def per_device(strain, templates, live_count, chi_edges, shifts):
    own_count = live_count[0, 0]
    slots = templates.shape[0]
    onehot_own = edge_onehot(chi_edges)
    live = (jnp.arange(slots, dtype=jnp.int32) < own_count).astype(jnp.float32)
    sigma2, fraction = prepare(templates, onehot_own)
    phase_table = local_table()
    seg_local = strain.shape[0]

    def one_round(carry, round_index):
        owner = round_index // seg_local
        which = round_index % seg_local
        mine = lax.dynamic_index_in_dim(strain, which, 0, keepdims=False)
        arrived = from_root(mine, "dt", owner)
        strain_blocks = lax.all_gather(arrived, "tmpl", axis=2, tiled=True)
        count = strain_blocks.shape[2]
        block_ids = jnp.arange(count, dtype=jnp.int32)
        partial_value = correlate(strain_blocks, templates, block_ids, phase_table)
        shift_row = lax.dynamic_index_in_dim(shifts, round_index, 0, keepdims=False)
        return (carry, statistic(partial_value, onehot_own, fraction, sigma2, shift_row, live))

    rounds = seg_local * lax.axis_size("dt")
    final_carry, best_local = lax.scan(one_round, jnp.int32(0), jnp.arange(rounds, dtype=jnp.int32))
    best = lax.pmax(best_local, "tmpl")
    return best[:, None, :]


def solution(mesh):
    in_specs = (
        P("dt", None, None, "tmpl", None),
        P(("dt", "tmpl"), None, None, None),
        P("dt", "tmpl"),
        P(("dt", "tmpl"), None),
        P(),
    )
    out_specs = P(None, "dt", None)
    return jax.shard_map(
        per_device, mesh=mesh, in_specs=in_specs, out_specs=out_specs, check_vma=False
    )
```

profile of v0, /device:TPU:0, one launch (start us, length us, event | category | flops | bytes accessed | tf_op | source)
XLA Modules:
  0.0 617.3 jit_solution(15847772550105661721)
XLA Ops:
  0.0 1.9 fusion.42
  3.0 1.3 negate_convert_fusion
  4.2 1.2 fusion.57
  5.5 1.3 copy.30
  6.9 574.7 %while.14 = (s32[]{:T(128)}, f32[8,8]{1,0:T(8,128)S(1)}, s32[8]{0:T(128)S(1)}, bf16[1,3,2,6,256]{4,2,1,3,0:T(2,128)(2,1)S(1)}, bf16[12,2,96,256]{3,2,0,1:T(8,128...) while((s32[]{:T(128)}, f32[8,8]{1,0:T(8,128)S(1)}, ...), condition=%wide.region_9.10_spmd.clone, body=%wide.region_3.9_spmd.clone.sunk | while | flops 2176280576 | bytes 47598672 | solution.py:141
  8.5 34.4 %psum.13 = bf16[3,2,6,256]{3,1,0,2:T(2,128)(2,1)S(1)} all-reduce(bf16[3,2,6,256]{3,1,0,2:T(2,128)(2,1)S(1)} %fusion.80), channel_id=1, replica_groups=mesh['dt'=8,'tmpl'=16] {'dt'}, use_global_device_ids=true, to_apply=%region_4.4 | all-reduce | flops 9216 | bytes 36864 | tf_op jit(solution)/shard_map/while/body/eval_jaxpr/psum | solution.py:24
  42.8 26.1 %all_gather.9 = bf16[3,2,96,256]{3,1,0,2:T(2,128)(2,1)S(1)} all-gather(bf16[3,2,6,256]{3,1,0,2:T(2,128)(2,1)S(1)} %psum.13), channel_id=1, replica_groups=mesh['dt'=8,'tmpl'=16] {'tmpl'}, dimensions={2}, use_global_device_ids=true | all-gather | bytes 313344 | tf_op jit(solution)/shard_map/while/body/eval_jaxpr/all_gather | solution.py:133
  70.7 2.1 fusion.83
  73.3 1.4 multiply_subtract_fusion.2
  74.7 3.9 fusion.85
  88.2 30.7 %psum.13 = bf16[3,2,6,256]{3,1,0,2:T(2,128)(2,1)S(1)} all-reduce(bf16[3,2,6,256]{3,1,0,2:T(2,128)(2,1)S(1)} %fusion.80), channel_id=1, replica_groups=mesh['dt'=8,'tmpl'=16] {'dt'}, use_global_device_ids=true, to_apply=%region_4.4 | all-reduce | flops 9216 | bytes 36864 | tf_op jit(solution)/shard_map/while/body/eval_jaxpr/psum | solution.py:24
  118.9 19.7 %all_gather.9 = bf16[3,2,96,256]{3,1,0,2:T(2,128)(2,1)S(1)} all-gather(bf16[3,2,6,256]{3,1,0,2:T(2,128)(2,1)S(1)} %psum.13), channel_id=1, replica_groups=mesh['dt'=8,'tmpl'=16] {'tmpl'}, dimensions={2}, use_global_device_ids=true | all-gather | bytes 313344 | tf_op jit(solution)/shard_map/while/body/eval_jaxpr/all_gather | solution.py:133
  139.4 1.0 add_convert_fusion.2
  140.4 2.1 fusion.83
  143.0 1.4 multiply_subtract_fusion.2
  144.5 3.9 fusion.85
  158.0 30.7 %psum.13 = bf16[3,2,6,256]{3,1,0,2:T(2,128)(2,1)S(1)} all-reduce(bf16[3,2,6,256]{3,1,0,2:T(2,128)(2,1)S(1)} %fusion.80), channel_id=1, replica_groups=mesh['dt'=8,'tmpl'=16] {'dt'}, use_global_device_ids=true, to_apply=%region_4.4 | all-reduce | flops 9216 | bytes 36864 | tf_op jit(solution)/shard_map/while/body/eval_jaxpr/psum | solution.py:24
  188.6 21.9 %all_gather.9 = bf16[3,2,96,256]{3,1,0,2:T(2,128)(2,1)S(1)} all-gather(bf16[3,2,6,256]{3,1,0,2:T(2,128)(2,1)S(1)} %psum.13), channel_id=1, replica_groups=mesh['dt'=8,'tmpl'=16] {'tmpl'}, dimensions={2}, use_global_device_ids=true | all-gather | bytes 313344 | tf_op jit(solution)/shard_map/while/body/eval_jaxpr/all_gather | solution.py:133
  211.3 1.0 add_convert_fusion.2
  212.4 2.1 fusion.83
  215.0 1.4 multiply_subtract_fusion.2
  216.4 3.9 fusion.85
  229.9 30.7 %psum.13 = bf16[3,2,6,256]{3,1,0,2:T(2,128)(2,1)S(1)} all-reduce(bf16[3,2,6,256]{3,1,0,2:T(2,128)(2,1)S(1)} %fusion.80), channel_id=1, replica_groups=mesh['dt'=8,'tmpl'=16] {'dt'}, use_global_device_ids=true, to_apply=%region_4.4 | all-reduce | flops 9216 | bytes 36864 | tf_op jit(solution)/shard_map/while/body/eval_jaxpr/psum | solution.py:24
  260.6 19.8 %all_gather.9 = bf16[3,2,96,256]{3,1,0,2:T(2,128)(2,1)S(1)} all-gather(bf16[3,2,6,256]{3,1,0,2:T(2,128)(2,1)S(1)} %psum.13), channel_id=1, replica_groups=mesh['dt'=8,'tmpl'=16] {'tmpl'}, dimensions={2}, use_global_device_ids=true | all-gather | bytes 313344 | tf_op jit(solution)/shard_map/while/body/eval_jaxpr/all_gather | solution.py:133
  282.1 2.1 fusion.83
  284.7 1.4 multiply_subtract_fusion.2
  286.2 3.9 fusion.85
  299.6 30.7 %psum.13 = bf16[3,2,6,256]{3,1,0,2:T(2,128)(2,1)S(1)} all-reduce(bf16[3,2,6,256]{3,1,0,2:T(2,128)(2,1)S(1)} %fusion.80), channel_id=1, replica_groups=mesh['dt'=8,'tmpl'=16] {'dt'}, use_global_device_ids=true, to_apply=%region_4.4 | all-reduce | flops 9216 | bytes 36864 | tf_op jit(solution)/shard_map/while/body/eval_jaxpr/psum | solution.py:24
  330.3 21.9 %all_gather.9 = bf16[3,2,96,256]{3,1,0,2:T(2,128)(2,1)S(1)} all-gather(bf16[3,2,6,256]{3,1,0,2:T(2,128)(2,1)S(1)} %psum.13), channel_id=1, replica_groups=mesh['dt'=8,'tmpl'=16] {'tmpl'}, dimensions={2}, use_global_device_ids=true | all-gather | bytes 313344 | tf_op jit(solution)/shard_map/while/body/eval_jaxpr/all_gather | solution.py:133
  354.0 2.1 fusion.83
  356.7 1.4 multiply_subtract_fusion.2
  358.1 3.9 fusion.85
  371.6 30.7 %psum.13 = bf16[3,2,6,256]{3,1,0,2:T(2,128)(2,1)S(1)} all-reduce(bf16[3,2,6,256]{3,1,0,2:T(2,128)(2,1)S(1)} %fusion.80), channel_id=1, replica_groups=mesh['dt'=8,'tmpl'=16] {'dt'}, use_global_device_ids=true, to_apply=%region_4.4 | all-reduce | flops 9216 | bytes 36864 | tf_op jit(solution)/shard_map/while/body/eval_jaxpr/psum | solution.py:24
  402.3 19.8 %all_gather.9 = bf16[3,2,96,256]{3,1,0,2:T(2,128)(2,1)S(1)} all-gather(bf16[3,2,6,256]{3,1,0,2:T(2,128)(2,1)S(1)} %psum.13), channel_id=1, replica_groups=mesh['dt'=8,'tmpl'=16] {'tmpl'}, dimensions={2}, use_global_device_ids=true | all-gather | bytes 313344 | tf_op jit(solution)/shard_map/while/body/eval_jaxpr/all_gather | solution.py:133
  423.8 2.1 fusion.83
  426.4 1.4 multiply_subtract_fusion.2
  427.8 3.9 fusion.85
  441.3 30.7 %psum.13 = bf16[3,2,6,256]{3,1,0,2:T(2,128)(2,1)S(1)} all-reduce(bf16[3,2,6,256]{3,1,0,2:T(2,128)(2,1)S(1)} %fusion.80), channel_id=1, replica_groups=mesh['dt'=8,'tmpl'=16] {'dt'}, use_global_device_ids=true, to_apply=%region_4.4 | all-reduce | flops 9216 | bytes 36864 | tf_op jit(solution)/shard_map/while/body/eval_jaxpr/psum | solution.py:24
  472.0 21.9 %all_gather.9 = bf16[3,2,96,256]{3,1,0,2:T(2,128)(2,1)S(1)} all-gather(bf16[3,2,6,256]{3,1,0,2:T(2,128)(2,1)S(1)} %psum.13), channel_id=1, replica_groups=mesh['dt'=8,'tmpl'=16] {'tmpl'}, dimensions={2}, use_global_device_ids=true | all-gather | bytes 313344 | tf_op jit(solution)/shard_map/while/body/eval_jaxpr/all_gather | solution.py:133
  495.7 2.1 fusion.83
  498.3 1.4 multiply_subtract_fusion.2
  499.8 3.9 fusion.85
  513.3 30.7 %psum.13 = bf16[3,2,6,256]{3,1,0,2:T(2,128)(2,1)S(1)} all-reduce(bf16[3,2,6,256]{3,1,0,2:T(2,128)(2,1)S(1)} %fusion.80), channel_id=1, replica_groups=mesh['dt'=8,'tmpl'=16] {'dt'}, use_global_device_ids=true, to_apply=%region_4.4 | all-reduce | flops 9216 | bytes 36864 | tf_op jit(solution)/shard_map/while/body/eval_jaxpr/psum | solution.py:24
  543.9 19.8 %all_gather.9 = bf16[3,2,96,256]{3,1,0,2:T(2,128)(2,1)S(1)} all-gather(bf16[3,2,6,256]{3,1,0,2:T(2,128)(2,1)S(1)} %psum.13), channel_id=1, replica_groups=mesh['dt'=8,'tmpl'=16] {'tmpl'}, dimensions={2}, use_global_device_ids=true | all-gather | bytes 313344 | tf_op jit(solution)/shard_map/while/body/eval_jaxpr/all_gather | solution.py:133
  565.5 2.1 fusion.83
  568.1 1.4 multiply_subtract_fusion.2
  569.5 3.9 fusion.85
  581.6 35.7 %pmax.7 = f32[8,1,8]{2,0,1:T(8,128)} all-reduce(f32[8,1,8]{2,0,1:T(8,128)S(1)} %bitcast.107), channel_id=1, replica_groups=mesh['dt'=8,'tmpl'=16] {'tmpl'}, use_global_device_ids=true, to_apply=%region_10.11 | all-reduce | flops 64 | bytes 512 | tf_op jit(solution)/shard_map/pmax | solution.py:142
  (178 shorter events, 41.4 us)
Async XLA Ops:
  0.0 6.8 %copy-start.1 = (bf16[1,3,2,6,256]{4,2,3,1,0:T(2,128)(2,1)S(1)}, bf16[1,3,2,6,256]{4,2,3,1,0:T(2,128)(2,1)}, u32[]{:S(2)}) copy-start(bf16[1,3,2,6,256]{4,2,3,1,0:T(2,128)(2,1)} %param.7) | copy-start | bytes 55300
  0.0 6.9 %copy-start = (s32[8,3]{0,1:T(4,128)S(1)}, s32[8,3]{0,1:T(4,128)}, u32[]{:S(2)}) copy-start(s32[8,3]{0,1:T(4,128)} %param.11) | copy-start | bytes 292
where the time goes:
time: 619 us; the launch traced here: 617 us
  blocking collectives  456 us (74%)
  loops' own time  53.5 us (9%)
  matrix products  47.6 us (8%)
  other arithmetic  43.7 us (7%)
  local copies, waits for them, and re-layouts  16.7 us (3%)
    psum x8, blocking collectives, from_root(): return lax.psum(jnp.where(mine, shard, jnp.zeros_like(shard)), axis)  249 us
    all_gather x8, blocking collectives, one_round(): strain_blocks = lax.all_gather(arrived, 'tmpl', axis=2, tiled=True)  171 us
    another operation x1, loops' own time, per_device(): lax.scan(one_round, jnp.int32(0), jnp.arange(rounds, dtype=jnp.int32))  53.5 us
    pmax x1, blocking collectives, per_device(): best = lax.pmax(best_local, 'tmpl')  35.7 us
    dot_general x8, matrix products, statistic(): jnp.einsum('kbj,dkjt->dkbt', onehot, partial_value, precision=lax.Precisi...  30.9 us
    dot_general x8, matrix products, correlate(): raw = jnp.dot(flat, phase_table, preferred_element_type=jnp.float32)  16.5 us

commit v1 on v0

v1 whole, which is shorter than its diff:
```python
import math

import ml_dtypes
import numpy as np

import jax
import jax.numpy as jnp
from jax import lax
from jax.experimental import pallas as pl
from jax.experimental.pallas import tpu as pltpu
from jax.sharding import PartitionSpec as P

FB = 256
NBLK = 96
NFFT = 1048576
FLOW = 5120
STRIDE = 4097
NBIN = 16
TW = 128
MARGIN = 64
WIN = 16
NWIN = TW // WIN
NDET = 3
SEGS = 8
SLOTS = 12
NSL = 16
JS = NBLK // NSL
ROWS = NDET * SEGS
EPSILON = 1e-05
TWO_PI = 2.0 * math.pi
AXES = ("dt", "tmpl")


def place_of(index):
    dt, tm = divmod(index, 16)
    return (dt // 2, (tm // 8) * 2 + dt % 2, (tm // 2) % 4, tm % 2)


def index_of(x, y, z, core):
    return (x * 2 + y % 2) * 16 + (y // 2) * 8 + z * 2 + core


def near(a):
    return a ^ 1


def far(a):
    return 3 - a


def swap_with(value, axis, partner):
    pairs = []
    for index in range(128):
        place = list(place_of(index))
        place[axis] = partner(place[axis])
        pairs.append((index, index_of(*place)))
    return lax.ppermute(value, AXES, pairs)


def tables():
    n = FLOW + np.arange(NBLK * FB, dtype=np.int64)
    tau = np.arange(TW, dtype=np.int64)
    turns = (n[:, None] * tau[None, :] * STRIDE) % NFFT
    angle = turns.astype(np.float64) * (TWO_PI / NFFT)
    cosine, sine = np.cos(angle), np.sin(angle)
    whole = np.concatenate([-sine, cosine, sine], axis=1).astype(ml_dtypes.bfloat16)
    return whole.reshape(NSL, JS, FB, 3 * TW)


def gather_strain(shard):
    x = jnp.transpose(shard[0], (2, 1, 0, 3)).reshape(JS, 2 * NDET, 1, FB)
    for axis, partner in ((0, near), (0, far), (1, near)):
        x = jnp.concatenate([x, swap_with(x, axis, partner)], axis=2)
    x = x[None]
    y = swap_with(x, 1, far)
    y = jnp.concatenate([y[:, :, :, 4:], y[:, :, :, :4]], axis=3)
    x = jnp.concatenate([x, y], axis=0)
    x = x.reshape(2, JS, 2 * ROWS, FB)
    for axis, partner in ((2, near), (2, far), (3, near)):
        x = jnp.concatenate([x, swap_with(x, axis, partner)], axis=0)
    return x


def arrival_order():
    dt = lax.axis_index("dt")
    tm = lax.axis_index("tmpl")
    x, y_lo = dt // 2, dt % 2
    y_hi, z, core = tm // 8, (tm // 2) % 4, tm % 2
    p = jnp.arange(SEGS, dtype=jnp.int32)
    q = jnp.arange(NSL, dtype=jnp.int32)

    def ring(a, first, second):
        a = jnp.where(second == 1, 3 - a, a)
        return a ^ first

    segs = ring(x, p % 2, p // 2 % 2) * 2 + (y_lo ^ (p // 4))
    slices = (y_hi ^ (q % 2)) * 8 + ring(z, q // 2 % 2, q // 4 % 2) * 2 + (core ^ (q // 8))
    return segs, slices


def phase(turns):
    angle = turns.astype(jnp.float32) * jnp.float32(TWO_PI / NFFT)
    return jnp.stack([jnp.cos(angle), jnp.sin(angle)])


def kernel(
    sl_ref, segs_ref, live_ref, bin_ref, frac_ref, inv_ref, half_ref,
    strain_ref, table_ref, templ_ref, start_ref, local_ref, step_ref,
    out_ref, prod_ref, rot_ref, best_ref, *binned,
):
    g = pl.program_id(0)

    @pl.when(g == 0)
    def _():
        for ref in binned:
            ref[...] = jnp.zeros_like(ref)

    sc, ss = start_ref[0, 0], start_ref[0, 1]
    for half in range(2):
        cols = slice(half * 128, half * 128 + 128)
        lc, ls = local_ref[0, :, cols], local_ref[1, :, cols]
        rot_ref[0, :, cols] = sc * lc - ss * ls
        rot_ref[1, :, cols] = sc * ls + ss * lc

    def one_block(jj, slot):
        both = strain_ref[0, jj].astype(jnp.float32)
        raw_r, raw_i = both[:ROWS], both[ROWS:]
        rc, rs = rot_ref[0], rot_ref[1]
        sr = raw_r * rc - raw_i * rs
        si = raw_r * rs + raw_i * rc
        su = sr + si
        pc = jnp.concatenate([step_ref[0], step_ref[0]], axis=1)
        ps = jnp.concatenate([step_ref[1], step_ref[1]], axis=1)
        rot_ref[0] = rc * pc - rs * ps
        rot_ref[1] = rc * ps + rs * pc
        for pair in range(SLOTS // 2):
            real, imag = [], []
            for k in (2 * pair, 2 * pair + 1):
                h = templ_ref[0, jj, k:k + 1, :]
                v = templ_ref[0, jj, SLOTS + k:SLOTS + k + 1, :]
                w = templ_ref[0, jj, 2 * SLOTS + k:2 * SLOTS + k + 1, :]
                k1 = h * su
                real.append(k1 - si * w)
                imag.append(k1 - sr * v)
            rows = slice(2 * ROWS * pair, 2 * ROWS * (pair + 1))
            prod_ref[slot, rows, :FB] = jnp.concatenate(real, axis=0).astype(jnp.bfloat16)
            prod_ref[slot, rows, FB:] = jnp.concatenate(imag, axis=0).astype(jnp.bfloat16)
        weights = jnp.concatenate([table_ref[0, jj, :, TW:], table_ref[0, jj, :, :2 * TW]], axis=0)
        series = jnp.dot(prod_ref[slot], weights, preferred_element_type=jnp.float32)
        j = sl_ref[g] * JS + jj
        for k in range(SLOTS):
            b = bin_ref[k, j]
            binned[k][b] += series[k * ROWS:(k + 1) * ROWS]

    def two_blocks(m, carry):
        one_block(2 * m, 0)
        one_block(2 * m + 1, 1)
        return carry

    lax.fori_loop(0, JS // 2, two_blocks, 0)

    @pl.when(g == NSL - 1)
    def _():
        best = jnp.zeros((SEGS, TW), jnp.float32)
        for k in range(SLOTS):
            total = binned[k][0]
            for b in range(1, NBIN):
                total = total + binned[k][b]
            chi = jnp.zeros((ROWS, TW), jnp.float32)
            for b in range(NBIN):
                gap = binned[k][b] - frac_ref[k, b] * total
                gap = gap * gap
                chi = chi + (gap[:, :TW] + gap[:, TW:]) * inv_ref[k, b]
            power = total * total
            snr2 = (power[:, :TW] + power[:, TW:]) * half_ref[k]
            reduced = chi / (2.0 * NBIN - 2.0)
            cube = (1.0 + reduced * reduced * reduced) * 0.5
            factor = jnp.where(reduced > 1.0, jnp.exp(jnp.log(cube) * (-1.0 / 3.0)), 1.0)
            new2 = snr2 * factor
            net2 = new2[:SEGS] + new2[SEGS:2 * SEGS] + new2[2 * SEGS:]
            best = jnp.where(k < live_ref[0], jnp.maximum(best, net2), best)
        best = jnp.sqrt(best)
        best_ref[...] = jnp.concatenate(
            [jnp.max(best[:, w * WIN:(w + 1) * WIN], axis=1, keepdims=True) for w in range(NWIN)], axis=1
        )
        for p in range(SEGS):
            out_ref[pl.ds(segs_ref[p], 1), :] = best_ref[p:p + 1, :]


def search(sl, segs, live, bin_of, frac, inv, half, strain, templ, start, local, step):
    grid_spec = pltpu.PrefetchScalarGridSpec(
        num_scalar_prefetch=7,
        grid=(NSL,),
        in_specs=[
            pl.BlockSpec((1, JS, 2 * ROWS, FB), lambda g, sl, *_: (g, 0, 0, 0)),
            pl.BlockSpec((1, JS, FB, 3 * TW), lambda g, sl, *_: (sl[g], 0, 0, 0)),
            pl.BlockSpec((1, JS, 3 * SLOTS, FB), lambda g, sl, *_: (sl[g], 0, 0, 0)),
            pl.BlockSpec((1, 2, ROWS, TW), lambda g, sl, *_: (g, 0, 0, 0)),
            pl.BlockSpec((2, ROWS, FB), lambda g, sl, *_: (0, 0, 0)),
            pl.BlockSpec((2, ROWS, TW), lambda g, sl, *_: (0, 0, 0)),
        ],
        out_specs=pl.BlockSpec((SEGS, NWIN), lambda g, sl, *_: (0, 0)),
        scratch_shapes=[
            pltpu.VMEM((2, SLOTS * ROWS, 2 * FB), jnp.bfloat16),
            pltpu.VMEM((2, ROWS, FB), jnp.float32),
            pltpu.VMEM((SEGS, NWIN), jnp.float32),
        ] + [pltpu.VMEM((NBIN, ROWS, 2 * TW), jnp.float32) for _ in range(SLOTS)],
    )
    return pl.pallas_call(
        kernel,
        out_shape=jax.ShapeDtypeStruct((SEGS, NWIN), jnp.float32),
        grid_spec=grid_spec,
        compiler_params=pltpu.CompilerParams(
            dimension_semantics=("arbitrary",), vmem_limit_bytes=40 * 1024 * 1024
        ),
        name="search",
    )(sl, segs, live, bin_of, frac, inv, half, strain, tables(), templ, start, local, step)


def per_device(strain, templates, live_count, chi_edges, shifts):
    segs, slices = arrival_order()
    gathered = gather_strain(strain)

    blocks = jnp.arange(NBLK, dtype=jnp.int32)
    bin_of = jnp.sum((chi_edges[:, :, None] <= blocks[None, None, :]).astype(jnp.int32), axis=1)
    labels = jnp.arange(NBIN, dtype=jnp.int32)
    onehot = (bin_of[:, None, :] == labels[None, :, None]).astype(jnp.float32)
    wide = templates.astype(jnp.float32)
    block_power = jnp.sum(wide * wide, axis=(1, 3))
    sigma2 = jnp.sum(block_power, axis=1) + EPSILON
    in_bins = jnp.sum(onehot * block_power[:, None, :], axis=2)
    frac = (in_bins + EPSILON) / sigma2[:, None]
    inv = 1.0 / (frac * sigma2[:, None])
    half = 1.0 / (2.0 * sigma2)

    real, imag = wide[:, 0], wide[:, 1]
    templ = jnp.concatenate([real, real + imag, real - imag], axis=0)
    templ = jnp.transpose(templ, (1, 0, 2)).reshape(NSL, JS, 3 * SLOTS, FB)

    first = (MARGIN + jnp.take(shifts, segs, axis=0)).T.reshape(ROWS)
    bins = jnp.arange(FB, dtype=jnp.int32)
    local = phase((first[:, None] * bins[None, :] * STRIDE) % NFFT)
    starts = (FLOW // FB + slices * JS) * FB
    start = phase((first[None, :] * starts[:, None]) % NFFT)
    start = jnp.broadcast_to(jnp.transpose(start, (1, 0, 2))[..., None], (NSL, 2, ROWS, TW))
    step = phase(first * FB)
    step = jnp.broadcast_to(step[..., None], (2, ROWS, TW))

    best = search(
        slices, segs, live_count[0], bin_of, frac, inv, half, gathered, templ, start, local, step
    )
    for axis, partner in ((3, near), (2, near), (2, far), (1, lambda y: y ^ 2)):
        best = jnp.maximum(best, swap_with(best, axis, partner))
    return best[:, None, :]


def solution(mesh):
    in_specs = (
        P("dt", None, None, "tmpl", None),
        P(("dt", "tmpl"), None, None, None),
        P("dt", "tmpl"),
        P(("dt", "tmpl"), None),
        P(),
    )
    out_specs = P(None, "dt", None)
    return jax.shard_map(
        per_device, mesh=mesh, in_specs=in_specs, out_specs=out_specs, check_vma=False
    )
```

time: 619 us -> 83.8 us (0.14)
  blocking collectives: 456 us -> 0 us
  loops' own time: 53.5 us -> 0 us
  matrix products: 47.6 us -> 0 us
  other arithmetic: 43.7 us -> 4.63 us
  waiting for transfers between devices: 0 us -> 27.4 us
  Pallas kernels: 0 us -> 22.4 us
  starting transfers between devices: 0 us -> 21.3 us
  local copies, waits for them, and re-layouts: 16.7 us -> 6.63 us
    psum x8 -> x0, blocking collectives: 249 us -> none  [from_root(): return lax.psum(jnp.where(mine, shard, jnp.zeros_like(shard)), axis)]
    all_gather x8 -> x0, blocking collectives: 171 us -> none  [one_round(): strain_blocks = lax.all_gather(arrived, 'tmpl', axis=2, tiled=True)]
    another operation x1 -> x0, loops' own time: 53.5 us -> none  [per_device(): lax.scan(one_round, jnp.int32(0), jnp.arange(rounds, dtype=jnp.int32))]
    dot_general x17 -> x0, matrix products: 47.6 us -> none  [the longest x8 30.9 us: statistic(): jnp.einsum('kbj,dkjt->dkbt', onehot, partial_value, precision=lax.Precisi...]
    pmax x1 -> x0, blocking collectives: 35.7 us -> none  [per_device(): best = lax.pmax(best_local, 'tmpl')]
    ppermute x0 -> x11, waiting for transfers between devices: none -> 27.4 us  [swap_with(): return lax.ppermute(value, AXES, pairs)]
    pallas_call x0 -> x1, Pallas kernels: none -> 22.4 us  [search(): pl.pallas_call(kernel, out_shape=jax.ShapeDtypeStruct((SEGS, NWIN), jnp.f...]
    ppermute x0 -> x11, starting transfers between devices: none -> 21.3 us  [swap_with(): return lax.ppermute(value, AXES, pairs)]
  transfers between devices with their start and end apart: 0 -> 11, of which waited for: 0 -> 10; matrix products, arithmetic and copies ran while one was open for 0% -> 11% of each run, Pallas kernels for 0% -> 0%
where the time goes in v1:
time: 83.8 us; the launch traced here: 83.2 us
  waiting for transfers between devices  27.4 us (33%)
  Pallas kernels  22.4 us (27%)
  starting transfers between devices  21.3 us (25%)
  local copies, waits for them, and re-layouts  6.63 us (8%)
  other arithmetic  4.63 us (6%)
  between operations  0.94 us (1%)
    ppermute x11, waiting for transfers between devices, swap_with(): return lax.ppermute(value, AXES, pairs)  27.4 us
    pallas_call x1, Pallas kernels, search(): pl.pallas_call(kernel, out_shape=jax.ShapeDtypeStruct((SEGS, NWIN), jnp.f...  22.4 us
    ppermute x11, starting transfers between devices, swap_with(): return lax.ppermute(value, AXES, pairs)  21.3 us
    transpose x1, local copies, waits for them, and re-layouts, per_device(): templ = jnp.transpose(templ, (1, 0, 2)).reshape(NSL, JS, 3 * SLOTS, FB)  2.07 us
    convert_element_type x1, other arithmetic, per_device(): wide = templates.astype(jnp.float32)  1.72 us
  transfers between devices with their start and end apart: 11, of which 10 were waited for; matrix products, arithmetic and copies ran while one was open for 11% of the time, Pallas kernels for 0%

profile of v1, /device:TPU:0, one launch (start us, length us, event | category | flops | bytes accessed | tf_op | source)
XLA Modules:
  0.0 83.2 jit_solution(16626170201982001433)
XLA Ops:
  0.0 0.7 copy.34
  0.7 1.6 %collective-permute-start = (bf16[6,6,1,256]{3,0,1,2:T(8,128)(2,1)S(1)}, bf16[6,6,1,256]{3,0,1,2:T(8,128)(2,1)S(1)}, u32[]{:S(2)}, u32[]{:S(2)}) collective-permute-start(bf16[6,6,1,256]{3,0,1,2:T(8,128)(2,1)S(1)} %bitcast.43), channel_id=1, source_target_pairs={{0,32},{1,33},{2,34},{3,35},{4,36},{5,37},{6,38},{7,39},{8,40},{9,... | collective-permute-start | bytes 55304 | tf_op jit(solution)/shard_map/ppermute | solution.py:57
  2.4 0.8 copy.39
  3.1 0.6 gather_fusion
  3.7 0.1 fusion.13
  3.8 0.1 copy.40
  3.9 0.1 mul.202
  4.0 0.2 fusion.6
  4.2 0.3 collective-permute-done
  4.6 2.9 %collective-permute-start.1 = (bf16[6,6,2,256]{3,0,1,2:T(8,128)(2,1)S(1)}, bf16[6,6,2,256]{3,0,1,2:T(8,128)(2,1)S(1)}, u32[]{:S(2)}, u32[]{:S(2)}) collective-permute-start(bf16[6,6,2,256]{3,0,1,2:T(8,128)(2,1)S(1)} %pad_maximum_fusion.6), channel_id=1, source_target_pairs={{0,96},{1,97},{2,98},{3,99},{4,100},{5,101},{6,102},{7,103},{8,104... | collective-permute-start | bytes 110600 | tf_op jit(solution)/shard_map/ppermute | solution.py:57
  7.5 0.1 fusion.11
  7.6 2.3 %collective-permute-done.1 = bf16[6,6,2,256]{3,0,1,2:T(8,128)(2,1)S(1)} collective-permute-done((bf16[6,6,2,256]{3,0,1,2:T(8,128)(2,1)S(1)}, bf16[6,6,2,256]{3,0,1,2:T(8,128)(2,1)S(1)}, u32[]{:S(2)}, u32[]{:S(2)}) %collective-permute-start.1) | collective-permute-done | bytes 36896 | tf_op jit(solution)/shard_map/ppermute | solution.py:57
  10.0 1.7 %collective-permute-start.2 = (bf16[6,6,4,256]{3,0,1,2:T(8,128)(2,1)S(1)}, bf16[6,6,4,256]{3,0,1,2:T(8,128)(2,1)S(1)}, u32[]{:S(2)}, u32[]{:S(2)}) collective-permute-start(bf16[6,6,4,256]{3,0,1,2:T(8,128)(2,1)S(1)} %pad_maximum_fusion.5), channel_id=1, source_target_pairs={{0,16},{1,17},{2,18},{3,19},{4,20},{5,21},{6,22},{7,23},{8,24},{9,... | collective-permute-start | bytes 221192 | tf_op jit(solution)/shard_map/ppermute | solution.py:57
  11.8 2.9 %collective-permute-done.2 = bf16[6,6,4,256]{3,0,1,2:T(8,128)(2,1)S(1)} collective-permute-done((bf16[6,6,4,256]{3,0,1,2:T(8,128)(2,1)S(1)}, bf16[6,6,4,256]{3,0,1,2:T(8,128)(2,1)S(1)}, u32[]{:S(2)}, u32[]{:S(2)}) %collective-permute-start.2) | collective-permute-done | bytes 73760 | tf_op jit(solution)/shard_map/ppermute | solution.py:57
  14.7 3.2 %collective-permute-start.3 = (bf16[1,6,6,8,256]{4,1,2,3,0:T(8,128)(2,1)S(1)}, bf16[1,6,6,8,256]{4,1,2,3,0:T(8,128)(2,1)S(1)}, u32[]{:S(2)}, u32[]{:S(2)}) collective-permute-start(bf16[1,6,6,8,256]{4,1,2,3,0:T(8,128)(2,1)S(1)} %get-tuple-element.21), channel_id=1, source_target_pairs={{0,24},{1,25},{2,26},{3,27},{4,28},{5,29},{6,30},{7,31},{8,16},{9,... | collective-permute-start | bytes 442376 | tf_op jit(solution)/shard_map/ppermute | solution.py:57
  18.0 3.7 %collective-permute-done.3 = bf16[1,6,6,8,256]{4,1,2,3,0:T(8,128)(2,1)S(1)} collective-permute-done((bf16[1,6,6,8,256]{4,1,2,3,0:T(8,128)(2,1)S(1)}, bf16[1,6,6,8,256]{4,1,2,3,0:T(8,128)(2,1)S(1)}, u32[]{:S(2)}, u32[]{:S(2)}) %collective-permute-start.3) | collective-permute-done | bytes 147488 | tf_op jit(solution)/shard_map/ppermute | solution.py:57
  21.9 2.1 %collective-permute-start.4 = (bf16[2,6,48,256]{3,2,1,0:T(8,128)(2,1)S(1)}, bf16[2,6,48,256]{3,2,1,0:T(8,128)(2,1)S(1)}, u32[]{:S(2)}, u32[]{:S(2)}) collective-permute-start(bf16[2,6,48,256]{3,2,1,0:T(8,128)(2,1)S(1)} %pad_maximum_fusion.2), channel_id=1, source_target_pairs={{0,2},{1,3},{2,0},{3,1},{4,6},{5,7},{6,4},{7,5},{8,10},{9,11},{10,... | collective-permute-start | bytes 884744 | tf_op jit(solution)/shard_map/ppermute | solution.py:57
  23.9 1.7 %convert_element_type.51 = f32[12,2,96,256]{3,2,1,0:T(8,128)} convert(bf16[12,2,96,256]{3,2,1,0:T(8,128)(2,1)S(1)} %copy-done.1) | non-fusion elementwise | flops 589824 | bytes 3538944 | tf_op jit(solution)/shard_map/convert_element_type | solution.py:228
  25.7 0.1 copy.43
  25.7 0.1 sin.36
  25.8 0.1 copy.42
  25.9 0.1 cos.36
  26.0 1.5 %slice_bitcast_fusion.1 = f32[12,96,256]{2,1,0:T(8,128)S(1)} fusion(f32[12,2,96,256]{3,2,1,0:T(8,128)} %convert_element_type.51), kind=kLoop, calls=%fused_computation.5 | loop fusion | bytes 2359296 | tf_op jit(solution)/shard_map/squeeze | solution.py:236
  27.5 1.2 %collective-permute-done.4 = bf16[2,6,48,256]{3,2,1,0:T(8,128)(2,1)S(1)} collective-permute-done((bf16[2,6,48,256]{3,2,1,0:T(8,128)(2,1)S(1)}, bf16[2,6,48,256]{3,2,1,0:T(8,128)(2,1)S(1)}, u32[]{:S(2)}, u32[]{:S(2)}) %collective-permute-start.4) | collective-permute-done | bytes 294944 | tf_op jit(solution)/shard_map/ppermute | solution.py:57
  28.7 0.1 pad_maximum_fusion.1
  28.7 4.2 %collective-permute-start.5 = (bf16[4,6,48,256]{3,2,1,0:T(8,128)(2,1)S(1)}, bf16[4,6,48,256]{3,2,1,0:T(8,128)(2,1)S(1)}, u32[]{:S(2)}, u32[]{:S(2)}) collective-permute-start(bf16[4,6,48,256]{3,2,1,0:T(8,128)(2,1)S(1)} %pad_maximum_fusion.1), channel_id=1, source_target_pairs={{0,6},{1,7},{2,4},{3,5},{4,2},{5,3},{6,0},{7,1},{8,14},{9,15},{10,... | collective-permute-start | bytes 1769480 | tf_op jit(solution)/shard_map/ppermute | solution.py:57
  32.9 0.2 fusion.1
  33.2 0.4 maximum_bitcast_fusion
  33.5 7.5 %collective-permute-done.5 = bf16[4,6,48,256]{3,2,1,0:T(8,128)(2,1)S(1)} collective-permute-done((bf16[4,6,48,256]{3,2,1,0:T(8,128)(2,1)S(1)}, bf16[4,6,48,256]{3,2,1,0:T(8,128)(2,1)S(1)}, u32[]{:S(2)}, u32[]{:S(2)}) %collective-permute-start.5) | collective-permute-done | bytes 589856 | tf_op jit(solution)/shard_map/ppermute | solution.py:57
  41.0 0.1 pad_maximum_fusion
  41.1 0.1 collective-permute-start.6
  41.9 2.1 %copy.38 = f32[96,36,256]{2,1,0:T(8,128)S(1)} copy(f32[96,36,256]{2,0,1:T(8,128)S(1)} %maximum_bitcast_fusion) | data formatting | bytes 7077888 | tf_op jit(solution)/shard_map/transpose | solution.py:238
  44.0 0.1 convert_reduce_fusion.bin_ref
  44.2 0.6 multiply_reduce_fusion
  44.7 0.1 select_reduce_fusion
  44.8 0.1 multiply_divide_fusion
  45.0 0.1 constant_dynamic-update-slice_fusion.strain_ref
  45.1 0.2 broadcast_in_dim.61.start_ref
  45.2 0.1 broadcast_in_dim.62.step_ref
  45.3 22.4 %search.1 = f32[8,8]{1,0:T(8,128)S(1)} custom-call(s32[16]{0:T(128)S(1)} %get-tuple-element.12.sl_ref, s32[8]{0:T(128)S(1)} %get-tuple-element.10.segs_ref, s32[1]{0:T(128)} %bitcast.41.live_ref, s32[12,96]{1,0:T(8,128)S(1)} %convert_reduce_fusion.bin_ref, f32[12,16]{1,0:T(8,128)S(1)} %get-tuple-element.24.frac_ref, f32[12,16]{1,0:T(8,128)S(1)} %get-tuple-element.23.inv_ref, ...), custom_call_target="tpu_custom_call" | custom-call | tf_op jit(solution)/shard_map/search/pallas_call | solution.py:209
  67.7 0.6 collective-permute-start.7
  68.2 0.8 collective-permute-done.7
  69.1 3.6 %collective-permute-done.8 = f32[8,8]{1,0:T(8,128)S(1)} collective-permute-done((f32[8,8]{1,0:T(8,128)S(1)}, f32[8,8]{1,0:T(8,128)S(1)}, u32[]{:S(2)}, u32[]{:S(2)}) %collective-permute-start.8) | collective-permute-done | bytes 288 | tf_op jit(solution)/shard_map/ppermute | solution.py:57
  72.7 3.0 %collective-permute-start.9 = (f32[8,8]{1,0:T(8,128)S(1)}, f32[8,8]{1,0:T(8,128)S(1)}, u32[]{:S(2)}, u32[]{:S(2)}) collective-permute-start(f32[8,8]{1,0:T(8,128)S(1)} %max.13), channel_id=1, source_target_pairs={{0,6},{1,7},{2,4},{3,5},{4,2},{5,3},{6,0},{7,1},{8,14},{9,15},{10,... | collective-permute-start | bytes 776 | tf_op jit(solution)/shard_map/ppermute | solution.py:57
  75.7 1.8 %collective-permute-done.9 = f32[8,8]{1,0:T(8,128)S(1)} collective-permute-done((f32[8,8]{1,0:T(8,128)S(1)}, f32[8,8]{1,0:T(8,128)S(1)}, u32[]{:S(2)}, u32[]{:S(2)}) %collective-permute-start.9) | collective-permute-done | bytes 288 | tf_op jit(solution)/shard_map/ppermute | solution.py:57
  77.5 1.9 %collective-permute-start.10 = (f32[8,8]{1,0:T(8,128)S(1)}, f32[8,8]{1,0:T(8,128)S(1)}, u32[]{:S(2)}, u32[]{:S(2)}) collective-permute-start(f32[8,8]{1,0:T(8,128)S(1)} %max.14), channel_id=1, source_target_pairs={{0,8},{1,9},{2,10},{3,11},{4,12},{5,13},{6,14},{7,15},{8,0},{9,1},... | collective-permute-start | bytes 776 | tf_op jit(solution)/shard_map/ppermute | solution.py:57
  79.4 3.2 %collective-permute-done.10 = f32[8,8]{1,0:T(8,128)S(1)} collective-permute-done((f32[8,8]{1,0:T(8,128)S(1)}, f32[8,8]{1,0:T(8,128)S(1)}, u32[]{:S(2)}, u32[]{:S(2)}) %collective-permute-start.10) | collective-permute-done | bytes 288 | tf_op jit(solution)/shard_map/ppermute | solution.py:57
  82.6 0.6 max.15
  (33 shorter events, 0.5 us)
Async XLA Ops:
  0.7 3.8 %collective-permute-start = (bf16[6,6,1,256]{3,0,1,2:T(8,128)(2,1)S(1)}, bf16[6,6,1,256]{3,0,1,2:T(8,128)(2,1)S(1)}, u32[]{:S(2)}, u32[]{:S(2)}) collective-permute-start(bf16[6,6,1,256]{3,0,1,2:T(8,128)(2,1)S(1)} %bitcast.43), channel_id=1, source_target_pairs={{0,32},{1,33},{2,34},{3,35},{4,36},{5,37},{6,38},{7,39},{8,40},{9,... | collective-permute-start | bytes 55304 | tf_op jit(solution)/shard_map/ppermute | solution.py:57
  4.2 19.8 %copy-start.1 = (bf16[12,2,96,256]{3,2,1,0:T(8,128)(2,1)S(1)}, bf16[12,2,96,256]{3,2,1,0:T(8,128)(2,1)}, u32[]{:S(2)}) copy-start(bf16[12,2,96,256]{3,2,1,0:T(8,128)(2,1)} %param.7) | copy-start | bytes 3538948
  4.6 5.4 %collective-permute-start.1 = (bf16[6,6,2,256]{3,0,1,2:T(8,128)(2,1)S(1)}, bf16[6,6,2,256]{3,0,1,2:T(8,128)(2,1)S(1)}, u32[]{:S(2)}, u32[]{:S(2)}) collective-permute-start(bf16[6,6,2,256]{3,0,1,2:T(8,128)(2,1)S(1)} %pad_maximum_fusion.6), channel_id=1, source_target_pairs={{0,96},{1,97},{2,98},{3,99},{4,100},{5,101},{6,102},{7,103},{8,104... | collective-permute-start | bytes 110600 | tf_op jit(solution)/shard_map/ppermute | solution.py:57
  10.0 4.7 %collective-permute-start.2 = (bf16[6,6,4,256]{3,0,1,2:T(8,128)(2,1)S(1)}, bf16[6,6,4,256]{3,0,1,2:T(8,128)(2,1)S(1)}, u32[]{:S(2)}, u32[]{:S(2)}) collective-permute-start(bf16[6,6,4,256]{3,0,1,2:T(8,128)(2,1)S(1)} %pad_maximum_fusion.5), channel_id=1, source_target_pairs={{0,16},{1,17},{2,18},{3,19},{4,20},{5,21},{6,22},{7,23},{8,24},{9,... | collective-permute-start | bytes 221192 | tf_op jit(solution)/shard_map/ppermute | solution.py:57
  14.7 7.0 %collective-permute-start.3 = (bf16[1,6,6,8,256]{4,1,2,3,0:T(8,128)(2,1)S(1)}, bf16[1,6,6,8,256]{4,1,2,3,0:T(8,128)(2,1)S(1)}, u32[]{:S(2)}, u32[]{:S(2)}) collective-permute-start(bf16[1,6,6,8,256]{4,1,2,3,0:T(8,128)(2,1)S(1)} %get-tuple-element.21), channel_id=1, source_target_pairs={{0,24},{1,25},{2,26},{3,27},{4,28},{5,29},{6,30},{7,31},{8,16},{9,... | collective-permute-start | bytes 442376 | tf_op jit(solution)/shard_map/ppermute | solution.py:57
  21.9 6.8 %collective-permute-start.4 = (bf16[2,6,48,256]{3,2,1,0:T(8,128)(2,1)S(1)}, bf16[2,6,48,256]{3,2,1,0:T(8,128)(2,1)S(1)}, u32[]{:S(2)}, u32[]{:S(2)}) collective-permute-start(bf16[2,6,48,256]{3,2,1,0:T(8,128)(2,1)S(1)} %pad_maximum_fusion.2), channel_id=1, source_target_pairs={{0,2},{1,3},{2,0},{3,1},{4,6},{5,7},{6,4},{7,5},{8,10},{9,11},{10,... | collective-permute-start | bytes 884744 | tf_op jit(solution)/shard_map/ppermute | solution.py:57
  26.0 6.9 %copy-start = (f32[12,2,96,256]{3,2,1,0:T(8,128)S(1)}, f32[12,2,96,256]{3,2,1,0:T(8,128)}, u32[]{:S(2)}) copy-start(f32[12,2,96,256]{3,2,1,0:T(8,128)} %convert_element_type.51) | copy-start | bytes 7077892
  28.7 12.3 %collective-permute-start.5 = (bf16[4,6,48,256]{3,2,1,0:T(8,128)(2,1)S(1)}, bf16[4,6,48,256]{3,2,1,0:T(8,128)(2,1)S(1)}, u32[]{:S(2)}, u32[]{:S(2)}) collective-permute-start(bf16[4,6,48,256]{3,2,1,0:T(8,128)(2,1)S(1)} %pad_maximum_fusion.1), channel_id=1, source_target_pairs={{0,6},{1,7},{2,4},{3,5},{4,2},{5,3},{6,0},{7,1},{8,14},{9,15},{10,... | collective-permute-start | bytes 1769480 | tf_op jit(solution)/shard_map/ppermute | solution.py:57
  41.1 3.8 %collective-permute-start.6 = (bf16[8,6,48,256]{3,2,1,0:T(8,128)(2,1)S(1)}, bf16[8,6,48,256]{3,2,1,0:T(8,128)(2,1)S(1)}, u32[]{:S(2)}, u32[]{:S(2)}) collective-permute-start(bf16[8,6,48,256]{3,2,1,0:T(8,128)(2,1)S(1)} %pad_maximum_fusion), channel_id=1, source_target_pairs={{0,1},{1,0},{2,3},{3,2},{4,5},{5,4},{6,7},{7,6},{8,9},{9,8},{10,11... | collective-permute-start | bytes 3538952 | tf_op jit(solution)/shard_map/ppermute | solution.py:57
  41.9 2.1 %copy-start.3 = (s32[12,15]{1,0:T(8,128)S(1)}, s32[12,15]{1,0:T(8,128)}, u32[]{:S(2)}) copy-start(s32[12,15]{1,0:T(8,128)} %param.9) | copy-start | bytes 2164
  41.9 2.2 %copy-start.2 = (bf16[12,2,96,256]{3,2,1,0:T(8,128)(2,1)S(1)}, bf16[12,2,96,256]{3,2,1,0:T(8,128)(2,1)}, u32[]{:S(2)}) copy-start(bf16[12,2,96,256]{3,2,1,0:T(8,128)(2,1)} %param.7) | copy-start | bytes 3538948
  67.7 1.4 %collective-permute-start.7 = (f32[8,8]{1,0:T(8,128)S(1)}, f32[8,8]{1,0:T(8,128)S(1)}, u32[]{:S(2)}, u32[]{:S(2)}) collective-permute-start(f32[8,8]{1,0:T(8,128)S(1)} %search.1), channel_id=1, source_target_pairs={{0,1},{1,0},{2,3},{3,2},{4,5},{5,4},{6,7},{7,6},{8,9},{9,8},{10,11... | collective-permute-start | bytes 776 | tf_op jit(solution)/shard_map/ppermute | solution.py:57
  69.1 3.6 %collective-permute-start.8 = (f32[8,8]{1,0:T(8,128)S(1)}, f32[8,8]{1,0:T(8,128)S(1)}, u32[]{:S(2)}, u32[]{:S(2)}) collective-permute-start(f32[8,8]{1,0:T(8,128)S(1)} %max.12), channel_id=1, source_target_pairs={{0,2},{1,3},{2,0},{3,1},{4,6},{5,7},{6,4},{7,5},{8,10},{9,11},{10,... | collective-permute-start | bytes 776 | tf_op jit(solution)/shard_map/ppermute | solution.py:57
  72.7 4.8 %collective-permute-start.9 = (f32[8,8]{1,0:T(8,128)S(1)}, f32[8,8]{1,0:T(8,128)S(1)}, u32[]{:S(2)}, u32[]{:S(2)}) collective-permute-start(f32[8,8]{1,0:T(8,128)S(1)} %max.13), channel_id=1, source_target_pairs={{0,6},{1,7},{2,4},{3,5},{4,2},{5,3},{6,0},{7,1},{8,14},{9,15},{10,... | collective-permute-start | bytes 776 | tf_op jit(solution)/shard_map/ppermute | solution.py:57
  77.5 5.1 %collective-permute-start.10 = (f32[8,8]{1,0:T(8,128)S(1)}, f32[8,8]{1,0:T(8,128)S(1)}, u32[]{:S(2)}, u32[]{:S(2)}) collective-permute-start(f32[8,8]{1,0:T(8,128)S(1)} %max.14), channel_id=1, source_target_pairs={{0,8},{1,9},{2,10},{3,11},{4,12},{5,13},{6,14},{7,15},{8,0},{9,1},... | collective-permute-start | bytes 776 | tf_op jit(solution)/shard_map/ppermute | solution.py:57

commit v2 on v1

--- a/solution.py
+++ b/solution.py
@@ -48,37 +48,73 @@
     return 3 - a
 
 
-def swap_with(value, axis, partner):
-    pairs = []
-    for index in range(128):
-        place = list(place_of(index))
-        place[axis] = partner(place[axis])
-        pairs.append((index, index_of(*place)))
+def swap_with(value, move):
+    pairs = [(index, index_of(*move(*place_of(index)))) for index in range(128)]
     return lax.ppermute(value, AXES, pairs)
 
 
+def x_near(x, y, z, core):
+    return (near(x), y, z, core)
+
+
+def x_far(x, y, z, core):
+    return (far(x), y, z, core)
+
+
+def y_near(x, y, z, core):
+    return (x, near(y), z, core)
+
+
+def y_far(x, y, z, core):
+    return (x, far(y), z, core)
+
+
+def z_near(x, y, z, core):
+    return (x, y, near(z), core)
+
+
+def z_far(x, y, z, core):
+    return (x, y, far(z), core)
+
+
+def y_across(x, y, z, core):
+    return (x, y ^ 2, z, core)
+
+
+def other_core(x, y, z, core):
+    return (x, y, z, core ^ 1)
+
+
+def by_core(first, second):
+    return lambda x, y, z, core: (second if core else first)(x, y, z, core)
+
+
 def tables():
-    n = FLOW + np.arange(NBLK * FB, dtype=np.int64)
     tau = np.arange(TW, dtype=np.int64)
-    turns = (n[:, None] * tau[None, :] * STRIDE) % NFFT
-    angle = turns.astype(np.float64) * (TWO_PI / NFFT)
+    bins = np.arange(FB, dtype=np.int64)
+    angle = ((bins[:, None] * tau[None, :] * STRIDE) % NFFT).astype(np.float64) * (TWO_PI / NFFT)
     cosine, sine = np.cos(angle), np.sin(angle)
-    whole = np.concatenate([-sine, cosine, sine], axis=1).astype(ml_dtypes.bfloat16)
-    return whole.reshape(NSL, JS, FB, 3 * TW)
+    local = np.block([[cosine, sine], [-sine, cosine]]).astype(ml_dtypes.bfloat16)
+    base = FLOW + np.arange(NBLK, dtype=np.int64) * FB
+    angle = ((base[:, None] * tau[None, :] * STRIDE) % NFFT).astype(np.float64) * (TWO_PI / NFFT)
+    turn = np.stack([np.cos(angle), np.sin(angle)], axis=1).astype(np.float32)
+    return local, turn.reshape(NSL, JS, 2, TW)
 
 
 def gather_strain(shard):
+    core = lax.axis_index("tmpl") % 2
     x = jnp.transpose(shard[0], (2, 1, 0, 3)).reshape(JS, 2 * NDET, 1, FB)
-    for axis, partner in ((0, near), (0, far), (1, near)):
-        x = jnp.concatenate([x, swap_with(x, axis, partner)], axis=2)
+    for move in (x_near, x_far, y_near):
+        x = jnp.concatenate([x, swap_with(x, move)], axis=2)
     x = x[None]
-    y = swap_with(x, 1, far)
-    y = jnp.concatenate([y[:, :, :, 4:], y[:, :, :, :4]], axis=3)
-    x = jnp.concatenate([x, y], axis=0)
-    x = x.reshape(2, JS, 2 * ROWS, FB)
-    for axis, partner in ((2, near), (2, far), (3, near)):
-        x = jnp.concatenate([x, swap_with(x, axis, partner)], axis=0)
-    return x
+    for moves, turned in (((y_far, z_near), 0), ((z_near, z_far), None), ((z_far, y_far), 1)):
+        y = swap_with(x, by_core(*moves))
+        if turned is not None:
+            other = jnp.concatenate([y[:, :, :, 4:], y[:, :, :, :4]], axis=3)
+            y = jnp.where(core == turned, other, y)
+        x = jnp.concatenate([x, y], axis=0)
+    x = x.reshape(NSL // 2, JS, 2 * ROWS, FB)
+    return jnp.concatenate([x, swap_with(x, other_core)], axis=0)
 
 
 def arrival_order():
@@ -94,8 +130,11 @@
         return a ^ first
 
     segs = ring(x, p % 2, p // 2 % 2) * 2 + (y_lo ^ (p // 4))
-    slices = (y_hi ^ (q % 2)) * 8 + ring(z, q // 2 % 2, q // 4 % 2) * 2 + (core ^ (q // 8))
-    return segs, slices
+    bits = (q % 2, q // 2 % 2, q // 4 % 2)
+    from_core = core ^ (q // 8)
+    even = (y_hi ^ bits[0]) * 8 + ring(z, bits[1], bits[2]) * 2
+    odd = (y_hi ^ bits[2]) * 8 + ring(z, bits[0], bits[1]) * 2 + 1
+    return segs, jnp.where(from_core == 0, even, odd)
 
 
 def phase(turns):
@@ -105,7 +144,7 @@
 
 def kernel(
     sl_ref, segs_ref, live_ref, bin_ref, frac_ref, inv_ref, half_ref,
-    strain_ref, table_ref, templ_ref, start_ref, local_ref, step_ref,
+    strain_ref, table_ref, turn_ref, templ_ref, start_ref, local_ref, step_ref,
     out_ref, prod_ref, rot_ref, best_ref, *binned,
 ):
     g = pl.program_id(0)
@@ -122,7 +161,7 @@
         rot_ref[0, :, cols] = sc * lc - ss * ls
         rot_ref[1, :, cols] = sc * ls + ss * lc
 
-    def one_block(jj, slot):
+    def product(jj):
         both = strain_ref[0, jj].astype(jnp.float32)
         raw_r, raw_i = both[:ROWS], both[ROWS:]
         rc, rs = rot_ref[0], rot_ref[1]
@@ -142,22 +181,28 @@
                 k1 = h * su
                 real.append(k1 - si * w)
                 imag.append(k1 - sr * v)
-            rows = slice(2 * ROWS * pair, 2 * ROWS * (pair + 1))
-            prod_ref[slot, rows, :FB] = jnp.concatenate(real, axis=0).astype(jnp.bfloat16)
-            prod_ref[slot, rows, FB:] = jnp.concatenate(imag, axis=0).astype(jnp.bfloat16)
-        weights = jnp.concatenate([table_ref[0, jj, :, TW:], table_ref[0, jj, :, :2 * TW]], axis=0)
-        series = jnp.dot(prod_ref[slot], weights, preferred_element_type=jnp.float32)
+            rows = slice(jj * SLOTS * ROWS + 2 * ROWS * pair, jj * SLOTS * ROWS + 2 * ROWS * (pair + 1))
+            prod_ref[rows, :FB] = jnp.concatenate(real, axis=0).astype(jnp.bfloat16)
+            prod_ref[rows, FB:] = jnp.concatenate(imag, axis=0).astype(jnp.bfloat16)
+
+    def post(jj, series):
         j = sl_ref[g] * JS + jj
+        c = turn_ref[0, jj, 0:1, :]
+        s = turn_ref[0, jj, 1:2, :]
         for k in range(SLOTS):
             b = bin_ref[k, j]
-            binned[k][b] += series[k * ROWS:(k + 1) * ROWS]
-
-    def two_blocks(m, carry):
-        one_block(2 * m, 0)
-        one_block(2 * m + 1, 1)
-        return carry
-
-    lax.fori_loop(0, JS // 2, two_blocks, 0)
+            re = series[k * ROWS:(k + 1) * ROWS, :TW]
+            im = series[k * ROWS:(k + 1) * ROWS, TW:]
+            binned[k][b, :, :TW] += c * re - s * im
+            binned[k][b, :, TW:] += c * im + s * re
+
+    half = JS // 2 * SLOTS * ROWS
+    for jj in range(JS):
+        product(jj)
+    for h in range(2):
+        series = jnp.dot(prod_ref[h * half:(h + 1) * half], table_ref[...], preferred_element_type=jnp.float32)
+        for m in range(JS // 2):
+            post(h * (JS // 2) + m, series[m * SLOTS * ROWS:(m + 1) * SLOTS * ROWS])
 
     @pl.when(g == NSL - 1)
     def _():
@@ -193,7 +238,8 @@
         grid=(NSL,),
         in_specs=[
             pl.BlockSpec((1, JS, 2 * ROWS, FB), lambda g, sl, *_: (g, 0, 0, 0)),
-            pl.BlockSpec((1, JS, FB, 3 * TW), lambda g, sl, *_: (sl[g], 0, 0, 0)),
+            pl.BlockSpec((2 * FB, 2 * TW), lambda g, sl, *_: (0, 0)),
+            pl.BlockSpec((1, JS, 2, TW), lambda g, sl, *_: (sl[g], 0, 0, 0)),
             pl.BlockSpec((1, JS, 3 * SLOTS, FB), lambda g, sl, *_: (sl[g], 0, 0, 0)),
             pl.BlockSpec((1, 2, ROWS, TW), lambda g, sl, *_: (g, 0, 0, 0)),
             pl.BlockSpec((2, ROWS, FB), lambda g, sl, *_: (0, 0, 0)),
@@ -201,7 +247,7 @@
         ],
         out_specs=pl.BlockSpec((SEGS, NWIN), lambda g, sl, *_: (0, 0)),
         scratch_shapes=[
-            pltpu.VMEM((2, SLOTS * ROWS, 2 * FB), jnp.bfloat16),
+            pltpu.VMEM((JS * SLOTS * ROWS, 2 * FB), jnp.bfloat16),
             pltpu.VMEM((2, ROWS, FB), jnp.float32),
             pltpu.VMEM((SEGS, NWIN), jnp.float32),
         ] + [pltpu.VMEM((NBIN, ROWS, 2 * TW), jnp.float32) for _ in range(SLOTS)],
@@ -214,7 +260,7 @@
             dimension_semantics=("arbitrary",), vmem_limit_bytes=40 * 1024 * 1024
         ),
         name="search",
-    )(sl, segs, live, bin_of, frac, inv, half, strain, tables(), templ, start, local, step)
+    )(sl, segs, live, bin_of, frac, inv, half, strain, *tables(), templ, start, local, step)
 
 
 def per_device(strain, templates, live_count, chi_edges, shifts):
@@ -249,8 +295,8 @@
     best = search(
         slices, segs, live_count[0], bin_of, frac, inv, half, gathered, templ, start, local, step
     )
-    for axis, partner in ((3, near), (2, near), (2, far), (1, lambda y: y ^ 2)):
-        best = jnp.maximum(best, swap_with(best, axis, partner))
+    for move in (other_core, z_near, z_far, y_across):
+        best = jnp.maximum(best, swap_with(best, move))
     return best[:, None, :]
 
 

time: 83.8 us -> 87.1 us (1.039)
  other arithmetic: 4.63 us -> 11.5 us
  Pallas kernels: 22.4 us -> 15.9 us
  waiting for transfers between devices: 27.4 us -> 30.6 us
  starting transfers between devices: 21.3 us -> 18.7 us
  local copies, waits for them, and re-layouts: 6.63 us -> 9.14 us
    pallas_call x1, Pallas kernels: 22.4 us -> 15.9 us  [search(): pl.pallas_call(kernel, out_shape=jax.ShapeDtypeStruct((SEGS, NWIN), jnp.f...]
    ppermute x11, waiting for transfers between devices: 27.4 us -> 30.6 us  [swap_with(): return lax.ppermute(value, AXES, pairs)]
    ppermute x11, starting transfers between devices: 21.3 us -> 18.7 us  [swap_with(): return lax.ppermute(value, AXES, pairs)]
    concatenate x1 -> x3, other arithmetic: 0.03 us -> 2.25 us  [gather_strain(): x = jnp.concatenate([x, y], axis=0)]
    transpose x1, local copies, waits for them, and re-layouts: 2.07 us -> 3.94 us  [per_device(): templ = jnp.transpose(templ, (1, 0, 2)).reshape(NSL, JS, 3 * SLOTS, FB)]
    transpose x1, other arithmetic: 0.37 us -> 2.21 us  [per_device(): templ = jnp.transpose(templ, (1, 0, 2)).reshape(NSL, JS, 3 * SLOTS, FB)]
    add x1, other arithmetic: 0.22 us -> 1.62 us  [per_device(): templ = jnp.concatenate([real, real + imag, real - imag], axis=0)]
    slice x1 -> x2, local copies, waits for them, and re-layouts: 0.01 us -> 1.19 us  [gather_strain(): other = jnp.concatenate([y[:, :, :, 4:], y[:, :, :, :4]], axis=3)]
  transfers between devices with their start and end apart: 11 -> 11, of which waited for: 10 -> 9; matrix products, arithmetic and copies ran while one was open for 11% -> 16% of each run, Pallas kernels for 0% -> 0%
where the time goes in v2:
time: 87.1 us; the launch traced here: 86.8 us
  waiting for transfers between devices  30.6 us (35%)
  starting transfers between devices  18.7 us (21%)
  Pallas kernels  15.9 us (18%)
  other arithmetic  11.5 us (13%)
  local copies, waits for them, and re-layouts  9.14 us (10%)
  between operations  1 us (1%)
    ppermute x11, waiting for transfers between devices, swap_with(): return lax.ppermute(value, AXES, pairs)  30.6 us
    ppermute x11, starting transfers between devices, swap_with(): return lax.ppermute(value, AXES, pairs)  18.7 us
    pallas_call x1, Pallas kernels, search(): pl.pallas_call(kernel, out_shape=jax.ShapeDtypeStruct((SEGS, NWIN), jnp.f...  15.9 us
    transpose x1, local copies, waits for them, and re-layouts, per_device(): templ = jnp.transpose(templ, (1, 0, 2)).reshape(NSL, JS, 3 * SLOTS, FB)  3.94 us
    concatenate x3, other arithmetic, gather_strain(): x = jnp.concatenate([x, y], axis=0)  2.25 us
    transpose x1, other arithmetic, per_device(): templ = jnp.transpose(templ, (1, 0, 2)).reshape(NSL, JS, 3 * SLOTS, FB)  2.21 us
  transfers between devices with their start and end apart: 11, of which 9 were waited for; matrix products, arithmetic and copies ran while one was open for 16% of the time, Pallas kernels for 0%

profile of v2, /device:TPU:0, one launch (start us, length us, event | category | flops | bytes accessed | tf_op | source)
XLA Modules:
  0.0 86.8 jit_solution(4764653442524338138)
XLA Ops:
  0.0 0.7 copy.51
  0.7 1.6 %collective-permute-start = (bf16[6,6,1,256]{3,0,1,2:T(8,128)(2,1)S(1)}, bf16[6,6,1,256]{3,0,1,2:T(8,128)(2,1)S(1)}, u32[]{:S(2)}, u32[]{:S(2)}) collective-permute-start(bf16[6,6,1,256]{3,0,1,2:T(8,128)(2,1)S(1)} %bitcast.49), channel_id=1, source_target_pairs={{0,32},{1,33},{2,34},{3,35},{4,36},{5,37},{6,38},{7,39},{8,40},{9,... | collective-permute-start | bytes 55304 | tf_op jit(solution)/shard_map/ppermute | solution.py:53
  2.3 1.5 %convert_element_type.51 = f32[12,2,96,256]{3,2,1,0:T(8,128)S(1)} convert(bf16[12,2,96,256]{3,2,1,0:T(8,128)(2,1)} %param.8) | non-fusion elementwise | flops 589824 | bytes 3538944 | tf_op jit(solution)/shard_map/convert_element_type | solution.py:274
  3.8 1.6 %fusion.1 = (f32[12,96,256]{2,1,0:T(8,128)}, f32[12,96,256]{2,1,0:T(8,128)}) fusion(f32[12,2,96,256]{3,2,1,0:T(8,128)S(1)} %convert_element_type.51), kind=kLoop, calls=%fused_computation.8 | loop fusion | flops 589824 | bytes 4718592 | tf_op jit(solution)/shard_map/add | solution.py:283
  5.5 1.1 %slice_bitcast_fusion.1 = f32[12,96,256]{2,1,0:T(8,128)} fusion(f32[12,2,96,256]{3,2,1,0:T(8,128)S(1)} %convert_element_type.51), kind=kLoop, calls=%fused_computation.5 | loop fusion | bytes 2359296 | tf_op jit(solution)/shard_map/squeeze | solution.py:282
  6.7 0.6 gather_fusion
  7.3 0.1 fusion.14
  7.4 2.2 %collective-permute-start.1 = (bf16[6,6,2,256]{3,0,1,2:T(8,128)(2,1)S(1)}, bf16[6,6,2,256]{3,0,1,2:T(8,128)(2,1)S(1)}, u32[]{:S(2)}, u32[]{:S(2)}) collective-permute-start(bf16[6,6,2,256]{3,0,1,2:T(8,128)(2,1)S(1)} %pad_maximum_fusion.5), channel_id=1, source_target_pairs={{0,96},{1,97},{2,98},{3,99},{4,100},{5,101},{6,102},{7,103},{8,104... | collective-permute-start | bytes 110600 | tf_op jit(solution)/shard_map/ppermute | solution.py:53
  9.7 0.1 mul.218
  9.8 3.0 %collective-permute-done.1 = bf16[6,6,2,256]{3,0,1,2:T(8,128)(2,1)S(1)} collective-permute-done((bf16[6,6,2,256]{3,0,1,2:T(8,128)(2,1)S(1)}, bf16[6,6,2,256]{3,0,1,2:T(8,128)(2,1)S(1)}, u32[]{:S(2)}, u32[]{:S(2)}) %collective-permute-start.1) | collective-permute-done | bytes 36896 | tf_op jit(solution)/shard_map/ppermute | solution.py:53
  12.8 1.7 %collective-permute-start.2 = (bf16[6,6,4,256]{3,0,1,2:T(8,128)(2,1)S(1)}, bf16[6,6,4,256]{3,0,1,2:T(8,128)(2,1)S(1)}, u32[]{:S(2)}, u32[]{:S(2)}) collective-permute-start(bf16[6,6,4,256]{3,0,1,2:T(8,128)(2,1)S(1)} %pad_maximum_fusion.4), channel_id=1, source_target_pairs={{0,16},{1,17},{2,18},{3,19},{4,20},{5,21},{6,22},{7,23},{8,24},{9,... | collective-permute-start | bytes 221192 | tf_op jit(solution)/shard_map/ppermute | solution.py:53
  14.5 0.7 fusion.12
  15.2 2.3 %collective-permute-done.2 = bf16[6,6,4,256]{3,0,1,2:T(8,128)(2,1)S(1)} collective-permute-done((bf16[6,6,4,256]{3,0,1,2:T(8,128)(2,1)S(1)}, bf16[6,6,4,256]{3,0,1,2:T(8,128)(2,1)S(1)}, u32[]{:S(2)}, u32[]{:S(2)}) %collective-permute-start.2) | collective-permute-done | bytes 73760 | tf_op jit(solution)/shard_map/ppermute | solution.py:53
  17.5 0.8 fusion.32
  18.4 3.0 %collective-permute-start.3 = (bf16[1,6,6,8,256]{4,1,2,3,0:T(8,128)(2,1)}, bf16[1,6,6,8,256]{4,1,2,3,0:T(8,128)(2,1)}, u32[]{:S(2)}, u32[]{:S(2)}) collective-permute-start(bf16[1,6,6,8,256]{4,1,2,3,0:T(8,128)(2,1)} %get-tuple-element.27), channel_id=1, source_target_pairs={{0,24},{1,3},{2,26},{3,1},{4,28},{5,7},{6,30},{7,5},{8,16},{9,11},... | collective-permute-start | bytes 442376 | tf_op jit(solution)/shard_map/ppermute | solution.py:53
  21.4 2.2 %maximum_bitcast_fusion = f32[96,36,256]{2,0,1:T(8,128)S(1)} fusion(f32[12,96,256]{2,1,0:T(8,128)} %get-tuple-element.22, f32[12,96,256]{2,1,0:T(8,128)} %get-tuple-element.21, f32[12,96,256]{2,1,0:T(8,128)} %slice_bitcast_fusion.1), kind=kLoop, calls=%fused_computation.1 | loop fusion | flops 1769472 | bytes 7077888 | tf_op jit(solution)/shard_map/transpose | solution.py:284
  24.3 3.9 %copy.57 = f32[96,36,256]{2,1,0:T(8,128)} copy(f32[96,36,256]{2,0,1:T(8,128)S(1)} %maximum_bitcast_fusion) | data formatting | bytes 7077888 | tf_op jit(solution)/shard_map/transpose | solution.py:284
  28.3 1.0 %fusion.36 = (bf16[1,6,6,4,256]{4,1,2,3,0:T(8,128)(2,1)S(1)}, bf16[1,6,6,4,256]{4,1,2,3,0:T(8,128)(2,1)S(1)}) fusion(bf16[1,6,6,8,256]{4,1,2,3,0:T(8,128)(2,1)} %collective-permute-done.3), kind=kLoop, calls=%fused_computation.125 | loop fusion | bytes 294912 | tf_op jit(solution)/shard_map/slice | solution.py:113
  29.3 1.0 %pad_maximum_fusion.2 = bf16[2,6,6,8,256]{4,1,2,3,0:T(8,128)(2,1)S(1)} fusion(bf16[1,6,6,8,256]{4,1,2,3,0:T(8,128)(2,1)S(1)} %maximum_select_fusion.1, bf16[1,6,6,8,256]{4,1,2,3,0:T(8,128)(2,1)} %get-tuple-element.27), kind=kLoop, calls=%fused_computation.12 | loop fusion | flops 147456 | bytes 589824 | tf_op jit(solution)/shard_map/concatenate | solution.py:115
  30.3 2.0 %collective-permute-start.4 = (bf16[2,6,6,8,256]{4,1,2,3,0:T(8,128)(2,1)S(1)}, bf16[2,6,6,8,256]{4,1,2,3,0:T(8,128)(2,1)S(1)}, u32[]{:S(2)}, u32[]{:S(2)}) collective-permute-start(bf16[2,6,6,8,256]{4,1,2,3,0:T(8,128)(2,1)S(1)} %pad_maximum_fusion.2), channel_id=1, source_target_pairs={{0,2},{1,7},{2,0},{3,5},{4,6},{5,3},{6,4},{7,1},{8,10},{9,15},{10,... | collective-permute-start | bytes 884744 | tf_op jit(solution)/shard_map/ppermute | solution.py:53
  32.5 0.1 sin.36
  32.6 0.1 cos.36
  32.7 5.5 %collective-permute-done.4 = bf16[2,6,6,8,256]{4,1,2,3,0:T(8,128)(2,1)S(1)} collective-permute-done((bf16[2,6,6,8,256]{4,1,2,3,0:T(8,128)(2,1)S(1)}, bf16[2,6,6,8,256]{4,1,2,3,0:T(8,128)(2,1)S(1)}, u32[]{:S(2)}, u32[]{:S(2)}) %collective-permute-start.4) | collective-permute-done | bytes 294944 | tf_op jit(solution)/shard_map/ppermute | solution.py:53
  38.2 1.1 %pad_maximum_fusion.1 = bf16[4,6,6,8,256]{4,1,2,3,0:T(8,128)(2,1)S(1)} fusion(bf16[2,6,6,8,256]{4,1,2,3,0:T(8,128)(2,1)S(1)} %collective-permute-done.4, bf16[1,6,6,8,256]{4,1,2,3,0:T(8,128)(2,1)S(1)} %maximum_select_fusion.1, bf16[1,6,6,8,256]{4,1,2,3,0:T(8,128)(2,1)} %get-tuple-element.27), kind=kLoop, calls=%fused_computation.9 | loop fusion | flops 589824 | bytes 1179648 | tf_op jit(solution)/shard_map/concatenate | solution.py:115
  39.3 0.2 copy.55
  39.5 4.1 %collective-permute-start.5 = (bf16[4,6,6,8,256]{4,3,2,1,0:T(8,128)(2,1)S(1)}, bf16[4,6,6,8,256]{4,3,2,1,0:T(8,128)(2,1)S(1)}, u32[]{:S(2)}, u32[]{:S(2)}) collective-permute-start(bf16[4,6,6,8,256]{4,3,2,1,0:T(8,128)(2,1)S(1)} %copy.55), channel_id=1, source_target_pairs={{0,6},{1,25},{2,4},{3,27},{4,2},{5,29},{6,0},{7,31},{8,14},{9,17},... | collective-permute-start | bytes 1769480 | tf_op jit(solution)/shard_map/ppermute | solution.py:53
  43.7 0.1 constant_dynamic-update-slice_fusion.2
  43.9 7.6 %collective-permute-done.5 = bf16[4,6,6,8,256]{4,3,2,1,0:T(8,128)(2,1)S(1)} collective-permute-done((bf16[4,6,6,8,256]{4,3,2,1,0:T(8,128)(2,1)S(1)}, bf16[4,6,6,8,256]{4,3,2,1,0:T(8,128)(2,1)S(1)}, u32[]{:S(2)}, u32[]{:S(2)}) %collective-permute-start.5) | collective-permute-done | bytes 589856 | tf_op jit(solution)/shard_map/ppermute | solution.py:53
  51.5 0.2 fusion.35
  51.7 0.4 constant_dynamic-update-slice_fusion.1
  52.1 0.1 pad_maximum_fusion
  52.3 0.1 collective-permute-start.6
  52.4 0.2 fusion.7
  52.6 0.1 convert_reduce_fusion.bin_ref
  52.7 0.3 copy-done.3
  53.0 0.6 multiply_reduce_fusion
  53.5 0.1 select_reduce_fusion
  53.7 1.5 %collective-permute-done.6 = bf16[8,6,48,256]{3,2,1,0:T(8,128)(2,1)S(1)} collective-permute-done((bf16[8,6,48,256]{3,2,1,0:T(8,128)(2,1)S(1)}, bf16[8,6,48,256]{3,2,1,0:T(8,128)(2,1)S(1)}, u32[]{:S(2)}, u32[]{:S(2)}) %collective-permute-start.6) | collective-permute-done | bytes 1179680 | tf_op jit(solution)/shard_map/ppermute | solution.py:53
  55.3 0.2 broadcast_in_dim.63.start_ref
  55.5 15.9 %search.1 = f32[8,8]{1,0:T(8,128)S(1)} custom-call(s32[16]{0:T(128)S(1)} %get-tuple-element.12.sl_ref, s32[8]{0:T(128)S(1)} %get-tuple-element.10.segs_ref, s32[1]{0:T(128)} %bitcast.47.live_ref, s32[12,96]{1,0:T(8,128)S(1)} %convert_reduce_fusion.bin_ref, f32[12,16]{1,0:T(8,128)S(1)} %get-tuple-element.30.frac_ref, f32[12,16]{1,0:T(8,128)S(1)} %get-tuple-element.29.inv_ref, ...), custom_call_target="tpu_custom_call" | custom-call | tf_op jit(solution)/shard_map/search/pallas_call | solution.py:255
  71.4 0.2 collective-permute-start.7
  71.7 1.0 %collective-permute-done.7 = f32[8,8]{1,0:T(8,128)S(1)} collective-permute-done((f32[8,8]{1,0:T(8,128)S(1)}, f32[8,8]{1,0:T(8,128)S(1)}, u32[]{:S(2)}, u32[]{:S(2)}) %collective-permute-start.7) | collective-permute-done | bytes 288 | tf_op jit(solution)/shard_map/ppermute | solution.py:53
  72.7 3.6 %collective-permute-done.8 = f32[8,8]{1,0:T(8,128)S(1)} collective-permute-done((f32[8,8]{1,0:T(8,128)S(1)}, f32[8,8]{1,0:T(8,128)S(1)}, u32[]{:S(2)}, u32[]{:S(2)}) %collective-permute-start.8) | collective-permute-done | bytes 288 | tf_op jit(solution)/shard_map/ppermute | solution.py:53
  76.3 3.3 %collective-permute-start.9 = (f32[8,8]{1,0:T(8,128)S(1)}, f32[8,8]{1,0:T(8,128)S(1)}, u32[]{:S(2)}, u32[]{:S(2)}) collective-permute-start(f32[8,8]{1,0:T(8,128)S(1)} %max.13), channel_id=1, source_target_pairs={{0,6},{1,7},{2,4},{3,5},{4,2},{5,3},{6,0},{7,1},{8,14},{9,15},{10,... | collective-permute-start | bytes 776 | tf_op jit(solution)/shard_map/ppermute | solution.py:53
  79.5 1.6 %collective-permute-done.9 = f32[8,8]{1,0:T(8,128)S(1)} collective-permute-done((f32[8,8]{1,0:T(8,128)S(1)}, f32[8,8]{1,0:T(8,128)S(1)}, u32[]{:S(2)}, u32[]{:S(2)}) %collective-permute-start.9) | collective-permute-done | bytes 288 | tf_op jit(solution)/shard_map/ppermute | solution.py:53
  81.1 0.6 collective-permute-start.10
  81.8 4.5 %collective-permute-done.10 = f32[8,8]{1,0:T(8,128)S(1)} collective-permute-done((f32[8,8]{1,0:T(8,128)S(1)}, f32[8,8]{1,0:T(8,128)S(1)}, u32[]{:S(2)}, u32[]{:S(2)}) %collective-permute-start.10) | collective-permute-done | bytes 288 | tf_op jit(solution)/shard_map/ppermute | solution.py:53
  86.3 0.6 max.15
  (49 shorter events, 1.0 us)
Async XLA Ops:
  0.7 6.7 %collective-permute-start = (bf16[6,6,1,256]{3,0,1,2:T(8,128)(2,1)S(1)}, bf16[6,6,1,256]{3,0,1,2:T(8,128)(2,1)S(1)}, u32[]{:S(2)}, u32[]{:S(2)}) collective-permute-start(bf16[6,6,1,256]{3,0,1,2:T(8,128)(2,1)S(1)} %bitcast.49), channel_id=1, source_target_pairs={{0,32},{1,33},{2,34},{3,35},{4,36},{5,37},{6,38},{7,39},{8,40},{9,... | collective-permute-start | bytes 55304 | tf_op jit(solution)/shard_map/ppermute | solution.py:53
  5.5 1.1 %copy-start.10 = (s32[8,3]{0,1:T(4,128)S(1)}, s32[8,3]{0,1:T(4,128)}, u32[]{:S(2)}) copy-start(s32[8,3]{0,1:T(4,128)} %param.11) | copy-start | bytes 292
  7.4 5.4 %collective-permute-start.1 = (bf16[6,6,2,256]{3,0,1,2:T(8,128)(2,1)S(1)}, bf16[6,6,2,256]{3,0,1,2:T(8,128)(2,1)S(1)}, u32[]{:S(2)}, u32[]{:S(2)}) collective-permute-start(bf16[6,6,2,256]{3,0,1,2:T(8,128)(2,1)S(1)} %pad_maximum_fusion.5), channel_id=1, source_target_pairs={{0,96},{1,97},{2,98},{3,99},{4,100},{5,101},{6,102},{7,103},{8,104... | collective-permute-start | bytes 110600 | tf_op jit(solution)/shard_map/ppermute | solution.py:53
  9.8 11.6 %copy-start.8 = (s32[24]{0:T(128)}, s32[24]{0:T(128)S(1)}, u32[]{:S(2)}) copy-start(s32[24]{0:T(128)S(1)} %mul.218) | copy-start | bytes 292
  12.8 4.7 %collective-permute-start.2 = (bf16[6,6,4,256]{3,0,1,2:T(8,128)(2,1)S(1)}, bf16[6,6,4,256]{3,0,1,2:T(8,128)(2,1)S(1)}, u32[]{:S(2)}, u32[]{:S(2)}) collective-permute-start(bf16[6,6,4,256]{3,0,1,2:T(8,128)(2,1)S(1)} %pad_maximum_fusion.4), channel_id=1, source_target_pairs={{0,16},{1,17},{2,18},{3,19},{4,20},{5,21},{6,22},{7,23},{8,24},{9,... | collective-permute-start | bytes 221192 | tf_op jit(solution)/shard_map/ppermute | solution.py:53
  18.4 9.9 %collective-permute-start.3 = (bf16[1,6,6,8,256]{4,1,2,3,0:T(8,128)(2,1)}, bf16[1,6,6,8,256]{4,1,2,3,0:T(8,128)(2,1)}, u32[]{:S(2)}, u32[]{:S(2)}) collective-permute-start(bf16[1,6,6,8,256]{4,1,2,3,0:T(8,128)(2,1)} %get-tuple-element.27), channel_id=1, source_target_pairs={{0,24},{1,3},{2,26},{3,1},{4,28},{5,7},{6,30},{7,5},{8,16},{9,11},... | collective-permute-start | bytes 442376 | tf_op jit(solution)/shard_map/ppermute | solution.py:53
  24.2 4.0 %copy-start.5 = (f32[1,16,24]{2,1,0:T(8,128)S(1)}, f32[1,16,24]{2,1,0:T(8,128)}, u32[]{:S(2)}) copy-start(f32[1,16,24]{2,1,0:T(8,128)} %get-tuple-element.31) | copy-start | bytes 4612
  24.3 4.0 %copy-start.6 = (f32[1,16,24]{2,1,0:T(8,128)S(1)}, f32[1,16,24]{2,1,0:T(8,128)}, u32[]{:S(2)}) copy-start(f32[1,16,24]{2,1,0:T(8,128)} %get-tuple-element.32) | copy-start | bytes 4612
  28.2 15.4 %copy-start.4 = (bf16[6,6,8,256]{3,0,1,2:T(8,128)(2,1)S(1)}, bf16[6,6,8,256]{3,0,1,2:T(8,128)(2,1)}, u32[]{:S(2)}) copy-start(bf16[6,6,8,256]{3,0,1,2:T(8,128)(2,1)} %get-tuple-element.28) | copy-start | bytes 442372
  30.3 7.9 %collective-permute-start.4 = (bf16[2,6,6,8,256]{4,1,2,3,0:T(8,128)(2,1)S(1)}, bf16[2,6,6,8,256]{4,1,2,3,0:T(8,128)(2,1)S(1)}, u32[]{:S(2)}, u32[]{:S(2)}) collective-permute-start(bf16[2,6,6,8,256]{4,1,2,3,0:T(8,128)(2,1)S(1)} %pad_maximum_fusion.2), channel_id=1, source_target_pairs={{0,2},{1,7},{2,0},{3,5},{4,6},{5,3},{6,4},{7,1},{8,10},{9,15},{10,... | collective-permute-start | bytes 884744 | tf_op jit(solution)/shard_map/ppermute | solution.py:53
  39.5 12.0 %collective-permute-start.5 = (bf16[4,6,6,8,256]{4,3,2,1,0:T(8,128)(2,1)S(1)}, bf16[4,6,6,8,256]{4,3,2,1,0:T(8,128)(2,1)S(1)}, u32[]{:S(2)}, u32[]{:S(2)}) collective-permute-start(bf16[4,6,6,8,256]{4,3,2,1,0:T(8,128)(2,1)S(1)} %copy.55), channel_id=1, source_target_pairs={{0,6},{1,25},{2,4},{3,27},{4,2},{5,29},{6,0},{7,31},{8,14},{9,17},... | collective-permute-start | bytes 1769480 | tf_op jit(solution)/shard_map/ppermute | solution.py:53
  51.7 0.7 copy-start.9
  51.7 0.9 %copy-start.7 = (s32[12,15]{1,0:T(8,128)S(1)}, s32[12,15]{1,0:T(8,128)}, u32[]{:S(2)}) copy-start(s32[12,15]{1,0:T(8,128)} %param.10) | copy-start | bytes 2164
  51.7 1.3 %copy-start.3 = (bf16[12,2,96,256]{3,2,1,0:T(8,128)(2,1)S(1)}, bf16[12,2,96,256]{3,2,1,0:T(8,128)(2,1)}, u32[]{:S(2)}) copy-start(bf16[12,2,96,256]{3,2,1,0:T(8,128)(2,1)} %param.8) | copy-start | bytes 3538948
  52.1 3.4 %copy-start.2 = (f32[16,6,2,128]{3,2,1,0:T(2,128)S(1)}, f32[16,6,2,128]{3,2,1,0:T(2,128)}, u32[]{:S(2)}) copy-start(f32[16,6,2,128]{3,2,1,0:T(2,128)} %constant.251.clone.turn_ref) | copy-start | bytes 294916
  52.3 3.3 %copy-start = (f32[96,36,256]{2,1,0:T(8,128)S(1)}, f32[96,36,256]{2,1,0:T(8,128)}, u32[]{:S(2)}) copy-start(f32[96,36,256]{2,1,0:T(8,128)} %copy.57) | copy-start | bytes 10616836
  52.3 3.3 %copy-start.1 = (bf16[512,256]{1,0:T(8,128)(2,1)S(1)}, bf16[512,256]{1,0:T(8,128)(2,1)}, u32[]{:S(2)}) copy-start(bf16[512,256]{1,0:T(8,128)(2,1)} %constant.250.clone.table_ref) | copy-start | bytes 786436
  52.3 2.9 %collective-permute-start.6 = (bf16[8,6,48,256]{3,2,1,0:T(8,128)(2,1)S(1)}, bf16[8,6,48,256]{3,2,1,0:T(8,128)(2,1)S(1)}, u32[]{:S(2)}, u32[]{:S(2)}) collective-permute-start(bf16[8,6,48,256]{3,2,1,0:T(8,128)(2,1)S(1)} %pad_maximum_fusion), channel_id=1, source_target_pairs={{0,1},{1,0},{2,3},{3,2},{4,5},{5,4},{6,7},{7,6},{8,9},{9,8},{10,11... | collective-permute-start | bytes 3538952 | tf_op jit(solution)/shard_map/ppermute | solution.py:53
  71.4 1.2 %collective-permute-start.7 = (f32[8,8]{1,0:T(8,128)S(1)}, f32[8,8]{1,0:T(8,128)S(1)}, u32[]{:S(2)}, u32[]{:S(2)}) collective-permute-start(f32[8,8]{1,0:T(8,128)S(1)} %search.1), channel_id=1, source_target_pairs={{0,1},{1,0},{2,3},{3,2},{4,5},{5,4},{6,7},{7,6},{8,9},{9,8},{10,11... | collective-permute-start | bytes 776 | tf_op jit(solution)/shard_map/ppermute | solution.py:53
  72.7 3.6 %collective-permute-start.8 = (f32[8,8]{1,0:T(8,128)S(1)}, f32[8,8]{1,0:T(8,128)S(1)}, u32[]{:S(2)}, u32[]{:S(2)}) collective-permute-start(f32[8,8]{1,0:T(8,128)S(1)} %max.12), channel_id=1, source_target_pairs={{0,2},{1,3},{2,0},{3,1},{4,6},{5,7},{6,4},{7,5},{8,10},{9,11},{10,... | collective-permute-start | bytes 776 | tf_op jit(solution)/shard_map/ppermute | solution.py:53
  76.3 4.8 %collective-permute-start.9 = (f32[8,8]{1,0:T(8,128)S(1)}, f32[8,8]{1,0:T(8,128)S(1)}, u32[]{:S(2)}, u32[]{:S(2)}) collective-permute-start(f32[8,8]{1,0:T(8,128)S(1)} %max.13), channel_id=1, source_target_pairs={{0,6},{1,7},{2,4},{3,5},{4,2},{5,3},{6,0},{7,1},{8,14},{9,15},{10,... | collective-permute-start | bytes 776 | tf_op jit(solution)/shard_map/ppermute | solution.py:53
  81.1 5.1 %collective-permute-start.10 = (f32[8,8]{1,0:T(8,128)S(1)}, f32[8,8]{1,0:T(8,128)S(1)}, u32[]{:S(2)}, u32[]{:S(2)}) collective-permute-start(f32[8,8]{1,0:T(8,128)S(1)} %max.14), channel_id=1, source_target_pairs={{0,8},{1,9},{2,10},{3,11},{4,12},{5,13},{6,14},{7,15},{8,0},{9,1},... | collective-permute-start | bytes 776 | tf_op jit(solution)/shard_map/ppermute | solution.py:53

commit v3 on v2

--- a/solution.py
+++ b/solution.py
@@ -40,53 +40,13 @@
     return (x * 2 + y % 2) * 16 + (y // 2) * 8 + z * 2 + core
 
 
-def near(a):
-    return a ^ 1
-
-
-def far(a):
-    return 3 - a
+def across(dx=0, dy=0, dz=0, dcore=0):
+    return lambda x, y, z, core: (x ^ dx, y ^ dy, z ^ dz, core ^ dcore)
 
 
 def swap_with(value, move):
     pairs = [(index, index_of(*move(*place_of(index)))) for index in range(128)]
     return lax.ppermute(value, AXES, pairs)
-
-
-def x_near(x, y, z, core):
-    return (near(x), y, z, core)
-
-
-def x_far(x, y, z, core):
-    return (far(x), y, z, core)
-
-
-def y_near(x, y, z, core):
-    return (x, near(y), z, core)
-
-
-def y_far(x, y, z, core):
-    return (x, far(y), z, core)
-
-
-def z_near(x, y, z, core):
-    return (x, y, near(z), core)
-
-
-def z_far(x, y, z, core):
-    return (x, y, far(z), core)
-
-
-def y_across(x, y, z, core):
-    return (x, y ^ 2, z, core)
-
-
-def other_core(x, y, z, core):
-    return (x, y, z, core ^ 1)
-
-
-def by_core(first, second):
-    return lambda x, y, z, core: (second if core else first)(x, y, z, core)
 
 
 def tables():
@@ -102,39 +62,28 @@
 
 
 def gather_strain(shard):
-    core = lax.axis_index("tmpl") % 2
     x = jnp.transpose(shard[0], (2, 1, 0, 3)).reshape(JS, 2 * NDET, 1, FB)
-    for move in (x_near, x_far, y_near):
-        x = jnp.concatenate([x, swap_with(x, move)], axis=2)
-    x = x[None]
-    for moves, turned in (((y_far, z_near), 0), ((z_near, z_far), None), ((z_far, y_far), 1)):
-        y = swap_with(x, by_core(*moves))
-        if turned is not None:
-            other = jnp.concatenate([y[:, :, :, 4:], y[:, :, :, :4]], axis=3)
-            y = jnp.where(core == turned, other, y)
-        x = jnp.concatenate([x, y], axis=0)
-    x = x.reshape(NSL // 2, JS, 2 * ROWS, FB)
-    return jnp.concatenate([x, swap_with(x, other_core)], axis=0)
+    got = {0: x}
+    for dx in (2, 3, 1):
+        got[dx] = swap_with(x, across(dx=dx))
+    x = jnp.concatenate([got[dx] for dx in range(4)], axis=2)
+    x = jnp.concatenate([x, swap_with(x, across(dy=1))], axis=2)
+    x = x.reshape(1, JS, 2 * ROWS, FB)
+    got = {(0, 0): x}
+    for dy, dz in ((0, 2), (2, 0), (2, 2), (0, 3), (2, 3), (2, 1), (0, 1)):
+        got[dy, dz] = swap_with(x, across(dy=dy, dz=dz))
+    x = jnp.concatenate([got[dy, dz] for dy in (0, 2) for dz in range(4)], axis=0)
+    return jnp.concatenate([x, swap_with(x, across(dcore=1))], axis=0)
 
 
 def arrival_order():
     dt = lax.axis_index("dt")
     tm = lax.axis_index("tmpl")
-    x, y_lo = dt // 2, dt % 2
-    y_hi, z, core = tm // 8, (tm // 2) % 4, tm % 2
     p = jnp.arange(SEGS, dtype=jnp.int32)
     q = jnp.arange(NSL, dtype=jnp.int32)
-
-    def ring(a, first, second):
-        a = jnp.where(second == 1, 3 - a, a)
-        return a ^ first
-
-    segs = ring(x, p % 2, p // 2 % 2) * 2 + (y_lo ^ (p // 4))
-    bits = (q % 2, q // 2 % 2, q // 4 % 2)
-    from_core = core ^ (q // 8)
-    even = (y_hi ^ bits[0]) * 8 + ring(z, bits[1], bits[2]) * 2
-    odd = (y_hi ^ bits[2]) * 8 + ring(z, bits[0], bits[1]) * 2 + 1
-    return segs, jnp.where(from_core == 0, even, odd)
+    segs = ((dt // 2) ^ (p % 4)) * 2 + ((dt % 2) ^ (p // 4))
+    slices = ((tm // 8) ^ (q // 4 % 2)) * 8 + ((tm // 2 % 4) ^ (q % 4)) * 2 + ((tm % 2) ^ (q // 8))
+    return segs, slices
 
 
 def phase(turns):
@@ -145,7 +94,7 @@
 def kernel(
     sl_ref, segs_ref, live_ref, bin_ref, frac_ref, inv_ref, half_ref,
     strain_ref, table_ref, turn_ref, templ_ref, start_ref, local_ref, step_ref,
-    out_ref, prod_ref, rot_ref, best_ref, *binned,
+    out_ref, prod_ref, rot_ref, best_ref, wide_ref, *binned,
 ):
     g = pl.program_id(0)
 
@@ -153,6 +102,12 @@
     def _():
         for ref in binned:
             ref[...] = jnp.zeros_like(ref)
+        for k in range(SLOTS):
+            h = templ_ref[k, 0].astype(jnp.float32)
+            i = templ_ref[k, 1].astype(jnp.float32)
+            wide_ref[k, 0] = h
+            wide_ref[k, 1] = h + i
+            wide_ref[k, 2] = h - i
 
     sc, ss = start_ref[0, 0], start_ref[0, 1]
     for half in range(2):
@@ -162,6 +117,7 @@
         rot_ref[1, :, cols] = sc * ls + ss * lc
 
     def product(jj):
+        j = sl_ref[g] * JS + jj
         both = strain_ref[0, jj].astype(jnp.float32)
         raw_r, raw_i = both[:ROWS], both[ROWS:]
         rc, rs = rot_ref[0], rot_ref[1]
@@ -175,9 +131,9 @@
         for pair in range(SLOTS // 2):
             real, imag = [], []
             for k in (2 * pair, 2 * pair + 1):
-                h = templ_ref[0, jj, k:k + 1, :]
-                v = templ_ref[0, jj, SLOTS + k:SLOTS + k + 1, :]
-                w = templ_ref[0, jj, 2 * SLOTS + k:2 * SLOTS + k + 1, :]
+                h = wide_ref[k, 0, pl.ds(j, 1), :]
+                v = wide_ref[k, 1, pl.ds(j, 1), :]
+                w = wide_ref[k, 2, pl.ds(j, 1), :]
                 k1 = h * su
                 real.append(k1 - si * w)
                 imag.append(k1 - sr * v)
@@ -240,7 +196,7 @@
             pl.BlockSpec((1, JS, 2 * ROWS, FB), lambda g, sl, *_: (g, 0, 0, 0)),
             pl.BlockSpec((2 * FB, 2 * TW), lambda g, sl, *_: (0, 0)),
             pl.BlockSpec((1, JS, 2, TW), lambda g, sl, *_: (sl[g], 0, 0, 0)),
-            pl.BlockSpec((1, JS, 3 * SLOTS, FB), lambda g, sl, *_: (sl[g], 0, 0, 0)),
+            pl.BlockSpec((SLOTS, 2, NBLK, FB), lambda g, sl, *_: (0, 0, 0, 0)),
             pl.BlockSpec((1, 2, ROWS, TW), lambda g, sl, *_: (g, 0, 0, 0)),
             pl.BlockSpec((2, ROWS, FB), lambda g, sl, *_: (0, 0, 0)),
             pl.BlockSpec((2, ROWS, TW), lambda g, sl, *_: (0, 0, 0)),
@@ -250,6 +206,7 @@
             pltpu.VMEM((JS * SLOTS * ROWS, 2 * FB), jnp.bfloat16),
             pltpu.VMEM((2, ROWS, FB), jnp.float32),
             pltpu.VMEM((SEGS, NWIN), jnp.float32),
+            pltpu.VMEM((SLOTS, 3, NBLK, FB), jnp.float32),
         ] + [pltpu.VMEM((NBIN, ROWS, 2 * TW), jnp.float32) for _ in range(SLOTS)],
     )
     return pl.pallas_call(
@@ -257,7 +214,7 @@
         out_shape=jax.ShapeDtypeStruct((SEGS, NWIN), jnp.float32),
         grid_spec=grid_spec,
         compiler_params=pltpu.CompilerParams(
-            dimension_semantics=("arbitrary",), vmem_limit_bytes=40 * 1024 * 1024
+            dimension_semantics=("arbitrary",), vmem_limit_bytes=24 * 1024 * 1024
         ),
         name="search",
     )(sl, segs, live, bin_of, frac, inv, half, strain, *tables(), templ, start, local, step)
@@ -279,10 +236,6 @@
     inv = 1.0 / (frac * sigma2[:, None])
     half = 1.0 / (2.0 * sigma2)
 
-    real, imag = wide[:, 0], wide[:, 1]
-    templ = jnp.concatenate([real, real + imag, real - imag], axis=0)
-    templ = jnp.transpose(templ, (1, 0, 2)).reshape(NSL, JS, 3 * SLOTS, FB)
-
     first = (MARGIN + jnp.take(shifts, segs, axis=0)).T.reshape(ROWS)
     bins = jnp.arange(FB, dtype=jnp.int32)
     local = phase((first[:, None] * bins[None, :] * STRIDE) % NFFT)
@@ -293,9 +246,9 @@
     step = jnp.broadcast_to(step[..., None], (2, ROWS, TW))
 
     best = search(
-        slices, segs, live_count[0], bin_of, frac, inv, half, gathered, templ, start, local, step
-    )
-    for move in (other_core, z_near, z_far, y_across):
+        slices, segs, live_count[0], bin_of, frac, inv, half, gathered, templates, start, local, step
+    )
+    for move in (across(dcore=1), across(dz=1), across(dz=3), across(dy=2)):
         best = jnp.maximum(best, swap_with(best, move))
     return best[:, None, :]
 

time: 87.1 us -> 75.8 us (0.87)
  other arithmetic: 11.5 us -> 2 us
  local copies, waits for them, and re-layouts: 9.14 us -> 3.1 us
  starting transfers between devices: 18.7 us -> 23.2 us
    ppermute x11 -> x16, starting transfers between devices: 18.7 us -> 23.2 us  [swap_with(): return lax.ppermute(value, AXES, pairs)]
    transpose x1 -> x0, local copies, waits for them, and re-layouts: 3.94 us -> none  [per_device(): templ = jnp.transpose(templ, (1, 0, 2)).reshape(NSL, JS, 3 * SLOTS, FB)]
    concatenate x5 -> x1, other arithmetic: 2.29 us -> 0.03 us  [gather_strain(): x = jnp.concatenate([got[dx] for dx in range(4)], axis=2)]
    transpose x1 -> x0, other arithmetic: 2.21 us -> none  [per_device(): templ = jnp.transpose(templ, (1, 0, 2)).reshape(NSL, JS, 3 * SLOTS, FB)]
    add x1 -> x0, other arithmetic: 1.62 us -> none  [per_device(): templ = jnp.concatenate([real, real + imag, real - imag], axis=0)]
    convert_element_type x1 -> x0, other arithmetic: 1.53 us -> none  [per_device(): wide = templates.astype(jnp.float32)]
    slice x2 -> x0, local copies, waits for them, and re-layouts: 1.19 us -> none  [gather_strain(): other = jnp.concatenate([y[:, :, :, 4:], y[:, :, :, :4]], axis=3)]
    squeeze x1 -> x0, local copies, waits for them, and re-layouts: 1.09 us -> none  [per_device(): real, imag = (wide[:, 0], wide[:, 1])]
  transfers between devices with their start and end apart: 11 -> 16, of which waited for: 9 -> 10; matrix products, arithmetic and copies ran while one was open for 16% -> 4% of each run, Pallas kernels for 0% -> 0%
where the time goes in v3:
time: 75.8 us; the launch traced here: 75.7 us
  waiting for transfers between devices  29.9 us (39%)
  starting transfers between devices  23.2 us (31%)
  Pallas kernels  16.5 us (22%)
  local copies, waits for them, and re-layouts  3.1 us (4%)
  other arithmetic  2 us (3%)
  between operations  0.95 us (1%)
    ppermute x16, waiting for transfers between devices, swap_with(): return lax.ppermute(value, AXES, pairs)  29.9 us
    ppermute x16, starting transfers between devices, swap_with(): return lax.ppermute(value, AXES, pairs)  23.2 us
    pallas_call x1, Pallas kernels, search(): pl.pallas_call(kernel, out_shape=jax.ShapeDtypeStruct((SEGS, NWIN), jnp.f...  16.5 us
    unnamed x22, local copies, waits for them, and re-layouts  1.71 us
  transfers between devices with their start and end apart: 16, of which 10 were waited for; matrix products, arithmetic and copies ran while one was open for 4% of the time, Pallas kernels for 0%

profile of v3, /device:TPU:0, one launch (start us, length us, event | category | flops | bytes accessed | tf_op | source)
XLA Modules:
  0.0 75.7 jit_solution(9436262015038553045)
XLA Ops:
  0.0 0.7 copy.27
  0.7 1.6 %collective-permute-start = (bf16[6,6,1,256]{3,0,1,2:T(8,128)(2,1)S(1)}, bf16[6,6,1,256]{3,0,1,2:T(8,128)(2,1)S(1)}, u32[]{:S(2)}, u32[]{:S(2)}) collective-permute-start(bf16[6,6,1,256]{3,0,1,2:T(8,128)(2,1)S(1)} %bitcast.20), channel_id=1, source_target_pairs={{0,32},{1,33},{2,34},{3,35},{4,36},{5,37},{6,38},{7,39},{8,40},{9,... | collective-permute-start | bytes 55304 | tf_op jit(solution)/shard_map/ppermute | solution.py:49
  2.3 2.7 %collective-permute-start.1 = (bf16[6,6,1,256]{3,0,1,2:T(8,128)(2,1)S(1)}, bf16[6,6,1,256]{3,0,1,2:T(8,128)(2,1)S(1)}, u32[]{:S(2)}, u32[]{:S(2)}) collective-permute-start(bf16[6,6,1,256]{3,0,1,2:T(8,128)(2,1)S(1)} %bitcast.21), channel_id=1, source_target_pairs={{0,64},{1,65},{2,66},{3,67},{4,68},{5,69},{6,70},{7,71},{8,72},{9,... | collective-permute-start | bytes 55304 | tf_op jit(solution)/shard_map/ppermute | solution.py:49
  5.0 0.4 collective-permute-start.2
  5.5 0.8 %copy.29 = s32[8,3]{1,0:T(8,128)S(1)} copy(s32[8,3]{0,1:T(4,128)} %param.11) | data formatting | bytes 192 | tf_op args[4]
  6.3 0.6 gather_fusion
  6.8 0.1 fusion.13
  6.9 0.1 copy.30
  7.1 0.1 mul.202
  7.2 0.1 fusion.11
  7.3 0.1 copy.33
  7.4 0.1 sin.36
  7.5 0.1 copy.32
  7.6 0.1 cos.36
  7.7 2.4 %collective-permute-done.2 = bf16[6,6,1,256]{3,0,1,2:T(8,128)(2,1)S(1)} collective-permute-done((bf16[6,6,1,256]{3,0,1,2:T(8,128)(2,1)S(1)}, bf16[6,6,1,256]{3,0,1,2:T(8,128)(2,1)S(1)}, u32[]{:S(2)}, u32[]{:S(2)}) %collective-permute-start.2) | collective-permute-done | bytes 18464 | tf_op jit(solution)/shard_map/ppermute | solution.py:49
  10.1 1.7 %collective-permute-start.3 = (bf16[6,6,4,256]{3,0,1,2:T(8,128)(2,1)S(1)}, bf16[6,6,4,256]{3,0,1,2:T(8,128)(2,1)S(1)}, u32[]{:S(2)}, u32[]{:S(2)}) collective-permute-start(bf16[6,6,4,256]{3,0,1,2:T(8,128)(2,1)S(1)} %pad_maximum_fusion), channel_id=1, source_target_pairs={{0,16},{1,17},{2,18},{3,19},{4,20},{5,21},{6,22},{7,23},{8,24},{9,... | collective-permute-start | bytes 221192 | tf_op jit(solution)/shard_map/ppermute | solution.py:49
  11.8 3.0 %collective-permute-done.3 = bf16[6,6,4,256]{3,0,1,2:T(8,128)(2,1)S(1)} collective-permute-done((bf16[6,6,4,256]{3,0,1,2:T(8,128)(2,1)S(1)}, bf16[6,6,4,256]{3,0,1,2:T(8,128)(2,1)S(1)}, u32[]{:S(2)}, u32[]{:S(2)}) %collective-permute-start.3) | collective-permute-done | bytes 73760 | tf_op jit(solution)/shard_map/ppermute | solution.py:49
  14.8 0.1 constant_dynamic-update-slice_fusion.12
  14.9 2.0 %collective-permute-start.4 = (bf16[1,6,48,256]{3,2,1,0:T(8,128)(2,1)S(1)}, bf16[1,6,48,256]{3,2,1,0:T(8,128)(2,1)S(1)}, u32[]{:S(2)}, u32[]{:S(2)}) collective-permute-start(bf16[1,6,48,256]{3,2,1,0:T(8,128)(2,1)S(1)} %get-tuple-element.14), channel_id=1, source_target_pairs={{0,2},{1,3},{2,0},{3,1},{4,6},{5,7},{6,4},{7,5},{8,10},{9,11},{10,... | collective-permute-start | bytes 442376 | tf_op jit(solution)/shard_map/ppermute | solution.py:49
  17.5 3.7 %collective-permute-start.5 = (bf16[1,6,48,256]{3,2,1,0:T(8,128)(2,1)S(1)}, bf16[1,6,48,256]{3,2,1,0:T(8,128)(2,1)S(1)}, u32[]{:S(2)}, u32[]{:S(2)}) collective-permute-start(bf16[1,6,48,256]{3,2,1,0:T(8,128)(2,1)S(1)} %get-tuple-element.14), channel_id=1, source_target_pairs={{0,4},{1,5},{2,6},{3,7},{4,0},{5,1},{6,2},{7,3},{8,12},{9,13},{10,... | collective-permute-start | bytes 442376 | tf_op jit(solution)/shard_map/ppermute | solution.py:49
  21.2 0.1 collective-permute-start.6
  21.3 3.3 %collective-permute-start.7 = (bf16[1,6,48,256]{3,2,1,0:T(8,128)(2,1)S(1)}, bf16[1,6,48,256]{3,2,1,0:T(8,128)(2,1)S(1)}, u32[]{:S(2)}, u32[]{:S(2)}) collective-permute-start(bf16[1,6,48,256]{3,2,1,0:T(8,128)(2,1)S(1)} %get-tuple-element.14), channel_id=1, source_target_pairs={{0,8},{1,9},{2,10},{3,11},{4,12},{5,13},{6,14},{7,15},{8,0},{9,1},... | collective-permute-start | bytes 442376 | tf_op jit(solution)/shard_map/ppermute | solution.py:49
  24.6 7.0 %collective-permute-start.9 = (bf16[1,6,48,256]{3,2,1,0:T(8,128)(2,1)S(1)}, bf16[1,6,48,256]{3,2,1,0:T(8,128)(2,1)S(1)}, u32[]{:S(2)}, u32[]{:S(2)}) collective-permute-start(bf16[1,6,48,256]{3,2,1,0:T(8,128)(2,1)S(1)} %get-tuple-element.14), channel_id=1, source_target_pairs={{0,12},{1,13},{2,14},{3,15},{4,8},{5,9},{6,10},{7,11},{8,4},{9,5},... | collective-permute-start | bytes 442376 | tf_op jit(solution)/shard_map/ppermute | solution.py:49
  31.6 0.1 collective-permute-start.10
  31.8 1.8 %collective-permute-done.8 = bf16[1,6,48,256]{3,2,1,0:T(8,128)(2,1)S(1)} collective-permute-done((bf16[1,6,48,256]{3,2,1,0:T(8,128)(2,1)S(1)}, bf16[1,6,48,256]{3,2,1,0:T(8,128)(2,1)S(1)}, u32[]{:S(2)}, u32[]{:S(2)}) %collective-permute-start.8) | collective-permute-done | bytes 147488 | tf_op jit(solution)/shard_map/ppermute | solution.py:49
  33.6 3.9 %collective-permute-done.9 = bf16[1,6,48,256]{3,2,1,0:T(8,128)(2,1)S(1)} collective-permute-done((bf16[1,6,48,256]{3,2,1,0:T(8,128)(2,1)S(1)}, bf16[1,6,48,256]{3,2,1,0:T(8,128)(2,1)S(1)}, u32[]{:S(2)}, u32[]{:S(2)}) %collective-permute-start.9) | collective-permute-done | bytes 147488 | tf_op jit(solution)/shard_map/ppermute | solution.py:49
  37.6 0.0 copy-start.1
  37.6 0.0 copy-start.2
  37.6 2.9 %collective-permute-done.10 = bf16[1,6,48,256]{3,2,1,0:T(8,128)(2,1)S(1)} collective-permute-done((bf16[1,6,48,256]{3,2,1,0:T(8,128)(2,1)S(1)}, bf16[1,6,48,256]{3,2,1,0:T(8,128)(2,1)S(1)}, u32[]{:S(2)}, u32[]{:S(2)}) %collective-permute-start.10) | collective-permute-done | bytes 147488 | tf_op jit(solution)/shard_map/ppermute | solution.py:49
  40.5 0.1 collective-permute-start.11
  40.6 0.2 fusion.6
  40.8 0.1 convert_reduce_fusion.bin_ref
  40.9 0.6 fusion
  41.5 0.1 select_reduce_fusion
  41.6 0.1 multiply_divide_fusion
  41.7 1.8 %collective-permute-done.11 = bf16[8,6,48,256]{3,2,1,0:T(8,128)(2,1)S(1)} collective-permute-done((bf16[8,6,48,256]{3,2,1,0:T(8,128)(2,1)S(1)}, bf16[8,6,48,256]{3,2,1,0:T(8,128)(2,1)S(1)}, u32[]{:S(2)}, u32[]{:S(2)}) %collective-permute-start.11) | collective-permute-done | bytes 1179680 | tf_op jit(solution)/shard_map/ppermute | solution.py:49
  43.4 0.1 constant_dynamic-update-slice_fusion.13.strain_ref
  43.5 0.2 broadcast_in_dim.13.start_ref
  43.7 0.1 broadcast_in_dim.14.step_ref
  43.7 16.5 %search.1 = f32[8,8]{1,0:T(8,128)S(1)} custom-call(s32[16]{0:T(128)S(1)} %get-tuple-element.12.sl_ref, s32[8]{0:T(128)S(1)} %get-tuple-element.10.segs_ref, s32[1]{0:T(128)} %bitcast.19.live_ref, s32[12,96]{1,0:T(8,128)S(1)} %convert_reduce_fusion.bin_ref, f32[12,16]{1,0:T(8,128)S(1)} %get-tuple-element.30.frac_ref, f32[12,16]{1,0:T(8,128)S(1)} %get-tuple-element.29.inv_ref, ...), custom_call_target="tpu_custom_call" | custom-call | tf_op jit(solution)/shard_map/search/pallas_call | solution.py:212
  60.3 0.2 collective-permute-start.12
  60.5 1.0 %collective-permute-done.12 = f32[8,8]{1,0:T(8,128)S(1)} collective-permute-done((f32[8,8]{1,0:T(8,128)S(1)}, f32[8,8]{1,0:T(8,128)S(1)}, u32[]{:S(2)}, u32[]{:S(2)}) %collective-permute-start.12) | collective-permute-done | bytes 288 | tf_op jit(solution)/shard_map/ppermute | solution.py:49
  61.5 3.6 %collective-permute-done.13 = f32[8,8]{1,0:T(8,128)S(1)} collective-permute-done((f32[8,8]{1,0:T(8,128)S(1)}, f32[8,8]{1,0:T(8,128)S(1)}, u32[]{:S(2)}, u32[]{:S(2)}) %collective-permute-start.13) | collective-permute-done | bytes 288 | tf_op jit(solution)/shard_map/ppermute | solution.py:49
  65.1 0.1 collective-permute-start.14
  65.2 4.7 %collective-permute-done.14 = f32[8,8]{1,0:T(8,128)S(1)} collective-permute-done((f32[8,8]{1,0:T(8,128)S(1)}, f32[8,8]{1,0:T(8,128)S(1)}, u32[]{:S(2)}, u32[]{:S(2)}) %collective-permute-start.14) | collective-permute-done | bytes 288 | tf_op jit(solution)/shard_map/ppermute | solution.py:49
  69.9 0.3 collective-permute-start.15
  70.3 4.8 %collective-permute-done.15 = f32[8,8]{1,0:T(8,128)S(1)} collective-permute-done((f32[8,8]{1,0:T(8,128)S(1)}, f32[8,8]{1,0:T(8,128)S(1)}, u32[]{:S(2)}, u32[]{:S(2)}) %collective-permute-start.15) | collective-permute-done | bytes 288 | tf_op jit(solution)/shard_map/ppermute | solution.py:49
  75.1 0.6 max.15
  (41 shorter events, 0.4 us)
Async XLA Ops:
  0.7 6.9 %collective-permute-start = (bf16[6,6,1,256]{3,0,1,2:T(8,128)(2,1)S(1)}, bf16[6,6,1,256]{3,0,1,2:T(8,128)(2,1)S(1)}, u32[]{:S(2)}, u32[]{:S(2)}) collective-permute-start(bf16[6,6,1,256]{3,0,1,2:T(8,128)(2,1)S(1)} %bitcast.20), channel_id=1, source_target_pairs={{0,32},{1,33},{2,34},{3,35},{4,36},{5,37},{6,38},{7,39},{8,40},{9,... | collective-permute-start | bytes 55304 | tf_op jit(solution)/shard_map/ppermute | solution.py:49
  2.3 5.4 %collective-permute-start.1 = (bf16[6,6,1,256]{3,0,1,2:T(8,128)(2,1)S(1)}, bf16[6,6,1,256]{3,0,1,2:T(8,128)(2,1)S(1)}, u32[]{:S(2)}, u32[]{:S(2)}) collective-permute-start(bf16[6,6,1,256]{3,0,1,2:T(8,128)(2,1)S(1)} %bitcast.21), channel_id=1, source_target_pairs={{0,64},{1,65},{2,66},{3,67},{4,68},{5,69},{6,70},{7,71},{8,72},{9,... | collective-permute-start | bytes 55304 | tf_op jit(solution)/shard_map/ppermute | solution.py:49
  5.0 5.0 %collective-permute-start.2 = (bf16[6,6,1,256]{3,0,1,2:T(8,128)(2,1)S(1)}, bf16[6,6,1,256]{3,0,1,2:T(8,128)(2,1)S(1)}, u32[]{:S(2)}, u32[]{:S(2)}) collective-permute-start(bf16[6,6,1,256]{3,0,1,2:T(8,128)(2,1)S(1)} %bitcast.22), channel_id=1, source_target_pairs={{0,96},{1,97},{2,98},{3,99},{4,100},{5,101},{6,102},{7,103},{8,104... | collective-permute-start | bytes 55304 | tf_op jit(solution)/shard_map/ppermute | solution.py:49
  7.1 33.6 %copy-start.3 = (s32[12,15]{1,0:T(8,128)S(1)}, s32[12,15]{1,0:T(8,128)}, u32[]{:S(2)}) copy-start(s32[12,15]{1,0:T(8,128)} %param.10) | copy-start | bytes 2164
  7.3 33.6 %copy-start = (bf16[12,2,96,256]{3,2,1,0:T(8,128)(2,1)S(1)}, bf16[12,2,96,256]{3,2,1,0:T(8,128)(2,1)}, u32[]{:S(2)}) copy-start(bf16[12,2,96,256]{3,2,1,0:T(8,128)(2,1)} %templ_ref.1) | copy-start | bytes 3538948
  10.1 4.7 %collective-permute-start.3 = (bf16[6,6,4,256]{3,0,1,2:T(8,128)(2,1)S(1)}, bf16[6,6,4,256]{3,0,1,2:T(8,128)(2,1)S(1)}, u32[]{:S(2)}, u32[]{:S(2)}) collective-permute-start(bf16[6,6,4,256]{3,0,1,2:T(8,128)(2,1)S(1)} %pad_maximum_fusion), channel_id=1, source_target_pairs={{0,16},{1,17},{2,18},{3,19},{4,20},{5,21},{6,22},{7,23},{8,24},{9,... | collective-permute-start | bytes 221192 | tf_op jit(solution)/shard_map/ppermute | solution.py:49
  14.9 9.7 %collective-permute-start.4 = (bf16[1,6,48,256]{3,2,1,0:T(8,128)(2,1)S(1)}, bf16[1,6,48,256]{3,2,1,0:T(8,128)(2,1)S(1)}, u32[]{:S(2)}, u32[]{:S(2)}) collective-permute-start(bf16[1,6,48,256]{3,2,1,0:T(8,128)(2,1)S(1)} %get-tuple-element.14), channel_id=1, source_target_pairs={{0,2},{1,3},{2,0},{3,1},{4,6},{5,7},{6,4},{7,5},{8,10},{9,11},{10,... | collective-permute-start | bytes 442376 | tf_op jit(solution)/shard_map/ppermute | solution.py:49
  17.5 14.1 %collective-permute-start.5 = (bf16[1,6,48,256]{3,2,1,0:T(8,128)(2,1)S(1)}, bf16[1,6,48,256]{3,2,1,0:T(8,128)(2,1)S(1)}, u32[]{:S(2)}, u32[]{:S(2)}) collective-permute-start(bf16[1,6,48,256]{3,2,1,0:T(8,128)(2,1)S(1)} %get-tuple-element.14), channel_id=1, source_target_pairs={{0,4},{1,5},{2,6},{3,7},{4,0},{5,1},{6,2},{7,3},{8,12},{9,13},{10,... | collective-permute-start | bytes 442376 | tf_op jit(solution)/shard_map/ppermute | solution.py:49
  21.2 10.5 %collective-permute-start.6 = (bf16[1,6,48,256]{3,2,1,0:T(8,128)(2,1)S(1)}, bf16[1,6,48,256]{3,2,1,0:T(8,128)(2,1)S(1)}, u32[]{:S(2)}, u32[]{:S(2)}) collective-permute-start(bf16[1,6,48,256]{3,2,1,0:T(8,128)(2,1)S(1)} %get-tuple-element.14), channel_id=1, source_target_pairs={{0,6},{1,7},{2,4},{3,5},{4,2},{5,3},{6,0},{7,1},{8,14},{9,15},{10,... | collective-permute-start | bytes 442376 | tf_op jit(solution)/shard_map/ppermute | solution.py:49
  21.3 10.5 %collective-permute-start.7 = (bf16[1,6,48,256]{3,2,1,0:T(8,128)(2,1)S(1)}, bf16[1,6,48,256]{3,2,1,0:T(8,128)(2,1)S(1)}, u32[]{:S(2)}, u32[]{:S(2)}) collective-permute-start(bf16[1,6,48,256]{3,2,1,0:T(8,128)(2,1)S(1)} %get-tuple-element.14), channel_id=1, source_target_pairs={{0,8},{1,9},{2,10},{3,11},{4,12},{5,13},{6,14},{7,15},{8,0},{9,1},... | collective-permute-start | bytes 442376 | tf_op jit(solution)/shard_map/ppermute | solution.py:49
  24.6 9.0 %collective-permute-start.8 = (bf16[1,6,48,256]{3,2,1,0:T(8,128)(2,1)S(1)}, bf16[1,6,48,256]{3,2,1,0:T(8,128)(2,1)S(1)}, u32[]{:S(2)}, u32[]{:S(2)}) collective-permute-start(bf16[1,6,48,256]{3,2,1,0:T(8,128)(2,1)S(1)} %get-tuple-element.14), channel_id=1, source_target_pairs={{0,10},{1,11},{2,8},{3,9},{4,14},{5,15},{6,12},{7,13},{8,2},{9,3},... | collective-permute-start | bytes 442376 | tf_op jit(solution)/shard_map/ppermute | solution.py:49
  24.6 13.0 %collective-permute-start.9 = (bf16[1,6,48,256]{3,2,1,0:T(8,128)(2,1)S(1)}, bf16[1,6,48,256]{3,2,1,0:T(8,128)(2,1)S(1)}, u32[]{:S(2)}, u32[]{:S(2)}) collective-permute-start(bf16[1,6,48,256]{3,2,1,0:T(8,128)(2,1)S(1)} %get-tuple-element.14), channel_id=1, source_target_pairs={{0,12},{1,13},{2,14},{3,15},{4,8},{5,9},{6,10},{7,11},{8,4},{9,5},... | collective-permute-start | bytes 442376 | tf_op jit(solution)/shard_map/ppermute | solution.py:49
  31.6 8.8 %collective-permute-start.10 = (bf16[1,6,48,256]{3,2,1,0:T(8,128)(2,1)S(1)}, bf16[1,6,48,256]{3,2,1,0:T(8,128)(2,1)S(1)}, u32[]{:S(2)}, u32[]{:S(2)}) collective-permute-start(bf16[1,6,48,256]{3,2,1,0:T(8,128)(2,1)S(1)} %get-tuple-element.14), channel_id=1, source_target_pairs={{0,14},{1,15},{2,12},{3,13},{4,10},{5,11},{6,8},{7,9},{8,6},{9,7},... | collective-permute-start | bytes 442376 | tf_op jit(solution)/shard_map/ppermute | solution.py:49
  37.6 6.2 %copy-start.1 = (bf16[512,256]{1,0:T(8,128)(2,1)S(1)}, bf16[512,256]{1,0:T(8,128)(2,1)}, u32[]{:S(2)}) copy-start(bf16[512,256]{1,0:T(8,128)(2,1)} %constant.205.clone.table_ref) | copy-start | bytes 786436
  37.6 6.2 %copy-start.2 = (f32[16,6,2,128]{3,2,1,0:T(2,128)S(1)}, f32[16,6,2,128]{3,2,1,0:T(2,128)}, u32[]{:S(2)}) copy-start(f32[16,6,2,128]{3,2,1,0:T(2,128)} %constant.206.clone.turn_ref) | copy-start | bytes 294916
  40.5 2.9 %collective-permute-start.11 = (bf16[8,6,48,256]{3,2,1,0:T(8,128)(2,1)S(1)}, bf16[8,6,48,256]{3,2,1,0:T(8,128)(2,1)S(1)}, u32[]{:S(2)}, u32[]{:S(2)}) collective-permute-start(bf16[8,6,48,256]{3,2,1,0:T(8,128)(2,1)S(1)} %get-tuple-element.15), channel_id=1, source_target_pairs={{0,1},{1,0},{2,3},{3,2},{4,5},{5,4},{6,7},{7,6},{8,9},{9,8},{10,11... | collective-permute-start | bytes 3538952 | tf_op jit(solution)/shard_map/ppermute | solution.py:49
  60.3 1.2 %collective-permute-start.12 = (f32[8,8]{1,0:T(8,128)S(1)}, f32[8,8]{1,0:T(8,128)S(1)}, u32[]{:S(2)}, u32[]{:S(2)}) collective-permute-start(f32[8,8]{1,0:T(8,128)S(1)} %search.1), channel_id=1, source_target_pairs={{0,1},{1,0},{2,3},{3,2},{4,5},{5,4},{6,7},{7,6},{8,9},{9,8},{10,11... | collective-permute-start | bytes 776 | tf_op jit(solution)/shard_map/ppermute | solution.py:49
  61.5 3.6 %collective-permute-start.13 = (f32[8,8]{1,0:T(8,128)S(1)}, f32[8,8]{1,0:T(8,128)S(1)}, u32[]{:S(2)}, u32[]{:S(2)}) collective-permute-start(f32[8,8]{1,0:T(8,128)S(1)} %max.12), channel_id=1, source_target_pairs={{0,2},{1,3},{2,0},{3,1},{4,6},{5,7},{6,4},{7,5},{8,10},{9,11},{10,... | collective-permute-start | bytes 776 | tf_op jit(solution)/shard_map/ppermute | solution.py:49
  65.1 4.8 %collective-permute-start.14 = (f32[8,8]{1,0:T(8,128)S(1)}, f32[8,8]{1,0:T(8,128)S(1)}, u32[]{:S(2)}, u32[]{:S(2)}) collective-permute-start(f32[8,8]{1,0:T(8,128)S(1)} %max.13), channel_id=1, source_target_pairs={{0,6},{1,7},{2,4},{3,5},{4,2},{5,3},{6,0},{7,1},{8,14},{9,15},{10,... | collective-permute-start | bytes 776 | tf_op jit(solution)/shard_map/ppermute | solution.py:49
  69.9 5.1 %collective-permute-start.15 = (f32[8,8]{1,0:T(8,128)S(1)}, f32[8,8]{1,0:T(8,128)S(1)}, u32[]{:S(2)}, u32[]{:S(2)}) collective-permute-start(f32[8,8]{1,0:T(8,128)S(1)} %max.14), channel_id=1, source_target_pairs={{0,8},{1,9},{2,10},{3,11},{4,12},{5,13},{6,14},{7,15},{8,0},{9,1},... | collective-permute-start | bytes 776 | tf_op jit(solution)/shard_map/ppermute | solution.py:49

commit v4 on v3

v4 whole, which is shorter than its diff:
```python
import functools
import math

import ml_dtypes
import numpy as np

import jax
import jax.numpy as jnp
from jax import lax
from jax.experimental import pallas as pl
from jax.experimental.pallas import tpu as pltpu
from jax.sharding import PartitionSpec as P

FB = 256
NBLK = 96
NFFT = 1048576
FLOW = 5120
STRIDE = 4097
NBIN = 16
TW = 128
MARGIN = 64
WIN = 16
NWIN = TW // WIN
NDET = 3
SEGS = 8
SLOTS = 12
NSL = 16
JS = NBLK // NSL
ROWS = NDET * SEGS
EPSILON = 1e-05
TWO_PI = 2.0 * math.pi
AXES = ("dt", "tmpl")
VMEM = 16 * 1024 * 1024


def place_of(index):
    dt, tm = divmod(index, 16)
    return (dt // 2, (tm // 8) * 2 + dt % 2, (tm // 2) % 4, tm % 2)


def index_of(x, y, z, core):
    return (x * 2 + y % 2) * 16 + (y // 2) * 8 + z * 2 + core


def across(dx=0, dy=0, dz=0, dcore=0):
    return lambda x, y, z, core: (x ^ dx, y ^ dy, z ^ dz, core ^ dcore)


def swap_with(value, move):
    pairs = [(index, index_of(*move(*place_of(index)))) for index in range(128)]
    return lax.ppermute(value, AXES, pairs)


def tables():
    tau = np.arange(TW, dtype=np.int64)
    bins = np.arange(FB, dtype=np.int64)
    angle = ((bins[:, None] * tau[None, :] * STRIDE) % NFFT).astype(np.float64) * (TWO_PI / NFFT)
    cosine, sine = np.cos(angle), np.sin(angle)
    local = np.block([[cosine, sine], [-sine, cosine]]).astype(ml_dtypes.bfloat16)
    base = FLOW + np.arange(NBLK, dtype=np.int64) * FB
    angle = ((base[:, None] * tau[None, :] * STRIDE) % NFFT).astype(np.float64) * (TWO_PI / NFFT)
    turn = np.stack([np.cos(angle), np.sin(angle)], axis=1).astype(np.float32)
    return local, turn.reshape(NSL, JS, 2, TW)


def phase(turns):
    angle = turns.astype(jnp.float32) * jnp.float32(TWO_PI / NFFT)
    return jnp.stack([jnp.cos(angle), jnp.sin(angle)])


STEPS = (
    ({"dy": 2}, {"dz": 1}),
    ({"dz": 1}, {"dz": 3}),
    ({"dz": 3}, {"dy": 2}),
)


def step_move(step):
    first, second = across(**STEPS[step][0]), across(**STEPS[step][1])
    return lambda x, y, z, core: (second if core else first)(x, y, z, core)


def slice_of(piece, other):
    tm = lax.axis_index("tmpl")
    y_hi, z, core = tm // 8, (tm // 2) % 4, (tm % 2) ^ other
    change = []
    for which in range(2):
        dy = dz = 0
        for step in range(3):
            if piece >> step & 1:
                dy ^= STEPS[step][which].get("dy", 0) // 2
                dz ^= STEPS[step][which].get("dz", 0)
        change.append((dy, dz))
    dy = jnp.where(core == 0, change[0][0], change[1][0])
    dz = jnp.where(core == 0, change[0][1], change[1][1])
    return (y_hi ^ dy) * 8 + (z ^ dz) * 2 + core


def segment_at(place):
    dt = lax.axis_index("dt")
    return ((dt // 2) ^ (place % 4)) * 2 + ((dt % 2) ^ (place // 4))


def widen_kernel(templ_ref, wide_ref, *binned):
    for ref in binned:
        ref[...] = jnp.zeros_like(ref)
    for k in range(SLOTS):
        h = templ_ref[k, 0].astype(jnp.float32)
        i = templ_ref[k, 1].astype(jnp.float32)
        wide_ref[k, 0] = h
        wide_ref[k, 1] = h + i
        wide_ref[k, 2] = h - i


def whole():
    return pl.BlockSpec(memory_space=pltpu.VMEM)


BINNED = [jax.ShapeDtypeStruct((NBIN, ROWS, 2 * TW), jnp.float32)] * SLOTS


def widen(templates):
    outs = pl.pallas_call(
        widen_kernel,
        out_shape=[jax.ShapeDtypeStruct((SLOTS, 3, NBLK, FB), jnp.float32)] + BINNED,
        in_specs=[whole()],
        out_specs=[whole()] * (1 + SLOTS),
        compiler_params=pltpu.CompilerParams(vmem_limit_bytes=VMEM),
        cost_estimate=pl.CostEstimate(flops=10**6, bytes_accessed=10**6, transcendentals=0),
        name="widen",
    )(templates)
    return outs[0], outs[1:]


def bins_kernel(parts, last, *refs):
    count = len(parts)
    pieces, refs = refs[:count], refs[count:]
    bin_vmem, table_ref, turn_ref, wide_ref, start_ref, local_ref, step_ref = refs[:7]
    refs = refs[7:]
    if last:
        stat_vmem, refs = refs[0], refs[1:]
    refs = refs[SLOTS:]
    binned, refs = refs[:SLOTS], refs[SLOTS:]
    if last:
        out_ref, refs = refs[0], refs[1:]
    prod_ref, rot_ref, bin_ref, sems = refs[:4]
    copies = [pltpu.make_async_copy(bin_vmem, bin_ref, sems.at[0])]
    if last:
        stat_ref, best_ref = refs[4:]
        copies.append(pltpu.make_async_copy(stat_vmem, stat_ref, sems.at[1]))
    for copy in copies:
        copy.start()

    def product(piece_ref, c, jj):
        j = c * JS + jj
        both = piece_ref[0, jj].astype(jnp.float32)
        raw_r, raw_i = both[:ROWS], both[ROWS:]
        rc, rs = rot_ref[0], rot_ref[1]
        sr = raw_r * rc - raw_i * rs
        si = raw_r * rs + raw_i * rc
        su = sr + si
        if jj < JS - 1:
            pc = jnp.concatenate([step_ref[0], step_ref[0]], axis=1)
            ps = jnp.concatenate([step_ref[1], step_ref[1]], axis=1)
            rot_ref[0] = rc * pc - rs * ps
            rot_ref[1] = rc * ps + rs * pc
        for pair in range(SLOTS // 2):
            real, imag = [], []
            for k in (2 * pair, 2 * pair + 1):
                h = wide_ref[k, 0, pl.ds(j, 1), :]
                v = wide_ref[k, 1, pl.ds(j, 1), :]
                w = wide_ref[k, 2, pl.ds(j, 1), :]
                k1 = h * su
                real.append(k1 - si * w)
                imag.append(k1 - sr * v)
            base = jj * SLOTS * ROWS + 2 * ROWS * pair
            rows = slice(base, base + 2 * ROWS)
            prod_ref[rows, :FB] = jnp.concatenate(real, axis=0).astype(jnp.bfloat16)
            prod_ref[rows, FB:] = jnp.concatenate(imag, axis=0).astype(jnp.bfloat16)

    def post(c, jj, series):
        j = c * JS + jj
        cos = turn_ref[c, jj, 0:1, :]
        sin = turn_ref[c, jj, 1:2, :]
        for k in range(SLOTS):
            b = bin_ref[k, j]
            re = series[k * ROWS:(k + 1) * ROWS, :TW]
            im = series[k * ROWS:(k + 1) * ROWS, TW:]
            binned[k][b, :, :TW] += cos * re - sin * im
            binned[k][b, :, TW:] += cos * im + sin * re

    for number, (piece_ref, part) in enumerate(zip(pieces, parts)):
        c = slice_of(*part)
        sc, ss = start_ref[c, 0], start_ref[c, 1]
        for half in range(2):
            cols = slice(half * TW, half * TW + TW)
            lc, ls = local_ref[0, :, cols], local_ref[1, :, cols]
            rot_ref[0, :, cols] = sc * lc - ss * ls
            rot_ref[1, :, cols] = sc * ls + ss * lc
        for jj in range(JS):
            product(piece_ref, c, jj)
        if number == 0:
            for copy in copies:
                copy.wait()
        half = JS // 2
        size = half * SLOTS * ROWS
        for h in range(2):
            series = jnp.dot(
                prod_ref[h * size:(h + 1) * size], table_ref[...], preferred_element_type=jnp.float32
            )
            for m in range(half):
                post(c, h * half + m, series[m * SLOTS * ROWS:(m + 1) * SLOTS * ROWS])

    if last:
        best = jnp.zeros((SEGS, TW), jnp.float32)
        for k in range(SLOTS):
            total = binned[k][0]
            for b in range(1, NBIN):
                total = total + binned[k][b]
            chi = jnp.zeros((ROWS, TW), jnp.float32)
            for b in range(NBIN):
                gap = binned[k][b] - stat_ref[k, b] * total
                gap = gap * gap
                chi = chi + (gap[:, :TW] + gap[:, TW:]) * stat_ref[k, NBIN + b]
            power = total * total
            snr2 = (power[:, :TW] + power[:, TW:]) * stat_ref[k, 2 * NBIN]
            reduced = chi / (2.0 * NBIN - 2.0)
            cube = (1.0 + reduced * reduced * reduced) * 0.5
            factor = jnp.where(reduced > 1.0, jnp.exp(jnp.log(cube) * (-1.0 / 3.0)), 1.0)
            new2 = snr2 * factor
            net2 = new2[:SEGS] + new2[SEGS:2 * SEGS] + new2[2 * SEGS:]
            best = jnp.where(stat_ref[k, 2 * NBIN + 1] > 0.5, jnp.maximum(best, net2), best)
        best = jnp.sqrt(best)
        best_ref[...] = jnp.concatenate(
            [jnp.max(best[:, w * WIN:(w + 1) * WIN], axis=1, keepdims=True) for w in range(NWIN)], axis=1
        )
        for place in range(SEGS):
            out_ref[pl.ds(segment_at(place), 1), :] = best_ref[place:place + 1, :]


def add_bins(pieces, parts, shared, binned, stat=None):
    last = stat is not None
    operands = [*pieces, *shared] + ([stat] if last else []) + list(binned)
    first = len(operands) - SLOTS
    out_shape = list(BINNED)
    scratch = [
        pltpu.VMEM((JS * SLOTS * ROWS, 2 * FB), jnp.bfloat16),
        pltpu.VMEM((2, ROWS, FB), jnp.float32),
        pltpu.SMEM((SLOTS, NBLK), jnp.int32),
        pltpu.SemaphoreType.DMA((2,)),
    ]
    if last:
        out_shape.append(jax.ShapeDtypeStruct((SEGS, NWIN), jnp.float32))
        scratch += [pltpu.SMEM((SLOTS, 2 * NBIN + 2), jnp.float32), pltpu.VMEM((SEGS, NWIN), jnp.float32)]
    flops = len(parts) * 2 * JS * SLOTS * ROWS * 2 * FB * 2 * TW
    return pl.pallas_call(
        functools.partial(bins_kernel, parts, last),
        out_shape=out_shape,
        in_specs=[whole()] * len(operands),
        out_specs=[whole()] * len(out_shape),
        scratch_shapes=scratch,
        input_output_aliases={first + k: k for k in range(SLOTS)},
        compiler_params=pltpu.CompilerParams(vmem_limit_bytes=VMEM),
        cost_estimate=pl.CostEstimate(flops=2 * flops, bytes_accessed=10**6, transcendentals=0),
        name="last_bins" if last else "add_bins",
    )(*operands)


def per_device(strain, templates, live_count, chi_edges, shifts):
    wide, binned = widen(templates)

    x = jnp.transpose(strain[0], (2, 1, 0, 3)).reshape(JS, 2 * NDET, 1, FB)
    got = {0: x}
    for dx in (2, 3, 1):
        got[dx] = swap_with(x, across(dx=dx))
    x = jnp.concatenate([got[dx] for dx in range(4)], axis=2)
    x = jnp.concatenate([x, swap_with(x, across(dy=1))], axis=2)
    own = [x.reshape(1, JS, 2 * ROWS, FB)]

    blocks = jnp.arange(NBLK, dtype=jnp.int32)
    bin_of = jnp.sum((chi_edges[:, :, None] <= blocks[None, None, :]).astype(jnp.int32), axis=1)
    labels = jnp.arange(NBIN, dtype=jnp.int32)
    onehot = (bin_of[:, None, :] == labels[None, :, None]).astype(jnp.float32)
    full = templates.astype(jnp.float32)
    block_power = jnp.sum(full * full, axis=(1, 3))
    sigma2 = jnp.sum(block_power, axis=1) + EPSILON
    in_bins = jnp.sum(onehot * block_power[:, None, :], axis=2)
    frac = (in_bins + EPSILON) / sigma2[:, None]
    inv = 1.0 / (frac * sigma2[:, None])
    half = 1.0 / (2.0 * sigma2)
    live = (jnp.arange(SLOTS, dtype=jnp.int32) < live_count[0, 0]).astype(jnp.float32)
    stat = jnp.concatenate([frac, inv, half[:, None], live[:, None]], axis=1)

    order = segment_at(jnp.arange(SEGS, dtype=jnp.int32))
    first = (MARGIN + jnp.take(shifts, order, axis=0)).T.reshape(ROWS)
    bins = jnp.arange(FB, dtype=jnp.int32)
    local = phase((first[:, None] * bins[None, :] * STRIDE) % NFFT)
    starts = (FLOW // FB + jnp.arange(NSL, dtype=jnp.int32) * JS) * FB
    start = phase((first[None, :] * starts[:, None]) % NFFT)
    start = jnp.broadcast_to(jnp.transpose(start, (1, 0, 2))[..., None], (NSL, 2, ROWS, TW))
    step = phase(first * FB)
    step = jnp.broadcast_to(step[..., None], (2, ROWS, TW))
    table, turn = tables()
    shared = (bin_of, table, turn, wide, start, local, step)

    others = [swap_with(own[0], across(dcore=1))]
    for number in range(3):
        fresh = [swap_with(piece, step_move(number)) for piece in own]
        own += fresh
        others += [swap_with(piece, across(dcore=1)) for piece in fresh]
    for p in range(7):
        binned = add_bins((own[p], others[p]), ((p, 0), (p, 1)), shared, binned)
    binned = add_bins((own[7],), ((7, 0),), shared, binned)
    best = add_bins((others[7],), ((7, 1),), shared, binned, stat)[-1]
    for move in (across(dcore=1), across(dz=1), across(dz=3), across(dy=2)):
        best = jnp.maximum(best, swap_with(best, move))
    return best[:, None, :]


def solution(mesh):
    in_specs = (
        P("dt", None, None, "tmpl", None),
        P(("dt", "tmpl"), None, None, None),
        P("dt", "tmpl"),
        P(("dt", "tmpl"), None),
        P(),
    )
    out_specs = P(None, "dt", None)
    return jax.shard_map(
        per_device, mesh=mesh, in_specs=in_specs, out_specs=out_specs, check_vma=False
    )
```

time: 75.8 us -> 73.2 us (0.966)
  waiting for transfers between devices: 29.9 us -> 12.2 us
  starting transfers between devices: 23.2 us -> 31.6 us
  Pallas kernels: 16.5 us -> 21.1 us
  other arithmetic: 2 us -> 4.06 us
    ppermute x16 -> x23, waiting for transfers between devices: 29.9 us -> 12.2 us  [swap_with(): return lax.ppermute(value, AXES, pairs)]
    ppermute x16 -> x23, starting transfers between devices: 23.2 us -> 31.6 us  [swap_with(): return lax.ppermute(value, AXES, pairs)]
    pallas_call x1 -> x10, Pallas kernels: 16.5 us -> 21.1 us  [the longest x9 20.6 us: add_bins(): pl.pallas_call(functools.partial(bins_kernel, parts, last), out_shape=out...]
    reduce_sum x1, other arithmetic: 0.55 us -> 1.84 us  [per_device(): block_power = jnp.sum(full * full, axis=(1, 3))]
    unnamed x22 -> x12, local copies, waits for them, and re-layouts: 1.71 us -> 1.62 us
  transfers between devices with their start and end apart: 16 -> 23, of which waited for: 10 -> 7; matrix products, arithmetic and copies ran while one was open for 4% -> 8% of each run, Pallas kernels for 0% -> 25%
where the time goes in v4:
time: 73.2 us; the launch traced here: 73 us
  starting transfers between devices  31.6 us (43%)
  Pallas kernels  21.1 us (29%)
  waiting for transfers between devices  12.2 us (17%)
  other arithmetic  4.06 us (6%)
  local copies, waits for them, and re-layouts  3.06 us (4%)
  between operations  0.97 us (1%)
    ppermute x23, starting transfers between devices, swap_with(): return lax.ppermute(value, AXES, pairs)  31.6 us
    pallas_call x9, Pallas kernels, add_bins(): pl.pallas_call(functools.partial(bins_kernel, parts, last), out_shape=out...  20.6 us
    ppermute x23, waiting for transfers between devices, swap_with(): return lax.ppermute(value, AXES, pairs)  12.2 us
    reduce_sum x1, other arithmetic, per_device(): block_power = jnp.sum(full * full, axis=(1, 3))  1.84 us
    unnamed x12, local copies, waits for them, and re-layouts  1.62 us
  transfers between devices with their start and end apart: 23, of which 7 were waited for; matrix products, arithmetic and copies ran while one was open for 8% of the time, Pallas kernels for 25%

profile of v4, /device:TPU:0, one launch (start us, length us, event | category | flops | bytes accessed | tf_op | source)
XLA Modules:
  0.0 73.0 jit_solution(8689050592589655105)
XLA Ops:
  0.0 0.8 %copy.138 = bf16[1,3,2,6,256]{4,3,1,2,0:T(8,128)(2,1)S(1)} copy(bf16[1,3,2,6,256]{4,2,3,1,0:T(2,128)(2,1)} %param.7) | data formatting | bytes 36864 | tf_op args[0]
  0.9 1.6 %collective-permute-start = (bf16[6,6,1,256]{3,0,1,2:T(8,128)(2,1)S(1)}, bf16[6,6,1,256]{3,0,1,2:T(8,128)(2,1)S(1)}, u32[]{:S(2)}, u32[]{:S(2)}) collective-permute-start(bf16[6,6,1,256]{3,0,1,2:T(8,128)(2,1)S(1)} %bitcast.27), channel_id=1, source_target_pairs={{0,32},{1,33},{2,34},{3,35},{4,36},{5,37},{6,38},{7,39},{8,40},{9,... | collective-permute-start | bytes 55304 | tf_op jit(solution)/shard_map/ppermute | solution.py:51
  2.4 2.7 %collective-permute-start.1 = (bf16[6,6,1,256]{3,0,1,2:T(8,128)(2,1)S(1)}, bf16[6,6,1,256]{3,0,1,2:T(8,128)(2,1)S(1)}, u32[]{:S(2)}, u32[]{:S(2)}) collective-permute-start(bf16[6,6,1,256]{3,0,1,2:T(8,128)(2,1)S(1)} %bitcast.28), channel_id=1, source_target_pairs={{0,64},{1,65},{2,66},{3,67},{4,68},{5,69},{6,70},{7,71},{8,72},{9,... | collective-permute-start | bytes 55304 | tf_op jit(solution)/shard_map/ppermute | solution.py:51
  5.2 0.4 collective-permute-start.2
  5.6 0.8 %copy.140 = s32[8,3]{1,0:T(8,128)S(1)} copy(s32[8,3]{0,1:T(4,128)} %param.11) | data formatting | bytes 192 | tf_op args[4]
  6.4 0.6 gather_fusion
  6.9 0.1 fusion.14
  7.3 0.2 fusion.6
  7.4 0.1 fusion.12
  7.6 0.8 %convert_reduce_fusion.refs_2_.refs_1_ = s32[12,96]{1,0:T(8,128)S(1)} fusion(s32[12,15]{1,0:T(8,128)} %param.10), kind=kLoop, calls=%fused_computation.8 | loop fusion | flops 50688 | bytes 5328 | tf_op jit(solution)/shard_map/reduce_sum | solution.py:281
  8.4 1.8 %fusion.1 = (f32[12,96]{1,0:T(8,128)S(1)}, f32[12]{0:T(128)S(1)}) fusion(bf16[12,2,96,256]{3,2,1,0:T(8,128)(2,1)} %templ_ref.1), kind=kLoop, calls=%fused_computation.3 | loop fusion | flops 2358132 | bytes 1184304 | tf_op jit(solution)/shard_map/reduce_sum | solution.py:285
  10.2 0.1 copy.145
  11.0 0.1 select_reduce_fusion
  11.7 1.7 %collective-permute-start.3 = (bf16[6,6,4,256]{3,0,1,2:T(8,128)(2,1)S(1)}, bf16[6,6,4,256]{3,0,1,2:T(8,128)(2,1)S(1)}, u32[]{:S(2)}, u32[]{:S(2)}) collective-permute-start(bf16[6,6,4,256]{3,0,1,2:T(8,128)(2,1)S(1)} %pad_maximum_fusion), channel_id=1, source_target_pairs={{0,16},{1,17},{2,18},{3,19},{4,20},{5,21},{6,22},{7,23},{8,24},{9,... | collective-permute-start | bytes 221192 | tf_op jit(solution)/shard_map/ppermute | solution.py:51
  13.4 2.9 %collective-permute-done.3 = bf16[6,6,4,256]{3,0,1,2:T(8,128)(2,1)S(1)} collective-permute-done((bf16[6,6,4,256]{3,0,1,2:T(8,128)(2,1)S(1)}, bf16[6,6,4,256]{3,0,1,2:T(8,128)(2,1)S(1)}, u32[]{:S(2)}, u32[]{:S(2)}) %collective-permute-start.3) | collective-permute-done | bytes 73760 | tf_op jit(solution)/shard_map/ppermute | solution.py:51
  16.4 0.1 collective-permute-start.18
  16.5 3.4 %collective-permute-start.4 = (bf16[1,6,48,256]{3,2,1,0:T(8,128)(2,1)S(1)}, bf16[1,6,48,256]{3,2,1,0:T(8,128)(2,1)S(1)}, u32[]{:S(2)}, u32[]{:S(2)}) collective-permute-start(bf16[1,6,48,256]{3,2,1,0:T(8,128)(2,1)S(1)} %bitcast.23), channel_id=1, source_target_pairs={{0,8},{1,3},{2,10},{3,1},{4,12},{5,7},{6,14},{7,5},{8,0},{9,11},{1... | collective-permute-start | bytes 442376 | tf_op jit(solution)/shard_map/ppermute | solution.py:51
  19.9 1.9 %collective-permute-start.8 = (bf16[1,6,48,256]{3,2,1,0:T(8,128)(2,1)S(1)}, bf16[1,6,48,256]{3,2,1,0:T(8,128)(2,1)S(1)}, u32[]{:S(2)}, u32[]{:S(2)}) collective-permute-start(bf16[1,6,48,256]{3,2,1,0:T(8,128)(2,1)S(1)} %bitcast.24), channel_id=1, source_target_pairs={{0,2},{1,7},{2,0},{3,5},{4,6},{5,3},{6,4},{7,1},{8,10},{9,15},{10,... | collective-permute-start | bytes 442376 | tf_op jit(solution)/shard_map/ppermute | solution.py:51
  21.8 0.5 widen.1
  22.4 2.6 %collective-permute-start.13 = (bf16[1,6,48,256]{3,2,1,0:T(8,128)(2,1)S(1)}, bf16[1,6,48,256]{3,2,1,0:T(8,128)(2,1)S(1)}, u32[]{:S(2)}, u32[]{:S(2)}) collective-permute-start(bf16[1,6,48,256]{3,2,1,0:T(8,128)(2,1)S(1)} %bitcast.25), channel_id=1, source_target_pairs={{0,6},{1,9},{2,4},{3,11},{4,2},{5,13},{6,0},{7,15},{8,14},{9,1},{1... | collective-permute-start | bytes 442376 | tf_op jit(solution)/shard_map/ppermute | solution.py:51
  25.0 1.0 %collective-permute-start.5 = (bf16[1,6,48,256]{3,2,1,0:T(8,128)(2,1)S(1)}, bf16[1,6,48,256]{3,2,1,0:T(8,128)(2,1)S(1)}, u32[]{:S(2)}, u32[]{:S(2)}) collective-permute-start(bf16[1,6,48,256]{3,2,1,0:T(8,128)(2,1)S(1)} %collective-permute-done.4.refs_0_), channel_id=1, source_target_pairs={{0,2},{1,7},{2,0},{3,5},{4,6},{5,3},{6,4},{7,1},{8,10},{9,15},{10,... | collective-permute-start | bytes 442376 | tf_op jit(solution)/shard_map/ppermute | solution.py:51
  26.0 2.4 %collective-permute-start.11 = (bf16[1,6,48,256]{3,2,1,0:T(8,128)(2,1)S(1)}, bf16[1,6,48,256]{3,2,1,0:T(8,128)(2,1)S(1)}, u32[]{:S(2)}, u32[]{:S(2)}) collective-permute-start(bf16[1,6,48,256]{3,2,1,0:T(8,128)(2,1)S(1)} %collective-permute-done.4.refs_0_), channel_id=1, source_target_pairs={{0,6},{1,9},{2,4},{3,11},{4,2},{5,13},{6,0},{7,15},{8,14},{9,1},{1... | collective-permute-start | bytes 442376 | tf_op jit(solution)/shard_map/ppermute | solution.py:51
  28.4 3.1 %collective-permute-start.16 = (bf16[1,6,48,256]{3,2,1,0:T(8,128)(2,1)S(1)}, bf16[1,6,48,256]{3,2,1,0:T(8,128)(2,1)S(1)}, u32[]{:S(2)}, u32[]{:S(2)}) collective-permute-start(bf16[1,6,48,256]{3,2,1,0:T(8,128)(2,1)S(1)} %collective-permute-done.8.refs_0_), channel_id=1, source_target_pairs={{0,1},{1,0},{2,3},{3,2},{4,5},{5,4},{6,7},{7,6},{8,9},{9,8},{10,11... | collective-permute-start | bytes 442376 | tf_op jit(solution)/shard_map/ppermute | solution.py:51
  31.5 0.2 broadcast_in_dim.13.refs_6_.refs_5_
  31.8 2.3 %add_bins.8 = (f32[16,24,256]{2,1,0:T(8,128)S(1)}, f32[16,24,256]{2,1,0:T(8,128)S(1)}, f32[16,24,256]{2,1,0:T(8,128)S(1)}, f32[16,24,256]{2,1,0:T(8,128)S(1)}, f...) custom-call(bf16[1,6,48,256]{3,2,1,0:T(8,128)(2,1)S(1)} %bitcast.26,, ...), custom_call_target="tpu_custom_call", output_to_operand_aliasing={{0}: (9, {}), {1}: (10, {}), {2}: (11, {}), {3}: (12, {}), ... | custom-call | flops 1811939328 | bytes 1000000 | tf_op jit(solution)/shard_map/add_bins/pallas_call | solution.py:256
  34.1 0.4 collective-permute-start.9
  34.5 0.5 collective-permute-start.15
  35.0 2.3 %add_bins.9 = (f32[16,24,256]{2,1,0:T(8,128)S(1)}, f32[16,24,256]{2,1,0:T(8,128)S(1)}, f32[16,24,256]{2,1,0:T(8,128)S(1)}, f32[16,24,256]{2,1,0:T(8,128)S(1)}, f...) custom-call(bf16[1,6,48,256]{3,2,1,0:T(8,128)(2,1)S(1)} %collective-, ...), custom_call_target="tpu_custom_call", output_to_operand_aliasing={{0}: (9, {}), {1}: (10, {}), {2}: (11, {}), {3}: (12, {}), ... | custom-call | flops 1811939328 | bytes 1000000 | tf_op jit(solution)/shard_map/add_bins/pallas_call | solution.py:256
  37.3 3.0 %collective-permute-start.6 = (bf16[1,6,48,256]{3,2,1,0:T(8,128)(2,1)S(1)}, bf16[1,6,48,256]{3,2,1,0:T(8,128)(2,1)S(1)}, u32[]{:S(2)}, u32[]{:S(2)}) collective-permute-start(bf16[1,6,48,256]{3,2,1,0:T(8,128)(2,1)S(1)} %collective-permute-done.5.refs_0_), channel_id=1, source_target_pairs={{0,6},{1,9},{2,4},{3,11},{4,2},{5,13},{6,0},{7,15},{8,14},{9,1},{1... | collective-permute-start | bytes 442376 | tf_op jit(solution)/shard_map/ppermute | solution.py:51
  40.3 0.2 collective-permute-done.9.refs_0_
  40.5 0.3 collective-permute-start.10
  40.9 2.3 %add_bins.10 = (f32[16,24,256]{2,1,0:T(8,128)S(1)}, f32[16,24,256]{2,1,0:T(8,128)S(1)}, f32[16,24,256]{2,1,0:T(8,128)S(1)}, f32[16,24,256]{2,1,0:T(8,128)S(1)}, ...) custom-call(bf16[1,6,48,256]{3,2,1,0:T(8,128)(2,1)S(1)} %collective-, ...), custom_call_target="tpu_custom_call", output_to_operand_aliasing={{0}: (9, {}), {1}: (10, {}), {2}: (11, {}), {3}: (12, {}), ... | custom-call | flops 1811939328 | bytes 1000000 | tf_op jit(solution)/shard_map/add_bins/pallas_call | solution.py:256
  43.2 0.5 collective-permute-done.6.refs_0_
  43.7 2.3 %add_bins.11 = (f32[16,24,256]{2,1,0:T(8,128)S(1)}, f32[16,24,256]{2,1,0:T(8,128)S(1)}, f32[16,24,256]{2,1,0:T(8,128)S(1)}, f32[16,24,256]{2,1,0:T(8,128)S(1)}, ...) custom-call(bf16[1,6,48,256]{3,2,1,0:T(8,128)(2,1)S(1)} %collective-, ...), custom_call_target="tpu_custom_call", output_to_operand_aliasing={{0}: (9, {}), {1}: (10, {}), {2}: (11, {}), {3}: (12, {}), ... | custom-call | flops 1811939328 | bytes 1000000 | tf_op jit(solution)/shard_map/add_bins/pallas_call | solution.py:256
  46.1 2.3 %add_bins.12 = (f32[16,24,256]{2,1,0:T(8,128)S(1)}, f32[16,24,256]{2,1,0:T(8,128)S(1)}, f32[16,24,256]{2,1,0:T(8,128)S(1)}, f32[16,24,256]{2,1,0:T(8,128)S(1)}, ...) custom-call(bf16[1,6,48,256]{3,2,1,0:T(8,128)(2,1)S(1)} %collective-, ...), custom_call_target="tpu_custom_call", output_to_operand_aliasing={{0}: (9, {}), {1}: (10, {}), {2}: (11, {}), {3}: (12, {}), ... | custom-call | flops 1811939328 | bytes 1000000 | tf_op jit(solution)/shard_map/add_bins/pallas_call | solution.py:256
  48.4 2.3 %add_bins.13 = (f32[16,24,256]{2,1,0:T(8,128)S(1)}, f32[16,24,256]{2,1,0:T(8,128)S(1)}, f32[16,24,256]{2,1,0:T(8,128)S(1)}, f32[16,24,256]{2,1,0:T(8,128)S(1)}, ...) custom-call(bf16[1,6,48,256]{3,2,1,0:T(8,128)(2,1)S(1)} %collective-, ...), custom_call_target="tpu_custom_call", output_to_operand_aliasing={{0}: (9, {}), {1}: (10, {}), {2}: (11, {}), {3}: (12, {}), ... | custom-call | flops 1811939328 | bytes 1000000 | tf_op jit(solution)/shard_map/add_bins/pallas_call | solution.py:256
  50.8 2.4 %add_bins.14 = (f32[16,24,256]{2,1,0:T(8,128)S(1)}, f32[16,24,256]{2,1,0:T(8,128)S(1)}, f32[16,24,256]{2,1,0:T(8,128)S(1)}, f32[16,24,256]{2,1,0:T(8,128)S(1)}, ...) custom-call(bf16[1,6,48,256]{3,2,1,0:T(8,128)(2,1)S(1)} %collective-, ...), custom_call_target="tpu_custom_call", output_to_operand_aliasing={{0}: (9, {}), {1}: (10, {}), {2}: (11, {}), {3}: (12, {}), ... | custom-call | flops 1811939328 | bytes 1000000 | tf_op jit(solution)/shard_map/add_bins/pallas_call | solution.py:256
  53.1 1.4 %add_bins.15 = (f32[16,24,256]{2,1,0:T(8,128)S(1)}, f32[16,24,256]{2,1,0:T(8,128)S(1)}, f32[16,24,256]{2,1,0:T(8,128)S(1)}, f32[16,24,256]{2,1,0:T(8,128)S(1)}, ...) custom-call(bf16[1,6,48,256]{3,2,1,0:T(8,128)(2,1)S(1)} %collective-, ...), custom_call_target="tpu_custom_call", output_to_operand_aliasing={{0}: (8, {}), {1}: (9, {}), {2}: (10, {}), {3}: (11, {}), {... | custom-call | flops 905969664 | bytes 1000000 | tf_op jit(solution)/shard_map/add_bins/pallas_call | solution.py:256
  54.6 2.8 %last_bins.1 = (f32[16,24,256]{2,1,0:T(8,128)S(1)}, f32[16,24,256]{2,1,0:T(8,128)S(1)}, f32[16,24,256]{2,1,0:T(8,128)S(1)}, f32[16,24,256]{2,1,0:T(8,128)S(1)}, ...) custom-call(bf16[1,6,48,256]{3,2,1,0:T(8,128)(2,1)S(1)} %collective-, ...), custom_call_target="tpu_custom_call", output_to_operand_aliasing={{0}: (9, {}), {1}: (10, {}), {2}: (11, {}), {3}: (12, {}), ... | custom-call | flops 905969664 | bytes 1000000 | tf_op jit(solution)/shard_map/last_bins/pallas_call | solution.py:256
  57.5 0.6 collective-permute-start.19
  58.1 0.8 %collective-permute-done.19 = f32[8,8]{1,0:T(8,128)S(1)} collective-permute-done((f32[8,8]{1,0:T(8,128)S(1)}, f32[8,8]{1,0:T(8,128)S(1)}, u32[]{:S(2)}, u32[]{:S(2)}) %collective-permute-start.19) | collective-permute-done | bytes 288 | tf_op jit(solution)/shard_map/ppermute | solution.py:51
  58.9 0.4 collective-permute-start.20
  59.3 3.2 %collective-permute-done.20 = f32[8,8]{1,0:T(8,128)S(1)} collective-permute-done((f32[8,8]{1,0:T(8,128)S(1)}, f32[8,8]{1,0:T(8,128)S(1)}, u32[]{:S(2)}, u32[]{:S(2)}) %collective-permute-start.20) | collective-permute-done | bytes 288 | tf_op jit(solution)/shard_map/ppermute | solution.py:51
  62.5 2.9 %collective-permute-start.21 = (f32[8,8]{1,0:T(8,128)S(1)}, f32[8,8]{1,0:T(8,128)S(1)}, u32[]{:S(2)}, u32[]{:S(2)}) collective-permute-start(f32[8,8]{1,0:T(8,128)S(1)} %max.13), channel_id=1, source_target_pairs={{0,6},{1,7},{2,4},{3,5},{4,2},{5,3},{6,0},{7,1},{8,14},{9,15},{10,... | collective-permute-start | bytes 776 | tf_op jit(solution)/shard_map/ppermute | solution.py:51
  65.4 1.9 %collective-permute-done.21 = f32[8,8]{1,0:T(8,128)S(1)} collective-permute-done((f32[8,8]{1,0:T(8,128)S(1)}, f32[8,8]{1,0:T(8,128)S(1)}, u32[]{:S(2)}, u32[]{:S(2)}) %collective-permute-start.21) | collective-permute-done | bytes 288 | tf_op jit(solution)/shard_map/ppermute | solution.py:51
  67.3 2.5 %collective-permute-start.22 = (f32[8,8]{1,0:T(8,128)S(1)}, f32[8,8]{1,0:T(8,128)S(1)}, u32[]{:S(2)}, u32[]{:S(2)}) collective-permute-start(f32[8,8]{1,0:T(8,128)S(1)} %max.14), channel_id=1, source_target_pairs={{0,8},{1,9},{2,10},{3,11},{4,12},{5,13},{6,14},{7,15},{8,0},{9,1},... | collective-permute-start | bytes 776 | tf_op jit(solution)/shard_map/ppermute | solution.py:51
  69.8 2.6 %collective-permute-done.22 = f32[8,8]{1,0:T(8,128)S(1)} collective-permute-done((f32[8,8]{1,0:T(8,128)S(1)}, f32[8,8]{1,0:T(8,128)S(1)}, u32[]{:S(2)}, u32[]{:S(2)}) %collective-permute-start.22) | collective-permute-done | bytes 288 | tf_op jit(solution)/shard_map/ppermute | solution.py:51
  72.4 0.6 max.15
  (56 shorter events, 1.1 us)
Async XLA Ops:
  0.0 31.7 %copy-start = (bf16[512,256]{1,0:T(8,128)(2,1)S(1)}, bf16[512,256]{1,0:T(8,128)(2,1)}, u32[]{:S(2)}) copy-start(bf16[512,256]{1,0:T(8,128)(2,1)} %constant.131.clone.refs_3_.refs_2_) | copy-start | bytes 786436
  0.0 31.7 %copy-start.1 = (f32[16,6,2,128]{3,2,1,0:T(2,128)S(1)}, f32[16,6,2,128]{3,2,1,0:T(2,128)}, u32[]{:S(2)}) copy-start(f32[16,6,2,128]{3,2,1,0:T(2,128)} %constant.132.clone.refs_4_.refs_3_) | copy-start | bytes 294916
  0.0 21.8 %copy-start.2 = (bf16[12,2,96,256]{3,2,1,0:T(8,128)(2,1)S(1)}, bf16[12,2,96,256]{3,2,1,0:T(8,128)(2,1)}, u32[]{:S(2)}) copy-start(bf16[12,2,96,256]{3,2,1,0:T(8,128)(2,1)} %templ_ref.1) | copy-start | bytes 3538948
  0.9 10.8 %collective-permute-start = (bf16[6,6,1,256]{3,0,1,2:T(8,128)(2,1)S(1)}, bf16[6,6,1,256]{3,0,1,2:T(8,128)(2,1)S(1)}, u32[]{:S(2)}, u32[]{:S(2)}) collective-permute-start(bf16[6,6,1,256]{3,0,1,2:T(8,128)(2,1)S(1)} %bitcast.27), channel_id=1, source_target_pairs={{0,32},{1,33},{2,34},{3,35},{4,36},{5,37},{6,38},{7,39},{8,40},{9,... | collective-permute-start | bytes 55304 | tf_op jit(solution)/shard_map/ppermute | solution.py:51
  2.4 9.2 %collective-permute-start.1 = (bf16[6,6,1,256]{3,0,1,2:T(8,128)(2,1)S(1)}, bf16[6,6,1,256]{3,0,1,2:T(8,128)(2,1)S(1)}, u32[]{:S(2)}, u32[]{:S(2)}) collective-permute-start(bf16[6,6,1,256]{3,0,1,2:T(8,128)(2,1)S(1)} %bitcast.28), channel_id=1, source_target_pairs={{0,64},{1,65},{2,66},{3,67},{4,68},{5,69},{6,70},{7,71},{8,72},{9,... | collective-permute-start | bytes 55304 | tf_op jit(solution)/shard_map/ppermute | solution.py:51
  5.2 6.5 %collective-permute-start.2 = (bf16[6,6,1,256]{3,0,1,2:T(8,128)(2,1)S(1)}, bf16[6,6,1,256]{3,0,1,2:T(8,128)(2,1)S(1)}, u32[]{:S(2)}, u32[]{:S(2)}) collective-permute-start(bf16[6,6,1,256]{3,0,1,2:T(8,128)(2,1)S(1)} %bitcast.29), channel_id=1, source_target_pairs={{0,96},{1,97},{2,98},{3,99},{4,100},{5,101},{6,102},{7,103},{8,104... | collective-permute-start | bytes 55304 | tf_op jit(solution)/shard_map/ppermute | solution.py:51
  11.7 4.7 %collective-permute-start.3 = (bf16[6,6,4,256]{3,0,1,2:T(8,128)(2,1)S(1)}, bf16[6,6,4,256]{3,0,1,2:T(8,128)(2,1)S(1)}, u32[]{:S(2)}, u32[]{:S(2)}) collective-permute-start(bf16[6,6,4,256]{3,0,1,2:T(8,128)(2,1)S(1)} %pad_maximum_fusion), channel_id=1, source_target_pairs={{0,16},{1,17},{2,18},{3,19},{4,20},{5,21},{6,22},{7,23},{8,24},{9,... | collective-permute-start | bytes 221192 | tf_op jit(solution)/shard_map/ppermute | solution.py:51
  16.4 9.6 %collective-permute-start.18 = (bf16[1,6,48,256]{3,2,1,0:T(8,128)(2,1)S(1)}, bf16[1,6,48,256]{3,2,1,0:T(8,128)(2,1)S(1)}, u32[]{:S(2)}, u32[]{:S(2)}) collective-permute-start(bf16[1,6,48,256]{3,2,1,0:T(8,128)(2,1)S(1)} %bitcast.22), channel_id=1, source_target_pairs={{0,1},{1,0},{2,3},{3,2},{4,5},{5,4},{6,7},{7,6},{8,9},{9,8},{10,11... | collective-permute-start | bytes 442376 | tf_op jit(solution)/shard_map/ppermute | solution.py:51
  16.5 8.5 %collective-permute-start.4 = (bf16[1,6,48,256]{3,2,1,0:T(8,128)(2,1)S(1)}, bf16[1,6,48,256]{3,2,1,0:T(8,128)(2,1)S(1)}, u32[]{:S(2)}, u32[]{:S(2)}) collective-permute-start(bf16[1,6,48,256]{3,2,1,0:T(8,128)(2,1)S(1)} %bitcast.23), channel_id=1, source_target_pairs={{0,8},{1,3},{2,10},{3,1},{4,12},{5,7},{6,14},{7,5},{8,0},{9,11},{1... | collective-permute-start | bytes 442376 | tf_op jit(solution)/shard_map/ppermute | solution.py:51
  19.9 8.5 %collective-permute-start.8 = (bf16[1,6,48,256]{3,2,1,0:T(8,128)(2,1)S(1)}, bf16[1,6,48,256]{3,2,1,0:T(8,128)(2,1)S(1)}, u32[]{:S(2)}, u32[]{:S(2)}) collective-permute-start(bf16[1,6,48,256]{3,2,1,0:T(8,128)(2,1)S(1)} %bitcast.24), channel_id=1, source_target_pairs={{0,2},{1,7},{2,0},{3,5},{4,6},{5,3},{6,4},{7,1},{8,10},{9,15},{10,... | collective-permute-start | bytes 442376 | tf_op jit(solution)/shard_map/ppermute | solution.py:51
  22.4 11.7 %collective-permute-start.13 = (bf16[1,6,48,256]{3,2,1,0:T(8,128)(2,1)S(1)}, bf16[1,6,48,256]{3,2,1,0:T(8,128)(2,1)S(1)}, u32[]{:S(2)}, u32[]{:S(2)}) collective-permute-start(bf16[1,6,48,256]{3,2,1,0:T(8,128)(2,1)S(1)} %bitcast.25), channel_id=1, source_target_pairs={{0,6},{1,9},{2,4},{3,11},{4,2},{5,13},{6,0},{7,15},{8,14},{9,1},{1... | collective-permute-start | bytes 442376 | tf_op jit(solution)/shard_map/ppermute | solution.py:51
  25.0 9.4 %collective-permute-start.17 = (bf16[1,6,48,256]{3,2,1,0:T(8,128)(2,1)S(1)}, bf16[1,6,48,256]{3,2,1,0:T(8,128)(2,1)S(1)}, u32[]{:S(2)}, u32[]{:S(2)}) collective-permute-start(bf16[1,6,48,256]{3,2,1,0:T(8,128)(2,1)S(1)} %collective-permute-done.4.refs_0_), channel_id=1, source_target_pairs={{0,1},{1,0},{2,3},{3,2},{4,5},{5,4},{6,7},{7,6},{8,9},{9,8},{10,11... | collective-permute-start | bytes 442376 | tf_op jit(solution)/shard_map/ppermute | solution.py:51
  25.0 9.5 %collective-permute-start.5 = (bf16[1,6,48,256]{3,2,1,0:T(8,128)(2,1)S(1)}, bf16[1,6,48,256]{3,2,1,0:T(8,128)(2,1)S(1)}, u32[]{:S(2)}, u32[]{:S(2)}) collective-permute-start(bf16[1,6,48,256]{3,2,1,0:T(8,128)(2,1)S(1)} %collective-permute-done.4.refs_0_), channel_id=1, source_target_pairs={{0,2},{1,7},{2,0},{3,5},{4,6},{5,3},{6,4},{7,1},{8,10},{9,15},{10,... | collective-permute-start | bytes 442376 | tf_op jit(solution)/shard_map/ppermute | solution.py:51
  26.0 14.3 %collective-permute-start.11 = (bf16[1,6,48,256]{3,2,1,0:T(8,128)(2,1)S(1)}, bf16[1,6,48,256]{3,2,1,0:T(8,128)(2,1)S(1)}, u32[]{:S(2)}, u32[]{:S(2)}) collective-permute-start(bf16[1,6,48,256]{3,2,1,0:T(8,128)(2,1)S(1)} %collective-permute-done.4.refs_0_), channel_id=1, source_target_pairs={{0,6},{1,9},{2,4},{3,11},{4,2},{5,13},{6,0},{7,15},{8,14},{9,1},{1... | collective-permute-start | bytes 442376 | tf_op jit(solution)/shard_map/ppermute | solution.py:51
  28.4 8.8 %collective-permute-start.16 = (bf16[1,6,48,256]{3,2,1,0:T(8,128)(2,1)S(1)}, bf16[1,6,48,256]{3,2,1,0:T(8,128)(2,1)S(1)}, u32[]{:S(2)}, u32[]{:S(2)}) collective-permute-start(bf16[1,6,48,256]{3,2,1,0:T(8,128)(2,1)S(1)} %collective-permute-done.8.refs_0_), channel_id=1, source_target_pairs={{0,1},{1,0},{2,3},{3,2},{4,5},{5,4},{6,7},{7,6},{8,9},{9,8},{10,11... | collective-permute-start | bytes 442376 | tf_op jit(solution)/shard_map/ppermute | solution.py:51
  34.1 6.4 %collective-permute-start.9 = (bf16[1,6,48,256]{3,2,1,0:T(8,128)(2,1)S(1)}, bf16[1,6,48,256]{3,2,1,0:T(8,128)(2,1)S(1)}, u32[]{:S(2)}, u32[]{:S(2)}) collective-permute-start(bf16[1,6,48,256]{3,2,1,0:T(8,128)(2,1)S(1)} %collective-permute-done.8.refs_0_), channel_id=1, source_target_pairs={{0,6},{1,9},{2,4},{3,11},{4,2},{5,13},{6,0},{7,15},{8,14},{9,1},{1... | collective-permute-start | bytes 442376 | tf_op jit(solution)/shard_map/ppermute | solution.py:51
  34.5 11.6 %collective-permute-start.14 = (bf16[1,6,48,256]{3,2,1,0:T(8,128)(2,1)S(1)}, bf16[1,6,48,256]{3,2,1,0:T(8,128)(2,1)S(1)}, u32[]{:S(2)}, u32[]{:S(2)}) collective-permute-start(bf16[1,6,48,256]{3,2,1,0:T(8,128)(2,1)S(1)} %collective-permute-done.13.refs_0_), channel_id=1, source_target_pairs={{0,1},{1,0},{2,3},{3,2},{4,5},{5,4},{6,7},{7,6},{8,9},{9,8},{10,11... | collective-permute-start | bytes 442376 | tf_op jit(solution)/shard_map/ppermute | solution.py:51
  34.5 9.2 %collective-permute-start.15 = (bf16[1,6,48,256]{3,2,1,0:T(8,128)(2,1)S(1)}, bf16[1,6,48,256]{3,2,1,0:T(8,128)(2,1)S(1)}, u32[]{:S(2)}, u32[]{:S(2)}) collective-permute-start(bf16[1,6,48,256]{3,2,1,0:T(8,128)(2,1)S(1)} %collective-permute-done.5.refs_0_), channel_id=1, source_target_pairs={{0,1},{1,0},{2,3},{3,2},{4,5},{5,4},{6,7},{7,6},{8,9},{9,8},{10,11... | collective-permute-start | bytes 442376 | tf_op jit(solution)/shard_map/ppermute | solution.py:51
  37.3 6.4 %collective-permute-start.6 = (bf16[1,6,48,256]{3,2,1,0:T(8,128)(2,1)S(1)}, bf16[1,6,48,256]{3,2,1,0:T(8,128)(2,1)S(1)}, u32[]{:S(2)}, u32[]{:S(2)}) collective-permute-start(bf16[1,6,48,256]{3,2,1,0:T(8,128)(2,1)S(1)} %collective-permute-done.5.refs_0_), channel_id=1, source_target_pairs={{0,6},{1,9},{2,4},{3,11},{4,2},{5,13},{6,0},{7,15},{8,14},{9,1},{1... | collective-permute-start | bytes 442376 | tf_op jit(solution)/shard_map/ppermute | solution.py:51
  40.3 8.1 %collective-permute-start.12 = (bf16[1,6,48,256]{3,2,1,0:T(8,128)(2,1)S(1)}, bf16[1,6,48,256]{3,2,1,0:T(8,128)(2,1)S(1)}, u32[]{:S(2)}, u32[]{:S(2)}) collective-permute-start(bf16[1,6,48,256]{3,2,1,0:T(8,128)(2,1)S(1)} %collective-permute-done.11.refs_0_), channel_id=1, source_target_pairs={{0,1},{1,0},{2,3},{3,2},{4,5},{5,4},{6,7},{7,6},{8,9},{9,8},{10,11... | collective-permute-start | bytes 442376 | tf_op jit(solution)/shard_map/ppermute | solution.py:51
  40.5 10.2 %collective-permute-start.10 = (bf16[1,6,48,256]{3,2,1,0:T(8,128)(2,1)S(1)}, bf16[1,6,48,256]{3,2,1,0:T(8,128)(2,1)S(1)}, u32[]{:S(2)}, u32[]{:S(2)}) collective-permute-start(bf16[1,6,48,256]{3,2,1,0:T(8,128)(2,1)S(1)} %collective-permute-done.9.refs_0_), channel_id=1, source_target_pairs={{0,1},{1,0},{2,3},{3,2},{4,5},{5,4},{6,7},{7,6},{8,9},{9,8},{10,11... | collective-permute-start | bytes 442376 | tf_op jit(solution)/shard_map/ppermute | solution.py:51
  43.7 10.9 %collective-permute-start.7 = (bf16[1,6,48,256]{3,2,1,0:T(8,128)(2,1)S(1)}, bf16[1,6,48,256]{3,2,1,0:T(8,128)(2,1)S(1)}, u32[]{:S(2)}, u32[]{:S(2)}) collective-permute-start(bf16[1,6,48,256]{3,2,1,0:T(8,128)(2,1)S(1)} %collective-permute-done.6.refs_0_), channel_id=1, source_target_pairs={{0,1},{1,0},{2,3},{3,2},{4,5},{5,4},{6,7},{7,6},{8,9},{9,8},{10,11... | collective-permute-start | bytes 442376 | tf_op jit(solution)/shard_map/ppermute | solution.py:51
  57.5 1.4 %collective-permute-start.19 = (f32[8,8]{1,0:T(8,128)S(1)}, f32[8,8]{1,0:T(8,128)S(1)}, u32[]{:S(2)}, u32[]{:S(2)}) collective-permute-start(f32[8,8]{1,0:T(8,128)S(1)} %get-tuple-element.224), channel_id=1, source_target_pairs={{0,1},{1,0},{2,3},{3,2},{4,5},{5,4},{6,7},{7,6},{8,9},{9,8},{10,11... | collective-permute-start | bytes 776 | tf_op jit(solution)/shard_map/ppermute | solution.py:51
  58.9 3.6 %collective-permute-start.20 = (f32[8,8]{1,0:T(8,128)S(1)}, f32[8,8]{1,0:T(8,128)S(1)}, u32[]{:S(2)}, u32[]{:S(2)}) collective-permute-start(f32[8,8]{1,0:T(8,128)S(1)} %max.12), channel_id=1, source_target_pairs={{0,2},{1,3},{2,0},{3,1},{4,6},{5,7},{6,4},{7,5},{8,10},{9,11},{10,... | collective-permute-start | bytes 776 | tf_op jit(solution)/shard_map/ppermute | solution.py:51
  62.5 4.8 %collective-permute-start.21 = (f32[8,8]{1,0:T(8,128)S(1)}, f32[8,8]{1,0:T(8,128)S(1)}, u32[]{:S(2)}, u32[]{:S(2)}) collective-permute-start(f32[8,8]{1,0:T(8,128)S(1)} %max.13), channel_id=1, source_target_pairs={{0,6},{1,7},{2,4},{3,5},{4,2},{5,3},{6,0},{7,1},{8,14},{9,15},{10,... | collective-permute-start | bytes 776 | tf_op jit(solution)/shard_map/ppermute | solution.py:51
  67.3 5.1 %collective-permute-start.22 = (f32[8,8]{1,0:T(8,128)S(1)}, f32[8,8]{1,0:T(8,128)S(1)}, u32[]{:S(2)}, u32[]{:S(2)}) collective-permute-start(f32[8,8]{1,0:T(8,128)S(1)} %max.14), channel_id=1, source_target_pairs={{0,8},{1,9},{2,10},{3,11},{4,12},{5,13},{6,14},{7,15},{8,0},{9,1},... | collective-permute-start | bytes 776 | tf_op jit(solution)/shard_map/ppermute | solution.py:51

commit v5 on v4

--- a/solution.py
+++ b/solution.py
@@ -20,6 +20,7 @@
 TW = 128
 MARGIN = 64
 WIN = 16
+LANES = 128
 NWIN = TW // WIN
 NDET = 3
 SEGS = 8
@@ -61,11 +62,6 @@
     angle = ((base[:, None] * tau[None, :] * STRIDE) % NFFT).astype(np.float64) * (TWO_PI / NFFT)
     turn = np.stack([np.cos(angle), np.sin(angle)], axis=1).astype(np.float32)
     return local, turn.reshape(NSL, JS, 2, TW)
-
-
-def phase(turns):
-    angle = turns.astype(jnp.float32) * jnp.float32(TWO_PI / NFFT)
-    return jnp.stack([jnp.cos(angle), jnp.sin(angle)])
 
 
 STEPS = (
@@ -101,15 +97,34 @@
     return ((dt // 2) ^ (place % 4)) * 2 + ((dt % 2) ^ (place // 4))
 
 
-def widen_kernel(templ_ref, wide_ref, *binned):
+def widen_kernel(templ_ref, edges_ref, live_ref, wide_ref, bin_ref, stat_ref, *binned):
     for ref in binned:
         ref[...] = jnp.zeros_like(ref)
+    lane = lax.broadcasted_iota(jnp.int32, (SLOTS, LANES), 1)
+    bin_of = jnp.zeros((SLOTS, LANES), jnp.int32)
+    for e in range(NBIN - 1):
+        bin_of = bin_of + (edges_ref[:, e:e + 1] <= lane).astype(jnp.int32)
+    bin_ref[...] = bin_of
+    block = lax.broadcasted_iota(jnp.int32, (NBLK, LANES), 0)
+    at_lane = lax.broadcasted_iota(jnp.int32, (1, LANES), 1)
     for k in range(SLOTS):
         h = templ_ref[k, 0].astype(jnp.float32)
         i = templ_ref[k, 1].astype(jnp.float32)
         wide_ref[k, 0] = h
         wide_ref[k, 1] = h + i
         wide_ref[k, 2] = h - i
+        power = jnp.sum(h * h + i * i, axis=1, keepdims=True)
+        upper = edges_ref[k:k + 1, :]
+        lower = jnp.where(at_lane == 0, 0, pltpu.roll(upper, 1, 1))
+        inside = jnp.where((block >= lower) & (block < upper), power, 0.0)
+        in_bins = jnp.sum(inside, axis=0, keepdims=True)
+        sigma2 = jnp.sum(power, axis=0, keepdims=True) + EPSILON
+        frac = (in_bins + EPSILON) / sigma2
+        inv = pltpu.roll(1.0 / (frac * sigma2), NBIN, 1)
+        live = (k < live_ref[...]).astype(jnp.float32)
+        row = jnp.where(at_lane == 2 * NBIN, 0.5 / sigma2, live)
+        row = jnp.where(at_lane < 2 * NBIN, inv, row)
+        stat_ref[k:k + 1, :] = jnp.where(at_lane < NBIN, frac, row)
 
 
 def whole():
@@ -119,41 +134,53 @@
 BINNED = [jax.ShapeDtypeStruct((NBIN, ROWS, 2 * TW), jnp.float32)] * SLOTS
 
 
-def widen(templates):
+def widen(templates, edges, live_count):
     outs = pl.pallas_call(
         widen_kernel,
-        out_shape=[jax.ShapeDtypeStruct((SLOTS, 3, NBLK, FB), jnp.float32)] + BINNED,
-        in_specs=[whole()],
-        out_specs=[whole()] * (1 + SLOTS),
+        out_shape=[
+            jax.ShapeDtypeStruct((SLOTS, 3, NBLK, FB), jnp.float32),
+            jax.ShapeDtypeStruct((SLOTS, LANES), jnp.int32),
+            jax.ShapeDtypeStruct((SLOTS, LANES), jnp.float32),
+        ] + BINNED,
+        in_specs=[whole()] * 3,
+        out_specs=[whole()] * (3 + SLOTS),
         compiler_params=pltpu.CompilerParams(vmem_limit_bytes=VMEM),
         cost_estimate=pl.CostEstimate(flops=10**6, bytes_accessed=10**6, transcendentals=0),
         name="widen",
-    )(templates)
-    return outs[0], outs[1:]
+    )(templates, edges, live_count)
+    return outs[0], outs[1], outs[2], outs[3:]
 
 
 def bins_kernel(parts, last, *refs):
     count = len(parts)
     pieces, refs = refs[:count], refs[count:]
-    bin_vmem, table_ref, turn_ref, wide_ref, start_ref, local_ref, step_ref = refs[:7]
-    refs = refs[7:]
+    bin_vmem, table_ref, turn_ref, wide_ref, phase_ref = refs[:5]
+    refs = refs[5:]
     if last:
         stat_vmem, refs = refs[0], refs[1:]
     refs = refs[SLOTS:]
     binned, refs = refs[:SLOTS], refs[SLOTS:]
     if last:
         out_ref, refs = refs[0], refs[1:]
-    prod_ref, rot_ref, bin_ref, sems = refs[:4]
+    prod_ref, rot_ref, step_ref, bin_ref, sems = refs[:5]
     copies = [pltpu.make_async_copy(bin_vmem, bin_ref, sems.at[0])]
     if last:
-        stat_ref, best_ref = refs[4:]
+        stat_ref, best_ref = refs[5:]
         copies.append(pltpu.make_async_copy(stat_vmem, stat_ref, sems.at[1]))
     for copy in copies:
         copy.start()
 
-    def product(piece_ref, c, jj):
+    lane = lax.broadcasted_iota(jnp.int32, (ROWS, LANES), 1)
+
+    def at_lane(part, place):
+        return jnp.sum(jnp.where(lane == place, phase_ref[part, :, FB:], 0.0), axis=1, keepdims=True)
+
+    for part in range(2):
+        step_ref[part] = jnp.broadcast_to(at_lane(part, NSL), (ROWS, TW))
+
+    def product(piece_ref, which, c, jj):
         j = c * JS + jj
-        both = piece_ref[0, jj].astype(jnp.float32)
+        both = piece_ref[which, jj].astype(jnp.float32)
         raw_r, raw_i = both[:ROWS], both[ROWS:]
         rc, rs = rot_ref[0], rot_ref[1]
         sr = raw_r * rc - raw_i * rs
@@ -189,27 +216,28 @@
             binned[k][b, :, :TW] += cos * re - sin * im
             binned[k][b, :, TW:] += cos * im + sin * re
 
-    for number, (piece_ref, part) in enumerate(zip(pieces, parts)):
-        c = slice_of(*part)
-        sc, ss = start_ref[c, 0], start_ref[c, 1]
-        for half in range(2):
-            cols = slice(half * TW, half * TW + TW)
-            lc, ls = local_ref[0, :, cols], local_ref[1, :, cols]
-            rot_ref[0, :, cols] = sc * lc - ss * ls
-            rot_ref[1, :, cols] = sc * ls + ss * lc
-        for jj in range(JS):
-            product(piece_ref, c, jj)
-        if number == 0:
-            for copy in copies:
-                copy.wait()
-        half = JS // 2
-        size = half * SLOTS * ROWS
-        for h in range(2):
-            series = jnp.dot(
-                prod_ref[h * size:(h + 1) * size], table_ref[...], preferred_element_type=jnp.float32
-            )
-            for m in range(half):
-                post(c, h * half + m, series[m * SLOTS * ROWS:(m + 1) * SLOTS * ROWS])
+    number = 0
+    for piece_ref, (first, amount, other) in zip(pieces, parts):
+        for which in range(amount):
+            c = slice_of(first + which, other)
+            sc, ss = at_lane(0, c), at_lane(1, c)
+            lc, ls = phase_ref[0, :, :FB], phase_ref[1, :, :FB]
+            rot_ref[0] = sc * lc - ss * ls
+            rot_ref[1] = sc * ls + ss * lc
+            for jj in range(JS):
+                product(piece_ref, which, c, jj)
+            if number == 0:
+                for copy in copies:
+                    copy.wait()
+            number += 1
+            half = JS // 2
+            size = half * SLOTS * ROWS
+            for h in range(2):
+                series = jnp.dot(
+                    prod_ref[h * size:(h + 1) * size], table_ref[...], preferred_element_type=jnp.float32
+                )
+                for m in range(half):
+                    post(c, h * half + m, series[m * SLOTS * ROWS:(m + 1) * SLOTS * ROWS])
 
     if last:
         best = jnp.zeros((SEGS, TW), jnp.float32)
@@ -246,13 +274,14 @@
     scratch = [
         pltpu.VMEM((JS * SLOTS * ROWS, 2 * FB), jnp.bfloat16),
         pltpu.VMEM((2, ROWS, FB), jnp.float32),
-        pltpu.SMEM((SLOTS, NBLK), jnp.int32),
+        pltpu.VMEM((2, ROWS, TW), jnp.float32),
+        pltpu.SMEM((SLOTS, LANES), jnp.int32),
         pltpu.SemaphoreType.DMA((2,)),
     ]
     if last:
         out_shape.append(jax.ShapeDtypeStruct((SEGS, NWIN), jnp.float32))
-        scratch += [pltpu.SMEM((SLOTS, 2 * NBIN + 2), jnp.float32), pltpu.VMEM((SEGS, NWIN), jnp.float32)]
-    flops = len(parts) * 2 * JS * SLOTS * ROWS * 2 * FB * 2 * TW
+        scratch += [pltpu.SMEM((SLOTS, LANES), jnp.float32), pltpu.VMEM((SEGS, NWIN), jnp.float32)]
+    flops = sum(part[1] for part in parts) * 2 * JS * SLOTS * ROWS * 2 * FB * 2 * TW
     return pl.pallas_call(
         functools.partial(bins_kernel, parts, last),
         out_shape=out_shape,
@@ -266,52 +295,59 @@
     )(*operands)
 
 
+def phases(shifts):
+    row = jnp.arange(ROWS, dtype=jnp.int32)
+    segment = segment_at(row % SEGS)
+    here = (jnp.arange(SEGS, dtype=jnp.int32)[None, :, None] == segment[:, None, None]) & (
+        jnp.arange(NDET, dtype=jnp.int32)[None, None, :] == (row // SEGS)[:, None, None]
+    )
+    first = MARGIN + jnp.sum(jnp.where(here, shifts[None], 0), axis=(1, 2))
+    lane = np.arange(FB + LANES, dtype=np.int32)
+    starts = (FLOW // FB + (lane - FB) * JS) * FB
+    rate = np.where(lane < FB, lane * STRIDE, np.where(lane < FB + NSL, starts, FB)).astype(np.int32)
+    angle = ((first[:, None] * rate[None, :]) % NFFT).astype(jnp.float32) * jnp.float32(TWO_PI / NFFT)
+    quarter = np.array([0.0, 0.5 * math.pi], np.float32)[:, None, None]
+    return jnp.cos(angle[None] - quarter)
+
+
 def per_device(strain, templates, live_count, chi_edges, shifts):
-    wide, binned = widen(templates)
+    edges = jnp.pad(chi_edges, ((0, 0), (0, LANES - NBIN + 1)), constant_values=NBLK)
+    wide, bin_of, stat, binned = widen(templates, edges, live_count)
+    table, turn = tables()
+    turned = phases(shifts)
 
     x = jnp.transpose(strain[0], (2, 1, 0, 3)).reshape(JS, 2 * NDET, 1, FB)
     got = {0: x}
     for dx in (2, 3, 1):
         got[dx] = swap_with(x, across(dx=dx))
     x = jnp.concatenate([got[dx] for dx in range(4)], axis=2)
+    x, wide, turned = lax.optimization_barrier((x, wide, turned))
     x = jnp.concatenate([x, swap_with(x, across(dy=1))], axis=2)
-    own = [x.reshape(1, JS, 2 * ROWS, FB)]
-
-    blocks = jnp.arange(NBLK, dtype=jnp.int32)
-    bin_of = jnp.sum((chi_edges[:, :, None] <= blocks[None, None, :]).astype(jnp.int32), axis=1)
-    labels = jnp.arange(NBIN, dtype=jnp.int32)
-    onehot = (bin_of[:, None, :] == labels[None, :, None]).astype(jnp.float32)
-    full = templates.astype(jnp.float32)
-    block_power = jnp.sum(full * full, axis=(1, 3))
-    sigma2 = jnp.sum(block_power, axis=1) + EPSILON
-    in_bins = jnp.sum(onehot * block_power[:, None, :], axis=2)
-    frac = (in_bins + EPSILON) / sigma2[:, None]
-    inv = 1.0 / (frac * sigma2[:, None])
-    half = 1.0 / (2.0 * sigma2)
-    live = (jnp.arange(SLOTS, dtype=jnp.int32) < live_count[0, 0]).astype(jnp.float32)
-    stat = jnp.concatenate([frac, inv, half[:, None], live[:, None]], axis=1)
-
-    order = segment_at(jnp.arange(SEGS, dtype=jnp.int32))
-    first = (MARGIN + jnp.take(shifts, order, axis=0)).T.reshape(ROWS)
-    bins = jnp.arange(FB, dtype=jnp.int32)
-    local = phase((first[:, None] * bins[None, :] * STRIDE) % NFFT)
-    starts = (FLOW // FB + jnp.arange(NSL, dtype=jnp.int32) * JS) * FB
-    start = phase((first[None, :] * starts[:, None]) % NFFT)
-    start = jnp.broadcast_to(jnp.transpose(start, (1, 0, 2))[..., None], (NSL, 2, ROWS, TW))
-    step = phase(first * FB)
-    step = jnp.broadcast_to(step[..., None], (2, ROWS, TW))
-    table, turn = tables()
-    shared = (bin_of, table, turn, wide, start, local, step)
-
-    others = [swap_with(own[0], across(dcore=1))]
-    for number in range(3):
-        fresh = [swap_with(piece, step_move(number)) for piece in own]
-        own += fresh
-        others += [swap_with(piece, across(dcore=1)) for piece in fresh]
-    for p in range(7):
-        binned = add_bins((own[p], others[p]), ((p, 0), (p, 1)), shared, binned)
-    binned = add_bins((own[7],), ((7, 0),), shared, binned)
-    best = add_bins((others[7],), ((7, 1),), shared, binned, stat)[-1]
+    shared = (bin_of, table, turn, wide, turned)
+
+    def to_core(piece):
+        return swap_with(piece, across(dcore=1))
+
+    def after(value, binned):
+        value, first = lax.optimization_barrier((value, binned[0]))
+        return value, [first, *binned[1:]]
+
+    p0 = x.reshape(1, JS, 2 * ROWS, FB)
+    q0 = to_core(p0)
+    p1 = swap_with(p0, step_move(0))
+    q1 = to_core(p1)
+    binned = add_bins((p0, q0), ((0, 1, 0), (0, 1, 1)), shared, binned)
+    p01, binned = after(jnp.concatenate([p0, p1], axis=0), binned)
+    p23 = swap_with(p01, step_move(1))
+    q23 = to_core(p23)
+    binned = add_bins((p1, q1), ((1, 1, 0), (1, 1, 1)), shared, binned)
+    (p01, p23), binned = after((p01, p23), binned)
+    p45 = swap_with(p01, step_move(2))
+    p67 = swap_with(p23, step_move(2))
+    q45, q67 = to_core(p45), to_core(p67)
+    binned = add_bins((p23, q23), ((2, 2, 0), (2, 2, 1)), shared, binned)
+    binned = add_bins((p45, q45), ((4, 2, 0), (4, 2, 1)), shared, binned)
+    best = add_bins((p67, q67), ((6, 2, 0), (6, 2, 1)), shared, binned, stat)[-1]
     for move in (across(dcore=1), across(dz=1), across(dz=3), across(dy=2)):
         best = jnp.maximum(best, swap_with(best, move))
     return best[:, None, :]

time: 73.2 us -> 76.1 us (1.040)
  waiting for transfers between devices: 12.2 us -> 24 us
  starting transfers between devices: 31.6 us -> 23.7 us
  Pallas kernels: 21.1 us -> 19.5 us
  local copies, waits for them, and re-layouts: 3.06 us -> 4.59 us
  other arithmetic: 4.06 us -> 3.26 us
    ppermute x23 -> x17, waiting for transfers between devices: 12.2 us -> 24 us  [swap_with(): return lax.ppermute(value, AXES, pairs)]
    ppermute x23 -> x17, starting transfers between devices: 31.6 us -> 23.7 us  [swap_with(): return lax.ppermute(value, AXES, pairs)]
    pallas_call x9 -> x5, Pallas kernels: 20.6 us -> 18.1 us  [add_bins(): pl.pallas_call(functools.partial(bins_kernel, parts, last), out_shape=out...]
    unnamed x12 -> x9, local copies, waits for them, and re-layouts: 1.62 us -> 3.84 us
    reduce_sum x3 -> x1, other arithmetic: 2.73 us -> 0.77 us  [phases(): first = MARGIN + jnp.sum(jnp.where(here, shifts[None], 0), axis=(1, 2))]
    pallas_call x1, Pallas kernels: 0.54 us -> 1.44 us  [widen(): pl.pallas_call(widen_kernel, out_shape=[jax.ShapeDtypeStruct((SLOTS, 3, N...]
    mul x1, other arithmetic: 0.01 us -> 0.77 us  [phases(): (first[:, None] * rate[None, :] % NFFT).astype(jnp.float32)]
  transfers between devices with their start and end apart: 23 -> 17, of which waited for: 7 -> 9; matrix products, arithmetic and copies ran while one was open for 8% -> 4% of each run, Pallas kernels for 25% -> 19%
where the time goes in v5:
time: 76.1 us; the launch traced here: 75.8 us
  waiting for transfers between devices  24 us (32%)
  starting transfers between devices  23.7 us (31%)
  Pallas kernels  19.5 us (26%)
  local copies, waits for them, and re-layouts  4.59 us (6%)
  other arithmetic  3.26 us (4%)
  between operations  0.8 us (1%)
    ppermute x17, waiting for transfers between devices, swap_with(): return lax.ppermute(value, AXES, pairs)  24 us
    ppermute x17, starting transfers between devices, swap_with(): return lax.ppermute(value, AXES, pairs)  23.7 us
    pallas_call x5, Pallas kernels, add_bins(): pl.pallas_call(functools.partial(bins_kernel, parts, last), out_shape=out...  18.1 us
    unnamed x9, local copies, waits for them, and re-layouts  3.84 us
  transfers between devices with their start and end apart: 17, of which 9 were waited for; matrix products, arithmetic and copies ran while one was open for 4% of the time, Pallas kernels for 19%

profile of v5, /device:TPU:0, one launch (start us, length us, event | category | flops | bytes accessed | tf_op | source)
XLA Modules:
  0.0 75.8 jit_solution(4173917242047104551)
XLA Ops:
  0.0 0.7 copy.76
  0.7 1.6 %collective-permute-start = (bf16[6,6,1,256]{3,0,1,2:T(8,128)(2,1)S(1)}, bf16[6,6,1,256]{3,0,1,2:T(8,128)(2,1)S(1)}, u32[]{:S(2)}, u32[]{:S(2)}) collective-permute-start(bf16[6,6,1,256]{3,0,1,2:T(8,128)(2,1)S(1)} %bitcast.15), channel_id=1, source_target_pairs={{0,32},{1,33},{2,34},{3,35},{4,36},{5,37},{6,38},{7,39},{8,40},{9,... | collective-permute-start | bytes 55304 | tf_op jit(solution)/shard_map/ppermute | solution.py:52
  2.3 2.7 %collective-permute-start.1 = (bf16[6,6,1,256]{3,0,1,2:T(8,128)(2,1)S(1)}, bf16[6,6,1,256]{3,0,1,2:T(8,128)(2,1)S(1)}, u32[]{:S(2)}, u32[]{:S(2)}) collective-permute-start(bf16[6,6,1,256]{3,0,1,2:T(8,128)(2,1)S(1)} %bitcast.16), channel_id=1, source_target_pairs={{0,64},{1,65},{2,66},{3,67},{4,68},{5,69},{6,70},{7,71},{8,72},{9,... | collective-permute-start | bytes 55304 | tf_op jit(solution)/shard_map/ppermute | solution.py:52
  5.0 0.4 collective-permute-start.2
  5.5 0.8 %select_reduce_fusion = s32[24]{0:T(128)S(1)} fusion(s32[8,3]{0,1:T(4,128)} %param.13, pred[24,3]{0,1:T(4,128)(4,1)S(1)} %iota_compare_fusion.1, pred[24,8]{0,1:T(8,128)(4,1)S(1)} %iota_compare_fusion), kind=kLoop, calls=%fused_computation.13 | loop fusion | flops 1704 | bytes 456 | tf_op jit(solution)/shard_map/reduce_sum | solution.py:304
  6.2 0.8 %fusion.1 = f32[24,384]{1,0:T(8,128)S(1)} fusion(s32[384]{0:T(512)} %constant.116, s32[24]{0:T(128)S(1)} %broadcast_add_fusion), kind=kLoop, calls=%fused_computation.11 | loop fusion | flops 129024 | bytes 38496 | tf_op jit(solution)/shard_map/mul | solution.py:308
  7.0 1.0 %add_cosine_fusion.refs_6_ = f32[2,24,384]{2,1,0:T(8,128)S(1)} fusion(f32[2]{0:T(128)} %constant.118, f32[24,384]{1,0:T(8,128)S(1)} %fusion.1), kind=kLoop, calls=%fused_computation.4 | loop fusion | flops 18432 | bytes 110600 | tf_op jit(solution)/shard_map/cos | solution.py:310
  8.7 0.7 pad.4.edges_ref
  9.4 1.3 %copy-done = bf16[12,2,96,256]{3,2,1,0:T(8,128)(2,1)S(1)} copy-done((bf16[12,2,96,256]{3,2,1,0:T(8,128)(2,1)S(1)}, bf16[12,2,96,256]{3,2,1,0:T(8,128)(2,1)}, u32[]{:S(2)}) %copy-start) | copy-done | bytes 1179672
  10.6 1.4 %widen.1 = (f32[12,3,96,256]{3,2,1,0:T(8,128)S(1)}, s32[12,128]{1,0:T(8,128)S(1)}, f32[12,128]{1,0:T(8,128)S(1)}, f32[16,24,256]{2,1,0:T(8,128)S(1)}, f32[16,24,...) custom-call(bf16[12,2,96,256]{3,2,1,0:T(8,128)(2,1)S(1)} %copy-done,, ...), custom_call_target="tpu_custom_call" | custom-call | flops 1000000 | bytes 1000000 | tf_op jit(solution)/shard_map/widen/pallas_call | solution.py:138
  12.1 0.0 collective-permute-done
  12.1 0.0 collective-permute-done.1
  12.1 0.0 collective-permute-done.2
  12.1 1.7 %collective-permute-start.3 = (bf16[6,6,4,256]{3,0,1,2:T(8,128)(2,1)S(1)}, bf16[6,6,4,256]{3,0,1,2:T(8,128)(2,1)S(1)}, u32[]{:S(2)}, u32[]{:S(2)}) collective-permute-start(bf16[6,6,4,256]{3,0,1,2:T(8,128)(2,1)S(1)} %pad_maximum_fusion.2), channel_id=1, source_target_pairs={{0,16},{1,17},{2,18},{3,19},{4,20},{5,21},{6,22},{7,23},{8,24},{9,... | collective-permute-start | bytes 221192 | tf_op jit(solution)/shard_map/ppermute | solution.py:52
  13.9 3.0 %collective-permute-done.3 = bf16[6,6,4,256]{3,0,1,2:T(8,128)(2,1)S(1)} collective-permute-done((bf16[6,6,4,256]{3,0,1,2:T(8,128)(2,1)S(1)}, bf16[6,6,4,256]{3,0,1,2:T(8,128)(2,1)S(1)}, u32[]{:S(2)}, u32[]{:S(2)}) %collective-permute-start.3) | collective-permute-done | bytes 73760 | tf_op jit(solution)/shard_map/ppermute | solution.py:52
  16.9 3.4 %collective-permute-start.4 = (bf16[1,6,48,256]{3,2,1,0:T(8,128)(2,1)S(1)}, bf16[1,6,48,256]{3,2,1,0:T(8,128)(2,1)S(1)}, u32[]{:S(2)}, u32[]{:S(2)}) collective-permute-start(bf16[1,6,48,256]{3,2,1,0:T(8,128)(2,1)S(1)} %bitcast.11), channel_id=1, source_target_pairs={{0,8},{1,3},{2,10},{3,1},{4,12},{5,7},{6,14},{7,5},{8,0},{9,11},{1... | collective-permute-start | bytes 442376 | tf_op jit(solution)/shard_map/ppermute | solution.py:52
  20.3 0.0 collective-permute-start.5
  20.3 3.4 %collective-permute-done.4.refs_0_ = bf16[1,6,48,256]{3,2,1,0:T(8,128)(2,1)S(1)} collective-permute-done((bf16[1,6,48,256]{3,2,1,0:T(8,128)(2,1)S(1)}, bf16[1,6,48,256]{3,2,1,0:T(8,128)(2,1)S(1)}, u32[]{:S(2)}, u32[]{:S(2)}) %collective-permute-start.4) | collective-permute-done | bytes 147488 | tf_op jit(solution)/shard_map/ppermute | solution.py:52
  23.7 0.0 collective-permute-start.7
  23.7 0.0 collective-permute-done.5.refs_1_
  23.7 0.9 %copy-done.1 = bf16[512,256]{1,0:T(8,128)(2,1)S(1)} copy-done((bf16[512,256]{1,0:T(8,128)(2,1)S(1)}, bf16[512,256]{1,0:T(8,128)(2,1)}, u32[]{:S(2)}) %copy-start.1) | copy-done | bytes 262168
  24.6 0.9 %copy-done.3 = f32[16,6,2,128]{3,2,1,0:T(2,128)S(1)} copy-done((f32[16,6,2,128]{3,2,1,0:T(2,128)S(1)}, f32[16,6,2,128]{3,2,1,0:T(2,128)}, u32[]{:S(2)}) %copy-start.3) | copy-done | bytes 98328
  25.5 2.3 %add_bins.4 = (f32[16,24,256]{2,1,0:T(8,128)S(1)}, f32[16,24,256]{2,1,0:T(8,128)S(1)}, f32[16,24,256]{2,1,0:T(8,128)S(1)}, f32[16,24,256]{2,1,0:T(8,128)S(1)}, f...) custom-call(bf16[1,6,48,256]{3,2,1,0:T(8,128)(2,1)S(1)} %bitcast.13,, ...), custom_call_target="tpu_custom_call", output_to_operand_aliasing={{0}: (7, {}), {1}: (8, {}), {2}: (9, {}), {3}: (10, {}), {4... | custom-call | flops 1811939328 | bytes 1000000 | tf_op jit(solution)/shard_map/add_bins/pallas_call | solution.py:285
  27.9 2.1 %collective-permute-start.6 = (bf16[2,6,48,256]{3,2,1,0:T(8,128)(2,1)S(1)}, bf16[2,6,48,256]{3,2,1,0:T(8,128)(2,1)S(1)}, u32[]{:S(2)}, u32[]{:S(2)}) collective-permute-start(bf16[2,6,48,256]{3,2,1,0:T(8,128)(2,1)S(1)} %pad_maximum_fusion), channel_id=1, source_target_pairs={{0,2},{1,7},{2,0},{3,5},{4,6},{5,3},{6,4},{7,1},{8,10},{9,15},{10,... | collective-permute-start | bytes 884744 | tf_op jit(solution)/shard_map/ppermute | solution.py:52
  30.0 0.0 collective-permute-done.7.refs_1_
  30.0 2.4 %add_bins.5 = (f32[16,24,256]{2,1,0:T(8,128)S(1)}, f32[16,24,256]{2,1,0:T(8,128)S(1)}, f32[16,24,256]{2,1,0:T(8,128)S(1)}, f32[16,24,256]{2,1,0:T(8,128)S(1)}, f...) custom-call(bf16[1,6,48,256]{3,2,1,0:T(8,128)(2,1)S(1)} %collective-, ...), custom_call_target="tpu_custom_call", output_to_operand_aliasing={{0}: (7, {}), {1}: (8, {}), {2}: (9, {}), {3}: (10, {}), {4... | custom-call | flops 1811939328 | bytes 1000000 | tf_op jit(solution)/shard_map/add_bins/pallas_call | solution.py:285
  32.4 2.3 %collective-permute-done.6.refs_0_ = bf16[2,6,48,256]{3,2,1,0:T(8,128)(2,1)S(1)} collective-permute-done((bf16[2,6,48,256]{3,2,1,0:T(8,128)(2,1)S(1)}, bf16[2,6,48,256]{3,2,1,0:T(8,128)(2,1)S(1)}, u32[]{:S(2)}, u32[]{:S(2)}) %collective-permute-start.6) | collective-permute-done | bytes 294944 | tf_op jit(solution)/shard_map/ppermute | solution.py:52
  34.7 4.1 %collective-permute-start.10 = (bf16[2,6,48,256]{3,2,1,0:T(8,128)(2,1)S(1)}, bf16[2,6,48,256]{3,2,1,0:T(8,128)(2,1)S(1)}, u32[]{:S(2)}, u32[]{:S(2)}) collective-permute-start(bf16[2,6,48,256]{3,2,1,0:T(8,128)(2,1)S(1)} %pad_maximum_fusion), channel_id=1, source_target_pairs={{0,6},{1,9},{2,4},{3,11},{4,2},{5,13},{6,0},{7,15},{8,14},{9,1},{1... | collective-permute-start | bytes 884744 | tf_op jit(solution)/shard_map/ppermute | solution.py:52
  38.8 0.0 collective-permute-start.8
  38.8 0.6 collective-permute-start.12
  39.4 4.1 %collective-permute-done.10.refs_0_ = bf16[2,6,48,256]{3,2,1,0:T(8,128)(2,1)S(1)} collective-permute-done((bf16[2,6,48,256]{3,2,1,0:T(8,128)(2,1)S(1)}, bf16[2,6,48,256]{3,2,1,0:T(8,128)(2,1)S(1)}, u32[]{:S(2)}, u32[]{:S(2)}) %collective-permute-start.10) | collective-permute-done | bytes 294944 | tf_op jit(solution)/shard_map/ppermute | solution.py:52
  43.5 0.0 collective-permute-start.11
  43.5 3.2 %collective-permute-done.8.refs_0_ = bf16[2,6,48,256]{3,2,1,0:T(8,128)(2,1)S(1)} collective-permute-done((bf16[2,6,48,256]{3,2,1,0:T(8,128)(2,1)S(1)}, bf16[2,6,48,256]{3,2,1,0:T(8,128)(2,1)S(1)}, u32[]{:S(2)}, u32[]{:S(2)}) %collective-permute-start.8) | collective-permute-done | bytes 294944 | tf_op jit(solution)/shard_map/ppermute | solution.py:52
  46.7 0.0 collective-permute-start.9
  46.7 0.0 collective-permute-done.12.refs_1_
  46.7 4.0 %add_bins.6 = (f32[16,24,256]{2,1,0:T(8,128)S(1)}, f32[16,24,256]{2,1,0:T(8,128)S(1)}, f32[16,24,256]{2,1,0:T(8,128)S(1)}, f32[16,24,256]{2,1,0:T(8,128)S(1)}, f...) custom-call(bf16[2,6,48,256]{3,2,1,0:T(8,128)(2,1)S(1)} %collective-, ...), custom_call_target="tpu_custom_call", output_to_operand_aliasing={{0}: (7, {}), {1}: (8, {}), {2}: (9, {}), {3}: (10, {}), {4... | custom-call | flops 3623878656 | bytes 1000000 | tf_op jit(solution)/shard_map/add_bins/pallas_call | solution.py:285
  50.8 4.1 %add_bins.7 = (f32[16,24,256]{2,1,0:T(8,128)S(1)}, f32[16,24,256]{2,1,0:T(8,128)S(1)}, f32[16,24,256]{2,1,0:T(8,128)S(1)}, f32[16,24,256]{2,1,0:T(8,128)S(1)}, f...) custom-call(bf16[2,6,48,256]{3,2,1,0:T(8,128)(2,1)S(1)} %collective-, ...), custom_call_target="tpu_custom_call", output_to_operand_aliasing={{0}: (7, {}), {1}: (8, {}), {2}: (9, {}), {3}: (10, {}), {4... | custom-call | flops 3623878656 | bytes 1000000 | tf_op jit(solution)/shard_map/add_bins/pallas_call | solution.py:285
  54.9 0.0 collective-permute-done.9.refs_1_
  54.9 5.3 %last_bins.1 = (f32[16,24,256]{2,1,0:T(8,128)S(1)}, f32[16,24,256]{2,1,0:T(8,128)S(1)}, f32[16,24,256]{2,1,0:T(8,128)S(1)}, f32[16,24,256]{2,1,0:T(8,128)S(1)}, ...) custom-call(bf16[2,6,48,256]{3,2,1,0:T(8,128)(2,1)S(1)} %collective-, ...), custom_call_target="tpu_custom_call", output_to_operand_aliasing={{0}: (8, {}), {1}: (9, {}), {2}: (10, {}), {3}: (11, {}), {... | custom-call | flops 3623878656 | bytes 1000000 | tf_op jit(solution)/shard_map/last_bins/pallas_call | solution.py:285
  60.2 0.6 collective-permute-start.13
  60.8 0.8 %collective-permute-done.13 = f32[8,8]{1,0:T(8,128)S(1)} collective-permute-done((f32[8,8]{1,0:T(8,128)S(1)}, f32[8,8]{1,0:T(8,128)S(1)}, u32[]{:S(2)}, u32[]{:S(2)}) %collective-permute-start.13) | collective-permute-done | bytes 288 | tf_op jit(solution)/shard_map/ppermute | solution.py:52
  61.6 0.0 collective-permute-start.14
  61.6 3.6 %collective-permute-done.14 = f32[8,8]{1,0:T(8,128)S(1)} collective-permute-done((f32[8,8]{1,0:T(8,128)S(1)}, f32[8,8]{1,0:T(8,128)S(1)}, u32[]{:S(2)}, u32[]{:S(2)}) %collective-permute-start.14) | collective-permute-done | bytes 288 | tf_op jit(solution)/shard_map/ppermute | solution.py:52
  65.3 3.2 %collective-permute-start.15 = (f32[8,8]{1,0:T(8,128)S(1)}, f32[8,8]{1,0:T(8,128)S(1)}, u32[]{:S(2)}, u32[]{:S(2)}) collective-permute-start(f32[8,8]{1,0:T(8,128)S(1)} %max.13), channel_id=1, source_target_pairs={{0,6},{1,7},{2,4},{3,5},{4,2},{5,3},{6,0},{7,1},{8,14},{9,15},{10,... | collective-permute-start | bytes 776 | tf_op jit(solution)/shard_map/ppermute | solution.py:52
  68.5 1.6 %collective-permute-done.15 = f32[8,8]{1,0:T(8,128)S(1)} collective-permute-done((f32[8,8]{1,0:T(8,128)S(1)}, f32[8,8]{1,0:T(8,128)S(1)}, u32[]{:S(2)}, u32[]{:S(2)}) %collective-permute-start.15) | collective-permute-done | bytes 288 | tf_op jit(solution)/shard_map/ppermute | solution.py:52
  70.1 3.2 %collective-permute-start.16 = (f32[8,8]{1,0:T(8,128)S(1)}, f32[8,8]{1,0:T(8,128)S(1)}, u32[]{:S(2)}, u32[]{:S(2)}) collective-permute-start(f32[8,8]{1,0:T(8,128)S(1)} %max.14), channel_id=1, source_target_pairs={{0,8},{1,9},{2,10},{3,11},{4,12},{5,13},{6,14},{7,15},{8,0},{9,1},... | collective-permute-start | bytes 776 | tf_op jit(solution)/shard_map/ppermute | solution.py:52
  73.2 2.0 %collective-permute-done.16 = f32[8,8]{1,0:T(8,128)S(1)} collective-permute-done((f32[8,8]{1,0:T(8,128)S(1)}, f32[8,8]{1,0:T(8,128)S(1)}, u32[]{:S(2)}, u32[]{:S(2)}) %collective-permute-start.16) | collective-permute-done | bytes 288 | tf_op jit(solution)/shard_map/ppermute | solution.py:52
  75.2 0.6 max.15
  (18 shorter events, 0.2 us)
Async XLA Ops:
  0.7 11.3 %collective-permute-start = (bf16[6,6,1,256]{3,0,1,2:T(8,128)(2,1)S(1)}, bf16[6,6,1,256]{3,0,1,2:T(8,128)(2,1)S(1)}, u32[]{:S(2)}, u32[]{:S(2)}) collective-permute-start(bf16[6,6,1,256]{3,0,1,2:T(8,128)(2,1)S(1)} %bitcast.15), channel_id=1, source_target_pairs={{0,32},{1,33},{2,34},{3,35},{4,36},{5,37},{6,38},{7,39},{8,40},{9,... | collective-permute-start | bytes 55304 | tf_op jit(solution)/shard_map/ppermute | solution.py:52
  2.3 9.8 %collective-permute-start.1 = (bf16[6,6,1,256]{3,0,1,2:T(8,128)(2,1)S(1)}, bf16[6,6,1,256]{3,0,1,2:T(8,128)(2,1)S(1)}, u32[]{:S(2)}, u32[]{:S(2)}) collective-permute-start(bf16[6,6,1,256]{3,0,1,2:T(8,128)(2,1)S(1)} %bitcast.16), channel_id=1, source_target_pairs={{0,64},{1,65},{2,66},{3,67},{4,68},{5,69},{6,70},{7,71},{8,72},{9,... | collective-permute-start | bytes 55304 | tf_op jit(solution)/shard_map/ppermute | solution.py:52
  5.0 7.1 %collective-permute-start.2 = (bf16[6,6,1,256]{3,0,1,2:T(8,128)(2,1)S(1)}, bf16[6,6,1,256]{3,0,1,2:T(8,128)(2,1)S(1)}, u32[]{:S(2)}, u32[]{:S(2)}) collective-permute-start(bf16[6,6,1,256]{3,0,1,2:T(8,128)(2,1)S(1)} %bitcast.17), channel_id=1, source_target_pairs={{0,96},{1,97},{2,98},{3,99},{4,100},{5,101},{6,102},{7,103},{8,104... | collective-permute-start | bytes 55304 | tf_op jit(solution)/shard_map/ppermute | solution.py:52
  9.4 1.3 %copy-start = (bf16[12,2,96,256]{3,2,1,0:T(8,128)(2,1)S(1)}, bf16[12,2,96,256]{3,2,1,0:T(8,128)(2,1)}, u32[]{:S(2)}) copy-start(bf16[12,2,96,256]{3,2,1,0:T(8,128)(2,1)} %templ_ref.1) | copy-start | bytes 3538948
  12.1 4.7 %collective-permute-start.3 = (bf16[6,6,4,256]{3,0,1,2:T(8,128)(2,1)S(1)}, bf16[6,6,4,256]{3,0,1,2:T(8,128)(2,1)S(1)}, u32[]{:S(2)}, u32[]{:S(2)}) collective-permute-start(bf16[6,6,4,256]{3,0,1,2:T(8,128)(2,1)S(1)} %pad_maximum_fusion.2), channel_id=1, source_target_pairs={{0,16},{1,17},{2,18},{3,19},{4,20},{5,21},{6,22},{7,23},{8,24},{9,... | collective-permute-start | bytes 221192 | tf_op jit(solution)/shard_map/ppermute | solution.py:52
  16.9 6.7 %collective-permute-start.4 = (bf16[1,6,48,256]{3,2,1,0:T(8,128)(2,1)S(1)}, bf16[1,6,48,256]{3,2,1,0:T(8,128)(2,1)S(1)}, u32[]{:S(2)}, u32[]{:S(2)}) collective-permute-start(bf16[1,6,48,256]{3,2,1,0:T(8,128)(2,1)S(1)} %bitcast.11), channel_id=1, source_target_pairs={{0,8},{1,3},{2,10},{3,1},{4,12},{5,7},{6,14},{7,5},{8,0},{9,11},{1... | collective-permute-start | bytes 442376 | tf_op jit(solution)/shard_map/ppermute | solution.py:52
  20.3 3.4 %collective-permute-start.5 = (bf16[1,6,48,256]{3,2,1,0:T(8,128)(2,1)S(1)}, bf16[1,6,48,256]{3,2,1,0:T(8,128)(2,1)S(1)}, u32[]{:S(2)}, u32[]{:S(2)}) collective-permute-start(bf16[1,6,48,256]{3,2,1,0:T(8,128)(2,1)S(1)} %bitcast.12), channel_id=1, source_target_pairs={{0,1},{1,0},{2,3},{3,2},{4,5},{5,4},{6,7},{7,6},{8,9},{9,8},{10,11... | collective-permute-start | bytes 442376 | tf_op jit(solution)/shard_map/ppermute | solution.py:52
  23.7 6.3 %collective-permute-start.7 = (bf16[1,6,48,256]{3,2,1,0:T(8,128)(2,1)S(1)}, bf16[1,6,48,256]{3,2,1,0:T(8,128)(2,1)S(1)}, u32[]{:S(2)}, u32[]{:S(2)}) collective-permute-start(bf16[1,6,48,256]{3,2,1,0:T(8,128)(2,1)S(1)} %collective-permute-done.4.refs_0_), channel_id=1, source_target_pairs={{0,1},{1,0},{2,3},{3,2},{4,5},{5,4},{6,7},{7,6},{8,9},{9,8},{10,11... | collective-permute-start | bytes 442376 | tf_op jit(solution)/shard_map/ppermute | solution.py:52
  23.7 1.0 %copy-start.1 = (bf16[512,256]{1,0:T(8,128)(2,1)S(1)}, bf16[512,256]{1,0:T(8,128)(2,1)}, u32[]{:S(2)}) copy-start(bf16[512,256]{1,0:T(8,128)(2,1)} %constant.108.clone.refs_3_) | copy-start | bytes 786436
  24.6 0.9 %copy-start.3 = (f32[16,6,2,128]{3,2,1,0:T(2,128)S(1)}, f32[16,6,2,128]{3,2,1,0:T(2,128)}, u32[]{:S(2)}) copy-start(f32[16,6,2,128]{3,2,1,0:T(2,128)} %constant.109.clone.refs_4_) | copy-start | bytes 294916
  25.5 4.5 %copy-start.2 = (bf16[512,256]{1,0:T(8,128)(2,1)S(1)}, bf16[512,256]{1,0:T(8,128)(2,1)}, u32[]{:S(2)}) copy-start(bf16[512,256]{1,0:T(8,128)(2,1)} %constant.108.clone.refs_3_) | copy-start | bytes 786436
  27.9 6.8 %collective-permute-start.6 = (bf16[2,6,48,256]{3,2,1,0:T(8,128)(2,1)S(1)}, bf16[2,6,48,256]{3,2,1,0:T(8,128)(2,1)S(1)}, u32[]{:S(2)}, u32[]{:S(2)}) collective-permute-start(bf16[2,6,48,256]{3,2,1,0:T(8,128)(2,1)S(1)} %pad_maximum_fusion), channel_id=1, source_target_pairs={{0,2},{1,7},{2,0},{3,5},{4,6},{5,3},{6,4},{7,1},{8,10},{9,15},{10,... | collective-permute-start | bytes 884744 | tf_op jit(solution)/shard_map/ppermute | solution.py:52
  34.7 8.8 %collective-permute-start.10 = (bf16[2,6,48,256]{3,2,1,0:T(8,128)(2,1)S(1)}, bf16[2,6,48,256]{3,2,1,0:T(8,128)(2,1)S(1)}, u32[]{:S(2)}, u32[]{:S(2)}) collective-permute-start(bf16[2,6,48,256]{3,2,1,0:T(8,128)(2,1)S(1)} %pad_maximum_fusion), channel_id=1, source_target_pairs={{0,6},{1,9},{2,4},{3,11},{4,2},{5,13},{6,0},{7,15},{8,14},{9,1},{1... | collective-permute-start | bytes 884744 | tf_op jit(solution)/shard_map/ppermute | solution.py:52
  38.8 7.9 %collective-permute-start.8 = (bf16[2,6,48,256]{3,2,1,0:T(8,128)(2,1)S(1)}, bf16[2,6,48,256]{3,2,1,0:T(8,128)(2,1)S(1)}, u32[]{:S(2)}, u32[]{:S(2)}) collective-permute-start(bf16[2,6,48,256]{3,2,1,0:T(8,128)(2,1)S(1)} %collective-permute-done.6.refs_0_), channel_id=1, source_target_pairs={{0,6},{1,9},{2,4},{3,11},{4,2},{5,13},{6,0},{7,15},{8,14},{9,1},{1... | collective-permute-start | bytes 884744 | tf_op jit(solution)/shard_map/ppermute | solution.py:52
  38.8 7.9 %collective-permute-start.12 = (bf16[2,6,48,256]{3,2,1,0:T(8,128)(2,1)S(1)}, bf16[2,6,48,256]{3,2,1,0:T(8,128)(2,1)S(1)}, u32[]{:S(2)}, u32[]{:S(2)}) collective-permute-start(bf16[2,6,48,256]{3,2,1,0:T(8,128)(2,1)S(1)} %collective-permute-done.6.refs_0_), channel_id=1, source_target_pairs={{0,1},{1,0},{2,3},{3,2},{4,5},{5,4},{6,7},{7,6},{8,9},{9,8},{10,11... | collective-permute-start | bytes 884744 | tf_op jit(solution)/shard_map/ppermute | solution.py:52
  43.5 7.3 %collective-permute-start.11 = (bf16[2,6,48,256]{3,2,1,0:T(8,128)(2,1)S(1)}, bf16[2,6,48,256]{3,2,1,0:T(8,128)(2,1)S(1)}, u32[]{:S(2)}, u32[]{:S(2)}) collective-permute-start(bf16[2,6,48,256]{3,2,1,0:T(8,128)(2,1)S(1)} %collective-permute-done.10.refs_0_), channel_id=1, source_target_pairs={{0,1},{1,0},{2,3},{3,2},{4,5},{5,4},{6,7},{7,6},{8,9},{9,8},{10,11... | collective-permute-start | bytes 884744 | tf_op jit(solution)/shard_map/ppermute | solution.py:52
  46.7 8.2 %collective-permute-start.9 = (bf16[2,6,48,256]{3,2,1,0:T(8,128)(2,1)S(1)}, bf16[2,6,48,256]{3,2,1,0:T(8,128)(2,1)S(1)}, u32[]{:S(2)}, u32[]{:S(2)}) collective-permute-start(bf16[2,6,48,256]{3,2,1,0:T(8,128)(2,1)S(1)} %collective-permute-done.8.refs_0_), channel_id=1, source_target_pairs={{0,1},{1,0},{2,3},{3,2},{4,5},{5,4},{6,7},{7,6},{8,9},{9,8},{10,11... | collective-permute-start | bytes 884744 | tf_op jit(solution)/shard_map/ppermute | solution.py:52
  60.2 1.5 %collective-permute-start.13 = (f32[8,8]{1,0:T(8,128)S(1)}, f32[8,8]{1,0:T(8,128)S(1)}, u32[]{:S(2)}, u32[]{:S(2)}) collective-permute-start(f32[8,8]{1,0:T(8,128)S(1)} %get-tuple-element.148), channel_id=1, source_target_pairs={{0,1},{1,0},{2,3},{3,2},{4,5},{5,4},{6,7},{7,6},{8,9},{9,8},{10,11... | collective-permute-start | bytes 776 | tf_op jit(solution)/shard_map/ppermute | solution.py:52
  61.6 3.6 %collective-permute-start.14 = (f32[8,8]{1,0:T(8,128)S(1)}, f32[8,8]{1,0:T(8,128)S(1)}, u32[]{:S(2)}, u32[]{:S(2)}) collective-permute-start(f32[8,8]{1,0:T(8,128)S(1)} %max.12), channel_id=1, source_target_pairs={{0,2},{1,3},{2,0},{3,1},{4,6},{5,7},{6,4},{7,5},{8,10},{9,11},{10,... | collective-permute-start | bytes 776 | tf_op jit(solution)/shard_map/ppermute | solution.py:52
  65.3 4.8 %collective-permute-start.15 = (f32[8,8]{1,0:T(8,128)S(1)}, f32[8,8]{1,0:T(8,128)S(1)}, u32[]{:S(2)}, u32[]{:S(2)}) collective-permute-start(f32[8,8]{1,0:T(8,128)S(1)} %max.13), channel_id=1, source_target_pairs={{0,6},{1,7},{2,4},{3,5},{4,2},{5,3},{6,0},{7,1},{8,14},{9,15},{10,... | collective-permute-start | bytes 776 | tf_op jit(solution)/shard_map/ppermute | solution.py:52
  70.1 5.1 %collective-permute-start.16 = (f32[8,8]{1,0:T(8,128)S(1)}, f32[8,8]{1,0:T(8,128)S(1)}, u32[]{:S(2)}, u32[]{:S(2)}) collective-permute-start(f32[8,8]{1,0:T(8,128)S(1)} %max.14), channel_id=1, source_target_pairs={{0,8},{1,9},{2,10},{3,11},{4,12},{5,13},{6,14},{7,15},{8,0},{9,1},... | collective-permute-start | bytes 776 | tf_op jit(solution)/shard_map/ppermute | solution.py:52

commit v6 on v5

--- a/solution.py
+++ b/solution.py
@@ -97,24 +97,55 @@
     return ((dt // 2) ^ (place % 4)) * 2 + ((dt % 2) ^ (place // 4))
 
 
-def widen_kernel(templ_ref, edges_ref, live_ref, wide_ref, bin_ref, stat_ref, *binned):
+def lane_rates():
+    lane = np.arange(FB + LANES, dtype=np.int32)
+    starts = (FLOW // FB + (lane - FB) * JS) * FB
+    return np.where(lane < FB, lane * STRIDE, np.where(lane < FB + NSL, starts, FB)).astype(np.int32)[None]
+
+
+def prepare_kernel(
+    templ_hbm, edges_hbm, live_hbm, shifts_hbm, rate_hbm, table_hbm, turn_hbm,
+    wide_ref, bin_ref, stat_ref, phase_ref, table_ref, turn_ref, *refs,
+):
+    binned, (templ_ref, edges_ref, live_ref, shifts_ref, rate_ref, upper_ref, first_ref, sems) = refs[:SLOTS], refs[SLOTS:]
+    moves = [(edges_hbm, edges_ref), (live_hbm, live_ref), (shifts_hbm, shifts_ref), (rate_hbm, rate_ref)]
+    moves += [(templ_hbm.at[k], templ_ref.at[k]) for k in range(SLOTS)]
+    moves += [(table_hbm, table_ref), (turn_hbm, turn_ref)]
+    copies = [pltpu.make_async_copy(a, b, sems.at[n]) for n, (a, b) in enumerate(moves)]
+    for copy in copies:
+        copy.start()
     for ref in binned:
         ref[...] = jnp.zeros_like(ref)
+    for copy in copies[:4]:
+        copy.wait()
+
+    for place in range(SEGS):
+        first_ref[place:place + 1, :] = shifts_ref[pl.ds(segment_at(place), 1), :]
+    ordered = first_ref[...] + MARGIN
+    first = jnp.concatenate([ordered[:, d:d + 1] for d in range(NDET)], axis=0)
+    turns = (first * rate_ref[...]) & (NFFT - 1)
+    angle = turns.astype(jnp.float32) * jnp.float32(TWO_PI / NFFT)
+    phase_ref[0] = jnp.cos(angle)
+    phase_ref[1] = jnp.sin(angle)
+
     lane = lax.broadcasted_iota(jnp.int32, (SLOTS, LANES), 1)
     bin_of = jnp.zeros((SLOTS, LANES), jnp.int32)
     for e in range(NBIN - 1):
         bin_of = bin_of + (edges_ref[:, e:e + 1] <= lane).astype(jnp.int32)
     bin_ref[...] = bin_of
+    upper_ref[...] = jnp.full((SLOTS, LANES), NBLK, jnp.int32)
+    upper_ref[:, :NBIN - 1] = edges_ref[...]
     block = lax.broadcasted_iota(jnp.int32, (NBLK, LANES), 0)
     at_lane = lax.broadcasted_iota(jnp.int32, (1, LANES), 1)
     for k in range(SLOTS):
+        copies[4 + k].wait()
         h = templ_ref[k, 0].astype(jnp.float32)
         i = templ_ref[k, 1].astype(jnp.float32)
         wide_ref[k, 0] = h
         wide_ref[k, 1] = h + i
         wide_ref[k, 2] = h - i
         power = jnp.sum(h * h + i * i, axis=1, keepdims=True)
-        upper = edges_ref[k:k + 1, :]
+        upper = upper_ref[k:k + 1, :]
         lower = jnp.where(at_lane == 0, 0, pltpu.roll(upper, 1, 1))
         inside = jnp.where((block >= lower) & (block < upper), power, 0.0)
         in_bins = jnp.sum(inside, axis=0, keepdims=True)
@@ -125,6 +156,8 @@
         row = jnp.where(at_lane == 2 * NBIN, 0.5 / sigma2, live)
         row = jnp.where(at_lane < 2 * NBIN, inv, row)
         stat_ref[k:k + 1, :] = jnp.where(at_lane < NBIN, frac, row)
+    for copy in copies[4 + SLOTS:]:
+        copy.wait()
 
 
 def whole():
@@ -134,21 +167,36 @@
 BINNED = [jax.ShapeDtypeStruct((NBIN, ROWS, 2 * TW), jnp.float32)] * SLOTS
 
 
-def widen(templates, edges, live_count):
+def prepare(templates, edges, live_count, shifts):
+    table, turn = tables()
+    operands = (templates, edges, live_count, shifts, lane_rates(), table, turn)
     outs = pl.pallas_call(
-        widen_kernel,
+        prepare_kernel,
         out_shape=[
             jax.ShapeDtypeStruct((SLOTS, 3, NBLK, FB), jnp.float32),
             jax.ShapeDtypeStruct((SLOTS, LANES), jnp.int32),
             jax.ShapeDtypeStruct((SLOTS, LANES), jnp.float32),
+            jax.ShapeDtypeStruct((2, ROWS, FB + LANES), jnp.float32),
+            jax.ShapeDtypeStruct(table.shape, table.dtype),
+            jax.ShapeDtypeStruct(turn.shape, turn.dtype),
         ] + BINNED,
-        in_specs=[whole()] * 3,
-        out_specs=[whole()] * (3 + SLOTS),
+        in_specs=[pl.BlockSpec(memory_space=pl.ANY)] * len(operands),
+        out_specs=[whole()] * (6 + SLOTS),
+        scratch_shapes=[
+            pltpu.VMEM(templates.shape, templates.dtype),
+            pltpu.VMEM(edges.shape, jnp.int32),
+            pltpu.VMEM(live_count.shape, jnp.int32),
+            pltpu.VMEM(shifts.shape, jnp.int32),
+            pltpu.VMEM((1, FB + LANES), jnp.int32),
+            pltpu.VMEM((SLOTS, LANES), jnp.int32),
+            pltpu.VMEM(shifts.shape, jnp.int32),
+            pltpu.SemaphoreType.DMA((6 + SLOTS,)),
+        ],
         compiler_params=pltpu.CompilerParams(vmem_limit_bytes=VMEM),
         cost_estimate=pl.CostEstimate(flops=10**6, bytes_accessed=10**6, transcendentals=0),
-        name="widen",
-    )(templates, edges, live_count)
-    return outs[0], outs[1], outs[2], outs[3:]
+        name="prepare",
+    )(*operands)
+    return outs[:6], outs[6:]
 
 
 def bins_kernel(parts, last, *refs):
@@ -295,33 +343,15 @@
     )(*operands)
 
 
-def phases(shifts):
-    row = jnp.arange(ROWS, dtype=jnp.int32)
-    segment = segment_at(row % SEGS)
-    here = (jnp.arange(SEGS, dtype=jnp.int32)[None, :, None] == segment[:, None, None]) & (
-        jnp.arange(NDET, dtype=jnp.int32)[None, None, :] == (row // SEGS)[:, None, None]
-    )
-    first = MARGIN + jnp.sum(jnp.where(here, shifts[None], 0), axis=(1, 2))
-    lane = np.arange(FB + LANES, dtype=np.int32)
-    starts = (FLOW // FB + (lane - FB) * JS) * FB
-    rate = np.where(lane < FB, lane * STRIDE, np.where(lane < FB + NSL, starts, FB)).astype(np.int32)
-    angle = ((first[:, None] * rate[None, :]) % NFFT).astype(jnp.float32) * jnp.float32(TWO_PI / NFFT)
-    quarter = np.array([0.0, 0.5 * math.pi], np.float32)[:, None, None]
-    return jnp.cos(angle[None] - quarter)
-
-
 def per_device(strain, templates, live_count, chi_edges, shifts):
-    edges = jnp.pad(chi_edges, ((0, 0), (0, LANES - NBIN + 1)), constant_values=NBLK)
-    wide, bin_of, stat, binned = widen(templates, edges, live_count)
-    table, turn = tables()
-    turned = phases(shifts)
+    (wide, bin_of, stat, turned, table, turn), binned = prepare(templates, chi_edges, live_count, shifts)
 
     x = jnp.transpose(strain[0], (2, 1, 0, 3)).reshape(JS, 2 * NDET, 1, FB)
     got = {0: x}
     for dx in (2, 3, 1):
         got[dx] = swap_with(x, across(dx=dx))
     x = jnp.concatenate([got[dx] for dx in range(4)], axis=2)
-    x, wide, turned = lax.optimization_barrier((x, wide, turned))
+    x, wide = lax.optimization_barrier((x, wide))
     x = jnp.concatenate([x, swap_with(x, across(dy=1))], axis=2)
     shared = (bin_of, table, turn, wide, turned)
 
@@ -335,17 +365,20 @@
     p0 = x.reshape(1, JS, 2 * ROWS, FB)
     q0 = to_core(p0)
     p1 = swap_with(p0, step_move(0))
+    binned = add_bins((p0, q0), ((0, 1, 0), (0, 1, 1)), shared, binned)
+    p1, binned = after(p1, binned)
     q1 = to_core(p1)
-    binned = add_bins((p0, q0), ((0, 1, 0), (0, 1, 1)), shared, binned)
-    p01, binned = after(jnp.concatenate([p0, p1], axis=0), binned)
+    p01 = jnp.concatenate([p0, p1], axis=0)
     p23 = swap_with(p01, step_move(1))
+    binned = add_bins((p1, q1), ((1, 1, 0), (1, 1, 1)), shared, binned)
+    p23, binned = after(p23, binned)
     q23 = to_core(p23)
-    binned = add_bins((p1, q1), ((1, 1, 0), (1, 1, 1)), shared, binned)
-    (p01, p23), binned = after((p01, p23), binned)
+    p01, p23 = lax.optimization_barrier((p01, p23))
     p45 = swap_with(p01, step_move(2))
     p67 = swap_with(p23, step_move(2))
+    binned = add_bins((p23, q23), ((2, 2, 0), (2, 2, 1)), shared, binned)
+    (p45, p67), binned = after((p45, p67), binned)
     q45, q67 = to_core(p45), to_core(p67)
-    binned = add_bins((p23, q23), ((2, 2, 0), (2, 2, 1)), shared, binned)
     binned = add_bins((p45, q45), ((4, 2, 0), (4, 2, 1)), shared, binned)
     best = add_bins((p67, q67), ((6, 2, 0), (6, 2, 1)), shared, binned, stat)[-1]
     for move in (across(dcore=1), across(dz=1), across(dz=3), across(dy=2)):

time: 76.1 us -> 74.7 us (0.982)
  waiting for transfers between devices: 24 us -> 19.6 us
  Pallas kernels: 19.5 us -> 23.3 us
  other arithmetic: 3.26 us -> 0.71 us
  local copies, waits for them, and re-layouts: 4.59 us -> 6.01 us
    ppermute x17, waiting for transfers between devices: 24 us -> 19.6 us  [swap_with(): return lax.ppermute(value, AXES, pairs)]
    pallas_call x1, Pallas kernels: 1.44 us -> 5.31 us  [prepare(): pl.pallas_call(prepare_kernel, out_shape=[jax.ShapeDtypeStruct((SLOTS, 3,...]
    unnamed x9 -> x12, local copies, waits for them, and re-layouts: 3.84 us -> 5.97 us
    cos x1 -> x0, other arithmetic: 0.98 us -> none  [phases(): return jnp.cos(angle[None] - quarter)]
    mul x1 -> x0, other arithmetic: 0.77 us -> none  [phases(): (first[:, None] * rate[None, :] % NFFT).astype(jnp.float32)]
    reduce_sum x1 -> x0, other arithmetic: 0.77 us -> none  [phases(): first = MARGIN + jnp.sum(jnp.where(here, shifts[None], 0), axis=(1, 2))]
  transfers between devices with their start and end apart: 17 -> 17, of which waited for: 9 -> 10; matrix products, arithmetic and copies ran while one was open for 4% -> 1% of each run, Pallas kernels for 19% -> 24%
where the time goes in v6:
time: 74.7 us; the launch traced here: 74.3 us
  starting transfers between devices  23.8 us (32%)
  Pallas kernels  23.3 us (31%)
  waiting for transfers between devices  19.6 us (26%)
  local copies, waits for them, and re-layouts  6.01 us (8%)
  between operations  0.79 us (1%)
    ppermute x17, starting transfers between devices, swap_with(): return lax.ppermute(value, AXES, pairs)  23.8 us
    ppermute x17, waiting for transfers between devices, swap_with(): return lax.ppermute(value, AXES, pairs)  19.6 us
    pallas_call x5, Pallas kernels, add_bins(): pl.pallas_call(functools.partial(bins_kernel, parts, last), out_shape=out...  18 us
    unnamed x12, local copies, waits for them, and re-layouts  5.97 us
    pallas_call x1, Pallas kernels, prepare(): pl.pallas_call(prepare_kernel, out_shape=[jax.ShapeDtypeStruct((SLOTS, 3,...  5.31 us
  transfers between devices with their start and end apart: 17, of which 10 were waited for; matrix products, arithmetic and copies ran while one was open for 1% of the time, Pallas kernels for 24%

profile of v6, /device:TPU:0, one launch (start us, length us, event | category | flops | bytes accessed | tf_op | source)
XLA Modules:
  0.0 74.3 jit_solution(932769477341886893)
XLA Ops:
  0.0 0.7 copy.71
  0.7 1.6 %collective-permute-start = (bf16[6,6,1,256]{3,0,1,2:T(8,128)(2,1)S(1)}, bf16[6,6,1,256]{3,0,1,2:T(8,128)(2,1)S(1)}, u32[]{:S(2)}, u32[]{:S(2)}) collective-permute-start(bf16[6,6,1,256]{3,0,1,2:T(8,128)(2,1)S(1)} %bitcast.15), channel_id=1, source_target_pairs={{0,32},{1,33},{2,34},{3,35},{4,36},{5,37},{6,38},{7,39},{8,40},{9,... | collective-permute-start | bytes 55304 | tf_op jit(solution)/shard_map/ppermute | solution.py:52
  2.3 2.7 %collective-permute-start.1 = (bf16[6,6,1,256]{3,0,1,2:T(8,128)(2,1)S(1)}, bf16[6,6,1,256]{3,0,1,2:T(8,128)(2,1)S(1)}, u32[]{:S(2)}, u32[]{:S(2)}) collective-permute-start(bf16[6,6,1,256]{3,0,1,2:T(8,128)(2,1)S(1)} %bitcast.16), channel_id=1, source_target_pairs={{0,64},{1,65},{2,66},{3,67},{4,68},{5,69},{6,70},{7,71},{8,72},{9,... | collective-permute-start | bytes 55304 | tf_op jit(solution)/shard_map/ppermute | solution.py:52
  5.0 0.4 collective-permute-start.2
  5.4 0.8 %copy.72.shifts_hbm = s32[8,3]{1,0:T(8,128)S(1)} copy(s32[8,3]{0,1:T(4,128)} %param.12) | data formatting | bytes 192 | tf_op args[4]
  6.8 0.0 copy-start
  6.8 1.3 %copy-done = bf16[12,2,96,256]{3,2,1,0:T(8,128)(2,1)S(1)} copy-done((bf16[12,2,96,256]{3,2,1,0:T(8,128)(2,1)S(1)}, bf16[12,2,96,256]{3,2,1,0:T(8,128)(2,1)}, u32[]{:S(2)}) %copy-start) | copy-done | bytes 1179672
  8.1 0.9 %copy-done.1 = bf16[512,256]{1,0:T(8,128)(2,1)S(1)} copy-done((bf16[512,256]{1,0:T(8,128)(2,1)S(1)}, bf16[512,256]{1,0:T(8,128)(2,1)}, u32[]{:S(2)}) %copy-start.1) | copy-done | bytes 262168
  9.1 0.9 %copy-done.2 = f32[16,6,2,128]{3,2,1,0:T(2,128)S(1)} copy-done((f32[16,6,2,128]{3,2,1,0:T(2,128)S(1)}, f32[16,6,2,128]{3,2,1,0:T(2,128)}, u32[]{:S(2)}) %copy-start.2) | copy-done | bytes 98328
  10.0 0.7 copy-done.3
  10.7 0.7 copy-done.4
  11.3 5.3 %prepare.1 = (f32[12,3,96,256]{3,2,1,0:T(8,128)S(1)}, s32[12,128]{1,0:T(8,128)S(1)}, f32[12,128]{1,0:T(8,128)S(1)}, f32[2,24,384]{2,1,0:T(8,128)S(1)}, bf16[512,...) custom-call(bf16[12,2,96,256]{3,2,1,0:T(8,128)(2,1)S(1)} %copy-done,, ...), custom_call_target="tpu_custom_call" | custom-call | flops 1000000 | bytes 1000000 | tf_op jit(solution)/shard_map/prepare/pallas_call | solution.py:173
  16.6 0.0 collective-permute-done
  16.7 0.0 collective-permute-done.1
  16.7 1.7 %collective-permute-start.3 = (bf16[6,6,4,256]{3,0,1,2:T(8,128)(2,1)S(1)}, bf16[6,6,4,256]{3,0,1,2:T(8,128)(2,1)S(1)}, u32[]{:S(2)}, u32[]{:S(2)}) collective-permute-start(bf16[6,6,4,256]{3,0,1,2:T(8,128)(2,1)S(1)} %pad_maximum_fusion.2), channel_id=1, source_target_pairs={{0,16},{1,17},{2,18},{3,19},{4,20},{5,21},{6,22},{7,23},{8,24},{9,... | collective-permute-start | bytes 221192 | tf_op jit(solution)/shard_map/ppermute | solution.py:52
  18.5 3.0 %collective-permute-done.3 = bf16[6,6,4,256]{3,0,1,2:T(8,128)(2,1)S(1)} collective-permute-done((bf16[6,6,4,256]{3,0,1,2:T(8,128)(2,1)S(1)}, bf16[6,6,4,256]{3,0,1,2:T(8,128)(2,1)S(1)}, u32[]{:S(2)}, u32[]{:S(2)}) %collective-permute-start.3) | collective-permute-done | bytes 73760 | tf_op jit(solution)/shard_map/ppermute | solution.py:52
  21.5 0.1 collective-permute-start.5
  21.6 3.4 %collective-permute-start.4 = (bf16[1,6,48,256]{3,2,1,0:T(8,128)(2,1)S(1)}, bf16[1,6,48,256]{3,2,1,0:T(8,128)(2,1)S(1)}, u32[]{:S(2)}, u32[]{:S(2)}) collective-permute-start(bf16[1,6,48,256]{3,2,1,0:T(8,128)(2,1)S(1)} %bitcast.12), channel_id=1, source_target_pairs={{0,8},{1,3},{2,10},{3,1},{4,12},{5,7},{6,14},{7,5},{8,0},{9,11},{1... | collective-permute-start | bytes 442376 | tf_op jit(solution)/shard_map/ppermute | solution.py:52
  25.0 0.0 collective-permute-done.5.refs_1_
  25.0 2.3 %add_bins.4 = (f32[16,24,256]{2,1,0:T(8,128)S(1)}, f32[16,24,256]{2,1,0:T(8,128)S(1)}, f32[16,24,256]{2,1,0:T(8,128)S(1)}, f32[16,24,256]{2,1,0:T(8,128)S(1)}, f...) custom-call(bf16[1,6,48,256]{3,2,1,0:T(8,128)(2,1)S(1)} %bitcast.13,, ...), custom_call_target="tpu_custom_call", output_to_operand_aliasing={{0}: (7, {}), {1}: (8, {}), {2}: (9, {}), {3}: (10, {}), {4... | custom-call | flops 1811939328 | bytes 1000000 | tf_op jit(solution)/shard_map/add_bins/pallas_call | solution.py:333
  27.3 1.0 %collective-permute-done.4.refs_0_ = bf16[1,6,48,256]{3,2,1,0:T(8,128)(2,1)S(1)} collective-permute-done((bf16[1,6,48,256]{3,2,1,0:T(8,128)(2,1)S(1)}, bf16[1,6,48,256]{3,2,1,0:T(8,128)(2,1)S(1)}, u32[]{:S(2)}, u32[]{:S(2)}) %collective-permute-start.4) | collective-permute-done | bytes 147488 | tf_op jit(solution)/shard_map/ppermute | solution.py:52
  28.3 0.0 collective-permute-start.7
  28.4 2.1 %collective-permute-start.6 = (bf16[2,6,48,256]{3,2,1,0:T(8,128)(2,1)S(1)}, bf16[2,6,48,256]{3,2,1,0:T(8,128)(2,1)S(1)}, u32[]{:S(2)}, u32[]{:S(2)}) collective-permute-start(bf16[2,6,48,256]{3,2,1,0:T(8,128)(2,1)S(1)} %pad_maximum_fusion), channel_id=1, source_target_pairs={{0,2},{1,7},{2,0},{3,5},{4,6},{5,3},{6,4},{7,1},{8,10},{9,15},{10,... | collective-permute-start | bytes 884744 | tf_op jit(solution)/shard_map/ppermute | solution.py:52
  30.5 0.0 collective-permute-done.7.refs_1_
  30.5 2.4 %add_bins.5 = (f32[16,24,256]{2,1,0:T(8,128)S(1)}, f32[16,24,256]{2,1,0:T(8,128)S(1)}, f32[16,24,256]{2,1,0:T(8,128)S(1)}, f32[16,24,256]{2,1,0:T(8,128)S(1)}, f...) custom-call(bf16[1,6,48,256]{3,2,1,0:T(8,128)(2,1)S(1)} %collective-, ...), custom_call_target="tpu_custom_call", output_to_operand_aliasing={{0}: (7, {}), {1}: (8, {}), {2}: (9, {}), {3}: (10, {}), {4... | custom-call | flops 1811939328 | bytes 1000000 | tf_op jit(solution)/shard_map/add_bins/pallas_call | solution.py:333
  32.8 2.4 %collective-permute-done.6.refs_0_ = bf16[2,6,48,256]{3,2,1,0:T(8,128)(2,1)S(1)} collective-permute-done((bf16[2,6,48,256]{3,2,1,0:T(8,128)(2,1)S(1)}, bf16[2,6,48,256]{3,2,1,0:T(8,128)(2,1)S(1)}, u32[]{:S(2)}, u32[]{:S(2)}) %collective-permute-start.6) | collective-permute-done | bytes 294944 | tf_op jit(solution)/shard_map/ppermute | solution.py:52
  35.2 1.7 %collective-permute-start.10 = (bf16[2,6,48,256]{3,2,1,0:T(8,128)(2,1)S(1)}, bf16[2,6,48,256]{3,2,1,0:T(8,128)(2,1)S(1)}, u32[]{:S(2)}, u32[]{:S(2)}) collective-permute-start(bf16[2,6,48,256]{3,2,1,0:T(8,128)(2,1)S(1)} %collective-permute-done.6.refs_0_), channel_id=1, source_target_pairs={{0,1},{1,0},{2,3},{3,2},{4,5},{5,4},{6,7},{7,6},{8,9},{9,8},{10,11... | collective-permute-start | bytes 884744 | tf_op jit(solution)/shard_map/ppermute | solution.py:52
  36.9 3.0 %collective-permute-start.8 = (bf16[2,6,48,256]{3,2,1,0:T(8,128)(2,1)S(1)}, bf16[2,6,48,256]{3,2,1,0:T(8,128)(2,1)S(1)}, u32[]{:S(2)}, u32[]{:S(2)}) collective-permute-start(bf16[2,6,48,256]{3,2,1,0:T(8,128)(2,1)S(1)} %pad_maximum_fusion), channel_id=1, source_target_pairs={{0,6},{1,9},{2,4},{3,11},{4,2},{5,13},{6,0},{7,15},{8,14},{9,1},{1... | collective-permute-start | bytes 884744 | tf_op jit(solution)/shard_map/ppermute | solution.py:52
  39.9 0.3 collective-permute-start.9
  40.2 0.0 collective-permute-done.10.refs_1_
  40.2 4.0 %add_bins.6 = (f32[16,24,256]{2,1,0:T(8,128)S(1)}, f32[16,24,256]{2,1,0:T(8,128)S(1)}, f32[16,24,256]{2,1,0:T(8,128)S(1)}, f32[16,24,256]{2,1,0:T(8,128)S(1)}, f...) custom-call(bf16[2,6,48,256]{3,2,1,0:T(8,128)(2,1)S(1)} %collective-, ...), custom_call_target="tpu_custom_call", output_to_operand_aliasing={{0}: (7, {}), {1}: (8, {}), {2}: (9, {}), {3}: (10, {}), {4... | custom-call | flops 3623878656 | bytes 1000000 | tf_op jit(solution)/shard_map/add_bins/pallas_call | solution.py:333
  44.2 0.7 collective-permute-done.8.refs_0_
  44.8 3.2 %collective-permute-done.9.refs_0_ = bf16[2,6,48,256]{3,2,1,0:T(8,128)(2,1)S(1)} collective-permute-done((bf16[2,6,48,256]{3,2,1,0:T(8,128)(2,1)S(1)}, bf16[2,6,48,256]{3,2,1,0:T(8,128)(2,1)S(1)}, u32[]{:S(2)}, u32[]{:S(2)}) %collective-permute-start.9) | collective-permute-done | bytes 294944 | tf_op jit(solution)/shard_map/ppermute | solution.py:52
  48.0 0.0 collective-permute-start.12
  48.0 0.5 collective-permute-start.11
  48.5 1.1 %collective-permute-done.12.refs_1_ = bf16[2,6,48,256]{3,2,1,0:T(8,128)(2,1)S(1)} collective-permute-done((bf16[2,6,48,256]{3,2,1,0:T(8,128)(2,1)S(1)}, bf16[2,6,48,256]{3,2,1,0:T(8,128)(2,1)S(1)}, u32[]{:S(2)}, u32[]{:S(2)}) %collective-permute-start.12) | collective-permute-done | bytes 294944 | tf_op jit(solution)/shard_map/ppermute | solution.py:52
  49.6 4.0 %add_bins.7 = (f32[16,24,256]{2,1,0:T(8,128)S(1)}, f32[16,24,256]{2,1,0:T(8,128)S(1)}, f32[16,24,256]{2,1,0:T(8,128)S(1)}, f32[16,24,256]{2,1,0:T(8,128)S(1)}, f...) custom-call(bf16[2,6,48,256]{3,2,1,0:T(8,128)(2,1)S(1)} %collective-, ...), custom_call_target="tpu_custom_call", output_to_operand_aliasing={{0}: (7, {}), {1}: (8, {}), {2}: (9, {}), {3}: (10, {}), {4... | custom-call | flops 3623878656 | bytes 1000000 | tf_op jit(solution)/shard_map/add_bins/pallas_call | solution.py:333
  53.6 0.0 collective-permute-done.11.refs_1_
  53.7 5.3 %last_bins.1 = (f32[16,24,256]{2,1,0:T(8,128)S(1)}, f32[16,24,256]{2,1,0:T(8,128)S(1)}, f32[16,24,256]{2,1,0:T(8,128)S(1)}, f32[16,24,256]{2,1,0:T(8,128)S(1)}, ...) custom-call(bf16[2,6,48,256]{3,2,1,0:T(8,128)(2,1)S(1)} %collective-, ...), custom_call_target="tpu_custom_call", output_to_operand_aliasing={{0}: (8, {}), {1}: (9, {}), {2}: (10, {}), {3}: (11, {}), {... | custom-call | flops 3623878656 | bytes 1000000 | tf_op jit(solution)/shard_map/last_bins/pallas_call | solution.py:333
  58.9 0.2 collective-permute-start.13
  59.1 1.0 %collective-permute-done.13 = f32[8,8]{1,0:T(8,128)S(1)} collective-permute-done((f32[8,8]{1,0:T(8,128)S(1)}, f32[8,8]{1,0:T(8,128)S(1)}, u32[]{:S(2)}, u32[]{:S(2)}) %collective-permute-start.13) | collective-permute-done | bytes 288 | tf_op jit(solution)/shard_map/ppermute | solution.py:52
  60.2 0.0 collective-permute-start.14
  60.2 3.6 %collective-permute-done.14 = f32[8,8]{1,0:T(8,128)S(1)} collective-permute-done((f32[8,8]{1,0:T(8,128)S(1)}, f32[8,8]{1,0:T(8,128)S(1)}, u32[]{:S(2)}, u32[]{:S(2)}) %collective-permute-start.14) | collective-permute-done | bytes 288 | tf_op jit(solution)/shard_map/ppermute | solution.py:52
  63.8 3.0 %collective-permute-start.15 = (f32[8,8]{1,0:T(8,128)S(1)}, f32[8,8]{1,0:T(8,128)S(1)}, u32[]{:S(2)}, u32[]{:S(2)}) collective-permute-start(f32[8,8]{1,0:T(8,128)S(1)} %max.13), channel_id=1, source_target_pairs={{0,6},{1,7},{2,4},{3,5},{4,2},{5,3},{6,0},{7,1},{8,14},{9,15},{10,... | collective-permute-start | bytes 776 | tf_op jit(solution)/shard_map/ppermute | solution.py:52
  66.7 1.9 %collective-permute-done.15 = f32[8,8]{1,0:T(8,128)S(1)} collective-permute-done((f32[8,8]{1,0:T(8,128)S(1)}, f32[8,8]{1,0:T(8,128)S(1)}, u32[]{:S(2)}, u32[]{:S(2)}) %collective-permute-start.15) | collective-permute-done | bytes 288 | tf_op jit(solution)/shard_map/ppermute | solution.py:52
  68.6 3.2 %collective-permute-start.16 = (f32[8,8]{1,0:T(8,128)S(1)}, f32[8,8]{1,0:T(8,128)S(1)}, u32[]{:S(2)}, u32[]{:S(2)}) collective-permute-start(f32[8,8]{1,0:T(8,128)S(1)} %max.14), channel_id=1, source_target_pairs={{0,8},{1,9},{2,10},{3,11},{4,12},{5,13},{6,14},{7,15},{8,0},{9,1},... | collective-permute-start | bytes 776 | tf_op jit(solution)/shard_map/ppermute | solution.py:52
  71.8 1.9 %collective-permute-done.16 = f32[8,8]{1,0:T(8,128)S(1)} collective-permute-done((f32[8,8]{1,0:T(8,128)S(1)}, f32[8,8]{1,0:T(8,128)S(1)}, u32[]{:S(2)}, u32[]{:S(2)}) %collective-permute-start.16) | collective-permute-done | bytes 288 | tf_op jit(solution)/shard_map/ppermute | solution.py:52
  73.7 0.6 max.15
  (12 shorter events, 0.2 us)
Async XLA Ops:
  0.7 15.9 %collective-permute-start = (bf16[6,6,1,256]{3,0,1,2:T(8,128)(2,1)S(1)}, bf16[6,6,1,256]{3,0,1,2:T(8,128)(2,1)S(1)}, u32[]{:S(2)}, u32[]{:S(2)}) collective-permute-start(bf16[6,6,1,256]{3,0,1,2:T(8,128)(2,1)S(1)} %bitcast.15), channel_id=1, source_target_pairs={{0,32},{1,33},{2,34},{3,35},{4,36},{5,37},{6,38},{7,39},{8,40},{9,... | collective-permute-start | bytes 55304 | tf_op jit(solution)/shard_map/ppermute | solution.py:52
  2.3 14.4 %collective-permute-start.1 = (bf16[6,6,1,256]{3,0,1,2:T(8,128)(2,1)S(1)}, bf16[6,6,1,256]{3,0,1,2:T(8,128)(2,1)S(1)}, u32[]{:S(2)}, u32[]{:S(2)}) collective-permute-start(bf16[6,6,1,256]{3,0,1,2:T(8,128)(2,1)S(1)} %bitcast.16), channel_id=1, source_target_pairs={{0,64},{1,65},{2,66},{3,67},{4,68},{5,69},{6,70},{7,71},{8,72},{9,... | collective-permute-start | bytes 55304 | tf_op jit(solution)/shard_map/ppermute | solution.py:52
  5.0 11.6 %collective-permute-start.2 = (bf16[6,6,1,256]{3,0,1,2:T(8,128)(2,1)S(1)}, bf16[6,6,1,256]{3,0,1,2:T(8,128)(2,1)S(1)}, u32[]{:S(2)}, u32[]{:S(2)}) collective-permute-start(bf16[6,6,1,256]{3,0,1,2:T(8,128)(2,1)S(1)} %bitcast.17), channel_id=1, source_target_pairs={{0,96},{1,97},{2,98},{3,99},{4,100},{5,101},{6,102},{7,103},{8,104... | collective-permute-start | bytes 55304 | tf_op jit(solution)/shard_map/ppermute | solution.py:52
  6.8 1.3 %copy-start = (bf16[12,2,96,256]{3,2,1,0:T(8,128)(2,1)S(1)}, bf16[12,2,96,256]{3,2,1,0:T(8,128)(2,1)}, u32[]{:S(2)}) copy-start(bf16[12,2,96,256]{3,2,1,0:T(8,128)(2,1)} %templ_hbm.1) | copy-start | bytes 3538948
  8.1 0.9 %copy-start.1 = (bf16[512,256]{1,0:T(8,128)(2,1)S(1)}, bf16[512,256]{1,0:T(8,128)(2,1)}, u32[]{:S(2)}) copy-start(bf16[512,256]{1,0:T(8,128)(2,1)} %constant.7.clone.table_hbm) | copy-start | bytes 786436
  9.1 0.9 %copy-start.2 = (f32[16,6,2,128]{3,2,1,0:T(2,128)S(1)}, f32[16,6,2,128]{3,2,1,0:T(2,128)}, u32[]{:S(2)}) copy-start(f32[16,6,2,128]{3,2,1,0:T(2,128)} %constant.8.clone.turn_hbm) | copy-start | bytes 294916
  10.0 0.7 copy-start.3
  10.7 0.7 copy-start.4
  16.7 4.7 %collective-permute-start.3 = (bf16[6,6,4,256]{3,0,1,2:T(8,128)(2,1)S(1)}, bf16[6,6,4,256]{3,0,1,2:T(8,128)(2,1)S(1)}, u32[]{:S(2)}, u32[]{:S(2)}) collective-permute-start(bf16[6,6,4,256]{3,0,1,2:T(8,128)(2,1)S(1)} %pad_maximum_fusion.2), channel_id=1, source_target_pairs={{0,16},{1,17},{2,18},{3,19},{4,20},{5,21},{6,22},{7,23},{8,24},{9,... | collective-permute-start | bytes 221192 | tf_op jit(solution)/shard_map/ppermute | solution.py:52
  21.5 3.5 %collective-permute-start.5 = (bf16[1,6,48,256]{3,2,1,0:T(8,128)(2,1)S(1)}, bf16[1,6,48,256]{3,2,1,0:T(8,128)(2,1)S(1)}, u32[]{:S(2)}, u32[]{:S(2)}) collective-permute-start(bf16[1,6,48,256]{3,2,1,0:T(8,128)(2,1)S(1)} %bitcast.11), channel_id=1, source_target_pairs={{0,1},{1,0},{2,3},{3,2},{4,5},{5,4},{6,7},{7,6},{8,9},{9,8},{10,11... | collective-permute-start | bytes 442376 | tf_op jit(solution)/shard_map/ppermute | solution.py:52
  21.6 6.7 %collective-permute-start.4 = (bf16[1,6,48,256]{3,2,1,0:T(8,128)(2,1)S(1)}, bf16[1,6,48,256]{3,2,1,0:T(8,128)(2,1)S(1)}, u32[]{:S(2)}, u32[]{:S(2)}) collective-permute-start(bf16[1,6,48,256]{3,2,1,0:T(8,128)(2,1)S(1)} %bitcast.12), channel_id=1, source_target_pairs={{0,8},{1,3},{2,10},{3,1},{4,12},{5,7},{6,14},{7,5},{8,0},{9,11},{1... | collective-permute-start | bytes 442376 | tf_op jit(solution)/shard_map/ppermute | solution.py:52
  28.3 2.1 %collective-permute-start.7 = (bf16[1,6,48,256]{3,2,1,0:T(8,128)(2,1)S(1)}, bf16[1,6,48,256]{3,2,1,0:T(8,128)(2,1)S(1)}, u32[]{:S(2)}, u32[]{:S(2)}) collective-permute-start(bf16[1,6,48,256]{3,2,1,0:T(8,128)(2,1)S(1)} %collective-permute-done.4.refs_0_), channel_id=1, source_target_pairs={{0,1},{1,0},{2,3},{3,2},{4,5},{5,4},{6,7},{7,6},{8,9},{9,8},{10,11... | collective-permute-start | bytes 442376 | tf_op jit(solution)/shard_map/ppermute | solution.py:52
  28.4 6.8 %collective-permute-start.6 = (bf16[2,6,48,256]{3,2,1,0:T(8,128)(2,1)S(1)}, bf16[2,6,48,256]{3,2,1,0:T(8,128)(2,1)S(1)}, u32[]{:S(2)}, u32[]{:S(2)}) collective-permute-start(bf16[2,6,48,256]{3,2,1,0:T(8,128)(2,1)S(1)} %pad_maximum_fusion), channel_id=1, source_target_pairs={{0,2},{1,7},{2,0},{3,5},{4,6},{5,3},{6,4},{7,1},{8,10},{9,15},{10,... | collective-permute-start | bytes 884744 | tf_op jit(solution)/shard_map/ppermute | solution.py:52
  35.2 5.0 %collective-permute-start.10 = (bf16[2,6,48,256]{3,2,1,0:T(8,128)(2,1)S(1)}, bf16[2,6,48,256]{3,2,1,0:T(8,128)(2,1)S(1)}, u32[]{:S(2)}, u32[]{:S(2)}) collective-permute-start(bf16[2,6,48,256]{3,2,1,0:T(8,128)(2,1)S(1)} %collective-permute-done.6.refs_0_), channel_id=1, source_target_pairs={{0,1},{1,0},{2,3},{3,2},{4,5},{5,4},{6,7},{7,6},{8,9},{9,8},{10,11... | collective-permute-start | bytes 884744 | tf_op jit(solution)/shard_map/ppermute | solution.py:52
  36.9 7.9 %collective-permute-start.8 = (bf16[2,6,48,256]{3,2,1,0:T(8,128)(2,1)S(1)}, bf16[2,6,48,256]{3,2,1,0:T(8,128)(2,1)S(1)}, u32[]{:S(2)}, u32[]{:S(2)}) collective-permute-start(bf16[2,6,48,256]{3,2,1,0:T(8,128)(2,1)S(1)} %pad_maximum_fusion), channel_id=1, source_target_pairs={{0,6},{1,9},{2,4},{3,11},{4,2},{5,13},{6,0},{7,15},{8,14},{9,1},{1... | collective-permute-start | bytes 884744 | tf_op jit(solution)/shard_map/ppermute | solution.py:52
  39.9 8.1 %collective-permute-start.9 = (bf16[2,6,48,256]{3,2,1,0:T(8,128)(2,1)S(1)}, bf16[2,6,48,256]{3,2,1,0:T(8,128)(2,1)S(1)}, u32[]{:S(2)}, u32[]{:S(2)}) collective-permute-start(bf16[2,6,48,256]{3,2,1,0:T(8,128)(2,1)S(1)} %collective-permute-done.6.refs_0_), channel_id=1, source_target_pairs={{0,6},{1,9},{2,4},{3,11},{4,2},{5,13},{6,0},{7,15},{8,14},{9,1},{1... | collective-permute-start | bytes 884744 | tf_op jit(solution)/shard_map/ppermute | solution.py:52
  48.0 1.6 %collective-permute-start.12 = (bf16[2,6,48,256]{3,2,1,0:T(8,128)(2,1)S(1)}, bf16[2,6,48,256]{3,2,1,0:T(8,128)(2,1)S(1)}, u32[]{:S(2)}, u32[]{:S(2)}) collective-permute-start(bf16[2,6,48,256]{3,2,1,0:T(8,128)(2,1)S(1)} %collective-permute-done.8.refs_0_), channel_id=1, source_target_pairs={{0,1},{1,0},{2,3},{3,2},{4,5},{5,4},{6,7},{7,6},{8,9},{9,8},{10,11... | collective-permute-start | bytes 884744 | tf_op jit(solution)/shard_map/ppermute | solution.py:52
  48.0 5.6 %collective-permute-start.11 = (bf16[2,6,48,256]{3,2,1,0:T(8,128)(2,1)S(1)}, bf16[2,6,48,256]{3,2,1,0:T(8,128)(2,1)S(1)}, u32[]{:S(2)}, u32[]{:S(2)}) collective-permute-start(bf16[2,6,48,256]{3,2,1,0:T(8,128)(2,1)S(1)} %collective-permute-done.9.refs_0_), channel_id=1, source_target_pairs={{0,1},{1,0},{2,3},{3,2},{4,5},{5,4},{6,7},{7,6},{8,9},{9,8},{10,11... | collective-permute-start | bytes 884744 | tf_op jit(solution)/shard_map/ppermute | solution.py:52
  58.9 1.2 %collective-permute-start.13 = (f32[8,8]{1,0:T(8,128)S(1)}, f32[8,8]{1,0:T(8,128)S(1)}, u32[]{:S(2)}, u32[]{:S(2)}) collective-permute-start(f32[8,8]{1,0:T(8,128)S(1)} %get-tuple-element.160), channel_id=1, source_target_pairs={{0,1},{1,0},{2,3},{3,2},{4,5},{5,4},{6,7},{7,6},{8,9},{9,8},{10,11... | collective-permute-start | bytes 776 | tf_op jit(solution)/shard_map/ppermute | solution.py:52
  60.2 3.6 %collective-permute-start.14 = (f32[8,8]{1,0:T(8,128)S(1)}, f32[8,8]{1,0:T(8,128)S(1)}, u32[]{:S(2)}, u32[]{:S(2)}) collective-permute-start(f32[8,8]{1,0:T(8,128)S(1)} %max.12), channel_id=1, source_target_pairs={{0,2},{1,3},{2,0},{3,1},{4,6},{5,7},{6,4},{7,5},{8,10},{9,11},{10,... | collective-permute-start | bytes 776 | tf_op jit(solution)/shard_map/ppermute | solution.py:52
  63.8 4.8 %collective-permute-start.15 = (f32[8,8]{1,0:T(8,128)S(1)}, f32[8,8]{1,0:T(8,128)S(1)}, u32[]{:S(2)}, u32[]{:S(2)}) collective-permute-start(f32[8,8]{1,0:T(8,128)S(1)} %max.13), channel_id=1, source_target_pairs={{0,6},{1,7},{2,4},{3,5},{4,2},{5,3},{6,0},{7,1},{8,14},{9,15},{10,... | collective-permute-start | bytes 776 | tf_op jit(solution)/shard_map/ppermute | solution.py:52
  68.6 5.1 %collective-permute-start.16 = (f32[8,8]{1,0:T(8,128)S(1)}, f32[8,8]{1,0:T(8,128)S(1)}, u32[]{:S(2)}, u32[]{:S(2)}) collective-permute-start(f32[8,8]{1,0:T(8,128)S(1)} %max.14), channel_id=1, source_target_pairs={{0,8},{1,9},{2,10},{3,11},{4,12},{5,13},{6,14},{7,15},{8,0},{9,1},... | collective-permute-start | bytes 776 | tf_op jit(solution)/shard_map/ppermute | solution.py:52

commit v7 on v5

v7 whole, which is shorter than its diff:
```python
import functools
import math

import jax
import jax.numpy as jnp
from jax import lax
from jax.experimental import pallas as pl
from jax.experimental.pallas import tpu as pltpu
from jax.sharding import PartitionSpec as P

FB = 256
NBLK = 96
NFFT = 1048576
FLOW = 5120
STRIDE = 4097
NBIN = 16
TW = 128
MARGIN = 64
WIN = 16
LANES = 128
SPREAD = 40
NWIN = TW // WIN
NDET = 3
SEGS = 8
SLOTS = 12
NSL = 16
JS = NBLK // NSL
ROWS = NDET * SEGS
EPSILON = 1e-05
TWO_PI = 2.0 * math.pi
AXES = ("dt", "tmpl")
VMEM = 16 * 1024 * 1024


def place_of(index):
    dt, tm = divmod(index, 16)
    return (dt // 2, (tm // 8) * 2 + dt % 2, (tm // 2) % 4, tm % 2)


def index_of(x, y, z, core):
    return (x * 2 + y % 2) * 16 + (y // 2) * 8 + z * 2 + core


def across(dx=0, dy=0, dz=0, dcore=0):
    return lambda x, y, z, core: (x ^ dx, y ^ dy, z ^ dz, core ^ dcore)


def swap_with(value, move):
    pairs = [(index, index_of(*move(*place_of(index)))) for index in range(128)]
    return lax.ppermute(value, AXES, pairs)


STEPS = (
    ({"dy": 3}, {"dz": 1}),
    ({"dz": 1}, {"dz": 3}),
    ({"dz": 3}, {"dy": 3}),
)


def step_move(step):
    first, second = across(**STEPS[step][0]), across(**STEPS[step][1])
    return lambda x, y, z, core: (second if core else first)(x, y, z, core)


def slice_of(piece, other):
    tm = lax.axis_index("tmpl")
    y_hi, z, core = tm // 8, (tm // 2) % 4, (tm % 2) ^ other
    change = []
    for which in range(2):
        dy = dz = 0
        for step in range(3):
            if piece >> step & 1:
                dy ^= STEPS[step][which].get("dy", 0) // 2
                dz ^= STEPS[step][which].get("dz", 0)
        change.append((dy, dz))
    dy = jnp.where(core == 0, change[0][0], change[1][0])
    dz = jnp.where(core == 0, change[0][1], change[1][1])
    return (y_hi ^ dy) * 8 + (z ^ dz) * 2 + core


def segment_at(place):
    return ((lax.axis_index("dt") // 2) ^ (place & 3)) * 2 + (place >> 2)


def circle(turns):
    turns = turns + NFFT // 8
    quarter = (turns >> 18) & 3
    rest = (turns & (NFFT // 4 - 1)) - NFFT // 8
    angle = rest.astype(jnp.float32) * jnp.float32(TWO_PI / NFFT)
    square = angle * angle
    cosine = 1.0 + square * (-1 / 2 + square * (1 / 24 + square * (-1 / 720 + square * (1 / 40320))))
    sine = angle * (1.0 + square * (-1 / 6 + square * (1 / 120 + square * (-1 / 5040 + square * (1 / 362880)))))
    odd = (quarter & 1) == 1
    real, imag = jnp.where(odd, -sine, cosine), jnp.where(odd, cosine, sine)
    return jnp.where(quarter >= 2, -real, real), jnp.where(quarter >= 2, -imag, imag)


def counted(shape, axis):
    return lax.broadcasted_iota(jnp.int32, shape, axis)


def tables_kernel(small_ref, bin_ref, phase_ref, table_ref, turn_ref, *binned):
    for ref in binned:
        ref[...] = jnp.zeros_like(ref)

    cosine, sine = circle(counted((FB, TW), 0) * counted((FB, TW), 1) * STRIDE)
    table_ref[:FB, :TW] = cosine.astype(jnp.bfloat16)
    table_ref[:FB, TW:] = sine.astype(jnp.bfloat16)
    table_ref[FB:, :TW] = (-sine).astype(jnp.bfloat16)
    table_ref[FB:, TW:] = cosine.astype(jnp.bfloat16)
    shape = (NSL, 8, TW)
    number = FLOW // FB + counted(shape, 0) * JS + counted(shape, 1)
    turn_ref[0], turn_ref[1] = circle(number * counted(shape, 2) * FB)

    place = counted((ROWS, LANES), 0) & (SEGS - 1)
    here = segment_at(place) == counted((ROWS, LANES), 1)
    spread = [jnp.broadcast_to(small_ref[SLOTS + d:SLOTS + d + 1, :], (SEGS, LANES)) for d in range(NDET)]
    held = jnp.where(here, jnp.concatenate(spread, axis=0), 0).astype(jnp.float32)
    first = MARGIN + jnp.sum(held, axis=1, keepdims=True).astype(jnp.int32)
    lane = counted((1, FB + LANES), 1)
    starts = (FLOW // FB + (lane - FB) * JS) * FB
    rate = jnp.where(lane < FB, lane * STRIDE, jnp.where(lane < FB + NSL, starts, FB))
    phase_ref[0], phase_ref[1] = circle(first * rate)

    lane = counted((SLOTS, LANES), 1)
    bin_of = jnp.zeros((SLOTS, LANES), jnp.int32)
    for e in range(NBIN - 1):
        bin_of = bin_of + (small_ref[:SLOTS, e:e + 1] <= lane).astype(jnp.int32)
    digit = counted((LANES, LANES), 0) - JS * counted((LANES, LANES), 1)
    held = (digit >= 0) & (digit < JS)
    weight = jnp.where(held, 1 << (4 * jnp.where(held, digit, 0)), 0).astype(jnp.float32)
    digits = bin_of.astype(jnp.float32).astype(jnp.bfloat16)
    bin_ref[...] = jnp.dot(digits, weight.astype(jnp.bfloat16), preferred_element_type=jnp.float32)


def templates_kernel(templ_ref, small_ref, wide_ref, spread_ref, stat_ref):
    stat_ref[...] = jnp.zeros_like(stat_ref)
    block = counted((NBLK, LANES), 0)
    at_lane = counted((1, LANES), 1)
    live_count = small_ref[SLOTS + NDET:SLOTS + NDET + 1, :]
    for k in range(SLOTS):
        h = templ_ref[k, 0].astype(jnp.float32)
        i = templ_ref[k, 1].astype(jnp.float32)
        wide_ref[k, 0] = h
        wide_ref[k, 1] = h + i
        wide_ref[k, 2] = h - i
        power = jnp.sum(h * h + i * i, axis=1, keepdims=True)
        upper = small_ref[k:k + 1, :]
        lower = jnp.where(at_lane == 0, 0, pltpu.roll(upper, 1, 1))
        inside = jnp.where((block >= lower) & (block < upper), power, 0.0)
        in_bins = jnp.sum(inside, axis=0, keepdims=True)
        sigma2 = jnp.sum(power, axis=0, keepdims=True) + EPSILON
        frac = (in_bins + EPSILON) / sigma2
        inv = pltpu.roll(1.0 / (frac * sigma2), NBIN, 1)
        live = (k < live_count).astype(jnp.float32)
        row = jnp.where(at_lane == 2 * NBIN, 0.5 / sigma2, live)
        row = jnp.where(at_lane < 2 * NBIN, inv, row)
        stat_ref[k:k + 1, :] = jnp.where(at_lane < NBIN, frac, row)
    columns = stat_ref[...].T
    for k in range(SLOTS):
        spread_ref[k] = jnp.broadcast_to(columns[:SPREAD, k:k + 1], (SPREAD, LANES))


def whole():
    return pl.BlockSpec(memory_space=pltpu.VMEM)


BINNED = [jax.ShapeDtypeStruct((NBIN, ROWS, 2 * TW), jnp.float32)] * SLOTS


def small_numbers(edges, live_count, shifts):
    return jnp.concatenate([
        jnp.pad(edges, ((0, 0), (0, LANES - NBIN + 1)), constant_values=NBLK),
        jnp.pad(shifts.T, ((0, 0), (0, LANES - SEGS))),
        jnp.broadcast_to(live_count, (1, LANES)),
    ], axis=0)


def prepare_tables(small):
    outs = pl.pallas_call(
        tables_kernel,
        out_shape=[
            jax.ShapeDtypeStruct((SLOTS, LANES), jnp.float32),
            jax.ShapeDtypeStruct((2, ROWS, FB + LANES), jnp.float32),
            jax.ShapeDtypeStruct((2 * FB, 2 * TW), jnp.bfloat16),
            jax.ShapeDtypeStruct((2, NSL, 8, TW), jnp.float32),
        ] + BINNED,
        in_specs=[whole()],
        out_specs=[whole()] * (4 + SLOTS),
        compiler_params=pltpu.CompilerParams(vmem_limit_bytes=VMEM),
        cost_estimate=pl.CostEstimate(flops=10**6, bytes_accessed=10**6, transcendentals=0),
        name="prepare_tables",
    )(small)
    return outs[:4], outs[4:]


def prepare_templates(templates, small):
    return pl.pallas_call(
        templates_kernel,
        out_shape=[
            jax.ShapeDtypeStruct((SLOTS, 3, NBLK, FB), jnp.float32),
            jax.ShapeDtypeStruct((SLOTS, SPREAD, LANES), jnp.float32),
        ],
        in_specs=[whole()] * 2,
        out_specs=[whole()] * 2,
        scratch_shapes=[pltpu.VMEM((LANES, LANES), jnp.float32)],
        compiler_params=pltpu.CompilerParams(vmem_limit_bytes=VMEM),
        cost_estimate=pl.CostEstimate(flops=10**6, bytes_accessed=10**6, transcendentals=0),
        name="prepare_templates",
    )(templates, small)


def bins_kernel(parts, last, *refs):
    count = len(parts)
    pieces, refs = refs[:count], refs[count:]
    bin_ref, table_ref, turn_ref, wide_ref, phase_ref = refs[:5]
    refs = refs[5:]
    if last:
        stat_ref, refs = refs[0], refs[1:]
    refs = refs[SLOTS:]
    binned, refs = refs[:SLOTS], refs[SLOTS:]
    if last:
        out_ref, refs = refs[0], refs[1:]
    prod_ref, rot_ref, step_ref = refs[:3]
    if last:
        best_ref = refs[3]

    lane = lax.broadcasted_iota(jnp.int32, (ROWS, LANES), 1)

    def at_lane(part, place):
        return jnp.sum(jnp.where(lane == place, phase_ref[part, :, FB:], 0.0), axis=1, keepdims=True)

    for part in range(2):
        step_ref[part] = jnp.broadcast_to(at_lane(part, NSL), (ROWS, TW))

    def product(piece_ref, which, c, jj):
        j = c * JS + jj
        both = piece_ref[which, jj].astype(jnp.float32)
        raw_r, raw_i = both[:ROWS], both[ROWS:]
        rc, rs = rot_ref[0], rot_ref[1]
        sr = raw_r * rc - raw_i * rs
        si = raw_r * rs + raw_i * rc
        su = sr + si
        if jj < JS - 1:
            pc = jnp.concatenate([step_ref[0], step_ref[0]], axis=1)
            ps = jnp.concatenate([step_ref[1], step_ref[1]], axis=1)
            rot_ref[0] = rc * pc - rs * ps
            rot_ref[1] = rc * ps + rs * pc
        for pair in range(SLOTS // 2):
            real, imag = [], []
            for k in (2 * pair, 2 * pair + 1):
                h = wide_ref[k, 0, pl.ds(j, 1), :]
                v = wide_ref[k, 1, pl.ds(j, 1), :]
                w = wide_ref[k, 2, pl.ds(j, 1), :]
                k1 = h * su
                real.append(k1 - si * w)
                imag.append(k1 - sr * v)
            base = jj * SLOTS * ROWS + 2 * ROWS * pair
            rows = slice(base, base + 2 * ROWS)
            prod_ref[rows, :FB] = jnp.concatenate(real, axis=0).astype(jnp.bfloat16)
            prod_ref[rows, FB:] = jnp.concatenate(imag, axis=0).astype(jnp.bfloat16)

    def post(c, jj, digits, series):
        cos = turn_ref[0, c, jj:jj + 1, :]
        sin = turn_ref[1, c, jj:jj + 1, :]
        for k in range(SLOTS):
            b = (digits[k] >> (4 * jj)) & (NBIN - 1)
            re = series[k * ROWS:(k + 1) * ROWS, :TW]
            im = series[k * ROWS:(k + 1) * ROWS, TW:]
            binned[k][b, :, :TW] += cos * re - sin * im
            binned[k][b, :, TW:] += cos * im + sin * re

    for piece_ref, (first, amount, other) in zip(pieces, parts):
        for which in range(amount):
            c = slice_of(first + which, other)
            sc, ss = at_lane(0, c), at_lane(1, c)
            slot_lane = lax.broadcasted_iota(jnp.int32, (SLOTS, LANES), 1)
            packed = jnp.sum(jnp.where(slot_lane == c, bin_ref[...], 0.0), axis=1, keepdims=True).astype(jnp.int32)
            digits = [packed[k, 0] for k in range(SLOTS)]
            lc, ls = phase_ref[0, :, :FB], phase_ref[1, :, :FB]
            rot_ref[0] = sc * lc - ss * ls
            rot_ref[1] = sc * ls + ss * lc
            for jj in range(JS):
                product(piece_ref, which, c, jj)
            half = JS // 2
            size = half * SLOTS * ROWS
            for h in range(2):
                series = jnp.dot(
                    prod_ref[h * size:(h + 1) * size], table_ref[...], preferred_element_type=jnp.float32
                )
                for m in range(half):
                    post(c, h * half + m, digits, series[m * SLOTS * ROWS:(m + 1) * SLOTS * ROWS])

    if last:
        best = jnp.zeros((SEGS, TW), jnp.float32)
        for k in range(SLOTS):
            total = binned[k][0]
            for b in range(1, NBIN):
                total = total + binned[k][b]
            chi = jnp.zeros((ROWS, TW), jnp.float32)
            for b in range(NBIN):
                share = jnp.concatenate([stat_ref[k, b:b + 1, :]] * 2, axis=1)
                gap = binned[k][b] - share * total
                gap = gap * gap
                chi = chi + (gap[:, :TW] + gap[:, TW:]) * stat_ref[k, NBIN + b:NBIN + b + 1, :]
            power = total * total
            snr2 = (power[:, :TW] + power[:, TW:]) * stat_ref[k, 2 * NBIN:2 * NBIN + 1, :]
            reduced = chi / (2.0 * NBIN - 2.0)
            cube = (1.0 + reduced * reduced * reduced) * 0.5
            factor = jnp.where(reduced > 1.0, jnp.exp(jnp.log(cube) * (-1.0 / 3.0)), 1.0)
            new2 = snr2 * factor
            net2 = new2[:SEGS] + new2[SEGS:2 * SEGS] + new2[2 * SEGS:]
            best = jnp.where(stat_ref[k, 2 * NBIN + 1:2 * NBIN + 2, :] > 0.5, jnp.maximum(best, net2), best)
        best = jnp.sqrt(best)
        best_ref[...] = jnp.concatenate(
            [jnp.max(best[:, w * WIN:(w + 1) * WIN], axis=1, keepdims=True) for w in range(NWIN)], axis=1
        )
        for place in range(SEGS):
            out_ref[pl.ds(segment_at(place), 1), :] = best_ref[place:place + 1, :]


def add_bins(pieces, parts, shared, binned, stat=None):
    last = stat is not None
    operands = [*pieces, *shared] + ([stat] if last else []) + list(binned)
    first = len(operands) - SLOTS
    out_shape = list(BINNED)
    scratch = [
        pltpu.VMEM((JS * SLOTS * ROWS, 2 * FB), jnp.bfloat16),
        pltpu.VMEM((2, ROWS, FB), jnp.float32),
        pltpu.VMEM((2, ROWS, TW), jnp.float32),
    ]
    if last:
        out_shape.append(jax.ShapeDtypeStruct((SEGS, NWIN), jnp.float32))
        scratch.append(pltpu.VMEM((SEGS, NWIN), jnp.float32))
    flops = sum(part[1] for part in parts) * 2 * JS * SLOTS * ROWS * 2 * FB * 2 * TW
    return pl.pallas_call(
        functools.partial(bins_kernel, parts, last),
        out_shape=out_shape,
        in_specs=[whole()] * len(operands),
        out_specs=[whole()] * len(out_shape),
        scratch_shapes=scratch,
        input_output_aliases={first + k: k for k in range(SLOTS)},
        compiler_params=pltpu.CompilerParams(vmem_limit_bytes=VMEM),
        cost_estimate=pl.CostEstimate(flops=2 * flops, bytes_accessed=10**6, transcendentals=0),
        name="last_bins" if last else "add_bins",
    )(*operands)


def per_device(strain, templates, live_count, chi_edges, shifts):
    small = small_numbers(chi_edges, live_count, shifts)
    (bin_of, turned, table, turn), binned = prepare_tables(small)
    wide, stat = prepare_templates(templates, small)

    x = jnp.transpose(strain[0], (2, 1, 0, 3)).reshape(JS, 2 * NDET, 1, FB)
    got = {0: x}
    for dx in (2, 3, 1):
        got[dx] = swap_with(x, across(dx=dx))
    x = jnp.concatenate([got[dx] for dx in range(4)], axis=2)
    x, turned = lax.optimization_barrier((x, turned))
    got = swap_with(x, across(dy=1))
    even = lax.axis_index("dt") % 2 == 0
    x, got, wide = lax.optimization_barrier((x, got, wide))
    x = jnp.concatenate([jnp.where(even, x, got), jnp.where(even, got, x)], axis=2)
    shared = (bin_of, table, turn, wide, turned)

    def to_core(piece):
        return swap_with(piece, across(dcore=1))

    def after(value, binned):
        value, first = lax.optimization_barrier((value, binned[0]))
        return value, [first, *binned[1:]]

    p0 = x.reshape(1, JS, 2 * ROWS, FB)
    q0 = to_core(p0)
    p1 = swap_with(p0, step_move(0))
    binned = add_bins((p0, q0), ((0, 1, 0), (0, 1, 1)), shared, binned)
    p1, binned = after(p1, binned)
    q1 = to_core(p1)
    p01 = jnp.concatenate([p0, p1], axis=0)
    p23 = swap_with(p01, step_move(1))
    binned = add_bins((p1, q1), ((1, 1, 0), (1, 1, 1)), shared, binned)
    p23, binned = after(p23, binned)
    q23 = to_core(p23)
    p01, p23 = lax.optimization_barrier((p01, p23))
    p45 = swap_with(p01, step_move(2))
    p67 = swap_with(p23, step_move(2))
    binned = add_bins((p23, q23), ((2, 2, 0), (2, 2, 1)), shared, binned)
    p45, binned = after(p45, binned)
    q45 = to_core(p45)
    binned = add_bins((p45,), ((4, 2, 0),), shared, binned)
    p67, binned = after(p67, binned)
    q67 = to_core(p67)
    binned = add_bins((q45,), ((4, 2, 1),), shared, binned)
    binned = add_bins((p67,), ((6, 2, 0),), shared, binned)
    best = add_bins((q67,), ((6, 2, 1),), shared, binned, stat)[-1]
    for move in (across(dcore=1), across(dz=1), across(dz=3), across(dy=2)):
        best = jnp.maximum(best, swap_with(best, move))
    return best[:, None, :]


def solution(mesh):
    in_specs = (
        P("dt", None, None, "tmpl", None),
        P(("dt", "tmpl"), None, None, None),
        P("dt", "tmpl"),
        P(("dt", "tmpl"), None),
        P(),
    )
    out_specs = P(None, "dt", None)
    return jax.shard_map(
        per_device, mesh=mesh, in_specs=in_specs, out_specs=out_specs, check_vma=False
    )
```

time: 76.1 us -> 71.4 us (0.938)
  waiting for transfers between devices: 24 us -> 16.3 us
  local copies, waits for them, and re-layouts: 4.59 us -> 12.1 us
  Pallas kernels: 19.5 us -> 17.1 us
  starting transfers between devices: 23.7 us -> 21.5 us
    unnamed x9 -> x29, local copies, waits for them, and re-layouts: 3.84 us -> 12 us
    ppermute x17, waiting for transfers between devices: 24 us -> 16.3 us  [swap_with(): return lax.ppermute(value, AXES, pairs)]
    pallas_call x5 -> x7, Pallas kernels: 18.1 us -> 14.7 us  [add_bins(): pl.pallas_call(functools.partial(bins_kernel, parts, last), out_shape=out...]
    ppermute x17, starting transfers between devices: 23.7 us -> 21.5 us  [swap_with(): return lax.ppermute(value, AXES, pairs)]
    cos x1 -> x0, other arithmetic: 0.98 us -> none  [phases(): return jnp.cos(angle[None] - quarter)]
    select_n x1, other arithmetic: 0.01 us -> 0.96 us  [per_device(): jnp.where(even, x, got)]
    pallas_call x1 -> x2, Pallas kernels: 1.44 us -> 2.36 us  [the longest x1 1.66 us: prepare_templates(): pl.pallas_call(templates_kernel, out_shape=[jax.ShapeDtypeStruct((SLOTS,...]
    concatenate x2 -> x3, other arithmetic: 0.07 us -> 0.86 us  [the longest x1 0.79 us: small_numbers(): jnp.concatenate([jnp.pad(edges, ((0, 0), (0, LANES - NBIN + 1)), constant...]
  transfers between devices with their start and end apart: 17 -> 17, of which waited for: 9 -> 8; matrix products, arithmetic and copies ran while one was open for 4% -> 1% of each run, Pallas kernels for 19% -> 20%
where the time goes in v7:
time: 71.4 us; the launch traced here: 70.9 us
  starting transfers between devices  21.5 us (30%)
  Pallas kernels  17.1 us (24%)
  waiting for transfers between devices  16.3 us (23%)
  local copies, waits for them, and re-layouts  12.1 us (17%)
  other arithmetic  3.09 us (4%)
  between operations  0.79 us (1%)
    ppermute x17, starting transfers between devices, swap_with(): return lax.ppermute(value, AXES, pairs)  21.5 us
    ppermute x17, waiting for transfers between devices, swap_with(): return lax.ppermute(value, AXES, pairs)  16.3 us
    pallas_call x7, Pallas kernels, add_bins(): pl.pallas_call(functools.partial(bins_kernel, parts, last), out_shape=out...  14.7 us
    unnamed x29, local copies, waits for them, and re-layouts  12 us
    pallas_call x1, Pallas kernels, prepare_templates(): pl.pallas_call(templates_kernel, out_shape=[jax.ShapeDtypeStruct((SLOTS,...  1.66 us
  transfers between devices with their start and end apart: 17, of which 8 were waited for; matrix products, arithmetic and copies ran while one was open for 1% of the time, Pallas kernels for 20%

profile of v7, /device:TPU:0, one launch (start us, length us, event | category | flops | bytes accessed | tf_op | source)
XLA Modules:
  0.0 70.9 jit_solution(1292488201408867329)
XLA Ops:
  0.0 0.7 %copy.91 = bf16[1,3,2,6,256]{4,3,1,2,0:T(8,128)(2,1)S(1)} copy(bf16[1,3,2,6,256]{4,2,3,1,0:T(2,128)(2,1)} %param.5) | data formatting | bytes 36864 | tf_op args[0]
  0.7 1.6 %collective-permute-start = (bf16[6,6,1,256]{3,0,1,2:T(8,128)(2,1)S(1)}, bf16[6,6,1,256]{3,0,1,2:T(8,128)(2,1)S(1)}, u32[]{:S(2)}, u32[]{:S(2)}) collective-permute-start(bf16[6,6,1,256]{3,0,1,2:T(8,128)(2,1)S(1)} %bitcast.20), channel_id=1, source_target_pairs={{0,32},{1,33},{2,34},{3,35},{4,36},{5,37},{6,38},{7,39},{8,40},{9,... | collective-permute-start | bytes 55304 | tf_op jit(solution)/shard_map/ppermute | solution.py:50
  2.3 2.7 %collective-permute-start.1 = (bf16[6,6,1,256]{3,0,1,2:T(8,128)(2,1)S(1)}, bf16[6,6,1,256]{3,0,1,2:T(8,128)(2,1)S(1)}, u32[]{:S(2)}, u32[]{:S(2)}) collective-permute-start(bf16[6,6,1,256]{3,0,1,2:T(8,128)(2,1)S(1)} %bitcast.21), channel_id=1, source_target_pairs={{0,64},{1,65},{2,66},{3,67},{4,68},{5,69},{6,70},{7,71},{8,72},{9,... | collective-permute-start | bytes 55304 | tf_op jit(solution)/shard_map/ppermute | solution.py:50
  5.0 0.4 collective-permute-start.2
  6.2 0.8 %fusion.small_ref = s32[16,128]{1,0:T(8,128)S(1)} fusion(s32[3,8]{1,0:T(4,128)} %bitcast.24, s32[12,15]{1,0:T(8,128)} %param.8, s32[16]{0:T(128)S(1)} %pad.16.clone), kind=kLoop, calls=%fused_computation.7 | loop fusion | flops 8192 | bytes 9072 | tf_op jit(solution)/shard_map/concatenate | solution.py:172
  6.9 0.7 prepare_tables.1
  7.7 0.7 %copy-done = f32[16,24,256]{2,1,0:T(8,128)} copy-done((f32[16,24,256]{2,1,0:T(8,128)}, f32[16,24,256]{2,1,0:T(8,128)S(1)}, u32[]{:S(2)}) %copy-start) | copy-done | bytes 393240
  8.4 0.8 %copy-done.2 = f32[16,24,256]{2,1,0:T(8,128)} copy-done((f32[16,24,256]{2,1,0:T(8,128)}, f32[16,24,256]{2,1,0:T(8,128)S(1)}, u32[]{:S(2)}) %copy-start.2) | copy-done | bytes 393240
  9.2 0.8 %copy-done.4 = f32[16,24,256]{2,1,0:T(8,128)} copy-done((f32[16,24,256]{2,1,0:T(8,128)}, f32[16,24,256]{2,1,0:T(8,128)S(1)}, u32[]{:S(2)}) %copy-start.4) | copy-done | bytes 393240
  9.9 0.7 copy-done.6
  10.6 0.7 copy-done.8
  11.3 0.6 copy-done.11
  11.9 0.7 pad_maximum_fusion.2
  12.6 1.7 %collective-permute-start.3 = (bf16[6,6,4,256]{3,0,1,2:T(8,128)(2,1)}, bf16[6,6,4,256]{3,0,1,2:T(8,128)(2,1)}, u32[]{:S(2)}, u32[]{:S(2)}) collective-permute-start(bf16[6,6,4,256]{3,0,1,2:T(8,128)(2,1)} %pad_maximum_fusion.2), channel_id=1, source_target_pairs={{0,16},{1,17},{2,18},{3,19},{4,20},{5,21},{6,22},{7,23},{8,24},{9,... | collective-permute-start | bytes 221192 | tf_op jit(solution)/shard_map/ppermute | solution.py:50
  14.3 1.3 %copy-done.13 = bf16[12,2,96,256]{3,2,1,0:T(8,128)(2,1)S(1)} copy-done((bf16[12,2,96,256]{3,2,1,0:T(8,128)(2,1)S(1)}, bf16[12,2,96,256]{3,2,1,0:T(8,128)(2,1)}, u32[]{:S(2)}) %copy-start.13) | copy-done | bytes 1179672
  15.5 1.7 %prepare_templates.1 = (f32[12,3,96,256]{3,2,1,0:T(8,128)S(1)}, f32[12,40,128]{2,1,0:T(8,128)S(1)}) custom-call(bf16[12,2,96,256]{3,2,1,0:T(8,128)(2,1)S(1)} %copy-done.13, s32[16,128]{1,0:T(8,128)S(1)} %fusion.small_ref), custom_call_target="tpu_custom_call" | custom-call | flops 1000000 | bytes 1000000 | tf_op jit(solution)/shard_map/prepare_templates/pallas_call | solution.py:198
  17.2 0.3 collective-permute-done.3
  17.5 1.0 %broadcast_select_fusion.1 = (bf16[6,6,4,256]{3,0,1,2:T(8,128)(2,1)S(1)}, bf16[6,6,4,256]{3,0,1,2:T(8,128)(2,1)S(1)}) fusion(bf16[6,6,4,256]{3,0,1,2:T(8,128)(2,1)} %pad_maximum_fusion.2, bf16[6,6,4,256]{3,0,1,2:T(8,128)(2,1)} %collective-permute-done.3, pred[]{:T(512)S(6)} %eq.5), kind=kLoop, calls=%fused_computation.5 | loop fusion | flops 73728 | bytes 294913 | tf_op jit(solution)/shard_map/jit(_where)/select_n | solution.py:363
  18.6 0.1 collective-permute-start.5
  18.7 3.2 %collective-permute-start.4 = (bf16[1,6,48,256]{3,2,1,0:T(8,128)(2,1)S(1)}, bf16[1,6,48,256]{3,2,1,0:T(8,128)(2,1)S(1)}, u32[]{:S(2)}, u32[]{:S(2)}) collective-permute-start(bf16[1,6,48,256]{3,2,1,0:T(8,128)(2,1)S(1)} %bitcast.17), channel_id=1, source_target_pairs={{0,24},{1,3},{2,26},{3,1},{4,28},{5,7},{6,30},{7,5},{8,16},{9,11},... | collective-permute-start | bytes 442376 | tf_op jit(solution)/shard_map/ppermute | solution.py:50
  21.9 1.0 %copy-done.1 = f32[16,24,256]{2,1,0:T(8,128)S(1)} copy-done((f32[16,24,256]{2,1,0:T(8,128)S(1)}, f32[16,24,256]{2,1,0:T(8,128)}, u32[]{:S(2)}) %copy-start.1) | copy-done | bytes 393240
  22.9 1.0 %copy-done.3 = f32[16,24,256]{2,1,0:T(8,128)S(1)} copy-done((f32[16,24,256]{2,1,0:T(8,128)S(1)}, f32[16,24,256]{2,1,0:T(8,128)}, u32[]{:S(2)}) %copy-start.3) | copy-done | bytes 393240
  23.9 1.0 %copy-done.5 = f32[16,24,256]{2,1,0:T(8,128)S(1)} copy-done((f32[16,24,256]{2,1,0:T(8,128)S(1)}, f32[16,24,256]{2,1,0:T(8,128)}, u32[]{:S(2)}) %copy-start.5) | copy-done | bytes 393240
  24.9 0.9 %copy-done.7 = bf16[512,256]{1,0:T(8,128)(2,1)S(1)} copy-done((bf16[512,256]{1,0:T(8,128)(2,1)S(1)}, bf16[512,256]{1,0:T(8,128)(2,1)}, u32[]{:S(2)}) %copy-start.7) | copy-done | bytes 262168
  25.8 0.9 %copy-done.9 = f32[2,16,8,128]{3,2,1,0:T(8,128)S(1)} copy-done((f32[2,16,8,128]{3,2,1,0:T(8,128)S(1)}, f32[2,16,8,128]{3,2,1,0:T(8,128)}, u32[]{:S(2)}) %copy-start.9) | copy-done | bytes 131096
  26.7 0.9 %copy-done.12 = f32[2,24,384]{2,1,0:T(8,128)S(1)} copy-done((f32[2,24,384]{2,1,0:T(8,128)S(1)}, f32[2,24,384]{2,1,0:T(8,128)}, u32[]{:S(2)}) %copy-start.12) | copy-done | bytes 73752
  27.6 1.7 %add_bins.6 = (f32[16,24,256]{2,1,0:T(8,128)S(1)}, f32[16,24,256]{2,1,0:T(8,128)S(1)}, f32[16,24,256]{2,1,0:T(8,128)S(1)}, f32[16,24,256]{2,1,0:T(8,128)S(1)}, f...) custom-call(bf16[1,6,48,256]{3,2,1,0:T(8,128)(2,1)S(1)} %bitcast.18,, ...), custom_call_target="tpu_custom_call", output_to_operand_aliasing={{0}: (7, {}), {1}: (8, {}), {2}: (9, {}), {3}: (10, {}), {4... | custom-call | flops 1811939328 | bytes 1000000 | tf_op jit(solution)/shard_map/add_bins/pallas_call | solution.py:336
  29.5 2.0 %collective-permute-start.6 = (bf16[2,6,48,256]{3,2,1,0:T(8,128)(2,1)S(1)}, bf16[2,6,48,256]{3,2,1,0:T(8,128)(2,1)S(1)}, u32[]{:S(2)}, u32[]{:S(2)}) collective-permute-start(bf16[2,6,48,256]{3,2,1,0:T(8,128)(2,1)S(1)} %pad_maximum_fusion), channel_id=1, source_target_pairs={{0,2},{1,7},{2,0},{3,5},{4,6},{5,3},{6,4},{7,1},{8,10},{9,15},{10,... | collective-permute-start | bytes 884744 | tf_op jit(solution)/shard_map/ppermute | solution.py:50
  31.5 1.7 %add_bins.7 = (f32[16,24,256]{2,1,0:T(8,128)S(1)}, f32[16,24,256]{2,1,0:T(8,128)S(1)}, f32[16,24,256]{2,1,0:T(8,128)S(1)}, f32[16,24,256]{2,1,0:T(8,128)S(1)}, f...) custom-call(bf16[1,6,48,256]{3,2,1,0:T(8,128)(2,1)S(1)} %collective-, ...), custom_call_target="tpu_custom_call", output_to_operand_aliasing={{0}: (7, {}), {1}: (8, {}), {2}: (9, {}), {3}: (10, {}), {4... | custom-call | flops 1811939328 | bytes 1000000 | tf_op jit(solution)/shard_map/add_bins/pallas_call | solution.py:336
  33.1 3.1 %collective-permute-done.6.refs_0_ = bf16[2,6,48,256]{3,2,1,0:T(8,128)(2,1)S(1)} collective-permute-done((bf16[2,6,48,256]{3,2,1,0:T(8,128)(2,1)S(1)}, bf16[2,6,48,256]{3,2,1,0:T(8,128)(2,1)S(1)}, u32[]{:S(2)}, u32[]{:S(2)}) %collective-permute-start.6) | collective-permute-done | bytes 294944 | tf_op jit(solution)/shard_map/ppermute | solution.py:50
  36.3 1.7 %collective-permute-start.10 = (bf16[2,6,48,256]{3,2,1,0:T(8,128)(2,1)S(1)}, bf16[2,6,48,256]{3,2,1,0:T(8,128)(2,1)S(1)}, u32[]{:S(2)}, u32[]{:S(2)}) collective-permute-start(bf16[2,6,48,256]{3,2,1,0:T(8,128)(2,1)S(1)} %collective-permute-done.6.refs_0_), channel_id=1, source_target_pairs={{0,1},{1,0},{2,3},{3,2},{4,5},{5,4},{6,7},{7,6},{8,9},{9,8},{10,11... | collective-permute-start | bytes 884744 | tf_op jit(solution)/shard_map/ppermute | solution.py:50
  37.9 3.0 %collective-permute-start.9 = (bf16[2,6,48,256]{3,2,1,0:T(8,128)(2,1)S(1)}, bf16[2,6,48,256]{3,2,1,0:T(8,128)(2,1)S(1)}, u32[]{:S(2)}, u32[]{:S(2)}) collective-permute-start(bf16[2,6,48,256]{3,2,1,0:T(8,128)(2,1)S(1)} %pad_maximum_fusion), channel_id=1, source_target_pairs={{0,6},{1,25},{2,4},{3,27},{4,2},{5,29},{6,0},{7,31},{8,14},{9,17},... | collective-permute-start | bytes 884744 | tf_op jit(solution)/shard_map/ppermute | solution.py:50
  40.9 0.3 collective-permute-start.8
  41.2 3.4 %add_bins.8 = (f32[16,24,256]{2,1,0:T(8,128)S(1)}, f32[16,24,256]{2,1,0:T(8,128)S(1)}, f32[16,24,256]{2,1,0:T(8,128)S(1)}, f32[16,24,256]{2,1,0:T(8,128)S(1)}, f...) custom-call(bf16[2,6,48,256]{3,2,1,0:T(8,128)(2,1)S(1)} %collective-, ...), custom_call_target="tpu_custom_call", output_to_operand_aliasing={{0}: (7, {}), {1}: (8, {}), {2}: (9, {}), {3}: (10, {}), {4... | custom-call | flops 3623878656 | bytes 1000000 | tf_op jit(solution)/shard_map/add_bins/pallas_call | solution.py:336
  44.5 1.3 %collective-permute-done.9.refs_0_ = bf16[2,6,48,256]{3,2,1,0:T(8,128)(2,1)S(1)} collective-permute-done((bf16[2,6,48,256]{3,2,1,0:T(8,128)(2,1)S(1)}, bf16[2,6,48,256]{3,2,1,0:T(8,128)(2,1)S(1)}, u32[]{:S(2)}, u32[]{:S(2)}) %collective-permute-start.9) | collective-permute-done | bytes 294944 | tf_op jit(solution)/shard_map/ppermute | solution.py:50
  45.9 1.7 %add_bins.9 = (f32[16,24,256]{2,1,0:T(8,128)S(1)}, f32[16,24,256]{2,1,0:T(8,128)S(1)}, f32[16,24,256]{2,1,0:T(8,128)S(1)}, f32[16,24,256]{2,1,0:T(8,128)S(1)}, f...) custom-call(bf16[2,6,48,256]{3,2,1,0:T(8,128)(2,1)S(1)} %collective-, ...), custom_call_target="tpu_custom_call", output_to_operand_aliasing={{0}: (6, {}), {1}: (7, {}), {2}: (8, {}), {3}: (9, {}), {4}... | custom-call | flops 1811939328 | bytes 1000000 | tf_op jit(solution)/shard_map/add_bins/pallas_call | solution.py:336
  47.6 1.4 %collective-permute-done.8.refs_0_ = bf16[2,6,48,256]{3,2,1,0:T(8,128)(2,1)S(1)} collective-permute-done((bf16[2,6,48,256]{3,2,1,0:T(8,128)(2,1)S(1)}, bf16[2,6,48,256]{3,2,1,0:T(8,128)(2,1)S(1)}, u32[]{:S(2)}, u32[]{:S(2)}) %collective-permute-start.8) | collective-permute-done | bytes 294944 | tf_op jit(solution)/shard_map/ppermute | solution.py:50
  49.0 1.7 %add_bins.10 = (f32[16,24,256]{2,1,0:T(8,128)S(1)}, f32[16,24,256]{2,1,0:T(8,128)S(1)}, f32[16,24,256]{2,1,0:T(8,128)S(1)}, f32[16,24,256]{2,1,0:T(8,128)S(1)}, ...) custom-call(bf16[2,6,48,256]{3,2,1,0:T(8,128)(2,1)S(1)} %collective-, ...), custom_call_target="tpu_custom_call", output_to_operand_aliasing={{0}: (6, {}), {1}: (7, {}), {2}: (8, {}), {3}: (9, {}), {4}... | custom-call | flops 1811939328 | bytes 1000000 | tf_op jit(solution)/shard_map/add_bins/pallas_call | solution.py:336
  50.7 1.8 %add_bins.11 = (f32[16,24,256]{2,1,0:T(8,128)S(1)}, f32[16,24,256]{2,1,0:T(8,128)S(1)}, f32[16,24,256]{2,1,0:T(8,128)S(1)}, f32[16,24,256]{2,1,0:T(8,128)S(1)}, ...) custom-call(bf16[2,6,48,256]{3,2,1,0:T(8,128)(2,1)S(1)} %collective-, ...), custom_call_target="tpu_custom_call", output_to_operand_aliasing={{0}: (6, {}), {1}: (7, {}), {2}: (8, {}), {3}: (9, {}), {4}... | custom-call | flops 1811939328 | bytes 1000000 | tf_op jit(solution)/shard_map/add_bins/pallas_call | solution.py:336
  52.5 2.8 %last_bins.1 = (f32[16,24,256]{2,1,0:T(8,128)S(1)}, f32[16,24,256]{2,1,0:T(8,128)S(1)}, f32[16,24,256]{2,1,0:T(8,128)S(1)}, f32[16,24,256]{2,1,0:T(8,128)S(1)}, ...) custom-call(bf16[2,6,48,256]{3,2,1,0:T(8,128)(2,1)S(1)} %collective-, ...), custom_call_target="tpu_custom_call", output_to_operand_aliasing={{0}: (7, {}), {1}: (8, {}), {2}: (9, {}), {3}: (10, {}), {4... | custom-call | flops 1811939328 | bytes 1000000 | tf_op jit(solution)/shard_map/last_bins/pallas_call | solution.py:336
  55.3 0.6 collective-permute-start.13
  55.9 0.8 %collective-permute-done.13 = f32[8,8]{1,0:T(8,128)S(1)} collective-permute-done((f32[8,8]{1,0:T(8,128)S(1)}, f32[8,8]{1,0:T(8,128)S(1)}, u32[]{:S(2)}, u32[]{:S(2)}) %collective-permute-start.13) | collective-permute-done | bytes 288 | tf_op jit(solution)/shard_map/ppermute | solution.py:50
  56.8 3.6 %collective-permute-done.14 = f32[8,8]{1,0:T(8,128)S(1)} collective-permute-done((f32[8,8]{1,0:T(8,128)S(1)}, f32[8,8]{1,0:T(8,128)S(1)}, u32[]{:S(2)}, u32[]{:S(2)}) %collective-permute-start.14) | collective-permute-done | bytes 288 | tf_op jit(solution)/shard_map/ppermute | solution.py:50
  60.4 2.9 %collective-permute-start.15 = (f32[8,8]{1,0:T(8,128)S(1)}, f32[8,8]{1,0:T(8,128)S(1)}, u32[]{:S(2)}, u32[]{:S(2)}) collective-permute-start(f32[8,8]{1,0:T(8,128)S(1)} %max.13), channel_id=1, source_target_pairs={{0,6},{1,7},{2,4},{3,5},{4,2},{5,3},{6,0},{7,1},{8,14},{9,15},{10,... | collective-permute-start | bytes 776 | tf_op jit(solution)/shard_map/ppermute | solution.py:50
  63.2 2.0 %collective-permute-done.15 = f32[8,8]{1,0:T(8,128)S(1)} collective-permute-done((f32[8,8]{1,0:T(8,128)S(1)}, f32[8,8]{1,0:T(8,128)S(1)}, u32[]{:S(2)}, u32[]{:S(2)}) %collective-permute-start.15) | collective-permute-done | bytes 288 | tf_op jit(solution)/shard_map/ppermute | solution.py:50
  65.2 1.4 %collective-permute-start.16 = (f32[8,8]{1,0:T(8,128)S(1)}, f32[8,8]{1,0:T(8,128)S(1)}, u32[]{:S(2)}, u32[]{:S(2)}) collective-permute-start(f32[8,8]{1,0:T(8,128)S(1)} %max.14), channel_id=1, source_target_pairs={{0,8},{1,9},{2,10},{3,11},{4,12},{5,13},{6,14},{7,15},{8,0},{9,1},... | collective-permute-start | bytes 776 | tf_op jit(solution)/shard_map/ppermute | solution.py:50
  66.6 3.7 %collective-permute-done.16 = f32[8,8]{1,0:T(8,128)S(1)} collective-permute-done((f32[8,8]{1,0:T(8,128)S(1)}, f32[8,8]{1,0:T(8,128)S(1)}, u32[]{:S(2)}, u32[]{:S(2)}) %collective-permute-start.16) | collective-permute-done | bytes 288 | tf_op jit(solution)/shard_map/ppermute | solution.py:50
  70.3 0.6 max.15
  (35 shorter events, 0.3 us)
Async XLA Ops:
  0.7 11.2 %collective-permute-start = (bf16[6,6,1,256]{3,0,1,2:T(8,128)(2,1)S(1)}, bf16[6,6,1,256]{3,0,1,2:T(8,128)(2,1)S(1)}, u32[]{:S(2)}, u32[]{:S(2)}) collective-permute-start(bf16[6,6,1,256]{3,0,1,2:T(8,128)(2,1)S(1)} %bitcast.20), channel_id=1, source_target_pairs={{0,32},{1,33},{2,34},{3,35},{4,36},{5,37},{6,38},{7,39},{8,40},{9,... | collective-permute-start | bytes 55304 | tf_op jit(solution)/shard_map/ppermute | solution.py:50
  2.3 9.6 %collective-permute-start.1 = (bf16[6,6,1,256]{3,0,1,2:T(8,128)(2,1)S(1)}, bf16[6,6,1,256]{3,0,1,2:T(8,128)(2,1)S(1)}, u32[]{:S(2)}, u32[]{:S(2)}) collective-permute-start(bf16[6,6,1,256]{3,0,1,2:T(8,128)(2,1)S(1)} %bitcast.21), channel_id=1, source_target_pairs={{0,64},{1,65},{2,66},{3,67},{4,68},{5,69},{6,70},{7,71},{8,72},{9,... | collective-permute-start | bytes 55304 | tf_op jit(solution)/shard_map/ppermute | solution.py:50
  5.0 6.9 %collective-permute-start.2 = (bf16[6,6,1,256]{3,0,1,2:T(8,128)(2,1)S(1)}, bf16[6,6,1,256]{3,0,1,2:T(8,128)(2,1)S(1)}, u32[]{:S(2)}, u32[]{:S(2)}) collective-permute-start(bf16[6,6,1,256]{3,0,1,2:T(8,128)(2,1)S(1)} %bitcast.22), channel_id=1, source_target_pairs={{0,96},{1,97},{2,98},{3,99},{4,100},{5,101},{6,102},{7,103},{8,104... | collective-permute-start | bytes 55304 | tf_op jit(solution)/shard_map/ppermute | solution.py:50
  7.6 0.8 %copy-start = (f32[16,24,256]{2,1,0:T(8,128)}, f32[16,24,256]{2,1,0:T(8,128)S(1)}, u32[]{:S(2)}) copy-start(f32[16,24,256]{2,1,0:T(8,128)S(1)} %get-tuple-element.130.refs_16_) | copy-start | bytes 1179652
  8.4 0.8 %copy-start.2 = (f32[16,24,256]{2,1,0:T(8,128)}, f32[16,24,256]{2,1,0:T(8,128)S(1)}, u32[]{:S(2)}) copy-start(f32[16,24,256]{2,1,0:T(8,128)S(1)} %get-tuple-element.131.refs_17_) | copy-start | bytes 1179652
  9.2 0.8 %copy-start.4 = (f32[16,24,256]{2,1,0:T(8,128)}, f32[16,24,256]{2,1,0:T(8,128)S(1)}, u32[]{:S(2)}) copy-start(f32[16,24,256]{2,1,0:T(8,128)S(1)} %get-tuple-element.132.refs_18_) | copy-start | bytes 1179652
  9.9 0.7 copy-start.6
  10.6 0.7 copy-start.8
  11.3 0.6 copy-start.11
  12.6 4.9 %collective-permute-start.3 = (bf16[6,6,4,256]{3,0,1,2:T(8,128)(2,1)}, bf16[6,6,4,256]{3,0,1,2:T(8,128)(2,1)}, u32[]{:S(2)}, u32[]{:S(2)}) collective-permute-start(bf16[6,6,4,256]{3,0,1,2:T(8,128)(2,1)} %pad_maximum_fusion.2), channel_id=1, source_target_pairs={{0,16},{1,17},{2,18},{3,19},{4,20},{5,21},{6,22},{7,23},{8,24},{9,... | collective-permute-start | bytes 221192 | tf_op jit(solution)/shard_map/ppermute | solution.py:50
  14.3 1.3 %copy-start.13 = (bf16[12,2,96,256]{3,2,1,0:T(8,128)(2,1)S(1)}, bf16[12,2,96,256]{3,2,1,0:T(8,128)(2,1)}, u32[]{:S(2)}) copy-start(bf16[12,2,96,256]{3,2,1,0:T(8,128)(2,1)} %templ_ref.1) | copy-start | bytes 3538948
  18.6 3.3 %collective-permute-start.5 = (bf16[1,6,48,256]{3,2,1,0:T(8,128)(2,1)S(1)}, bf16[1,6,48,256]{3,2,1,0:T(8,128)(2,1)S(1)}, u32[]{:S(2)}, u32[]{:S(2)}) collective-permute-start(bf16[1,6,48,256]{3,2,1,0:T(8,128)(2,1)S(1)} %bitcast.16), channel_id=1, source_target_pairs={{0,1},{1,0},{2,3},{3,2},{4,5},{5,4},{6,7},{7,6},{8,9},{9,8},{10,11... | collective-permute-start | bytes 442376 | tf_op jit(solution)/shard_map/ppermute | solution.py:50
  18.7 10.6 %collective-permute-start.4 = (bf16[1,6,48,256]{3,2,1,0:T(8,128)(2,1)S(1)}, bf16[1,6,48,256]{3,2,1,0:T(8,128)(2,1)S(1)}, u32[]{:S(2)}, u32[]{:S(2)}) collective-permute-start(bf16[1,6,48,256]{3,2,1,0:T(8,128)(2,1)S(1)} %bitcast.17), channel_id=1, source_target_pairs={{0,24},{1,3},{2,26},{3,1},{4,28},{5,7},{6,30},{7,5},{8,16},{9,11},... | collective-permute-start | bytes 442376 | tf_op jit(solution)/shard_map/ppermute | solution.py:50
  21.9 1.0 %copy-start.1 = (f32[16,24,256]{2,1,0:T(8,128)S(1)}, f32[16,24,256]{2,1,0:T(8,128)}, u32[]{:S(2)}) copy-start(f32[16,24,256]{2,1,0:T(8,128)} %copy-done) | copy-start | bytes 1179652
  22.9 1.0 %copy-start.3 = (f32[16,24,256]{2,1,0:T(8,128)S(1)}, f32[16,24,256]{2,1,0:T(8,128)}, u32[]{:S(2)}) copy-start(f32[16,24,256]{2,1,0:T(8,128)} %copy-done.2) | copy-start | bytes 1179652
  23.9 1.0 %copy-start.5 = (f32[16,24,256]{2,1,0:T(8,128)S(1)}, f32[16,24,256]{2,1,0:T(8,128)}, u32[]{:S(2)}) copy-start(f32[16,24,256]{2,1,0:T(8,128)} %copy-done.4) | copy-start | bytes 1179652
  24.9 0.9 %copy-start.7 = (bf16[512,256]{1,0:T(8,128)(2,1)S(1)}, bf16[512,256]{1,0:T(8,128)(2,1)}, u32[]{:S(2)}) copy-start(bf16[512,256]{1,0:T(8,128)(2,1)} %copy-done.6) | copy-start | bytes 786436
  25.8 0.9 %copy-start.9 = (f32[2,16,8,128]{3,2,1,0:T(8,128)S(1)}, f32[2,16,8,128]{3,2,1,0:T(8,128)}, u32[]{:S(2)}) copy-start(f32[2,16,8,128]{3,2,1,0:T(8,128)} %copy-done.8) | copy-start | bytes 393220
  26.7 0.9 %copy-start.12 = (f32[2,24,384]{2,1,0:T(8,128)S(1)}, f32[2,24,384]{2,1,0:T(8,128)}, u32[]{:S(2)}) copy-start(f32[2,24,384]{2,1,0:T(8,128)} %copy-done.11) | copy-start | bytes 221188
  29.3 2.1 %collective-permute-start.7 = (bf16[1,6,48,256]{3,2,1,0:T(8,128)(2,1)S(1)}, bf16[1,6,48,256]{3,2,1,0:T(8,128)(2,1)S(1)}, u32[]{:S(2)}, u32[]{:S(2)}) collective-permute-start(bf16[1,6,48,256]{3,2,1,0:T(8,128)(2,1)S(1)} %collective-permute-done.4.refs_0_), channel_id=1, source_target_pairs={{0,1},{1,0},{2,3},{3,2},{4,5},{5,4},{6,7},{7,6},{8,9},{9,8},{10,11... | collective-permute-start | bytes 442376 | tf_op jit(solution)/shard_map/ppermute | solution.py:50
  29.5 6.8 %collective-permute-start.6 = (bf16[2,6,48,256]{3,2,1,0:T(8,128)(2,1)S(1)}, bf16[2,6,48,256]{3,2,1,0:T(8,128)(2,1)S(1)}, u32[]{:S(2)}, u32[]{:S(2)}) collective-permute-start(bf16[2,6,48,256]{3,2,1,0:T(8,128)(2,1)S(1)} %pad_maximum_fusion), channel_id=1, source_target_pairs={{0,2},{1,7},{2,0},{3,5},{4,6},{5,3},{6,4},{7,1},{8,10},{9,15},{10,... | collective-permute-start | bytes 884744 | tf_op jit(solution)/shard_map/ppermute | solution.py:50
  31.5 9.7 %copy-start.10 = (f32[2,16,8,128]{3,2,1,0:T(8,128)S(1)}, f32[2,16,8,128]{3,2,1,0:T(8,128)}, u32[]{:S(2)}) copy-start(f32[2,16,8,128]{3,2,1,0:T(8,128)} %copy-done.8) | copy-start | bytes 393220
  36.3 4.9 %collective-permute-start.10 = (bf16[2,6,48,256]{3,2,1,0:T(8,128)(2,1)S(1)}, bf16[2,6,48,256]{3,2,1,0:T(8,128)(2,1)S(1)}, u32[]{:S(2)}, u32[]{:S(2)}) collective-permute-start(bf16[2,6,48,256]{3,2,1,0:T(8,128)(2,1)S(1)} %collective-permute-done.6.refs_0_), channel_id=1, source_target_pairs={{0,1},{1,0},{2,3},{3,2},{4,5},{5,4},{6,7},{7,6},{8,9},{9,8},{10,11... | collective-permute-start | bytes 884744 | tf_op jit(solution)/shard_map/ppermute | solution.py:50
  37.9 7.9 %collective-permute-start.9 = (bf16[2,6,48,256]{3,2,1,0:T(8,128)(2,1)S(1)}, bf16[2,6,48,256]{3,2,1,0:T(8,128)(2,1)S(1)}, u32[]{:S(2)}, u32[]{:S(2)}) collective-permute-start(bf16[2,6,48,256]{3,2,1,0:T(8,128)(2,1)S(1)} %pad_maximum_fusion), channel_id=1, source_target_pairs={{0,6},{1,25},{2,4},{3,27},{4,2},{5,29},{6,0},{7,31},{8,14},{9,17},... | collective-permute-start | bytes 884744 | tf_op jit(solution)/shard_map/ppermute | solution.py:50
  40.9 8.1 %collective-permute-start.8 = (bf16[2,6,48,256]{3,2,1,0:T(8,128)(2,1)S(1)}, bf16[2,6,48,256]{3,2,1,0:T(8,128)(2,1)S(1)}, u32[]{:S(2)}, u32[]{:S(2)}) collective-permute-start(bf16[2,6,48,256]{3,2,1,0:T(8,128)(2,1)S(1)} %collective-permute-done.6.refs_0_), channel_id=1, source_target_pairs={{0,6},{1,25},{2,4},{3,27},{4,2},{5,29},{6,0},{7,31},{8,14},{9,17},... | collective-permute-start | bytes 884744 | tf_op jit(solution)/shard_map/ppermute | solution.py:50
  45.9 3.2 %collective-permute-start.12 = (bf16[2,6,48,256]{3,2,1,0:T(8,128)(2,1)S(1)}, bf16[2,6,48,256]{3,2,1,0:T(8,128)(2,1)S(1)}, u32[]{:S(2)}, u32[]{:S(2)}) collective-permute-start(bf16[2,6,48,256]{3,2,1,0:T(8,128)(2,1)S(1)} %collective-permute-done.9.refs_0_), channel_id=1, source_target_pairs={{0,1},{1,0},{2,3},{3,2},{4,5},{5,4},{6,7},{7,6},{8,9},{9,8},{10,11... | collective-permute-start | bytes 884744 | tf_op jit(solution)/shard_map/ppermute | solution.py:50
  49.0 3.5 %collective-permute-start.11 = (bf16[2,6,48,256]{3,2,1,0:T(8,128)(2,1)S(1)}, bf16[2,6,48,256]{3,2,1,0:T(8,128)(2,1)S(1)}, u32[]{:S(2)}, u32[]{:S(2)}) collective-permute-start(bf16[2,6,48,256]{3,2,1,0:T(8,128)(2,1)S(1)} %collective-permute-done.8.refs_0_), channel_id=1, source_target_pairs={{0,1},{1,0},{2,3},{3,2},{4,5},{5,4},{6,7},{7,6},{8,9},{9,8},{10,11... | collective-permute-start | bytes 884744 | tf_op jit(solution)/shard_map/ppermute | solution.py:50
  55.3 1.4 %collective-permute-start.13 = (f32[8,8]{1,0:T(8,128)S(1)}, f32[8,8]{1,0:T(8,128)S(1)}, u32[]{:S(2)}, u32[]{:S(2)}) collective-permute-start(f32[8,8]{1,0:T(8,128)S(1)} %get-tuple-element.216), channel_id=1, source_target_pairs={{0,1},{1,0},{2,3},{3,2},{4,5},{5,4},{6,7},{7,6},{8,9},{9,8},{10,11... | collective-permute-start | bytes 776 | tf_op jit(solution)/shard_map/ppermute | solution.py:50
  56.8 3.6 %collective-permute-start.14 = (f32[8,8]{1,0:T(8,128)S(1)}, f32[8,8]{1,0:T(8,128)S(1)}, u32[]{:S(2)}, u32[]{:S(2)}) collective-permute-start(f32[8,8]{1,0:T(8,128)S(1)} %max.12), channel_id=1, source_target_pairs={{0,2},{1,3},{2,0},{3,1},{4,6},{5,7},{6,4},{7,5},{8,10},{9,11},{10,... | collective-permute-start | bytes 776 | tf_op jit(solution)/shard_map/ppermute | solution.py:50
  60.4 4.8 %collective-permute-start.15 = (f32[8,8]{1,0:T(8,128)S(1)}, f32[8,8]{1,0:T(8,128)S(1)}, u32[]{:S(2)}, u32[]{:S(2)}) collective-permute-start(f32[8,8]{1,0:T(8,128)S(1)} %max.13), channel_id=1, source_target_pairs={{0,6},{1,7},{2,4},{3,5},{4,2},{5,3},{6,0},{7,1},{8,14},{9,15},{10,... | collective-permute-start | bytes 776 | tf_op jit(solution)/shard_map/ppermute | solution.py:50
  65.2 5.1 %collective-permute-start.16 = (f32[8,8]{1,0:T(8,128)S(1)}, f32[8,8]{1,0:T(8,128)S(1)}, u32[]{:S(2)}, u32[]{:S(2)}) collective-permute-start(f32[8,8]{1,0:T(8,128)S(1)} %max.14), channel_id=1, source_target_pairs={{0,8},{1,9},{2,10},{3,11},{4,12},{5,13},{6,14},{7,15},{8,0},{9,1},... | collective-permute-start | bytes 776 | tf_op jit(solution)/shard_map/ppermute | solution.py:50

commit v8 on v7

--- a/solution.py
+++ b/solution.py
@@ -351,14 +351,14 @@
     (bin_of, turned, table, turn), binned = prepare_tables(small)
     wide, stat = prepare_templates(templates, small)
 
-    x = jnp.transpose(strain[0], (2, 1, 0, 3)).reshape(JS, 2 * NDET, 1, FB)
+    shard, even = lax.optimization_barrier((strain[0], lax.axis_index("dt") % 2 == 0))
+    x = jnp.transpose(shard, (2, 1, 0, 3)).reshape(JS, 2 * NDET, 1, FB)
     got = {0: x}
     for dx in (2, 3, 1):
         got[dx] = swap_with(x, across(dx=dx))
     x = jnp.concatenate([got[dx] for dx in range(4)], axis=2)
     x, turned = lax.optimization_barrier((x, turned))
     got = swap_with(x, across(dy=1))
-    even = lax.axis_index("dt") % 2 == 0
     x, got, wide = lax.optimization_barrier((x, got, wide))
     x = jnp.concatenate([jnp.where(even, x, got), jnp.where(even, got, x)], axis=2)
     shared = (bin_of, table, turn, wide, turned)

time: 71.4 us -> 63.2 us (0.89)
  local copies, waits for them, and re-layouts: 12.1 us -> 2.12 us
  waiting for transfers between devices: 16.3 us -> 19.5 us
  other arithmetic: 3.09 us -> 1.51 us
    unnamed x29 -> x3, local copies, waits for them, and re-layouts: 12 us -> 2 us
    ppermute x17, waiting for transfers between devices: 16.3 us -> 19.5 us  [swap_with(): return lax.ppermute(value, AXES, pairs)]
    select_n x1, other arithmetic: 0.96 us -> 0.02 us  [per_device(): jnp.where(even, x, got)]
  transfers between devices with their start and end apart: 17 -> 17, of which waited for: 8 -> 10; matrix products, arithmetic and copies ran while one was open for 1% -> 1% of each run, Pallas kernels for 20% -> 23%
where the time goes in v8:
time: 63.2 us; the launch traced here: 63 us
  starting transfers between devices  21.9 us (35%)
  waiting for transfers between devices  19.5 us (31%)
  Pallas kernels  17.2 us (27%)
  local copies, waits for them, and re-layouts  2.12 us (3%)
  other arithmetic  1.51 us (2%)
  between operations  0.77 us (1%)
    ppermute x17, starting transfers between devices, swap_with(): return lax.ppermute(value, AXES, pairs)  21.9 us
    ppermute x17, waiting for transfers between devices, swap_with(): return lax.ppermute(value, AXES, pairs)  19.5 us
    pallas_call x7, Pallas kernels, add_bins(): pl.pallas_call(functools.partial(bins_kernel, parts, last), out_shape=out...  14.9 us
    unnamed x3, local copies, waits for them, and re-layouts  2 us
    pallas_call x1, Pallas kernels, prepare_templates(): pl.pallas_call(templates_kernel, out_shape=[jax.ShapeDtypeStruct((SLOTS,...  1.66 us
  transfers between devices with their start and end apart: 17, of which 10 were waited for; matrix products, arithmetic and copies ran while one was open for 1% of the time, Pallas kernels for 23%

profile of v8, /device:TPU:0, one launch (start us, length us, event | category | flops | bytes accessed | tf_op | source)
XLA Modules:
  0.0 63.0 jit_solution(10946813906989454061)
XLA Ops:
  0.0 0.7 %copy.97 = bf16[1,3,2,6,256]{4,3,1,2,0:T(8,128)(2,1)S(1)} copy(bf16[1,3,2,6,256]{4,2,3,1,0:T(2,128)(2,1)} %param.5) | data formatting | bytes 36864 | tf_op args[0]
  0.7 1.6 %collective-permute-start = (bf16[6,6,1,256]{3,0,1,2:T(8,128)(2,1)S(1)}, bf16[6,6,1,256]{3,0,1,2:T(8,128)(2,1)S(1)}, u32[]{:S(2)}, u32[]{:S(2)}) collective-permute-start(bf16[6,6,1,256]{3,0,1,2:T(8,128)(2,1)S(1)} %bitcast.21), channel_id=1, source_target_pairs={{0,32},{1,33},{2,34},{3,35},{4,36},{5,37},{6,38},{7,39},{8,40},{9,... | collective-permute-start | bytes 55304 | tf_op jit(solution)/shard_map/ppermute | solution.py:50
  2.3 2.7 %collective-permute-start.1 = (bf16[6,6,1,256]{3,0,1,2:T(8,128)(2,1)S(1)}, bf16[6,6,1,256]{3,0,1,2:T(8,128)(2,1)S(1)}, u32[]{:S(2)}, u32[]{:S(2)}) collective-permute-start(bf16[6,6,1,256]{3,0,1,2:T(8,128)(2,1)S(1)} %bitcast.22), channel_id=1, source_target_pairs={{0,64},{1,65},{2,66},{3,67},{4,68},{5,69},{6,70},{7,71},{8,72},{9,... | collective-permute-start | bytes 55304 | tf_op jit(solution)/shard_map/ppermute | solution.py:50
  5.0 0.4 collective-permute-start.2
  6.1 0.1 pad.16.clone
  6.2 0.8 %fusion.small_ref = s32[16,128]{1,0:T(8,128)S(1)} fusion(s32[3,8]{1,0:T(4,128)} %bitcast.25, s32[12,15]{1,0:T(8,128)} %param.8, s32[16]{0:T(128)S(1)} %pad.16.clone), kind=kLoop, calls=%fused_computation.8 | loop fusion | flops 8192 | bytes 9072 | tf_op jit(solution)/shard_map/concatenate | solution.py:172
  6.9 0.7 %prepare_tables.1 = (f32[12,128]{1,0:T(8,128)S(1)}, f32[2,24,384]{2,1,0:T(8,128)S(1)}, bf16[512,256]{1,0:T(8,128)(2,1)S(1)}, f32[2,16,8,128]{3,2,1,0:T(8,128)S(1...) custom-call(s32[16,128]{1,0:T(8,128)S(1)} %fusion.small_ref), custom_call_target="tpu_custom_call" | custom-call | flops 1000000 | bytes 1000000 | tf_op jit(solution)/shard_map/prepare_tables/pallas_call | solution.py:180
  7.7 0.0 collective-permute-done
  7.7 0.0 collective-permute-done.1
  7.7 2.4 %collective-permute-done.2 = bf16[6,6,1,256]{3,0,1,2:T(8,128)(2,1)S(1)} collective-permute-done((bf16[6,6,1,256]{3,0,1,2:T(8,128)(2,1)S(1)}, bf16[6,6,1,256]{3,0,1,2:T(8,128)(2,1)S(1)}, u32[]{:S(2)}, u32[]{:S(2)}) %collective-permute-start.2) | collective-permute-done | bytes 18464 | tf_op jit(solution)/shard_map/ppermute | solution.py:50
  10.1 1.7 %collective-permute-start.3 = (bf16[6,6,4,256]{3,0,1,2:T(8,128)(2,1)S(1)}, bf16[6,6,4,256]{3,0,1,2:T(8,128)(2,1)S(1)}, u32[]{:S(2)}, u32[]{:S(2)}) collective-permute-start(bf16[6,6,4,256]{3,0,1,2:T(8,128)(2,1)S(1)} %pad_maximum_fusion.2), channel_id=1, source_target_pairs={{0,16},{1,17},{2,18},{3,19},{4,20},{5,21},{6,22},{7,23},{8,24},{9,... | collective-permute-start | bytes 221192 | tf_op jit(solution)/shard_map/ppermute | solution.py:50
  11.8 1.3 %copy-done = bf16[12,2,96,256]{3,2,1,0:T(8,128)(2,1)S(1)} copy-done((bf16[12,2,96,256]{3,2,1,0:T(8,128)(2,1)S(1)}, bf16[12,2,96,256]{3,2,1,0:T(8,128)(2,1)}, u32[]{:S(2)}) %copy-start) | copy-done | bytes 1179672
  13.0 1.7 %prepare_templates.1 = (f32[12,3,96,256]{3,2,1,0:T(8,128)S(1)}, f32[12,40,128]{2,1,0:T(8,128)S(1)}) custom-call(bf16[12,2,96,256]{3,2,1,0:T(8,128)(2,1)S(1)} %copy-done, s32[16,128]{1,0:T(8,128)S(1)} %fusion.small_ref), custom_call_target="tpu_custom_call" | custom-call | flops 1000000 | bytes 1000000 | tf_op jit(solution)/shard_map/prepare_templates/pallas_call | solution.py:198
  14.7 0.1 collective-permute-done.3
  14.9 0.1 collective-permute-start.5
  15.0 3.1 %collective-permute-start.4 = (bf16[1,6,48,256]{3,2,1,0:T(8,128)(2,1)S(1)}, bf16[1,6,48,256]{3,2,1,0:T(8,128)(2,1)S(1)}, u32[]{:S(2)}, u32[]{:S(2)}) collective-permute-start(bf16[1,6,48,256]{3,2,1,0:T(8,128)(2,1)S(1)} %bitcast.18), channel_id=1, source_target_pairs={{0,24},{1,3},{2,26},{3,1},{4,28},{5,7},{6,30},{7,5},{8,16},{9,11},... | collective-permute-start | bytes 442376 | tf_op jit(solution)/shard_map/ppermute | solution.py:50
  18.1 0.0 collective-permute-done.5.refs_1_
  18.1 1.7 %add_bins.6 = (f32[16,24,256]{2,1,0:T(8,128)S(1)}, f32[16,24,256]{2,1,0:T(8,128)S(1)}, f32[16,24,256]{2,1,0:T(8,128)S(1)}, f32[16,24,256]{2,1,0:T(8,128)S(1)}, f...) custom-call(bf16[1,6,48,256]{3,2,1,0:T(8,128)(2,1)S(1)} %bitcast.19,, ...), custom_call_target="tpu_custom_call", output_to_operand_aliasing={{0}: (7, {}), {1}: (8, {}), {2}: (9, {}), {3}: (10, {}), {4... | custom-call | flops 1811939328 | bytes 1000000 | tf_op jit(solution)/shard_map/add_bins/pallas_call | solution.py:336
  19.8 1.6 %collective-permute-done.4.refs_0_ = bf16[1,6,48,256]{3,2,1,0:T(8,128)(2,1)S(1)} collective-permute-done((bf16[1,6,48,256]{3,2,1,0:T(8,128)(2,1)S(1)}, bf16[1,6,48,256]{3,2,1,0:T(8,128)(2,1)S(1)}, u32[]{:S(2)}, u32[]{:S(2)}) %collective-permute-start.4) | collective-permute-done | bytes 147488 | tf_op jit(solution)/shard_map/ppermute | solution.py:50
  21.5 0.0 collective-permute-start.7
  21.5 2.0 %collective-permute-start.6 = (bf16[2,6,48,256]{3,2,1,0:T(8,128)(2,1)S(1)}, bf16[2,6,48,256]{3,2,1,0:T(8,128)(2,1)S(1)}, u32[]{:S(2)}, u32[]{:S(2)}) collective-permute-start(bf16[2,6,48,256]{3,2,1,0:T(8,128)(2,1)S(1)} %pad_maximum_fusion), channel_id=1, source_target_pairs={{0,2},{1,7},{2,0},{3,5},{4,6},{5,3},{6,4},{7,1},{8,10},{9,15},{10,... | collective-permute-start | bytes 884744 | tf_op jit(solution)/shard_map/ppermute | solution.py:50
  23.5 0.0 collective-permute-done.7.refs_1_
  23.5 1.7 %add_bins.7 = (f32[16,24,256]{2,1,0:T(8,128)S(1)}, f32[16,24,256]{2,1,0:T(8,128)S(1)}, f32[16,24,256]{2,1,0:T(8,128)S(1)}, f32[16,24,256]{2,1,0:T(8,128)S(1)}, f...) custom-call(bf16[1,6,48,256]{3,2,1,0:T(8,128)(2,1)S(1)} %collective-, ...), custom_call_target="tpu_custom_call", output_to_operand_aliasing={{0}: (7, {}), {1}: (8, {}), {2}: (9, {}), {3}: (10, {}), {4... | custom-call | flops 1811939328 | bytes 1000000 | tf_op jit(solution)/shard_map/add_bins/pallas_call | solution.py:336
  25.2 3.1 %collective-permute-done.6.refs_0_ = bf16[2,6,48,256]{3,2,1,0:T(8,128)(2,1)S(1)} collective-permute-done((bf16[2,6,48,256]{3,2,1,0:T(8,128)(2,1)S(1)}, bf16[2,6,48,256]{3,2,1,0:T(8,128)(2,1)S(1)}, u32[]{:S(2)}, u32[]{:S(2)}) %collective-permute-start.6) | collective-permute-done | bytes 294944 | tf_op jit(solution)/shard_map/ppermute | solution.py:50
  28.3 1.7 %collective-permute-start.10 = (bf16[2,6,48,256]{3,2,1,0:T(8,128)(2,1)S(1)}, bf16[2,6,48,256]{3,2,1,0:T(8,128)(2,1)S(1)}, u32[]{:S(2)}, u32[]{:S(2)}) collective-permute-start(bf16[2,6,48,256]{3,2,1,0:T(8,128)(2,1)S(1)} %collective-permute-done.6.refs_0_), channel_id=1, source_target_pairs={{0,1},{1,0},{2,3},{3,2},{4,5},{5,4},{6,7},{7,6},{8,9},{9,8},{10,11... | collective-permute-start | bytes 884744 | tf_op jit(solution)/shard_map/ppermute | solution.py:50
  29.9 3.0 %collective-permute-start.9 = (bf16[2,6,48,256]{3,2,1,0:T(8,128)(2,1)S(1)}, bf16[2,6,48,256]{3,2,1,0:T(8,128)(2,1)S(1)}, u32[]{:S(2)}, u32[]{:S(2)}) collective-permute-start(bf16[2,6,48,256]{3,2,1,0:T(8,128)(2,1)S(1)} %pad_maximum_fusion), channel_id=1, source_target_pairs={{0,6},{1,25},{2,4},{3,27},{4,2},{5,29},{6,0},{7,31},{8,14},{9,17},... | collective-permute-start | bytes 884744 | tf_op jit(solution)/shard_map/ppermute | solution.py:50
  32.9 0.3 collective-permute-start.8
  33.2 0.0 collective-permute-done.10.refs_1_
  33.2 3.4 %add_bins.8 = (f32[16,24,256]{2,1,0:T(8,128)S(1)}, f32[16,24,256]{2,1,0:T(8,128)S(1)}, f32[16,24,256]{2,1,0:T(8,128)S(1)}, f32[16,24,256]{2,1,0:T(8,128)S(1)}, f...) custom-call(bf16[2,6,48,256]{3,2,1,0:T(8,128)(2,1)S(1)} %collective-, ...), custom_call_target="tpu_custom_call", output_to_operand_aliasing={{0}: (7, {}), {1}: (8, {}), {2}: (9, {}), {3}: (10, {}), {4... | custom-call | flops 3623878656 | bytes 1000000 | tf_op jit(solution)/shard_map/add_bins/pallas_call | solution.py:336
  36.6 1.3 %collective-permute-done.9.refs_0_ = bf16[2,6,48,256]{3,2,1,0:T(8,128)(2,1)S(1)} collective-permute-done((bf16[2,6,48,256]{3,2,1,0:T(8,128)(2,1)S(1)}, bf16[2,6,48,256]{3,2,1,0:T(8,128)(2,1)S(1)}, u32[]{:S(2)}, u32[]{:S(2)}) %collective-permute-start.9) | collective-permute-done | bytes 294944 | tf_op jit(solution)/shard_map/ppermute | solution.py:50
  37.9 0.0 collective-permute-start.12
  37.9 1.7 %add_bins.9 = (f32[16,24,256]{2,1,0:T(8,128)S(1)}, f32[16,24,256]{2,1,0:T(8,128)S(1)}, f32[16,24,256]{2,1,0:T(8,128)S(1)}, f32[16,24,256]{2,1,0:T(8,128)S(1)}, f...) custom-call(bf16[2,6,48,256]{3,2,1,0:T(8,128)(2,1)S(1)} %collective-, ...), custom_call_target="tpu_custom_call", output_to_operand_aliasing={{0}: (6, {}), {1}: (7, {}), {2}: (8, {}), {3}: (9, {}), {4}... | custom-call | flops 1811939328 | bytes 1000000 | tf_op jit(solution)/shard_map/add_bins/pallas_call | solution.py:336
  39.6 1.4 %collective-permute-done.8.refs_0_ = bf16[2,6,48,256]{3,2,1,0:T(8,128)(2,1)S(1)} collective-permute-done((bf16[2,6,48,256]{3,2,1,0:T(8,128)(2,1)S(1)}, bf16[2,6,48,256]{3,2,1,0:T(8,128)(2,1)S(1)}, u32[]{:S(2)}, u32[]{:S(2)}) %collective-permute-start.8) | collective-permute-done | bytes 294944 | tf_op jit(solution)/shard_map/ppermute | solution.py:50
  41.0 0.0 collective-permute-start.11
  41.0 0.0 collective-permute-done.12.refs_0_
  41.0 1.7 %add_bins.10 = (f32[16,24,256]{2,1,0:T(8,128)S(1)}, f32[16,24,256]{2,1,0:T(8,128)S(1)}, f32[16,24,256]{2,1,0:T(8,128)S(1)}, f32[16,24,256]{2,1,0:T(8,128)S(1)}, ...) custom-call(bf16[2,6,48,256]{3,2,1,0:T(8,128)(2,1)S(1)} %collective-, ...), custom_call_target="tpu_custom_call", output_to_operand_aliasing={{0}: (6, {}), {1}: (7, {}), {2}: (8, {}), {3}: (9, {}), {4}... | custom-call | flops 1811939328 | bytes 1000000 | tf_op jit(solution)/shard_map/add_bins/pallas_call | solution.py:336
  42.8 1.8 %add_bins.11 = (f32[16,24,256]{2,1,0:T(8,128)S(1)}, f32[16,24,256]{2,1,0:T(8,128)S(1)}, f32[16,24,256]{2,1,0:T(8,128)S(1)}, f32[16,24,256]{2,1,0:T(8,128)S(1)}, ...) custom-call(bf16[2,6,48,256]{3,2,1,0:T(8,128)(2,1)S(1)} %collective-, ...), custom_call_target="tpu_custom_call", output_to_operand_aliasing={{0}: (6, {}), {1}: (7, {}), {2}: (8, {}), {3}: (9, {}), {4}... | custom-call | flops 1811939328 | bytes 1000000 | tf_op jit(solution)/shard_map/add_bins/pallas_call | solution.py:336
  44.6 0.0 collective-permute-done.11.refs_0_
  44.6 2.9 %last_bins.1 = (f32[16,24,256]{2,1,0:T(8,128)S(1)}, f32[16,24,256]{2,1,0:T(8,128)S(1)}, f32[16,24,256]{2,1,0:T(8,128)S(1)}, f32[16,24,256]{2,1,0:T(8,128)S(1)}, ...) custom-call(bf16[2,6,48,256]{3,2,1,0:T(8,128)(2,1)S(1)} %collective-, ...), custom_call_target="tpu_custom_call", output_to_operand_aliasing={{0}: (7, {}), {1}: (8, {}), {2}: (9, {}), {3}: (10, {}), {4... | custom-call | flops 1811939328 | bytes 1000000 | tf_op jit(solution)/shard_map/last_bins/pallas_call | solution.py:336
  47.4 0.6 collective-permute-start.13
  48.0 0.8 %collective-permute-done.13 = f32[8,8]{1,0:T(8,128)S(1)} collective-permute-done((f32[8,8]{1,0:T(8,128)S(1)}, f32[8,8]{1,0:T(8,128)S(1)}, u32[]{:S(2)}, u32[]{:S(2)}) %collective-permute-start.13) | collective-permute-done | bytes 288 | tf_op jit(solution)/shard_map/ppermute | solution.py:50
  48.8 0.0 collective-permute-start.14
  48.8 3.6 %collective-permute-done.14 = f32[8,8]{1,0:T(8,128)S(1)} collective-permute-done((f32[8,8]{1,0:T(8,128)S(1)}, f32[8,8]{1,0:T(8,128)S(1)}, u32[]{:S(2)}, u32[]{:S(2)}) %collective-permute-start.14) | collective-permute-done | bytes 288 | tf_op jit(solution)/shard_map/ppermute | solution.py:50
  52.4 2.9 %collective-permute-start.15 = (f32[8,8]{1,0:T(8,128)S(1)}, f32[8,8]{1,0:T(8,128)S(1)}, u32[]{:S(2)}, u32[]{:S(2)}) collective-permute-start(f32[8,8]{1,0:T(8,128)S(1)} %max.13), channel_id=1, source_target_pairs={{0,6},{1,7},{2,4},{3,5},{4,2},{5,3},{6,0},{7,1},{8,14},{9,15},{10,... | collective-permute-start | bytes 776 | tf_op jit(solution)/shard_map/ppermute | solution.py:50
  55.3 1.9 %collective-permute-done.15 = f32[8,8]{1,0:T(8,128)S(1)} collective-permute-done((f32[8,8]{1,0:T(8,128)S(1)}, f32[8,8]{1,0:T(8,128)S(1)}, u32[]{:S(2)}, u32[]{:S(2)}) %collective-permute-start.15) | collective-permute-done | bytes 288 | tf_op jit(solution)/shard_map/ppermute | solution.py:50
  57.2 2.0 %collective-permute-start.16 = (f32[8,8]{1,0:T(8,128)S(1)}, f32[8,8]{1,0:T(8,128)S(1)}, u32[]{:S(2)}, u32[]{:S(2)}) collective-permute-start(f32[8,8]{1,0:T(8,128)S(1)} %max.14), channel_id=1, source_target_pairs={{0,8},{1,9},{2,10},{3,11},{4,12},{5,13},{6,14},{7,15},{8,0},{9,1},... | collective-permute-start | bytes 776 | tf_op jit(solution)/shard_map/ppermute | solution.py:50
  59.2 3.1 %collective-permute-done.16 = f32[8,8]{1,0:T(8,128)S(1)} collective-permute-done((f32[8,8]{1,0:T(8,128)S(1)}, f32[8,8]{1,0:T(8,128)S(1)}, u32[]{:S(2)}, u32[]{:S(2)}) %collective-permute-start.16) | collective-permute-done | bytes 288 | tf_op jit(solution)/shard_map/ppermute | solution.py:50
  62.4 0.6 max.15
  (9 shorter events, 0.2 us)
Async XLA Ops:
  0.7 6.9 %collective-permute-start = (bf16[6,6,1,256]{3,0,1,2:T(8,128)(2,1)S(1)}, bf16[6,6,1,256]{3,0,1,2:T(8,128)(2,1)S(1)}, u32[]{:S(2)}, u32[]{:S(2)}) collective-permute-start(bf16[6,6,1,256]{3,0,1,2:T(8,128)(2,1)S(1)} %bitcast.21), channel_id=1, source_target_pairs={{0,32},{1,33},{2,34},{3,35},{4,36},{5,37},{6,38},{7,39},{8,40},{9,... | collective-permute-start | bytes 55304 | tf_op jit(solution)/shard_map/ppermute | solution.py:50
  2.3 5.4 %collective-permute-start.1 = (bf16[6,6,1,256]{3,0,1,2:T(8,128)(2,1)S(1)}, bf16[6,6,1,256]{3,0,1,2:T(8,128)(2,1)S(1)}, u32[]{:S(2)}, u32[]{:S(2)}) collective-permute-start(bf16[6,6,1,256]{3,0,1,2:T(8,128)(2,1)S(1)} %bitcast.22), channel_id=1, source_target_pairs={{0,64},{1,65},{2,66},{3,67},{4,68},{5,69},{6,70},{7,71},{8,72},{9,... | collective-permute-start | bytes 55304 | tf_op jit(solution)/shard_map/ppermute | solution.py:50
  5.0 5.0 %collective-permute-start.2 = (bf16[6,6,1,256]{3,0,1,2:T(8,128)(2,1)S(1)}, bf16[6,6,1,256]{3,0,1,2:T(8,128)(2,1)S(1)}, u32[]{:S(2)}, u32[]{:S(2)}) collective-permute-start(bf16[6,6,1,256]{3,0,1,2:T(8,128)(2,1)S(1)} %bitcast.23), channel_id=1, source_target_pairs={{0,96},{1,97},{2,98},{3,99},{4,100},{5,101},{6,102},{7,103},{8,104... | collective-permute-start | bytes 55304 | tf_op jit(solution)/shard_map/ppermute | solution.py:50
  10.1 4.7 %collective-permute-start.3 = (bf16[6,6,4,256]{3,0,1,2:T(8,128)(2,1)S(1)}, bf16[6,6,4,256]{3,0,1,2:T(8,128)(2,1)S(1)}, u32[]{:S(2)}, u32[]{:S(2)}) collective-permute-start(bf16[6,6,4,256]{3,0,1,2:T(8,128)(2,1)S(1)} %pad_maximum_fusion.2), channel_id=1, source_target_pairs={{0,16},{1,17},{2,18},{3,19},{4,20},{5,21},{6,22},{7,23},{8,24},{9,... | collective-permute-start | bytes 221192 | tf_op jit(solution)/shard_map/ppermute | solution.py:50
  11.8 1.3 %copy-start = (bf16[12,2,96,256]{3,2,1,0:T(8,128)(2,1)S(1)}, bf16[12,2,96,256]{3,2,1,0:T(8,128)(2,1)}, u32[]{:S(2)}) copy-start(bf16[12,2,96,256]{3,2,1,0:T(8,128)(2,1)} %templ_ref.1) | copy-start | bytes 3538948
  14.9 3.2 %collective-permute-start.5 = (bf16[1,6,48,256]{3,2,1,0:T(8,128)(2,1)S(1)}, bf16[1,6,48,256]{3,2,1,0:T(8,128)(2,1)S(1)}, u32[]{:S(2)}, u32[]{:S(2)}) collective-permute-start(bf16[1,6,48,256]{3,2,1,0:T(8,128)(2,1)S(1)} %bitcast.17), channel_id=1, source_target_pairs={{0,1},{1,0},{2,3},{3,2},{4,5},{5,4},{6,7},{7,6},{8,9},{9,8},{10,11... | collective-permute-start | bytes 442376 | tf_op jit(solution)/shard_map/ppermute | solution.py:50
  15.0 6.4 %collective-permute-start.4 = (bf16[1,6,48,256]{3,2,1,0:T(8,128)(2,1)S(1)}, bf16[1,6,48,256]{3,2,1,0:T(8,128)(2,1)S(1)}, u32[]{:S(2)}, u32[]{:S(2)}) collective-permute-start(bf16[1,6,48,256]{3,2,1,0:T(8,128)(2,1)S(1)} %bitcast.18), channel_id=1, source_target_pairs={{0,24},{1,3},{2,26},{3,1},{4,28},{5,7},{6,30},{7,5},{8,16},{9,11},... | collective-permute-start | bytes 442376 | tf_op jit(solution)/shard_map/ppermute | solution.py:50
  21.5 2.0 %collective-permute-start.7 = (bf16[1,6,48,256]{3,2,1,0:T(8,128)(2,1)S(1)}, bf16[1,6,48,256]{3,2,1,0:T(8,128)(2,1)S(1)}, u32[]{:S(2)}, u32[]{:S(2)}) collective-permute-start(bf16[1,6,48,256]{3,2,1,0:T(8,128)(2,1)S(1)} %collective-permute-done.4.refs_0_), channel_id=1, source_target_pairs={{0,1},{1,0},{2,3},{3,2},{4,5},{5,4},{6,7},{7,6},{8,9},{9,8},{10,11... | collective-permute-start | bytes 442376 | tf_op jit(solution)/shard_map/ppermute | solution.py:50
  21.5 6.8 %collective-permute-start.6 = (bf16[2,6,48,256]{3,2,1,0:T(8,128)(2,1)S(1)}, bf16[2,6,48,256]{3,2,1,0:T(8,128)(2,1)S(1)}, u32[]{:S(2)}, u32[]{:S(2)}) collective-permute-start(bf16[2,6,48,256]{3,2,1,0:T(8,128)(2,1)S(1)} %pad_maximum_fusion), channel_id=1, source_target_pairs={{0,2},{1,7},{2,0},{3,5},{4,6},{5,3},{6,4},{7,1},{8,10},{9,15},{10,... | collective-permute-start | bytes 884744 | tf_op jit(solution)/shard_map/ppermute | solution.py:50
  28.3 4.9 %collective-permute-start.10 = (bf16[2,6,48,256]{3,2,1,0:T(8,128)(2,1)S(1)}, bf16[2,6,48,256]{3,2,1,0:T(8,128)(2,1)S(1)}, u32[]{:S(2)}, u32[]{:S(2)}) collective-permute-start(bf16[2,6,48,256]{3,2,1,0:T(8,128)(2,1)S(1)} %collective-permute-done.6.refs_0_), channel_id=1, source_target_pairs={{0,1},{1,0},{2,3},{3,2},{4,5},{5,4},{6,7},{7,6},{8,9},{9,8},{10,11... | collective-permute-start | bytes 884744 | tf_op jit(solution)/shard_map/ppermute | solution.py:50
  29.9 7.9 %collective-permute-start.9 = (bf16[2,6,48,256]{3,2,1,0:T(8,128)(2,1)S(1)}, bf16[2,6,48,256]{3,2,1,0:T(8,128)(2,1)S(1)}, u32[]{:S(2)}, u32[]{:S(2)}) collective-permute-start(bf16[2,6,48,256]{3,2,1,0:T(8,128)(2,1)S(1)} %pad_maximum_fusion), channel_id=1, source_target_pairs={{0,6},{1,25},{2,4},{3,27},{4,2},{5,29},{6,0},{7,31},{8,14},{9,17},... | collective-permute-start | bytes 884744 | tf_op jit(solution)/shard_map/ppermute | solution.py:50
  32.9 8.1 %collective-permute-start.8 = (bf16[2,6,48,256]{3,2,1,0:T(8,128)(2,1)S(1)}, bf16[2,6,48,256]{3,2,1,0:T(8,128)(2,1)S(1)}, u32[]{:S(2)}, u32[]{:S(2)}) collective-permute-start(bf16[2,6,48,256]{3,2,1,0:T(8,128)(2,1)S(1)} %collective-permute-done.6.refs_0_), channel_id=1, source_target_pairs={{0,6},{1,25},{2,4},{3,27},{4,2},{5,29},{6,0},{7,31},{8,14},{9,17},... | collective-permute-start | bytes 884744 | tf_op jit(solution)/shard_map/ppermute | solution.py:50
  37.9 3.2 %collective-permute-start.12 = (bf16[2,6,48,256]{3,2,1,0:T(8,128)(2,1)S(1)}, bf16[2,6,48,256]{3,2,1,0:T(8,128)(2,1)S(1)}, u32[]{:S(2)}, u32[]{:S(2)}) collective-permute-start(bf16[2,6,48,256]{3,2,1,0:T(8,128)(2,1)S(1)} %collective-permute-done.9.refs_0_), channel_id=1, source_target_pairs={{0,1},{1,0},{2,3},{3,2},{4,5},{5,4},{6,7},{7,6},{8,9},{9,8},{10,11... | collective-permute-start | bytes 884744 | tf_op jit(solution)/shard_map/ppermute | solution.py:50
  41.0 3.5 %collective-permute-start.11 = (bf16[2,6,48,256]{3,2,1,0:T(8,128)(2,1)S(1)}, bf16[2,6,48,256]{3,2,1,0:T(8,128)(2,1)S(1)}, u32[]{:S(2)}, u32[]{:S(2)}) collective-permute-start(bf16[2,6,48,256]{3,2,1,0:T(8,128)(2,1)S(1)} %collective-permute-done.8.refs_0_), channel_id=1, source_target_pairs={{0,1},{1,0},{2,3},{3,2},{4,5},{5,4},{6,7},{7,6},{8,9},{9,8},{10,11... | collective-permute-start | bytes 884744 | tf_op jit(solution)/shard_map/ppermute | solution.py:50
  47.4 1.4 %collective-permute-start.13 = (f32[8,8]{1,0:T(8,128)S(1)}, f32[8,8]{1,0:T(8,128)S(1)}, u32[]{:S(2)}, u32[]{:S(2)}) collective-permute-start(f32[8,8]{1,0:T(8,128)S(1)} %get-tuple-element.220), channel_id=1, source_target_pairs={{0,1},{1,0},{2,3},{3,2},{4,5},{5,4},{6,7},{7,6},{8,9},{9,8},{10,11... | collective-permute-start | bytes 776 | tf_op jit(solution)/shard_map/ppermute | solution.py:50
  48.8 3.6 %collective-permute-start.14 = (f32[8,8]{1,0:T(8,128)S(1)}, f32[8,8]{1,0:T(8,128)S(1)}, u32[]{:S(2)}, u32[]{:S(2)}) collective-permute-start(f32[8,8]{1,0:T(8,128)S(1)} %max.12), channel_id=1, source_target_pairs={{0,2},{1,3},{2,0},{3,1},{4,6},{5,7},{6,4},{7,5},{8,10},{9,11},{10,... | collective-permute-start | bytes 776 | tf_op jit(solution)/shard_map/ppermute | solution.py:50
  52.4 4.8 %collective-permute-start.15 = (f32[8,8]{1,0:T(8,128)S(1)}, f32[8,8]{1,0:T(8,128)S(1)}, u32[]{:S(2)}, u32[]{:S(2)}) collective-permute-start(f32[8,8]{1,0:T(8,128)S(1)} %max.13), channel_id=1, source_target_pairs={{0,6},{1,7},{2,4},{3,5},{4,2},{5,3},{6,0},{7,1},{8,14},{9,15},{10,... | collective-permute-start | bytes 776 | tf_op jit(solution)/shard_map/ppermute | solution.py:50
  57.2 5.1 %collective-permute-start.16 = (f32[8,8]{1,0:T(8,128)S(1)}, f32[8,8]{1,0:T(8,128)S(1)}, u32[]{:S(2)}, u32[]{:S(2)}) collective-permute-start(f32[8,8]{1,0:T(8,128)S(1)} %max.14), channel_id=1, source_target_pairs={{0,8},{1,9},{2,10},{3,11},{4,12},{5,13},{6,14},{7,15},{8,0},{9,1},... | collective-permute-start | bytes 776 | tf_op jit(solution)/shard_map/ppermute | solution.py:50

commit v9 on v8

--- a/solution.py
+++ b/solution.py
@@ -99,7 +99,8 @@
     return lax.broadcasted_iota(jnp.int32, shape, axis)
 
 
-def tables_kernel(small_ref, bin_ref, phase_ref, table_ref, turn_ref, *binned):
+def tables_kernel(small_ref, bin_ref, turned_ref, table_ref, turn_ref, *refs):
+    binned, (now_ref,) = refs[:SLOTS], refs[SLOTS:]
     for ref in binned:
         ref[...] = jnp.zeros_like(ref)
 
@@ -117,10 +118,19 @@
     spread = [jnp.broadcast_to(small_ref[SLOTS + d:SLOTS + d + 1, :], (SEGS, LANES)) for d in range(NDET)]
     held = jnp.where(here, jnp.concatenate(spread, axis=0), 0).astype(jnp.float32)
     first = MARGIN + jnp.sum(held, axis=1, keepdims=True).astype(jnp.int32)
-    lane = counted((1, FB + LANES), 1)
-    starts = (FLOW // FB + (lane - FB) * JS) * FB
-    rate = jnp.where(lane < FB, lane * STRIDE, jnp.where(lane < FB + NSL, starts, FB))
-    phase_ref[0], phase_ref[1] = circle(first * rate)
+    now_ref[0], now_ref[1] = circle(first * (FLOW + counted((1, FB), 1)) * STRIDE)
+    pc, ps = circle(jnp.broadcast_to(first * FB, (ROWS, TW)))
+    pc, ps = jnp.concatenate([pc, pc], axis=1), jnp.concatenate([ps, ps], axis=1)
+
+    def one_block(j, carry):
+        rc, rs = now_ref[0], now_ref[1]
+        turned_ref[j, 0] = rc
+        turned_ref[j, 1] = rs
+        now_ref[0] = rc * pc - rs * ps
+        now_ref[1] = rc * ps + rs * pc
+        return carry
+
+    lax.fori_loop(0, NBLK, one_block, 0)
 
     lane = counted((SLOTS, LANES), 1)
     bin_of = jnp.zeros((SLOTS, LANES), jnp.int32)
@@ -181,12 +191,13 @@
         tables_kernel,
         out_shape=[
             jax.ShapeDtypeStruct((SLOTS, LANES), jnp.float32),
-            jax.ShapeDtypeStruct((2, ROWS, FB + LANES), jnp.float32),
+            jax.ShapeDtypeStruct((NBLK, 2, ROWS, FB), jnp.float32),
             jax.ShapeDtypeStruct((2 * FB, 2 * TW), jnp.bfloat16),
             jax.ShapeDtypeStruct((2, NSL, 8, TW), jnp.float32),
         ] + BINNED,
         in_specs=[whole()],
         out_specs=[whole()] * (4 + SLOTS),
+        scratch_shapes=[pltpu.VMEM((2, ROWS, FB), jnp.float32)],
         compiler_params=pltpu.CompilerParams(vmem_limit_bytes=VMEM),
         cost_estimate=pl.CostEstimate(flops=10**6, bytes_accessed=10**6, transcendentals=0),
         name="prepare_tables",
@@ -213,7 +224,7 @@
 def bins_kernel(parts, last, *refs):
     count = len(parts)
     pieces, refs = refs[:count], refs[count:]
-    bin_ref, table_ref, turn_ref, wide_ref, phase_ref = refs[:5]
+    bin_ref, table_ref, turn_ref, wide_ref, turned_ref = refs[:5]
     refs = refs[5:]
     if last:
         stat_ref, refs = refs[0], refs[1:]
@@ -221,31 +232,18 @@
     binned, refs = refs[:SLOTS], refs[SLOTS:]
     if last:
         out_ref, refs = refs[0], refs[1:]
-    prod_ref, rot_ref, step_ref = refs[:3]
+    prod_ref = refs[0]
     if last:
-        best_ref = refs[3]
-
-    lane = lax.broadcasted_iota(jnp.int32, (ROWS, LANES), 1)
-
-    def at_lane(part, place):
-        return jnp.sum(jnp.where(lane == place, phase_ref[part, :, FB:], 0.0), axis=1, keepdims=True)
-
-    for part in range(2):
-        step_ref[part] = jnp.broadcast_to(at_lane(part, NSL), (ROWS, TW))
+        best_ref = refs[1]
 
     def product(piece_ref, which, c, jj):
         j = c * JS + jj
         both = piece_ref[which, jj].astype(jnp.float32)
         raw_r, raw_i = both[:ROWS], both[ROWS:]
-        rc, rs = rot_ref[0], rot_ref[1]
+        rc, rs = turned_ref[j, 0], turned_ref[j, 1]
         sr = raw_r * rc - raw_i * rs
         si = raw_r * rs + raw_i * rc
         su = sr + si
-        if jj < JS - 1:
-            pc = jnp.concatenate([step_ref[0], step_ref[0]], axis=1)
-            ps = jnp.concatenate([step_ref[1], step_ref[1]], axis=1)
-            rot_ref[0] = rc * pc - rs * ps
-            rot_ref[1] = rc * ps + rs * pc
         for pair in range(SLOTS // 2):
             real, imag = [], []
             for k in (2 * pair, 2 * pair + 1):
@@ -273,13 +271,9 @@
     for piece_ref, (first, amount, other) in zip(pieces, parts):
         for which in range(amount):
             c = slice_of(first + which, other)
-            sc, ss = at_lane(0, c), at_lane(1, c)
             slot_lane = lax.broadcasted_iota(jnp.int32, (SLOTS, LANES), 1)
             packed = jnp.sum(jnp.where(slot_lane == c, bin_ref[...], 0.0), axis=1, keepdims=True).astype(jnp.int32)
             digits = [packed[k, 0] for k in range(SLOTS)]
-            lc, ls = phase_ref[0, :, :FB], phase_ref[1, :, :FB]
-            rot_ref[0] = sc * lc - ss * ls
-            rot_ref[1] = sc * ls + ss * lc
             for jj in range(JS):
                 product(piece_ref, which, c, jj)
             half = JS // 2
@@ -326,8 +320,6 @@
     out_shape = list(BINNED)
     scratch = [
         pltpu.VMEM((JS * SLOTS * ROWS, 2 * FB), jnp.bfloat16),
-        pltpu.VMEM((2, ROWS, FB), jnp.float32),
-        pltpu.VMEM((2, ROWS, TW), jnp.float32),
     ]
     if last:
         out_shape.append(jax.ShapeDtypeStruct((SEGS, NWIN), jnp.float32))
@@ -378,13 +370,16 @@
     q1 = to_core(p1)
     p01 = jnp.concatenate([p0, p1], axis=0)
     p23 = swap_with(p01, step_move(1))
-    binned = add_bins((p1, q1), ((1, 1, 0), (1, 1, 1)), shared, binned)
+    binned = add_bins((p1,), ((1, 1, 0),), shared, binned)
     p23, binned = after(p23, binned)
-    q23 = to_core(p23)
     p01, p23 = lax.optimization_barrier((p01, p23))
     p45 = swap_with(p01, step_move(2))
     p67 = swap_with(p23, step_move(2))
-    binned = add_bins((p23, q23), ((2, 2, 0), (2, 2, 1)), shared, binned)
+    binned = add_bins((p23,), ((2, 2, 0),), shared, binned)
+    p23, binned = after(p23, binned)
+    q23 = to_core(p23)
+    binned = add_bins((q1,), ((1, 1, 1),), shared, binned)
+    binned = add_bins((q23,), ((2, 2, 1),), shared, binned)
     p45, binned = after(p45, binned)
     q45 = to_core(p45)
     binned = add_bins((p45,), ((4, 2, 0),), shared, binned)

time: 63.2 us -> 63 us (level)
    pallas_call x1, Pallas kernels: 0.71 us -> 2.03 us  [prepare_tables(): pl.pallas_call(tables_kernel, out_shape=[jax.ShapeDtypeStruct((SLOTS, LAN...]
    pallas_call x7 -> x9, Pallas kernels: 14.9 us -> 14 us  [add_bins(): pl.pallas_call(functools.partial(bins_kernel, parts, last), out_shape=out...]
  transfers between devices with their start and end apart: 17 -> 17, of which waited for: 10 -> 10; matrix products, arithmetic and copies ran while one was open for 1% -> 1% of each run, Pallas kernels for 23% -> 21%
where the time goes in v9:
time: 63 us; the launch traced here: 62.8 us
  starting transfers between devices  21.3 us (34%)
  waiting for transfers between devices  19.4 us (31%)
  Pallas kernels  17.7 us (28%)
  local copies, waits for them, and re-layouts  2.12 us (3%)
  other arithmetic  1.51 us (2%)
  between operations  0.75 us (1%)
    ppermute x17, starting transfers between devices, swap_with(): return lax.ppermute(value, AXES, pairs)  21.3 us
    ppermute x17, waiting for transfers between devices, swap_with(): return lax.ppermute(value, AXES, pairs)  19.4 us
    pallas_call x9, Pallas kernels, add_bins(): pl.pallas_call(functools.partial(bins_kernel, parts, last), out_shape=out...  14 us
    pallas_call x1, Pallas kernels, prepare_tables(): pl.pallas_call(tables_kernel, out_shape=[jax.ShapeDtypeStruct((SLOTS, LAN...  2.03 us
    unnamed x3, local copies, waits for them, and re-layouts  2 us
    pallas_call x1, Pallas kernels, prepare_templates(): pl.pallas_call(templates_kernel, out_shape=[jax.ShapeDtypeStruct((SLOTS,...  1.66 us
  transfers between devices with their start and end apart: 17, of which 10 were waited for; matrix products, arithmetic and copies ran while one was open for 1% of the time, Pallas kernels for 21%

profile of v9, /device:TPU:0, one launch (start us, length us, event | category | flops | bytes accessed | tf_op | source)
XLA Modules:
  0.0 62.8 jit_solution(4745832595595912465)
XLA Ops:
  0.0 0.7 %copy.121 = bf16[1,3,2,6,256]{4,3,1,2,0:T(8,128)(2,1)S(1)} copy(bf16[1,3,2,6,256]{4,2,3,1,0:T(2,128)(2,1)} %param.5) | data formatting | bytes 36864 | tf_op args[0]
  0.7 2.8 %collective-permute-start.2 = (bf16[6,6,1,256]{3,0,1,2:T(8,128)(2,1)S(1)}, bf16[6,6,1,256]{3,0,1,2:T(8,128)(2,1)S(1)}, u32[]{:S(2)}, u32[]{:S(2)}) collective-permute-start(bf16[6,6,1,256]{3,0,1,2:T(8,128)(2,1)S(1)} %bitcast.21), channel_id=1, source_target_pairs={{0,96},{1,97},{2,98},{3,99},{4,100},{5,101},{6,102},{7,103},{8,104... | collective-permute-start | bytes 55304 | tf_op jit(solution)/shard_map/ppermute | solution.py:50
  3.6 0.8 %collective-permute-start.1 = (bf16[6,6,1,256]{3,0,1,2:T(8,128)(2,1)S(1)}, bf16[6,6,1,256]{3,0,1,2:T(8,128)(2,1)S(1)}, u32[]{:S(2)}, u32[]{:S(2)}) collective-permute-start(bf16[6,6,1,256]{3,0,1,2:T(8,128)(2,1)S(1)} %bitcast.22), channel_id=1, source_target_pairs={{0,64},{1,65},{2,66},{3,67},{4,68},{5,69},{6,70},{7,71},{8,72},{9,... | collective-permute-start | bytes 55304 | tf_op jit(solution)/shard_map/ppermute | solution.py:50
  4.4 0.5 collective-permute-start
  5.5 0.1 pad.16.clone
  5.5 0.8 %fusion.small_ref = s32[16,128]{1,0:T(8,128)S(1)} fusion(s32[3,8]{1,0:T(4,128)} %bitcast.25, s32[12,15]{1,0:T(8,128)} %param.8, s32[16]{0:T(128)S(1)} %pad.16.clone), kind=kLoop, calls=%fused_computation.8 | loop fusion | flops 8192 | bytes 9072 | tf_op jit(solution)/shard_map/concatenate | solution.py:182
  6.3 2.0 %prepare_tables.1 = (f32[12,128]{1,0:T(8,128)S(1)}, f32[96,2,24,256]{3,2,1,0:T(8,128)S(1)}, bf16[512,256]{1,0:T(8,128)(2,1)S(1)}, f32[2,16,8,128]{3,2,1,0:T(8,12...) custom-call(s32[16,128]{1,0:T(8,128)S(1)} %fusion.small_ref), custom_call_target="tpu_custom_call" | custom-call | flops 1000000 | bytes 1000000 | tf_op jit(solution)/shard_map/prepare_tables/pallas_call | solution.py:190
  8.4 0.0 collective-permute-done.2
  8.4 0.5 collective-permute-done.1
  8.9 0.0 collective-permute-done
  8.9 1.7 %collective-permute-start.3 = (bf16[6,6,4,256]{3,0,1,2:T(8,128)(2,1)S(1)}, bf16[6,6,4,256]{3,0,1,2:T(8,128)(2,1)S(1)}, u32[]{:S(2)}, u32[]{:S(2)}) collective-permute-start(bf16[6,6,4,256]{3,0,1,2:T(8,128)(2,1)S(1)} %pad_maximum_fusion.2), channel_id=1, source_target_pairs={{0,16},{1,17},{2,18},{3,19},{4,20},{5,21},{6,22},{7,23},{8,24},{9,... | collective-permute-start | bytes 221192 | tf_op jit(solution)/shard_map/ppermute | solution.py:50
  10.6 1.3 %copy-done = bf16[12,2,96,256]{3,2,1,0:T(8,128)(2,1)S(1)} copy-done((bf16[12,2,96,256]{3,2,1,0:T(8,128)(2,1)S(1)}, bf16[12,2,96,256]{3,2,1,0:T(8,128)(2,1)}, u32[]{:S(2)}) %copy-start) | copy-done | bytes 1179672
  11.9 1.7 %prepare_templates.1 = (f32[12,3,96,256]{3,2,1,0:T(8,128)S(1)}, f32[12,40,128]{2,1,0:T(8,128)S(1)}) custom-call(bf16[12,2,96,256]{3,2,1,0:T(8,128)(2,1)S(1)} %copy-done, s32[16,128]{1,0:T(8,128)S(1)} %fusion.small_ref), custom_call_target="tpu_custom_call" | custom-call | flops 1000000 | bytes 1000000 | tf_op jit(solution)/shard_map/prepare_templates/pallas_call | solution.py:209
  13.5 0.1 collective-permute-done.3
  13.8 0.1 collective-permute-start.5
  13.9 3.1 %collective-permute-start.4 = (bf16[1,6,48,256]{3,2,1,0:T(8,128)(2,1)S(1)}, bf16[1,6,48,256]{3,2,1,0:T(8,128)(2,1)S(1)}, u32[]{:S(2)}, u32[]{:S(2)}) collective-permute-start(bf16[1,6,48,256]{3,2,1,0:T(8,128)(2,1)S(1)} %bitcast.18), channel_id=1, source_target_pairs={{0,24},{1,3},{2,26},{3,1},{4,28},{5,7},{6,30},{7,5},{8,16},{9,11},... | collective-permute-start | bytes 442376 | tf_op jit(solution)/shard_map/ppermute | solution.py:50
  17.0 0.0 collective-permute-done.5.refs_1_
  17.0 1.6 %add_bins.8 = (f32[16,24,256]{2,1,0:T(8,128)S(1)}, f32[16,24,256]{2,1,0:T(8,128)S(1)}, f32[16,24,256]{2,1,0:T(8,128)S(1)}, f32[16,24,256]{2,1,0:T(8,128)S(1)}, f...) custom-call(bf16[1,6,48,256]{3,2,1,0:T(8,128)(2,1)S(1)} %bitcast.19,, ...), custom_call_target="tpu_custom_call", output_to_operand_aliasing={{0}: (7, {}), {1}: (8, {}), {2}: (9, {}), {3}: (10, {}), {4... | custom-call | flops 1811939328 | bytes 1000000 | tf_op jit(solution)/shard_map/add_bins/pallas_call | solution.py:328
  18.6 1.7 %collective-permute-done.4.refs_0_ = bf16[1,6,48,256]{3,2,1,0:T(8,128)(2,1)S(1)} collective-permute-done((bf16[1,6,48,256]{3,2,1,0:T(8,128)(2,1)S(1)}, bf16[1,6,48,256]{3,2,1,0:T(8,128)(2,1)S(1)}, u32[]{:S(2)}, u32[]{:S(2)}) %collective-permute-start.4) | collective-permute-done | bytes 147488 | tf_op jit(solution)/shard_map/ppermute | solution.py:50
  20.3 2.0 %collective-permute-start.6 = (bf16[2,6,48,256]{3,2,1,0:T(8,128)(2,1)S(1)}, bf16[2,6,48,256]{3,2,1,0:T(8,128)(2,1)S(1)}, u32[]{:S(2)}, u32[]{:S(2)}) collective-permute-start(bf16[2,6,48,256]{3,2,1,0:T(8,128)(2,1)S(1)} %pad_maximum_fusion), channel_id=1, source_target_pairs={{0,2},{1,7},{2,0},{3,5},{4,6},{5,3},{6,4},{7,1},{8,10},{9,15},{10,... | collective-permute-start | bytes 884744 | tf_op jit(solution)/shard_map/ppermute | solution.py:50
  22.3 0.8 %add_bins.9 = (f32[16,24,256]{2,1,0:T(8,128)S(1)}, f32[16,24,256]{2,1,0:T(8,128)S(1)}, f32[16,24,256]{2,1,0:T(8,128)S(1)}, f32[16,24,256]{2,1,0:T(8,128)S(1)}, f...) custom-call(bf16[1,6,48,256]{3,2,1,0:T(8,128)(2,1)S(1)} %collective-, ...), custom_call_target="tpu_custom_call", output_to_operand_aliasing={{0}: (6, {}), {1}: (7, {}), {2}: (8, {}), {3}: (9, {}), {4}... | custom-call | flops 905969664 | bytes 1000000 | tf_op jit(solution)/shard_map/add_bins/pallas_call | solution.py:328
  23.1 4.0 %collective-permute-done.6.refs_0_ = bf16[2,6,48,256]{3,2,1,0:T(8,128)(2,1)S(1)} collective-permute-done((bf16[2,6,48,256]{3,2,1,0:T(8,128)(2,1)S(1)}, bf16[2,6,48,256]{3,2,1,0:T(8,128)(2,1)S(1)}, u32[]{:S(2)}, u32[]{:S(2)}) %collective-permute-start.6) | collective-permute-done | bytes 294944 | tf_op jit(solution)/shard_map/ppermute | solution.py:50
  27.1 1.6 %add_bins.10 = (f32[16,24,256]{2,1,0:T(8,128)S(1)}, f32[16,24,256]{2,1,0:T(8,128)S(1)}, f32[16,24,256]{2,1,0:T(8,128)S(1)}, f32[16,24,256]{2,1,0:T(8,128)S(1)}, ...) custom-call(bf16[2,6,48,256]{3,2,1,0:T(8,128)(2,1)S(1)} %collective-, ...), custom_call_target="tpu_custom_call", output_to_operand_aliasing={{0}: (6, {}), {1}: (7, {}), {2}: (8, {}), {3}: (9, {}), {4}... | custom-call | flops 1811939328 | bytes 1000000 | tf_op jit(solution)/shard_map/add_bins/pallas_call | solution.py:328
  28.7 0.1 collective-permute-start.9
  28.8 0.5 collective-permute-start.10
  29.3 4.0 %collective-permute-start.8 = (bf16[2,6,48,256]{3,2,1,0:T(8,128)(2,1)S(1)}, bf16[2,6,48,256]{3,2,1,0:T(8,128)(2,1)S(1)}, u32[]{:S(2)}, u32[]{:S(2)}) collective-permute-start(bf16[2,6,48,256]{3,2,1,0:T(8,128)(2,1)S(1)} %pad_maximum_fusion), channel_id=1, source_target_pairs={{0,6},{1,25},{2,4},{3,27},{4,2},{5,29},{6,0},{7,31},{8,14},{9,17},... | collective-permute-start | bytes 884744 | tf_op jit(solution)/shard_map/ppermute | solution.py:50
  33.3 0.0 collective-permute-start.7
  33.4 0.8 %add_bins.11 = (f32[16,24,256]{2,1,0:T(8,128)S(1)}, f32[16,24,256]{2,1,0:T(8,128)S(1)}, f32[16,24,256]{2,1,0:T(8,128)S(1)}, f32[16,24,256]{2,1,0:T(8,128)S(1)}, ...) custom-call(bf16[1,6,48,256]{3,2,1,0:T(8,128)(2,1)S(1)} %collective-, ...), custom_call_target="tpu_custom_call", output_to_operand_aliasing={{0}: (6, {}), {1}: (7, {}), {2}: (8, {}), {3}: (9, {}), {4}... | custom-call | flops 905969664 | bytes 1000000 | tf_op jit(solution)/shard_map/add_bins/pallas_call | solution.py:328
  34.2 0.0 collective-permute-done.9.refs_0_
  34.2 1.6 %add_bins.12 = (f32[16,24,256]{2,1,0:T(8,128)S(1)}, f32[16,24,256]{2,1,0:T(8,128)S(1)}, f32[16,24,256]{2,1,0:T(8,128)S(1)}, f32[16,24,256]{2,1,0:T(8,128)S(1)}, ...) custom-call(bf16[2,6,48,256]{3,2,1,0:T(8,128)(2,1)S(1)} %collective-, ...), custom_call_target="tpu_custom_call", output_to_operand_aliasing={{0}: (6, {}), {1}: (7, {}), {2}: (8, {}), {3}: (9, {}), {4}... | custom-call | flops 1811939328 | bytes 1000000 | tf_op jit(solution)/shard_map/add_bins/pallas_call | solution.py:328
  35.8 2.2 %collective-permute-done.8.refs_0_ = bf16[2,6,48,256]{3,2,1,0:T(8,128)(2,1)S(1)} collective-permute-done((bf16[2,6,48,256]{3,2,1,0:T(8,128)(2,1)S(1)}, bf16[2,6,48,256]{3,2,1,0:T(8,128)(2,1)S(1)}, u32[]{:S(2)}, u32[]{:S(2)}) %collective-permute-start.8) | collective-permute-done | bytes 294944 | tf_op jit(solution)/shard_map/ppermute | solution.py:50
  38.0 0.0 collective-permute-start.12
  38.0 1.6 %add_bins.13 = (f32[16,24,256]{2,1,0:T(8,128)S(1)}, f32[16,24,256]{2,1,0:T(8,128)S(1)}, f32[16,24,256]{2,1,0:T(8,128)S(1)}, f32[16,24,256]{2,1,0:T(8,128)S(1)}, ...) custom-call(bf16[2,6,48,256]{3,2,1,0:T(8,128)(2,1)S(1)} %collective-, ...), custom_call_target="tpu_custom_call", output_to_operand_aliasing={{0}: (6, {}), {1}: (7, {}), {2}: (8, {}), {3}: (9, {}), {4}... | custom-call | flops 1811939328 | bytes 1000000 | tf_op jit(solution)/shard_map/add_bins/pallas_call | solution.py:328
  39.6 1.6 %collective-permute-done.7.refs_0_ = bf16[2,6,48,256]{3,2,1,0:T(8,128)(2,1)S(1)} collective-permute-done((bf16[2,6,48,256]{3,2,1,0:T(8,128)(2,1)S(1)}, bf16[2,6,48,256]{3,2,1,0:T(8,128)(2,1)S(1)}, u32[]{:S(2)}, u32[]{:S(2)}) %collective-permute-start.7) | collective-permute-done | bytes 294944 | tf_op jit(solution)/shard_map/ppermute | solution.py:50
  41.3 0.0 collective-permute-start.11
  41.3 0.0 collective-permute-done.12.refs_0_
  41.3 1.6 %add_bins.14 = (f32[16,24,256]{2,1,0:T(8,128)S(1)}, f32[16,24,256]{2,1,0:T(8,128)S(1)}, f32[16,24,256]{2,1,0:T(8,128)S(1)}, f32[16,24,256]{2,1,0:T(8,128)S(1)}, ...) custom-call(bf16[2,6,48,256]{3,2,1,0:T(8,128)(2,1)S(1)} %collective-, ...), custom_call_target="tpu_custom_call", output_to_operand_aliasing={{0}: (6, {}), {1}: (7, {}), {2}: (8, {}), {3}: (9, {}), {4}... | custom-call | flops 1811939328 | bytes 1000000 | tf_op jit(solution)/shard_map/add_bins/pallas_call | solution.py:328
  42.9 1.6 %add_bins.15 = (f32[16,24,256]{2,1,0:T(8,128)S(1)}, f32[16,24,256]{2,1,0:T(8,128)S(1)}, f32[16,24,256]{2,1,0:T(8,128)S(1)}, f32[16,24,256]{2,1,0:T(8,128)S(1)}, ...) custom-call(bf16[2,6,48,256]{3,2,1,0:T(8,128)(2,1)S(1)} %collective-, ...), custom_call_target="tpu_custom_call", output_to_operand_aliasing={{0}: (6, {}), {1}: (7, {}), {2}: (8, {}), {3}: (9, {}), {4}... | custom-call | flops 1811939328 | bytes 1000000 | tf_op jit(solution)/shard_map/add_bins/pallas_call | solution.py:328
  44.5 0.0 collective-permute-done.11.refs_0_
  44.5 2.7 %last_bins.1 = (f32[16,24,256]{2,1,0:T(8,128)S(1)}, f32[16,24,256]{2,1,0:T(8,128)S(1)}, f32[16,24,256]{2,1,0:T(8,128)S(1)}, f32[16,24,256]{2,1,0:T(8,128)S(1)}, ...) custom-call(bf16[2,6,48,256]{3,2,1,0:T(8,128)(2,1)S(1)} %collective-, ...), custom_call_target="tpu_custom_call", output_to_operand_aliasing={{0}: (7, {}), {1}: (8, {}), {2}: (9, {}), {3}: (10, {}), {4... | custom-call | flops 1811939328 | bytes 1000000 | tf_op jit(solution)/shard_map/last_bins/pallas_call | solution.py:328
  47.2 0.6 collective-permute-start.13
  47.8 0.8 %collective-permute-done.13 = f32[8,8]{1,0:T(8,128)S(1)} collective-permute-done((f32[8,8]{1,0:T(8,128)S(1)}, f32[8,8]{1,0:T(8,128)S(1)}, u32[]{:S(2)}, u32[]{:S(2)}) %collective-permute-start.13) | collective-permute-done | bytes 288 | tf_op jit(solution)/shard_map/ppermute | solution.py:50
  48.6 3.6 %collective-permute-done.14 = f32[8,8]{1,0:T(8,128)S(1)} collective-permute-done((f32[8,8]{1,0:T(8,128)S(1)}, f32[8,8]{1,0:T(8,128)S(1)}, u32[]{:S(2)}, u32[]{:S(2)}) %collective-permute-start.14) | collective-permute-done | bytes 288 | tf_op jit(solution)/shard_map/ppermute | solution.py:50
  52.3 3.2 %collective-permute-start.15 = (f32[8,8]{1,0:T(8,128)S(1)}, f32[8,8]{1,0:T(8,128)S(1)}, u32[]{:S(2)}, u32[]{:S(2)}) collective-permute-start(f32[8,8]{1,0:T(8,128)S(1)} %max.13), channel_id=1, source_target_pairs={{0,6},{1,7},{2,4},{3,5},{4,2},{5,3},{6,0},{7,1},{8,14},{9,15},{10,... | collective-permute-start | bytes 776 | tf_op jit(solution)/shard_map/ppermute | solution.py:50
  55.5 1.6 %collective-permute-done.15 = f32[8,8]{1,0:T(8,128)S(1)} collective-permute-done((f32[8,8]{1,0:T(8,128)S(1)}, f32[8,8]{1,0:T(8,128)S(1)}, u32[]{:S(2)}, u32[]{:S(2)}) %collective-permute-start.15) | collective-permute-done | bytes 288 | tf_op jit(solution)/shard_map/ppermute | solution.py:50
  57.1 2.0 %collective-permute-start.16 = (f32[8,8]{1,0:T(8,128)S(1)}, f32[8,8]{1,0:T(8,128)S(1)}, u32[]{:S(2)}, u32[]{:S(2)}) collective-permute-start(f32[8,8]{1,0:T(8,128)S(1)} %max.14), channel_id=1, source_target_pairs={{0,8},{1,9},{2,10},{3,11},{4,12},{5,13},{6,14},{7,15},{8,0},{9,1},... | collective-permute-start | bytes 776 | tf_op jit(solution)/shard_map/ppermute | solution.py:50
  59.1 3.1 %collective-permute-done.16 = f32[8,8]{1,0:T(8,128)S(1)} collective-permute-done((f32[8,8]{1,0:T(8,128)S(1)}, f32[8,8]{1,0:T(8,128)S(1)}, u32[]{:S(2)}, u32[]{:S(2)}) %collective-permute-start.16) | collective-permute-done | bytes 288 | tf_op jit(solution)/shard_map/ppermute | solution.py:50
  62.2 0.6 max.15
  (11 shorter events, 0.2 us)
Async XLA Ops:
  0.7 7.6 %collective-permute-start.2 = (bf16[6,6,1,256]{3,0,1,2:T(8,128)(2,1)S(1)}, bf16[6,6,1,256]{3,0,1,2:T(8,128)(2,1)S(1)}, u32[]{:S(2)}, u32[]{:S(2)}) collective-permute-start(bf16[6,6,1,256]{3,0,1,2:T(8,128)(2,1)S(1)} %bitcast.21), channel_id=1, source_target_pairs={{0,96},{1,97},{2,98},{3,99},{4,100},{5,101},{6,102},{7,103},{8,104... | collective-permute-start | bytes 55304 | tf_op jit(solution)/shard_map/ppermute | solution.py:50
  3.6 5.3 %collective-permute-start.1 = (bf16[6,6,1,256]{3,0,1,2:T(8,128)(2,1)S(1)}, bf16[6,6,1,256]{3,0,1,2:T(8,128)(2,1)S(1)}, u32[]{:S(2)}, u32[]{:S(2)}) collective-permute-start(bf16[6,6,1,256]{3,0,1,2:T(8,128)(2,1)S(1)} %bitcast.22), channel_id=1, source_target_pairs={{0,64},{1,65},{2,66},{3,67},{4,68},{5,69},{6,70},{7,71},{8,72},{9,... | collective-permute-start | bytes 55304 | tf_op jit(solution)/shard_map/ppermute | solution.py:50
  4.4 4.5 %collective-permute-start = (bf16[6,6,1,256]{3,0,1,2:T(8,128)(2,1)S(1)}, bf16[6,6,1,256]{3,0,1,2:T(8,128)(2,1)S(1)}, u32[]{:S(2)}, u32[]{:S(2)}) collective-permute-start(bf16[6,6,1,256]{3,0,1,2:T(8,128)(2,1)S(1)} %bitcast.23), channel_id=1, source_target_pairs={{0,32},{1,33},{2,34},{3,35},{4,36},{5,37},{6,38},{7,39},{8,40},{9,... | collective-permute-start | bytes 55304 | tf_op jit(solution)/shard_map/ppermute | solution.py:50
  8.9 4.7 %collective-permute-start.3 = (bf16[6,6,4,256]{3,0,1,2:T(8,128)(2,1)S(1)}, bf16[6,6,4,256]{3,0,1,2:T(8,128)(2,1)S(1)}, u32[]{:S(2)}, u32[]{:S(2)}) collective-permute-start(bf16[6,6,4,256]{3,0,1,2:T(8,128)(2,1)S(1)} %pad_maximum_fusion.2), channel_id=1, source_target_pairs={{0,16},{1,17},{2,18},{3,19},{4,20},{5,21},{6,22},{7,23},{8,24},{9,... | collective-permute-start | bytes 221192 | tf_op jit(solution)/shard_map/ppermute | solution.py:50
  10.6 1.3 %copy-start = (bf16[12,2,96,256]{3,2,1,0:T(8,128)(2,1)S(1)}, bf16[12,2,96,256]{3,2,1,0:T(8,128)(2,1)}, u32[]{:S(2)}) copy-start(bf16[12,2,96,256]{3,2,1,0:T(8,128)(2,1)} %templ_ref.1) | copy-start | bytes 3538948
  13.8 3.2 %collective-permute-start.5 = (bf16[1,6,48,256]{3,2,1,0:T(8,128)(2,1)S(1)}, bf16[1,6,48,256]{3,2,1,0:T(8,128)(2,1)S(1)}, u32[]{:S(2)}, u32[]{:S(2)}) collective-permute-start(bf16[1,6,48,256]{3,2,1,0:T(8,128)(2,1)S(1)} %bitcast.17), channel_id=1, source_target_pairs={{0,1},{1,0},{2,3},{3,2},{4,5},{5,4},{6,7},{7,6},{8,9},{9,8},{10,11... | collective-permute-start | bytes 442376 | tf_op jit(solution)/shard_map/ppermute | solution.py:50
  13.9 6.4 %collective-permute-start.4 = (bf16[1,6,48,256]{3,2,1,0:T(8,128)(2,1)S(1)}, bf16[1,6,48,256]{3,2,1,0:T(8,128)(2,1)S(1)}, u32[]{:S(2)}, u32[]{:S(2)}) collective-permute-start(bf16[1,6,48,256]{3,2,1,0:T(8,128)(2,1)S(1)} %bitcast.18), channel_id=1, source_target_pairs={{0,24},{1,3},{2,26},{3,1},{4,28},{5,7},{6,30},{7,5},{8,16},{9,11},... | collective-permute-start | bytes 442376 | tf_op jit(solution)/shard_map/ppermute | solution.py:50
  20.3 6.8 %collective-permute-start.6 = (bf16[2,6,48,256]{3,2,1,0:T(8,128)(2,1)S(1)}, bf16[2,6,48,256]{3,2,1,0:T(8,128)(2,1)S(1)}, u32[]{:S(2)}, u32[]{:S(2)}) collective-permute-start(bf16[2,6,48,256]{3,2,1,0:T(8,128)(2,1)S(1)} %pad_maximum_fusion), channel_id=1, source_target_pairs={{0,2},{1,7},{2,0},{3,5},{4,6},{5,3},{6,4},{7,1},{8,10},{9,15},{10,... | collective-permute-start | bytes 884744 | tf_op jit(solution)/shard_map/ppermute | solution.py:50
  28.7 5.5 %collective-permute-start.9 = (bf16[2,6,48,256]{3,2,1,0:T(8,128)(2,1)S(1)}, bf16[2,6,48,256]{3,2,1,0:T(8,128)(2,1)S(1)}, u32[]{:S(2)}, u32[]{:S(2)}) collective-permute-start(bf16[2,6,48,256]{3,2,1,0:T(8,128)(2,1)S(1)} %collective-permute-done.6.refs_0_), channel_id=1, source_target_pairs={{0,1},{1,0},{2,3},{3,2},{4,5},{5,4},{6,7},{7,6},{8,9},{9,8},{10,11... | collective-permute-start | bytes 884744 | tf_op jit(solution)/shard_map/ppermute | solution.py:50
  28.8 4.5 %collective-permute-start.10 = (bf16[1,6,48,256]{3,2,1,0:T(8,128)(2,1)S(1)}, bf16[1,6,48,256]{3,2,1,0:T(8,128)(2,1)S(1)}, u32[]{:S(2)}, u32[]{:S(2)}) collective-permute-start(bf16[1,6,48,256]{3,2,1,0:T(8,128)(2,1)S(1)} %collective-permute-done.4.refs_0_), channel_id=1, source_target_pairs={{0,1},{1,0},{2,3},{3,2},{4,5},{5,4},{6,7},{7,6},{8,9},{9,8},{10,11... | collective-permute-start | bytes 442376 | tf_op jit(solution)/shard_map/ppermute | solution.py:50
  29.3 8.7 %collective-permute-start.8 = (bf16[2,6,48,256]{3,2,1,0:T(8,128)(2,1)S(1)}, bf16[2,6,48,256]{3,2,1,0:T(8,128)(2,1)S(1)}, u32[]{:S(2)}, u32[]{:S(2)}) collective-permute-start(bf16[2,6,48,256]{3,2,1,0:T(8,128)(2,1)S(1)} %pad_maximum_fusion), channel_id=1, source_target_pairs={{0,6},{1,25},{2,4},{3,27},{4,2},{5,29},{6,0},{7,31},{8,14},{9,17},... | collective-permute-start | bytes 884744 | tf_op jit(solution)/shard_map/ppermute | solution.py:50
  33.3 7.9 %collective-permute-start.7 = (bf16[2,6,48,256]{3,2,1,0:T(8,128)(2,1)S(1)}, bf16[2,6,48,256]{3,2,1,0:T(8,128)(2,1)S(1)}, u32[]{:S(2)}, u32[]{:S(2)}) collective-permute-start(bf16[2,6,48,256]{3,2,1,0:T(8,128)(2,1)S(1)} %collective-permute-done.6.refs_0_), channel_id=1, source_target_pairs={{0,6},{1,25},{2,4},{3,27},{4,2},{5,29},{6,0},{7,31},{8,14},{9,17},... | collective-permute-start | bytes 884744 | tf_op jit(solution)/shard_map/ppermute | solution.py:50
  38.0 3.2 %collective-permute-start.12 = (bf16[2,6,48,256]{3,2,1,0:T(8,128)(2,1)S(1)}, bf16[2,6,48,256]{3,2,1,0:T(8,128)(2,1)S(1)}, u32[]{:S(2)}, u32[]{:S(2)}) collective-permute-start(bf16[2,6,48,256]{3,2,1,0:T(8,128)(2,1)S(1)} %collective-permute-done.8.refs_0_), channel_id=1, source_target_pairs={{0,1},{1,0},{2,3},{3,2},{4,5},{5,4},{6,7},{7,6},{8,9},{9,8},{10,11... | collective-permute-start | bytes 884744 | tf_op jit(solution)/shard_map/ppermute | solution.py:50
  41.3 3.2 %collective-permute-start.11 = (bf16[2,6,48,256]{3,2,1,0:T(8,128)(2,1)S(1)}, bf16[2,6,48,256]{3,2,1,0:T(8,128)(2,1)S(1)}, u32[]{:S(2)}, u32[]{:S(2)}) collective-permute-start(bf16[2,6,48,256]{3,2,1,0:T(8,128)(2,1)S(1)} %collective-permute-done.7.refs_0_), channel_id=1, source_target_pairs={{0,1},{1,0},{2,3},{3,2},{4,5},{5,4},{6,7},{7,6},{8,9},{9,8},{10,11... | collective-permute-start | bytes 884744 | tf_op jit(solution)/shard_map/ppermute | solution.py:50
  47.2 1.4 %collective-permute-start.13 = (f32[8,8]{1,0:T(8,128)S(1)}, f32[8,8]{1,0:T(8,128)S(1)}, u32[]{:S(2)}, u32[]{:S(2)}) collective-permute-start(f32[8,8]{1,0:T(8,128)S(1)} %get-tuple-element.272), channel_id=1, source_target_pairs={{0,1},{1,0},{2,3},{3,2},{4,5},{5,4},{6,7},{7,6},{8,9},{9,8},{10,11... | collective-permute-start | bytes 776 | tf_op jit(solution)/shard_map/ppermute | solution.py:50
  48.6 3.6 %collective-permute-start.14 = (f32[8,8]{1,0:T(8,128)S(1)}, f32[8,8]{1,0:T(8,128)S(1)}, u32[]{:S(2)}, u32[]{:S(2)}) collective-permute-start(f32[8,8]{1,0:T(8,128)S(1)} %max.12), channel_id=1, source_target_pairs={{0,2},{1,3},{2,0},{3,1},{4,6},{5,7},{6,4},{7,5},{8,10},{9,11},{10,... | collective-permute-start | bytes 776 | tf_op jit(solution)/shard_map/ppermute | solution.py:50
  52.3 4.8 %collective-permute-start.15 = (f32[8,8]{1,0:T(8,128)S(1)}, f32[8,8]{1,0:T(8,128)S(1)}, u32[]{:S(2)}, u32[]{:S(2)}) collective-permute-start(f32[8,8]{1,0:T(8,128)S(1)} %max.13), channel_id=1, source_target_pairs={{0,6},{1,7},{2,4},{3,5},{4,2},{5,3},{6,0},{7,1},{8,14},{9,15},{10,... | collective-permute-start | bytes 776 | tf_op jit(solution)/shard_map/ppermute | solution.py:50
  57.1 5.1 %collective-permute-start.16 = (f32[8,8]{1,0:T(8,128)S(1)}, f32[8,8]{1,0:T(8,128)S(1)}, u32[]{:S(2)}, u32[]{:S(2)}) collective-permute-start(f32[8,8]{1,0:T(8,128)S(1)} %max.14), channel_id=1, source_target_pairs={{0,8},{1,9},{2,10},{3,11},{4,12},{5,13},{6,14},{7,15},{8,0},{9,1},... | collective-permute-start | bytes 776 | tf_op jit(solution)/shard_map/ppermute | solution.py:50

commit v10 on v9

--- a/solution.py
+++ b/solution.py
@@ -365,27 +365,21 @@
     p0 = x.reshape(1, JS, 2 * ROWS, FB)
     q0 = to_core(p0)
     p1 = swap_with(p0, step_move(0))
+    p2 = swap_with(p0, step_move(1))
     binned = add_bins((p0, q0), ((0, 1, 0), (0, 1, 1)), shared, binned)
-    p1, binned = after(p1, binned)
-    q1 = to_core(p1)
-    p01 = jnp.concatenate([p0, p1], axis=0)
-    p23 = swap_with(p01, step_move(1))
-    binned = add_bins((p1,), ((1, 1, 0),), shared, binned)
-    p23, binned = after(p23, binned)
-    p01, p23 = lax.optimization_barrier((p01, p23))
-    p45 = swap_with(p01, step_move(2))
-    p67 = swap_with(p23, step_move(2))
-    binned = add_bins((p23,), ((2, 2, 0),), shared, binned)
-    p23, binned = after(p23, binned)
-    q23 = to_core(p23)
-    binned = add_bins((q1,), ((1, 1, 1),), shared, binned)
-    binned = add_bins((q23,), ((2, 2, 1),), shared, binned)
-    p45, binned = after(p45, binned)
-    q45 = to_core(p45)
-    binned = add_bins((p45,), ((4, 2, 0),), shared, binned)
+    (p1, p2), binned = after((p1, p2), binned)
+    q1, q2 = to_core(p1), to_core(p2)
+    p3 = swap_with(p1, step_move(1))
+    p45 = swap_with(jnp.concatenate([p0, p1], axis=0), step_move(2))
+    binned = add_bins((p1, q1), ((1, 1, 0), (1, 1, 1)), shared, binned)
+    binned = add_bins((p2, q2), ((2, 1, 0), (2, 1, 1)), shared, binned)
+    (p3, p45), binned = after((p3, p45), binned)
+    p67 = swap_with(jnp.concatenate([p2, p3], axis=0), step_move(2))
+    q3, q45 = to_core(p3), to_core(p45)
+    binned = add_bins((p3, q3), ((3, 1, 0), (3, 1, 1)), shared, binned)
+    binned = add_bins((p45, q45), ((4, 2, 0), (4, 2, 1)), shared, binned)
     p67, binned = after(p67, binned)
     q67 = to_core(p67)
-    binned = add_bins((q45,), ((4, 2, 1),), shared, binned)
     binned = add_bins((p67,), ((6, 2, 0),), shared, binned)
     best = add_bins((q67,), ((6, 2, 1),), shared, binned, stat)[-1]
     for move in (across(dcore=1), across(dz=1), across(dz=3), across(dy=2)):

time: 63 us -> 61.8 us (0.981)
  waiting for transfers between devices: 19.4 us -> 17.6 us
    ppermute x17 -> x19, waiting for transfers between devices: 19.4 us -> 17.6 us  [swap_with(): return lax.ppermute(value, AXES, pairs)]
    ppermute x17 -> x19, starting transfers between devices: 21.3 us -> 21.9 us  [swap_with(): return lax.ppermute(value, AXES, pairs)]
    pallas_call x9 -> x7, Pallas kernels: 14 us -> 13.9 us  [add_bins(): pl.pallas_call(functools.partial(bins_kernel, parts, last), out_shape=out...]
  transfers between devices with their start and end apart: 17 -> 19, of which waited for: 10 -> 9; matrix products, arithmetic and copies ran while one was open for 1% -> 1% of each run, Pallas kernels for 21% -> 24%
where the time goes in v10:
time: 61.8 us; the launch traced here: 61.6 us
  starting transfers between devices  21.9 us (35%)
  Pallas kernels  17.6 us (28%)
  waiting for transfers between devices  17.6 us (28%)
  local copies, waits for them, and re-layouts  2.12 us (3%)
  other arithmetic  1.54 us (2%)
  between operations  0.77 us (1%)
    ppermute x19, starting transfers between devices, swap_with(): return lax.ppermute(value, AXES, pairs)  21.9 us
    ppermute x19, waiting for transfers between devices, swap_with(): return lax.ppermute(value, AXES, pairs)  17.6 us
    pallas_call x7, Pallas kernels, add_bins(): pl.pallas_call(functools.partial(bins_kernel, parts, last), out_shape=out...  13.9 us
    pallas_call x1, Pallas kernels, prepare_tables(): pl.pallas_call(tables_kernel, out_shape=[jax.ShapeDtypeStruct((SLOTS, LAN...  2.03 us
    unnamed x3, local copies, waits for them, and re-layouts  2 us
    pallas_call x1, Pallas kernels, prepare_templates(): pl.pallas_call(templates_kernel, out_shape=[jax.ShapeDtypeStruct((SLOTS,...  1.66 us
  transfers between devices with their start and end apart: 19, of which 9 were waited for; matrix products, arithmetic and copies ran while one was open for 1% of the time, Pallas kernels for 24%

profile of v10, /device:TPU:0, one launch (start us, length us, event | category | flops | bytes accessed | tf_op | source)
XLA Modules:
  0.0 61.6 jit_solution(8825462757935073034)
XLA Ops:
  0.0 0.7 %copy.97 = bf16[1,3,2,6,256]{4,3,1,2,0:T(8,128)(2,1)S(1)} copy(bf16[1,3,2,6,256]{4,2,3,1,0:T(2,128)(2,1)} %param.5) | data formatting | bytes 36864 | tf_op args[0]
  0.7 2.8 %collective-permute-start.2 = (bf16[6,6,1,256]{3,0,1,2:T(8,128)(2,1)S(1)}, bf16[6,6,1,256]{3,0,1,2:T(8,128)(2,1)S(1)}, u32[]{:S(2)}, u32[]{:S(2)}) collective-permute-start(bf16[6,6,1,256]{3,0,1,2:T(8,128)(2,1)S(1)} %bitcast.22), channel_id=1, source_target_pairs={{0,96},{1,97},{2,98},{3,99},{4,100},{5,101},{6,102},{7,103},{8,104... | collective-permute-start | bytes 55304 | tf_op jit(solution)/shard_map/ppermute | solution.py:50
  3.6 0.8 %collective-permute-start.1 = (bf16[6,6,1,256]{3,0,1,2:T(8,128)(2,1)S(1)}, bf16[6,6,1,256]{3,0,1,2:T(8,128)(2,1)S(1)}, u32[]{:S(2)}, u32[]{:S(2)}) collective-permute-start(bf16[6,6,1,256]{3,0,1,2:T(8,128)(2,1)S(1)} %bitcast.23), channel_id=1, source_target_pairs={{0,64},{1,65},{2,66},{3,67},{4,68},{5,69},{6,70},{7,71},{8,72},{9,... | collective-permute-start | bytes 55304 | tf_op jit(solution)/shard_map/ppermute | solution.py:50
  4.4 0.5 collective-permute-start
  5.5 0.1 pad.18.clone
  5.5 0.8 %fusion.small_ref = s32[16,128]{1,0:T(8,128)S(1)} fusion(s32[3,8]{1,0:T(4,128)} %bitcast.26, s32[12,15]{1,0:T(8,128)} %param.8, s32[16]{0:T(128)S(1)} %pad.18.clone), kind=kLoop, calls=%fused_computation.9 | loop fusion | flops 8192 | bytes 9072 | tf_op jit(solution)/shard_map/concatenate | solution.py:182
  6.3 2.0 %prepare_tables.1 = (f32[12,128]{1,0:T(8,128)S(1)}, f32[96,2,24,256]{3,2,1,0:T(8,128)S(1)}, bf16[512,256]{1,0:T(8,128)(2,1)S(1)}, f32[2,16,8,128]{3,2,1,0:T(8,12...) custom-call(s32[16,128]{1,0:T(8,128)S(1)} %fusion.small_ref), custom_call_target="tpu_custom_call" | custom-call | flops 1000000 | bytes 1000000 | tf_op jit(solution)/shard_map/prepare_tables/pallas_call | solution.py:190
  8.4 0.0 collective-permute-done.2
  8.4 0.5 collective-permute-done.1
  8.9 0.0 collective-permute-done
  8.9 1.7 %collective-permute-start.3 = (bf16[6,6,4,256]{3,0,1,2:T(8,128)(2,1)S(1)}, bf16[6,6,4,256]{3,0,1,2:T(8,128)(2,1)S(1)}, u32[]{:S(2)}, u32[]{:S(2)}) collective-permute-start(bf16[6,6,4,256]{3,0,1,2:T(8,128)(2,1)S(1)} %pad_maximum_fusion.3), channel_id=1, source_target_pairs={{0,16},{1,17},{2,18},{3,19},{4,20},{5,21},{6,22},{7,23},{8,24},{9,... | collective-permute-start | bytes 221192 | tf_op jit(solution)/shard_map/ppermute | solution.py:50
  10.6 1.3 %copy-done = bf16[12,2,96,256]{3,2,1,0:T(8,128)(2,1)S(1)} copy-done((bf16[12,2,96,256]{3,2,1,0:T(8,128)(2,1)S(1)}, bf16[12,2,96,256]{3,2,1,0:T(8,128)(2,1)}, u32[]{:S(2)}) %copy-start) | copy-done | bytes 1179672
  11.9 1.7 %prepare_templates.1 = (f32[12,3,96,256]{3,2,1,0:T(8,128)S(1)}, f32[12,40,128]{2,1,0:T(8,128)S(1)}) custom-call(bf16[12,2,96,256]{3,2,1,0:T(8,128)(2,1)S(1)} %copy-done, s32[16,128]{1,0:T(8,128)S(1)} %fusion.small_ref), custom_call_target="tpu_custom_call" | custom-call | flops 1000000 | bytes 1000000 | tf_op jit(solution)/shard_map/prepare_templates/pallas_call | solution.py:209
  13.5 0.1 collective-permute-done.3
  13.8 0.1 collective-permute-start.6
  13.9 2.0 %collective-permute-start.5 = (bf16[1,6,48,256]{3,2,1,0:T(8,128)(2,1)S(1)}, bf16[1,6,48,256]{3,2,1,0:T(8,128)(2,1)S(1)}, u32[]{:S(2)}, u32[]{:S(2)}) collective-permute-start(bf16[1,6,48,256]{3,2,1,0:T(8,128)(2,1)S(1)} %bitcast.18), channel_id=1, source_target_pairs={{0,2},{1,7},{2,0},{3,5},{4,6},{5,3},{6,4},{7,1},{8,10},{9,15},{10,... | collective-permute-start | bytes 442376 | tf_op jit(solution)/shard_map/ppermute | solution.py:50
  15.9 3.0 %collective-permute-start.4 = (bf16[1,6,48,256]{3,2,1,0:T(8,128)(2,1)S(1)}, bf16[1,6,48,256]{3,2,1,0:T(8,128)(2,1)S(1)}, u32[]{:S(2)}, u32[]{:S(2)}) collective-permute-start(bf16[1,6,48,256]{3,2,1,0:T(8,128)(2,1)S(1)} %bitcast.19), channel_id=1, source_target_pairs={{0,24},{1,3},{2,26},{3,1},{4,28},{5,7},{6,30},{7,5},{8,16},{9,11},... | collective-permute-start | bytes 442376 | tf_op jit(solution)/shard_map/ppermute | solution.py:50
  18.9 1.6 %add_bins.6 = (f32[16,24,256]{2,1,0:T(8,128)S(1)}, f32[16,24,256]{2,1,0:T(8,128)S(1)}, f32[16,24,256]{2,1,0:T(8,128)S(1)}, f32[16,24,256]{2,1,0:T(8,128)S(1)}, f...) custom-call(bf16[1,6,48,256]{3,2,1,0:T(8,128)(2,1)S(1)} %bitcast.20,, ...), custom_call_target="tpu_custom_call", output_to_operand_aliasing={{0}: (7, {}), {1}: (8, {}), {2}: (9, {}), {3}: (10, {}), {4... | custom-call | flops 1811939328 | bytes 1000000 | tf_op jit(solution)/shard_map/add_bins/pallas_call | solution.py:328
  20.5 0.0 collective-permute-done.5.refs_0_
  20.5 1.7 %collective-permute-done.4.refs_0_ = bf16[1,6,48,256]{3,2,1,0:T(8,128)(2,1)S(1)} collective-permute-done((bf16[1,6,48,256]{3,2,1,0:T(8,128)(2,1)S(1)}, bf16[1,6,48,256]{3,2,1,0:T(8,128)(2,1)S(1)}, u32[]{:S(2)}, u32[]{:S(2)}) %collective-permute-start.4) | collective-permute-done | bytes 147488 | tf_op jit(solution)/shard_map/ppermute | solution.py:50
  22.2 0.1 collective-permute-start.10
  22.3 0.1 collective-permute-start.7
  22.4 2.5 %collective-permute-start.9 = (bf16[1,6,48,256]{3,2,1,0:T(8,128)(2,1)S(1)}, bf16[1,6,48,256]{3,2,1,0:T(8,128)(2,1)S(1)}, u32[]{:S(2)}, u32[]{:S(2)}) collective-permute-start(bf16[1,6,48,256]{3,2,1,0:T(8,128)(2,1)S(1)} %collective-permute-done.5.refs_0_), channel_id=1, source_target_pairs={{0,1},{1,0},{2,3},{3,2},{4,5},{5,4},{6,7},{7,6},{8,9},{9,8},{10,11... | collective-permute-start | bytes 442376 | tf_op jit(solution)/shard_map/ppermute | solution.py:50
  25.0 1.5 %collective-permute-start.8 = (bf16[2,6,48,256]{3,2,1,0:T(8,128)(2,1)S(1)}, bf16[2,6,48,256]{3,2,1,0:T(8,128)(2,1)S(1)}, u32[]{:S(2)}, u32[]{:S(2)}) collective-permute-start(bf16[2,6,48,256]{3,2,1,0:T(8,128)(2,1)S(1)} %pad_maximum_fusion), channel_id=1, source_target_pairs={{0,6},{1,25},{2,4},{3,27},{4,2},{5,29},{6,0},{7,31},{8,14},{9,17},... | collective-permute-start | bytes 884744 | tf_op jit(solution)/shard_map/ppermute | solution.py:50
  26.5 0.0 collective-permute-done.10.refs_1_
  26.5 1.6 %add_bins.7 = (f32[16,24,256]{2,1,0:T(8,128)S(1)}, f32[16,24,256]{2,1,0:T(8,128)S(1)}, f32[16,24,256]{2,1,0:T(8,128)S(1)}, f32[16,24,256]{2,1,0:T(8,128)S(1)}, f...) custom-call(bf16[1,6,48,256]{3,2,1,0:T(8,128)(2,1)S(1)} %collective-, ...), custom_call_target="tpu_custom_call", output_to_operand_aliasing={{0}: (7, {}), {1}: (8, {}), {2}: (9, {}), {3}: (10, {}), {4... | custom-call | flops 1811939328 | bytes 1000000 | tf_op jit(solution)/shard_map/add_bins/pallas_call | solution.py:328
  28.1 1.6 %add_bins.8 = (f32[16,24,256]{2,1,0:T(8,128)S(1)}, f32[16,24,256]{2,1,0:T(8,128)S(1)}, f32[16,24,256]{2,1,0:T(8,128)S(1)}, f32[16,24,256]{2,1,0:T(8,128)S(1)}, f...) custom-call(bf16[1,6,48,256]{3,2,1,0:T(8,128)(2,1)S(1)} %collective-, ...), custom_call_target="tpu_custom_call", output_to_operand_aliasing={{0}: (7, {}), {1}: (8, {}), {2}: (9, {}), {3}: (10, {}), {4... | custom-call | flops 1811939328 | bytes 1000000 | tf_op jit(solution)/shard_map/add_bins/pallas_call | solution.py:328
  29.7 0.0 collective-permute-done.7.refs_0_
  29.7 3.3 %collective-permute-done.8.refs_0_ = bf16[2,6,48,256]{3,2,1,0:T(8,128)(2,1)S(1)} collective-permute-done((bf16[2,6,48,256]{3,2,1,0:T(8,128)(2,1)S(1)}, bf16[2,6,48,256]{3,2,1,0:T(8,128)(2,1)S(1)}, u32[]{:S(2)}, u32[]{:S(2)}) %collective-permute-start.8) | collective-permute-done | bytes 294944 | tf_op jit(solution)/shard_map/ppermute | solution.py:50
  33.0 0.5 collective-permute-start.12
  33.6 1.7 %collective-permute-start.11 = (bf16[2,6,48,256]{3,2,1,0:T(8,128)(2,1)S(1)}, bf16[2,6,48,256]{3,2,1,0:T(8,128)(2,1)S(1)}, u32[]{:S(2)}, u32[]{:S(2)}) collective-permute-start(bf16[2,6,48,256]{3,2,1,0:T(8,128)(2,1)S(1)} %pad_maximum_fusion.1), channel_id=1, source_target_pairs={{0,6},{1,25},{2,4},{3,27},{4,2},{5,29},{6,0},{7,31},{8,14},{9,17},... | collective-permute-start | bytes 884744 | tf_op jit(solution)/shard_map/ppermute | solution.py:50
  35.2 0.0 collective-permute-done.13.refs_1_
  35.2 1.6 %add_bins.9 = (f32[16,24,256]{2,1,0:T(8,128)S(1)}, f32[16,24,256]{2,1,0:T(8,128)S(1)}, f32[16,24,256]{2,1,0:T(8,128)S(1)}, f32[16,24,256]{2,1,0:T(8,128)S(1)}, f...) custom-call(bf16[1,6,48,256]{3,2,1,0:T(8,128)(2,1)S(1)} %collective-, ...), custom_call_target="tpu_custom_call", output_to_operand_aliasing={{0}: (7, {}), {1}: (8, {}), {2}: (9, {}), {3}: (10, {}), {4... | custom-call | flops 1811939328 | bytes 1000000 | tf_op jit(solution)/shard_map/add_bins/pallas_call | solution.py:328
  36.8 0.0 collective-permute-done.12.refs_1_
  36.8 3.3 %add_bins.10 = (f32[16,24,256]{2,1,0:T(8,128)S(1)}, f32[16,24,256]{2,1,0:T(8,128)S(1)}, f32[16,24,256]{2,1,0:T(8,128)S(1)}, f32[16,24,256]{2,1,0:T(8,128)S(1)}, ...) custom-call(bf16[2,6,48,256]{3,2,1,0:T(8,128)(2,1)S(1)} %collective-, ...), custom_call_target="tpu_custom_call", output_to_operand_aliasing={{0}: (7, {}), {1}: (8, {}), {2}: (9, {}), {3}: (10, {}), {4... | custom-call | flops 3623878656 | bytes 1000000 | tf_op jit(solution)/shard_map/add_bins/pallas_call | solution.py:328
  40.1 1.7 %collective-permute-done.11.refs_0_ = bf16[2,6,48,256]{3,2,1,0:T(8,128)(2,1)S(1)} collective-permute-done((bf16[2,6,48,256]{3,2,1,0:T(8,128)(2,1)S(1)}, bf16[2,6,48,256]{3,2,1,0:T(8,128)(2,1)S(1)}, u32[]{:S(2)}, u32[]{:S(2)}) %collective-permute-start.11) | collective-permute-done | bytes 294944 | tf_op jit(solution)/shard_map/ppermute | solution.py:50
  41.8 1.6 %add_bins.11 = (f32[16,24,256]{2,1,0:T(8,128)S(1)}, f32[16,24,256]{2,1,0:T(8,128)S(1)}, f32[16,24,256]{2,1,0:T(8,128)S(1)}, f32[16,24,256]{2,1,0:T(8,128)S(1)}, ...) custom-call(bf16[2,6,48,256]{3,2,1,0:T(8,128)(2,1)S(1)} %collective-, ...), custom_call_target="tpu_custom_call", output_to_operand_aliasing={{0}: (6, {}), {1}: (7, {}), {2}: (8, {}), {3}: (9, {}), {4}... | custom-call | flops 1811939328 | bytes 1000000 | tf_op jit(solution)/shard_map/add_bins/pallas_call | solution.py:328
  43.3 0.0 collective-permute-done.14.refs_0_
  43.3 2.7 %last_bins.1 = (f32[16,24,256]{2,1,0:T(8,128)S(1)}, f32[16,24,256]{2,1,0:T(8,128)S(1)}, f32[16,24,256]{2,1,0:T(8,128)S(1)}, f32[16,24,256]{2,1,0:T(8,128)S(1)}, ...) custom-call(bf16[2,6,48,256]{3,2,1,0:T(8,128)(2,1)S(1)} %collective-, ...), custom_call_target="tpu_custom_call", output_to_operand_aliasing={{0}: (7, {}), {1}: (8, {}), {2}: (9, {}), {3}: (10, {}), {4... | custom-call | flops 1811939328 | bytes 1000000 | tf_op jit(solution)/shard_map/last_bins/pallas_call | solution.py:328
  46.0 0.6 collective-permute-start.15
  46.6 0.8 %collective-permute-done.15 = f32[8,8]{1,0:T(8,128)S(1)} collective-permute-done((f32[8,8]{1,0:T(8,128)S(1)}, f32[8,8]{1,0:T(8,128)S(1)}, u32[]{:S(2)}, u32[]{:S(2)}) %collective-permute-start.15) | collective-permute-done | bytes 288 | tf_op jit(solution)/shard_map/ppermute | solution.py:50
  47.4 0.0 collective-permute-start.16
  47.4 3.6 %collective-permute-done.16 = f32[8,8]{1,0:T(8,128)S(1)} collective-permute-done((f32[8,8]{1,0:T(8,128)S(1)}, f32[8,8]{1,0:T(8,128)S(1)}, u32[]{:S(2)}, u32[]{:S(2)}) %collective-permute-start.16) | collective-permute-done | bytes 288 | tf_op jit(solution)/shard_map/ppermute | solution.py:50
  51.0 1.4 %collective-permute-start.17 = (f32[8,8]{1,0:T(8,128)S(1)}, f32[8,8]{1,0:T(8,128)S(1)}, u32[]{:S(2)}, u32[]{:S(2)}) collective-permute-start(f32[8,8]{1,0:T(8,128)S(1)} %max.13), channel_id=1, source_target_pairs={{0,6},{1,7},{2,4},{3,5},{4,2},{5,3},{6,0},{7,1},{8,14},{9,15},{10,... | collective-permute-start | bytes 776 | tf_op jit(solution)/shard_map/ppermute | solution.py:50
  52.5 3.4 %collective-permute-done.17 = f32[8,8]{1,0:T(8,128)S(1)} collective-permute-done((f32[8,8]{1,0:T(8,128)S(1)}, f32[8,8]{1,0:T(8,128)S(1)}, u32[]{:S(2)}, u32[]{:S(2)}) %collective-permute-start.17) | collective-permute-done | bytes 288 | tf_op jit(solution)/shard_map/ppermute | solution.py:50
  55.9 2.6 %collective-permute-start.18 = (f32[8,8]{1,0:T(8,128)S(1)}, f32[8,8]{1,0:T(8,128)S(1)}, u32[]{:S(2)}, u32[]{:S(2)}) collective-permute-start(f32[8,8]{1,0:T(8,128)S(1)} %max.14), channel_id=1, source_target_pairs={{0,8},{1,9},{2,10},{3,11},{4,12},{5,13},{6,14},{7,15},{8,0},{9,1},... | collective-permute-start | bytes 776 | tf_op jit(solution)/shard_map/ppermute | solution.py:50
  58.5 2.5 %collective-permute-done.18 = f32[8,8]{1,0:T(8,128)S(1)} collective-permute-done((f32[8,8]{1,0:T(8,128)S(1)}, f32[8,8]{1,0:T(8,128)S(1)}, u32[]{:S(2)}, u32[]{:S(2)}) %collective-permute-start.18) | collective-permute-done | bytes 288 | tf_op jit(solution)/shard_map/ppermute | solution.py:50
  61.0 0.6 max.15
  (14 shorter events, 0.2 us)
Async XLA Ops:
  0.7 7.6 %collective-permute-start.2 = (bf16[6,6,1,256]{3,0,1,2:T(8,128)(2,1)S(1)}, bf16[6,6,1,256]{3,0,1,2:T(8,128)(2,1)S(1)}, u32[]{:S(2)}, u32[]{:S(2)}) collective-permute-start(bf16[6,6,1,256]{3,0,1,2:T(8,128)(2,1)S(1)} %bitcast.22), channel_id=1, source_target_pairs={{0,96},{1,97},{2,98},{3,99},{4,100},{5,101},{6,102},{7,103},{8,104... | collective-permute-start | bytes 55304 | tf_op jit(solution)/shard_map/ppermute | solution.py:50
  3.6 5.3 %collective-permute-start.1 = (bf16[6,6,1,256]{3,0,1,2:T(8,128)(2,1)S(1)}, bf16[6,6,1,256]{3,0,1,2:T(8,128)(2,1)S(1)}, u32[]{:S(2)}, u32[]{:S(2)}) collective-permute-start(bf16[6,6,1,256]{3,0,1,2:T(8,128)(2,1)S(1)} %bitcast.23), channel_id=1, source_target_pairs={{0,64},{1,65},{2,66},{3,67},{4,68},{5,69},{6,70},{7,71},{8,72},{9,... | collective-permute-start | bytes 55304 | tf_op jit(solution)/shard_map/ppermute | solution.py:50
  4.4 4.5 %collective-permute-start = (bf16[6,6,1,256]{3,0,1,2:T(8,128)(2,1)S(1)}, bf16[6,6,1,256]{3,0,1,2:T(8,128)(2,1)S(1)}, u32[]{:S(2)}, u32[]{:S(2)}) collective-permute-start(bf16[6,6,1,256]{3,0,1,2:T(8,128)(2,1)S(1)} %bitcast.24), channel_id=1, source_target_pairs={{0,32},{1,33},{2,34},{3,35},{4,36},{5,37},{6,38},{7,39},{8,40},{9,... | collective-permute-start | bytes 55304 | tf_op jit(solution)/shard_map/ppermute | solution.py:50
  8.9 4.7 %collective-permute-start.3 = (bf16[6,6,4,256]{3,0,1,2:T(8,128)(2,1)S(1)}, bf16[6,6,4,256]{3,0,1,2:T(8,128)(2,1)S(1)}, u32[]{:S(2)}, u32[]{:S(2)}) collective-permute-start(bf16[6,6,4,256]{3,0,1,2:T(8,128)(2,1)S(1)} %pad_maximum_fusion.3), channel_id=1, source_target_pairs={{0,16},{1,17},{2,18},{3,19},{4,20},{5,21},{6,22},{7,23},{8,24},{9,... | collective-permute-start | bytes 221192 | tf_op jit(solution)/shard_map/ppermute | solution.py:50
  10.6 1.3 %copy-start = (bf16[12,2,96,256]{3,2,1,0:T(8,128)(2,1)S(1)}, bf16[12,2,96,256]{3,2,1,0:T(8,128)(2,1)}, u32[]{:S(2)}) copy-start(bf16[12,2,96,256]{3,2,1,0:T(8,128)(2,1)} %templ_ref.1) | copy-start | bytes 3538948
  13.8 5.1 %collective-permute-start.6 = (bf16[1,6,48,256]{3,2,1,0:T(8,128)(2,1)S(1)}, bf16[1,6,48,256]{3,2,1,0:T(8,128)(2,1)S(1)}, u32[]{:S(2)}, u32[]{:S(2)}) collective-permute-start(bf16[1,6,48,256]{3,2,1,0:T(8,128)(2,1)S(1)} %bitcast.17), channel_id=1, source_target_pairs={{0,1},{1,0},{2,3},{3,2},{4,5},{5,4},{6,7},{7,6},{8,9},{9,8},{10,11... | collective-permute-start | bytes 442376 | tf_op jit(solution)/shard_map/ppermute | solution.py:50
  13.9 6.6 %collective-permute-start.5 = (bf16[1,6,48,256]{3,2,1,0:T(8,128)(2,1)S(1)}, bf16[1,6,48,256]{3,2,1,0:T(8,128)(2,1)S(1)}, u32[]{:S(2)}, u32[]{:S(2)}) collective-permute-start(bf16[1,6,48,256]{3,2,1,0:T(8,128)(2,1)S(1)} %bitcast.18), channel_id=1, source_target_pairs={{0,2},{1,7},{2,0},{3,5},{4,6},{5,3},{6,4},{7,1},{8,10},{9,15},{10,... | collective-permute-start | bytes 442376 | tf_op jit(solution)/shard_map/ppermute | solution.py:50
  15.9 6.4 %collective-permute-start.4 = (bf16[1,6,48,256]{3,2,1,0:T(8,128)(2,1)S(1)}, bf16[1,6,48,256]{3,2,1,0:T(8,128)(2,1)S(1)}, u32[]{:S(2)}, u32[]{:S(2)}) collective-permute-start(bf16[1,6,48,256]{3,2,1,0:T(8,128)(2,1)S(1)} %bitcast.19), channel_id=1, source_target_pairs={{0,24},{1,3},{2,26},{3,1},{4,28},{5,7},{6,30},{7,5},{8,16},{9,11},... | collective-permute-start | bytes 442376 | tf_op jit(solution)/shard_map/ppermute | solution.py:50
  22.2 4.3 %collective-permute-start.10 = (bf16[1,6,48,256]{3,2,1,0:T(8,128)(2,1)S(1)}, bf16[1,6,48,256]{3,2,1,0:T(8,128)(2,1)S(1)}, u32[]{:S(2)}, u32[]{:S(2)}) collective-permute-start(bf16[1,6,48,256]{3,2,1,0:T(8,128)(2,1)S(1)} %collective-permute-done.4.refs_0_), channel_id=1, source_target_pairs={{0,1},{1,0},{2,3},{3,2},{4,5},{5,4},{6,7},{7,6},{8,9},{9,8},{10,11... | collective-permute-start | bytes 442376 | tf_op jit(solution)/shard_map/ppermute | solution.py:50
  22.3 7.4 %collective-permute-start.7 = (bf16[1,6,48,256]{3,2,1,0:T(8,128)(2,1)S(1)}, bf16[1,6,48,256]{3,2,1,0:T(8,128)(2,1)S(1)}, u32[]{:S(2)}, u32[]{:S(2)}) collective-permute-start(bf16[1,6,48,256]{3,2,1,0:T(8,128)(2,1)S(1)} %collective-permute-done.4.refs_0_), channel_id=1, source_target_pairs={{0,2},{1,7},{2,0},{3,5},{4,6},{5,3},{6,4},{7,1},{8,10},{9,15},{10,... | collective-permute-start | bytes 442376 | tf_op jit(solution)/shard_map/ppermute | solution.py:50
  22.4 5.7 %collective-permute-start.9 = (bf16[1,6,48,256]{3,2,1,0:T(8,128)(2,1)S(1)}, bf16[1,6,48,256]{3,2,1,0:T(8,128)(2,1)S(1)}, u32[]{:S(2)}, u32[]{:S(2)}) collective-permute-start(bf16[1,6,48,256]{3,2,1,0:T(8,128)(2,1)S(1)} %collective-permute-done.5.refs_0_), channel_id=1, source_target_pairs={{0,1},{1,0},{2,3},{3,2},{4,5},{5,4},{6,7},{7,6},{8,9},{9,8},{10,11... | collective-permute-start | bytes 442376 | tf_op jit(solution)/shard_map/ppermute | solution.py:50
  25.0 8.0 %collective-permute-start.8 = (bf16[2,6,48,256]{3,2,1,0:T(8,128)(2,1)S(1)}, bf16[2,6,48,256]{3,2,1,0:T(8,128)(2,1)S(1)}, u32[]{:S(2)}, u32[]{:S(2)}) collective-permute-start(bf16[2,6,48,256]{3,2,1,0:T(8,128)(2,1)S(1)} %pad_maximum_fusion), channel_id=1, source_target_pairs={{0,6},{1,25},{2,4},{3,27},{4,2},{5,29},{6,0},{7,31},{8,14},{9,17},... | collective-permute-start | bytes 884744 | tf_op jit(solution)/shard_map/ppermute | solution.py:50
  33.0 2.2 %collective-permute-start.13 = (bf16[1,6,48,256]{3,2,1,0:T(8,128)(2,1)S(1)}, bf16[1,6,48,256]{3,2,1,0:T(8,128)(2,1)S(1)}, u32[]{:S(2)}, u32[]{:S(2)}) collective-permute-start(bf16[1,6,48,256]{3,2,1,0:T(8,128)(2,1)S(1)} %collective-permute-done.7.refs_0_), channel_id=1, source_target_pairs={{0,1},{1,0},{2,3},{3,2},{4,5},{5,4},{6,7},{7,6},{8,9},{9,8},{10,11... | collective-permute-start | bytes 442376 | tf_op jit(solution)/shard_map/ppermute | solution.py:50
  33.0 3.8 %collective-permute-start.12 = (bf16[2,6,48,256]{3,2,1,0:T(8,128)(2,1)S(1)}, bf16[2,6,48,256]{3,2,1,0:T(8,128)(2,1)S(1)}, u32[]{:S(2)}, u32[]{:S(2)}) collective-permute-start(bf16[2,6,48,256]{3,2,1,0:T(8,128)(2,1)S(1)} %collective-permute-done.8.refs_0_), channel_id=1, source_target_pairs={{0,1},{1,0},{2,3},{3,2},{4,5},{5,4},{6,7},{7,6},{8,9},{9,8},{10,11... | collective-permute-start | bytes 884744 | tf_op jit(solution)/shard_map/ppermute | solution.py:50
  33.6 8.2 %collective-permute-start.11 = (bf16[2,6,48,256]{3,2,1,0:T(8,128)(2,1)S(1)}, bf16[2,6,48,256]{3,2,1,0:T(8,128)(2,1)S(1)}, u32[]{:S(2)}, u32[]{:S(2)}) collective-permute-start(bf16[2,6,48,256]{3,2,1,0:T(8,128)(2,1)S(1)} %pad_maximum_fusion.1), channel_id=1, source_target_pairs={{0,6},{1,25},{2,4},{3,27},{4,2},{5,29},{6,0},{7,31},{8,14},{9,17},... | collective-permute-start | bytes 884744 | tf_op jit(solution)/shard_map/ppermute | solution.py:50
  41.7 1.6 %collective-permute-start.14 = (bf16[2,6,48,256]{3,2,1,0:T(8,128)(2,1)S(1)}, bf16[2,6,48,256]{3,2,1,0:T(8,128)(2,1)S(1)}, u32[]{:S(2)}, u32[]{:S(2)}) collective-permute-start(bf16[2,6,48,256]{3,2,1,0:T(8,128)(2,1)S(1)} %collective-permute-done.11.refs_0_), channel_id=1, source_target_pairs={{0,1},{1,0},{2,3},{3,2},{4,5},{5,4},{6,7},{7,6},{8,9},{9,8},{10,11... | collective-permute-start | bytes 884744 | tf_op jit(solution)/shard_map/ppermute | solution.py:50
  46.0 1.4 %collective-permute-start.15 = (f32[8,8]{1,0:T(8,128)S(1)}, f32[8,8]{1,0:T(8,128)S(1)}, u32[]{:S(2)}, u32[]{:S(2)}) collective-permute-start(f32[8,8]{1,0:T(8,128)S(1)} %get-tuple-element.216), channel_id=1, source_target_pairs={{0,1},{1,0},{2,3},{3,2},{4,5},{5,4},{6,7},{7,6},{8,9},{9,8},{10,11... | collective-permute-start | bytes 776 | tf_op jit(solution)/shard_map/ppermute | solution.py:50
  47.4 3.6 %collective-permute-start.16 = (f32[8,8]{1,0:T(8,128)S(1)}, f32[8,8]{1,0:T(8,128)S(1)}, u32[]{:S(2)}, u32[]{:S(2)}) collective-permute-start(f32[8,8]{1,0:T(8,128)S(1)} %max.12), channel_id=1, source_target_pairs={{0,2},{1,3},{2,0},{3,1},{4,6},{5,7},{6,4},{7,5},{8,10},{9,11},{10,... | collective-permute-start | bytes 776 | tf_op jit(solution)/shard_map/ppermute | solution.py:50
  51.0 4.8 %collective-permute-start.17 = (f32[8,8]{1,0:T(8,128)S(1)}, f32[8,8]{1,0:T(8,128)S(1)}, u32[]{:S(2)}, u32[]{:S(2)}) collective-permute-start(f32[8,8]{1,0:T(8,128)S(1)} %max.13), channel_id=1, source_target_pairs={{0,6},{1,7},{2,4},{3,5},{4,2},{5,3},{6,0},{7,1},{8,14},{9,15},{10,... | collective-permute-start | bytes 776 | tf_op jit(solution)/shard_map/ppermute | solution.py:50
  55.9 5.1 %collective-permute-start.18 = (f32[8,8]{1,0:T(8,128)S(1)}, f32[8,8]{1,0:T(8,128)S(1)}, u32[]{:S(2)}, u32[]{:S(2)}) collective-permute-start(f32[8,8]{1,0:T(8,128)S(1)} %max.14), channel_id=1, source_target_pairs={{0,8},{1,9},{2,10},{3,11},{4,12},{5,13},{6,14},{7,15},{8,0},{9,1},... | collective-permute-start | bytes 776 | tf_op jit(solution)/shard_map/ppermute | solution.py:50

commit v11 on v10

--- a/solution.py
+++ b/solution.py
@@ -268,14 +268,14 @@
             binned[k][b, :, :TW] += cos * re - sin * im
             binned[k][b, :, TW:] += cos * im + sin * re
 
-    for piece_ref, (first, amount, other) in zip(pieces, parts):
+    for piece_ref, (first, amount, other, held) in zip(pieces, parts):
         for which in range(amount):
             c = slice_of(first + which, other)
             slot_lane = lax.broadcasted_iota(jnp.int32, (SLOTS, LANES), 1)
             packed = jnp.sum(jnp.where(slot_lane == c, bin_ref[...], 0.0), axis=1, keepdims=True).astype(jnp.int32)
             digits = [packed[k, 0] for k in range(SLOTS)]
             for jj in range(JS):
-                product(piece_ref, which, c, jj)
+                product(piece_ref, held + which, c, jj)
             half = JS // 2
             size = half * SLOTS * ROWS
             for h in range(2):
@@ -366,22 +366,22 @@
     q0 = to_core(p0)
     p1 = swap_with(p0, step_move(0))
     p2 = swap_with(p0, step_move(1))
-    binned = add_bins((p0, q0), ((0, 1, 0), (0, 1, 1)), shared, binned)
+    binned = add_bins((p0, q0), ((0, 1, 0, 0), (0, 1, 1, 0)), shared, binned)
     (p1, p2), binned = after((p1, p2), binned)
-    q1, q2 = to_core(p1), to_core(p2)
+    p12 = jnp.concatenate([p1, p2], axis=0)
+    q12 = to_core(p12)
     p3 = swap_with(p1, step_move(1))
-    p45 = swap_with(jnp.concatenate([p0, p1], axis=0), step_move(2))
-    binned = add_bins((p1, q1), ((1, 1, 0), (1, 1, 1)), shared, binned)
-    binned = add_bins((p2, q2), ((2, 1, 0), (2, 1, 1)), shared, binned)
-    (p3, p45), binned = after((p3, p45), binned)
-    p67 = swap_with(jnp.concatenate([p2, p3], axis=0), step_move(2))
-    q3, q45 = to_core(p3), to_core(p45)
-    binned = add_bins((p3, q3), ((3, 1, 0), (3, 1, 1)), shared, binned)
-    binned = add_bins((p45, q45), ((4, 2, 0), (4, 2, 1)), shared, binned)
-    p67, binned = after(p67, binned)
-    q67 = to_core(p67)
-    binned = add_bins((p67,), ((6, 2, 0),), shared, binned)
-    best = add_bins((q67,), ((6, 2, 1),), shared, binned, stat)[-1]
+    p456 = swap_with(jnp.concatenate([p0, p12], axis=0), step_move(2))
+    binned = add_bins((p12, q12), ((1, 1, 0, 0), (1, 1, 1, 0)), shared, binned)
+    p3, binned = after(p3, binned)
+    q3 = to_core(p3)
+    p7 = swap_with(p3, step_move(2))
+    binned = add_bins((p12, q12, p3), ((2, 1, 0, 1), (2, 1, 1, 1), (3, 1, 0, 0)), shared, binned)
+    (p456, p7), binned = after((p456, p7), binned)
+    p4567 = jnp.concatenate([p456, p7], axis=0)
+    q4567 = to_core(p4567)
+    binned = add_bins((p4567,), ((4, 4, 0, 0),), shared, binned)
+    best = add_bins((q3, q4567), ((3, 1, 1, 0), (4, 4, 1, 0)), shared, binned, stat)[-1]
     for move in (across(dcore=1), across(dz=1), across(dz=3), across(dy=2)):
         best = jnp.maximum(best, swap_with(best, move))
     return best[:, None, :]

time: 61.8 us -> 62.5 us (1.011)
    ppermute x19 -> x17, waiting for transfers between devices: 17.6 us -> 18.1 us  [swap_with(): return lax.ppermute(value, AXES, pairs)]
    ppermute x19 -> x17, starting transfers between devices: 21.9 us -> 22 us  [swap_with(): return lax.ppermute(value, AXES, pairs)]
    pallas_call x7 -> x5, Pallas kernels: 13.9 us -> 14 us  [add_bins(): pl.pallas_call(functools.partial(bins_kernel, parts, last), out_shape=out...]
    unnamed x3 -> x5, local copies, waits for them, and re-layouts: 2 us -> 2.04 us
  transfers between devices with their start and end apart: 19 -> 17, of which waited for: 9 -> 10; matrix products, arithmetic and copies ran while one was open for 1% -> 1% of each run, Pallas kernels for 24% -> 20%
where the time goes in v11:
time: 62.5 us; the launch traced here: 62.2 us
  starting transfers between devices  22 us (35%)
  waiting for transfers between devices  18.1 us (29%)
  Pallas kernels  17.7 us (28%)
  local copies, waits for them, and re-layouts  2.18 us (3%)
  other arithmetic  1.53 us (2%)
  between operations  0.78 us (1%)
    ppermute x17, starting transfers between devices, swap_with(): return lax.ppermute(value, AXES, pairs)  22 us
    ppermute x17, waiting for transfers between devices, swap_with(): return lax.ppermute(value, AXES, pairs)  18.1 us
    pallas_call x5, Pallas kernels, add_bins(): pl.pallas_call(functools.partial(bins_kernel, parts, last), out_shape=out...  14 us
    unnamed x5, local copies, waits for them, and re-layouts  2.04 us
    pallas_call x1, Pallas kernels, prepare_tables(): pl.pallas_call(tables_kernel, out_shape=[jax.ShapeDtypeStruct((SLOTS, LAN...  2.03 us
    pallas_call x1, Pallas kernels, prepare_templates(): pl.pallas_call(templates_kernel, out_shape=[jax.ShapeDtypeStruct((SLOTS,...  1.66 us
  transfers between devices with their start and end apart: 17, of which 10 were waited for; matrix products, arithmetic and copies ran while one was open for 1% of the time, Pallas kernels for 20%

profile of v11, /device:TPU:0, one launch (start us, length us, event | category | flops | bytes accessed | tf_op | source)
XLA Modules:
  0.0 62.2 jit_solution(8104652719517232055)
XLA Ops:
  0.0 0.7 %copy.73 = bf16[1,3,2,6,256]{4,3,1,2,0:T(8,128)(2,1)S(1)} copy(bf16[1,3,2,6,256]{4,2,3,1,0:T(2,128)(2,1)} %param.5) | data formatting | bytes 36864 | tf_op args[0]
  0.7 2.8 %collective-permute-start.2 = (bf16[6,6,1,256]{3,0,1,2:T(8,128)(2,1)S(1)}, bf16[6,6,1,256]{3,0,1,2:T(8,128)(2,1)S(1)}, u32[]{:S(2)}, u32[]{:S(2)}) collective-permute-start(bf16[6,6,1,256]{3,0,1,2:T(8,128)(2,1)S(1)} %bitcast.22), channel_id=1, source_target_pairs={{0,96},{1,97},{2,98},{3,99},{4,100},{5,101},{6,102},{7,103},{8,104... | collective-permute-start | bytes 55304 | tf_op jit(solution)/shard_map/ppermute | solution.py:50
  3.6 0.8 %collective-permute-start.1 = (bf16[6,6,1,256]{3,0,1,2:T(8,128)(2,1)S(1)}, bf16[6,6,1,256]{3,0,1,2:T(8,128)(2,1)S(1)}, u32[]{:S(2)}, u32[]{:S(2)}) collective-permute-start(bf16[6,6,1,256]{3,0,1,2:T(8,128)(2,1)S(1)} %bitcast.23), channel_id=1, source_target_pairs={{0,64},{1,65},{2,66},{3,67},{4,68},{5,69},{6,70},{7,71},{8,72},{9,... | collective-permute-start | bytes 55304 | tf_op jit(solution)/shard_map/ppermute | solution.py:50
  4.4 0.5 collective-permute-start
  5.5 0.1 pad.17.clone
  5.5 0.8 %fusion.small_ref = s32[16,128]{1,0:T(8,128)S(1)} fusion(s32[3,8]{1,0:T(4,128)} %bitcast.26, s32[12,15]{1,0:T(8,128)} %param.8, s32[16]{0:T(128)S(1)} %pad.17.clone), kind=kLoop, calls=%fused_computation.12 | loop fusion | flops 8192 | bytes 9072 | tf_op jit(solution)/shard_map/concatenate | solution.py:182
  6.3 2.0 %prepare_tables.1 = (f32[12,128]{1,0:T(8,128)S(1)}, f32[96,2,24,256]{3,2,1,0:T(8,128)S(1)}, bf16[512,256]{1,0:T(8,128)(2,1)S(1)}, f32[2,16,8,128]{3,2,1,0:T(8,12...) custom-call(s32[16,128]{1,0:T(8,128)S(1)} %fusion.small_ref), custom_call_target="tpu_custom_call" | custom-call | flops 1000000 | bytes 1000000 | tf_op jit(solution)/shard_map/prepare_tables/pallas_call | solution.py:190
  8.4 0.0 collective-permute-done.2
  8.4 0.5 collective-permute-done.1
  8.9 0.0 collective-permute-done
  8.9 1.7 %collective-permute-start.3 = (bf16[6,6,4,256]{3,0,1,2:T(8,128)(2,1)S(1)}, bf16[6,6,4,256]{3,0,1,2:T(8,128)(2,1)S(1)}, u32[]{:S(2)}, u32[]{:S(2)}) collective-permute-start(bf16[6,6,4,256]{3,0,1,2:T(8,128)(2,1)S(1)} %pad_maximum_fusion.2), channel_id=1, source_target_pairs={{0,16},{1,17},{2,18},{3,19},{4,20},{5,21},{6,22},{7,23},{8,24},{9,... | collective-permute-start | bytes 221192 | tf_op jit(solution)/shard_map/ppermute | solution.py:50
  10.6 0.0 copy-start
  10.6 1.3 %copy-done = bf16[12,2,96,256]{3,2,1,0:T(8,128)(2,1)S(1)} copy-done((bf16[12,2,96,256]{3,2,1,0:T(8,128)(2,1)S(1)}, bf16[12,2,96,256]{3,2,1,0:T(8,128)(2,1)}, u32[]{:S(2)}) %copy-start) | copy-done | bytes 1179672
  11.9 1.7 %prepare_templates.1 = (f32[12,3,96,256]{3,2,1,0:T(8,128)S(1)}, f32[12,40,128]{2,1,0:T(8,128)S(1)}) custom-call(bf16[12,2,96,256]{3,2,1,0:T(8,128)(2,1)S(1)} %copy-done, s32[16,128]{1,0:T(8,128)S(1)} %fusion.small_ref), custom_call_target="tpu_custom_call" | custom-call | flops 1000000 | bytes 1000000 | tf_op jit(solution)/shard_map/prepare_templates/pallas_call | solution.py:209
  13.5 0.1 collective-permute-done.3
  13.8 0.1 collective-permute-start.6
  13.9 2.0 %collective-permute-start.5 = (bf16[1,6,48,256]{3,2,1,0:T(8,128)(2,1)S(1)}, bf16[1,6,48,256]{3,2,1,0:T(8,128)(2,1)S(1)}, u32[]{:S(2)}, u32[]{:S(2)}) collective-permute-start(bf16[1,6,48,256]{3,2,1,0:T(8,128)(2,1)S(1)} %bitcast.18), channel_id=1, source_target_pairs={{0,2},{1,7},{2,0},{3,5},{4,6},{5,3},{6,4},{7,1},{8,10},{9,15},{10,... | collective-permute-start | bytes 442376 | tf_op jit(solution)/shard_map/ppermute | solution.py:50
  15.9 3.0 %collective-permute-start.4 = (bf16[1,6,48,256]{3,2,1,0:T(8,128)(2,1)S(1)}, bf16[1,6,48,256]{3,2,1,0:T(8,128)(2,1)S(1)}, u32[]{:S(2)}, u32[]{:S(2)}) collective-permute-start(bf16[1,6,48,256]{3,2,1,0:T(8,128)(2,1)S(1)} %bitcast.19), channel_id=1, source_target_pairs={{0,24},{1,3},{2,26},{3,1},{4,28},{5,7},{6,30},{7,5},{8,16},{9,11},... | collective-permute-start | bytes 442376 | tf_op jit(solution)/shard_map/ppermute | solution.py:50
  18.9 0.0 collective-permute-done.6.refs_1_
  18.9 1.6 %add_bins.4 = (f32[16,24,256]{2,1,0:T(8,128)S(1)}, f32[16,24,256]{2,1,0:T(8,128)S(1)}, f32[16,24,256]{2,1,0:T(8,128)S(1)}, f32[16,24,256]{2,1,0:T(8,128)S(1)}, f...) custom-call(bf16[1,6,48,256]{3,2,1,0:T(8,128)(2,1)S(1)} %bitcast.20,, ...), custom_call_target="tpu_custom_call", output_to_operand_aliasing={{0}: (7, {}), {1}: (8, {}), {2}: (9, {}), {3}: (10, {}), {4... | custom-call | flops 1811939328 | bytes 1000000 | tf_op jit(solution)/shard_map/add_bins/pallas_call | solution.py:328
  20.5 0.0 collective-permute-done.5
  20.5 1.7 %collective-permute-done.4 = bf16[1,6,48,256]{3,2,1,0:T(8,128)(2,1)S(1)} collective-permute-done((bf16[1,6,48,256]{3,2,1,0:T(8,128)(2,1)S(1)}, bf16[1,6,48,256]{3,2,1,0:T(8,128)(2,1)S(1)}, u32[]{:S(2)}, u32[]{:S(2)}) %collective-permute-start.4) | collective-permute-done | bytes 147488 | tf_op jit(solution)/shard_map/ppermute | solution.py:50
  22.2 0.2 collective-permute-start.8
  22.4 0.1 pad_maximum_fusion
  22.5 2.5 %collective-permute-start.10 = (bf16[3,6,48,256]{3,2,1,0:T(8,128)(2,1)S(1)}, bf16[3,6,48,256]{3,2,1,0:T(8,128)(2,1)S(1)}, u32[]{:S(2)}, u32[]{:S(2)}) collective-permute-start(bf16[3,6,48,256]{3,2,1,0:T(8,128)(2,1)S(1)} %pad_maximum_fusion), channel_id=1, source_target_pairs={{0,6},{1,25},{2,4},{3,27},{4,2},{5,29},{6,0},{7,31},{8,14},{9,17},... | collective-permute-start | bytes 1327112 | tf_op jit(solution)/shard_map/ppermute | solution.py:50
  25.0 1.0 %collective-permute-start.7 = (bf16[1,6,48,256]{3,2,1,0:T(8,128)(2,1)S(1)}, bf16[1,6,48,256]{3,2,1,0:T(8,128)(2,1)S(1)}, u32[]{:S(2)}, u32[]{:S(2)}) collective-permute-start(bf16[1,6,48,256]{3,2,1,0:T(8,128)(2,1)S(1)} %collective-permute-done.4), channel_id=1, source_target_pairs={{0,2},{1,7},{2,0},{3,5},{4,6},{5,3},{6,4},{7,1},{8,10},{9,15},{10,... | collective-permute-start | bytes 442376 | tf_op jit(solution)/shard_map/ppermute | solution.py:50
  26.0 0.0 collective-permute-done.8.refs_1_
  26.0 1.6 %add_bins.5 = (f32[16,24,256]{2,1,0:T(8,128)S(1)}, f32[16,24,256]{2,1,0:T(8,128)S(1)}, f32[16,24,256]{2,1,0:T(8,128)S(1)}, f32[16,24,256]{2,1,0:T(8,128)S(1)}, f...) custom-call(bf16[2,6,48,256]{3,2,1,0:T(8,128)(2,1)S(1)} %constant_dy, ...), custom_call_target="tpu_custom_call", output_to_operand_aliasing={{0}: (7, {}), {1}: (8, {}), {2}: (9, {}), {3}: (10, {}), {4... | custom-call | flops 1811939328 | bytes 1000000 | tf_op jit(solution)/shard_map/add_bins/pallas_call | solution.py:328
  27.6 2.5 %collective-permute-done.7.refs_2_ = bf16[1,6,48,256]{3,2,1,0:T(8,128)(2,1)S(1)} collective-permute-done((bf16[1,6,48,256]{3,2,1,0:T(8,128)(2,1)S(1)}, bf16[1,6,48,256]{3,2,1,0:T(8,128)(2,1)S(1)}, u32[]{:S(2)}, u32[]{:S(2)}) %collective-permute-start.7) | collective-permute-done | bytes 147488 | tf_op jit(solution)/shard_map/ppermute | solution.py:50
  30.1 0.8 %collective-permute-start.11 = (bf16[1,6,48,256]{3,2,1,0:T(8,128)(2,1)S(1)}, bf16[1,6,48,256]{3,2,1,0:T(8,128)(2,1)S(1)}, u32[]{:S(2)}, u32[]{:S(2)}) collective-permute-start(bf16[1,6,48,256]{3,2,1,0:T(8,128)(2,1)S(1)} %collective-permute-done.7.refs_2_), channel_id=1, source_target_pairs={{0,6},{1,25},{2,4},{3,27},{4,2},{5,29},{6,0},{7,31},{8,14},{9,17},... | collective-permute-start | bytes 442376 | tf_op jit(solution)/shard_map/ppermute | solution.py:50
  31.0 2.4 %add_bins.6 = (f32[16,24,256]{2,1,0:T(8,128)S(1)}, f32[16,24,256]{2,1,0:T(8,128)S(1)}, f32[16,24,256]{2,1,0:T(8,128)S(1)}, f32[16,24,256]{2,1,0:T(8,128)S(1)}, f...) custom-call(bf16[2,6,48,256]{3,2,1,0:T(8,128)(2,1)S(1)} %constant_dy, ...), custom_call_target="tpu_custom_call", output_to_operand_aliasing={{0}: (8, {}), {1}: (9, {}), {2}: (10, {}), {3}: (11, {}), {... | custom-call | flops 2717908992 | bytes 1000000 | tf_op jit(solution)/shard_map/add_bins/pallas_call | solution.py:328
  33.3 0.3 collective-permute-done.10
  33.7 2.8 %collective-permute-done.11 = bf16[1,6,48,256]{3,2,1,0:T(8,128)(2,1)S(1)} collective-permute-done((bf16[1,6,48,256]{3,2,1,0:T(8,128)(2,1)S(1)}, bf16[1,6,48,256]{3,2,1,0:T(8,128)(2,1)S(1)}, u32[]{:S(2)}, u32[]{:S(2)}) %collective-permute-start.11) | collective-permute-done | bytes 147488 | tf_op jit(solution)/shard_map/ppermute | solution.py:50
  36.6 1.6 %collective-permute-start.12 = (bf16[4,6,48,256]{3,2,1,0:T(8,128)(2,1)S(1)}, bf16[4,6,48,256]{3,2,1,0:T(8,128)(2,1)S(1)}, u32[]{:S(2)}, u32[]{:S(2)}) collective-permute-start(bf16[4,6,48,256]{3,2,1,0:T(8,128)(2,1)S(1)} %constant_dynamic-update-slice_fusion.2.refs_0_), channel_id=1, source_target_pairs={{0,1},{1,0},{2,3},{3,2},{4,5},{5,4},{6,7},{7,6},{8,9},{9,8},{10,11... | collective-permute-start | bytes 1769480 | tf_op jit(solution)/shard_map/ppermute | solution.py:50
  38.2 0.3 collective-permute-start.9
  38.5 3.2 %add_bins.7 = (f32[16,24,256]{2,1,0:T(8,128)S(1)}, f32[16,24,256]{2,1,0:T(8,128)S(1)}, f32[16,24,256]{2,1,0:T(8,128)S(1)}, f32[16,24,256]{2,1,0:T(8,128)S(1)}, f...) custom-call(bf16[4,6,48,256]{3,2,1,0:T(8,128)(2,1)S(1)} %constant_dy, ...), custom_call_target="tpu_custom_call", output_to_operand_aliasing={{0}: (6, {}), {1}: (7, {}), {2}: (8, {}), {3}: (9, {}), {4}... | custom-call | flops 3623878656 | bytes 1000000 | tf_op jit(solution)/shard_map/add_bins/pallas_call | solution.py:328
  41.6 0.0 collective-permute-done.9.refs_0_
  41.7 0.0 collective-permute-done.12.refs_1_
  41.7 5.2 %last_bins.1 = (f32[16,24,256]{2,1,0:T(8,128)S(1)}, f32[16,24,256]{2,1,0:T(8,128)S(1)}, f32[16,24,256]{2,1,0:T(8,128)S(1)}, f32[16,24,256]{2,1,0:T(8,128)S(1)}, ...) custom-call(bf16[1,6,48,256]{3,2,1,0:T(8,128)(2,1)S(1)} %collective-, ...), custom_call_target="tpu_custom_call", output_to_operand_aliasing={{0}: (8, {}), {1}: (9, {}), {2}: (10, {}), {3}: (11, {}), {... | custom-call | flops 4529848320 | bytes 1000000 | tf_op jit(solution)/shard_map/last_bins/pallas_call | solution.py:328
  46.9 0.3 collective-permute-start.13
  47.2 0.9 %collective-permute-done.13 = f32[8,8]{1,0:T(8,128)S(1)} collective-permute-done((f32[8,8]{1,0:T(8,128)S(1)}, f32[8,8]{1,0:T(8,128)S(1)}, u32[]{:S(2)}, u32[]{:S(2)}) %collective-permute-start.13) | collective-permute-done | bytes 288 | tf_op jit(solution)/shard_map/ppermute | solution.py:50
  48.1 0.6 collective-permute-start.14
  48.7 3.0 %collective-permute-done.14 = f32[8,8]{1,0:T(8,128)S(1)} collective-permute-done((f32[8,8]{1,0:T(8,128)S(1)}, f32[8,8]{1,0:T(8,128)S(1)}, u32[]{:S(2)}, u32[]{:S(2)}) %collective-permute-start.14) | collective-permute-done | bytes 288 | tf_op jit(solution)/shard_map/ppermute | solution.py:50
  51.7 2.5 %collective-permute-start.15 = (f32[8,8]{1,0:T(8,128)S(1)}, f32[8,8]{1,0:T(8,128)S(1)}, u32[]{:S(2)}, u32[]{:S(2)}) collective-permute-start(f32[8,8]{1,0:T(8,128)S(1)} %max.13), channel_id=1, source_target_pairs={{0,6},{1,7},{2,4},{3,5},{4,2},{5,3},{6,0},{7,1},{8,14},{9,15},{10,... | collective-permute-start | bytes 776 | tf_op jit(solution)/shard_map/ppermute | solution.py:50
  54.3 2.3 %collective-permute-done.15 = f32[8,8]{1,0:T(8,128)S(1)} collective-permute-done((f32[8,8]{1,0:T(8,128)S(1)}, f32[8,8]{1,0:T(8,128)S(1)}, u32[]{:S(2)}, u32[]{:S(2)}) %collective-permute-start.15) | collective-permute-done | bytes 288 | tf_op jit(solution)/shard_map/ppermute | solution.py:50
  56.5 1.3 %collective-permute-start.16 = (f32[8,8]{1,0:T(8,128)S(1)}, f32[8,8]{1,0:T(8,128)S(1)}, u32[]{:S(2)}, u32[]{:S(2)}) collective-permute-start(f32[8,8]{1,0:T(8,128)S(1)} %max.14), channel_id=1, source_target_pairs={{0,8},{1,9},{2,10},{3,11},{4,12},{5,13},{6,14},{7,15},{8,0},{9,1},... | collective-permute-start | bytes 776 | tf_op jit(solution)/shard_map/ppermute | solution.py:50
  57.8 3.8 %collective-permute-done.16 = f32[8,8]{1,0:T(8,128)S(1)} collective-permute-done((f32[8,8]{1,0:T(8,128)S(1)}, f32[8,8]{1,0:T(8,128)S(1)}, u32[]{:S(2)}, u32[]{:S(2)}) %collective-permute-start.16) | collective-permute-done | bytes 288 | tf_op jit(solution)/shard_map/ppermute | solution.py:50
  61.7 0.6 max.15
  (11 shorter events, 0.2 us)
Async XLA Ops:
  0.7 7.6 %collective-permute-start.2 = (bf16[6,6,1,256]{3,0,1,2:T(8,128)(2,1)S(1)}, bf16[6,6,1,256]{3,0,1,2:T(8,128)(2,1)S(1)}, u32[]{:S(2)}, u32[]{:S(2)}) collective-permute-start(bf16[6,6,1,256]{3,0,1,2:T(8,128)(2,1)S(1)} %bitcast.22), channel_id=1, source_target_pairs={{0,96},{1,97},{2,98},{3,99},{4,100},{5,101},{6,102},{7,103},{8,104... | collective-permute-start | bytes 55304 | tf_op jit(solution)/shard_map/ppermute | solution.py:50
  3.6 5.3 %collective-permute-start.1 = (bf16[6,6,1,256]{3,0,1,2:T(8,128)(2,1)S(1)}, bf16[6,6,1,256]{3,0,1,2:T(8,128)(2,1)S(1)}, u32[]{:S(2)}, u32[]{:S(2)}) collective-permute-start(bf16[6,6,1,256]{3,0,1,2:T(8,128)(2,1)S(1)} %bitcast.23), channel_id=1, source_target_pairs={{0,64},{1,65},{2,66},{3,67},{4,68},{5,69},{6,70},{7,71},{8,72},{9,... | collective-permute-start | bytes 55304 | tf_op jit(solution)/shard_map/ppermute | solution.py:50
  4.4 4.5 %collective-permute-start = (bf16[6,6,1,256]{3,0,1,2:T(8,128)(2,1)S(1)}, bf16[6,6,1,256]{3,0,1,2:T(8,128)(2,1)S(1)}, u32[]{:S(2)}, u32[]{:S(2)}) collective-permute-start(bf16[6,6,1,256]{3,0,1,2:T(8,128)(2,1)S(1)} %bitcast.24), channel_id=1, source_target_pairs={{0,32},{1,33},{2,34},{3,35},{4,36},{5,37},{6,38},{7,39},{8,40},{9,... | collective-permute-start | bytes 55304 | tf_op jit(solution)/shard_map/ppermute | solution.py:50
  8.9 4.7 %collective-permute-start.3 = (bf16[6,6,4,256]{3,0,1,2:T(8,128)(2,1)S(1)}, bf16[6,6,4,256]{3,0,1,2:T(8,128)(2,1)S(1)}, u32[]{:S(2)}, u32[]{:S(2)}) collective-permute-start(bf16[6,6,4,256]{3,0,1,2:T(8,128)(2,1)S(1)} %pad_maximum_fusion.2), channel_id=1, source_target_pairs={{0,16},{1,17},{2,18},{3,19},{4,20},{5,21},{6,22},{7,23},{8,24},{9,... | collective-permute-start | bytes 221192 | tf_op jit(solution)/shard_map/ppermute | solution.py:50
  10.6 1.3 %copy-start = (bf16[12,2,96,256]{3,2,1,0:T(8,128)(2,1)S(1)}, bf16[12,2,96,256]{3,2,1,0:T(8,128)(2,1)}, u32[]{:S(2)}) copy-start(bf16[12,2,96,256]{3,2,1,0:T(8,128)(2,1)} %templ_ref.1) | copy-start | bytes 3538948
  13.8 5.1 %collective-permute-start.6 = (bf16[1,6,48,256]{3,2,1,0:T(8,128)(2,1)S(1)}, bf16[1,6,48,256]{3,2,1,0:T(8,128)(2,1)S(1)}, u32[]{:S(2)}, u32[]{:S(2)}) collective-permute-start(bf16[1,6,48,256]{3,2,1,0:T(8,128)(2,1)S(1)} %bitcast.17), channel_id=1, source_target_pairs={{0,1},{1,0},{2,3},{3,2},{4,5},{5,4},{6,7},{7,6},{8,9},{9,8},{10,11... | collective-permute-start | bytes 442376 | tf_op jit(solution)/shard_map/ppermute | solution.py:50
  13.9 6.6 %collective-permute-start.5 = (bf16[1,6,48,256]{3,2,1,0:T(8,128)(2,1)S(1)}, bf16[1,6,48,256]{3,2,1,0:T(8,128)(2,1)S(1)}, u32[]{:S(2)}, u32[]{:S(2)}) collective-permute-start(bf16[1,6,48,256]{3,2,1,0:T(8,128)(2,1)S(1)} %bitcast.18), channel_id=1, source_target_pairs={{0,2},{1,7},{2,0},{3,5},{4,6},{5,3},{6,4},{7,1},{8,10},{9,15},{10,... | collective-permute-start | bytes 442376 | tf_op jit(solution)/shard_map/ppermute | solution.py:50
  15.9 6.4 %collective-permute-start.4 = (bf16[1,6,48,256]{3,2,1,0:T(8,128)(2,1)S(1)}, bf16[1,6,48,256]{3,2,1,0:T(8,128)(2,1)S(1)}, u32[]{:S(2)}, u32[]{:S(2)}) collective-permute-start(bf16[1,6,48,256]{3,2,1,0:T(8,128)(2,1)S(1)} %bitcast.19), channel_id=1, source_target_pairs={{0,24},{1,3},{2,26},{3,1},{4,28},{5,7},{6,30},{7,5},{8,16},{9,11},... | collective-permute-start | bytes 442376 | tf_op jit(solution)/shard_map/ppermute | solution.py:50
  22.2 3.8 %collective-permute-start.8 = (bf16[2,6,48,256]{3,2,1,0:T(8,128)(2,1)S(1)}, bf16[2,6,48,256]{3,2,1,0:T(8,128)(2,1)S(1)}, u32[]{:S(2)}, u32[]{:S(2)}) collective-permute-start(bf16[2,6,48,256]{3,2,1,0:T(8,128)(2,1)S(1)} %constant_dynamic-update-slice_fusion.refs_0_), channel_id=1, source_target_pairs={{0,1},{1,0},{2,3},{3,2},{4,5},{5,4},{6,7},{7,6},{8,9},{9,8},{10,11... | collective-permute-start | bytes 884744 | tf_op jit(solution)/shard_map/ppermute | solution.py:50
  22.5 11.2 %collective-permute-start.10 = (bf16[3,6,48,256]{3,2,1,0:T(8,128)(2,1)S(1)}, bf16[3,6,48,256]{3,2,1,0:T(8,128)(2,1)S(1)}, u32[]{:S(2)}, u32[]{:S(2)}) collective-permute-start(bf16[3,6,48,256]{3,2,1,0:T(8,128)(2,1)S(1)} %pad_maximum_fusion), channel_id=1, source_target_pairs={{0,6},{1,25},{2,4},{3,27},{4,2},{5,29},{6,0},{7,31},{8,14},{9,17},... | collective-permute-start | bytes 1327112 | tf_op jit(solution)/shard_map/ppermute | solution.py:50
  25.0 5.1 %collective-permute-start.7 = (bf16[1,6,48,256]{3,2,1,0:T(8,128)(2,1)S(1)}, bf16[1,6,48,256]{3,2,1,0:T(8,128)(2,1)S(1)}, u32[]{:S(2)}, u32[]{:S(2)}) collective-permute-start(bf16[1,6,48,256]{3,2,1,0:T(8,128)(2,1)S(1)} %collective-permute-done.4), channel_id=1, source_target_pairs={{0,2},{1,7},{2,0},{3,5},{4,6},{5,3},{6,4},{7,1},{8,10},{9,15},{10,... | collective-permute-start | bytes 442376 | tf_op jit(solution)/shard_map/ppermute | solution.py:50
  30.1 6.4 %collective-permute-start.11 = (bf16[1,6,48,256]{3,2,1,0:T(8,128)(2,1)S(1)}, bf16[1,6,48,256]{3,2,1,0:T(8,128)(2,1)S(1)}, u32[]{:S(2)}, u32[]{:S(2)}) collective-permute-start(bf16[1,6,48,256]{3,2,1,0:T(8,128)(2,1)S(1)} %collective-permute-done.7.refs_2_), channel_id=1, source_target_pairs={{0,6},{1,25},{2,4},{3,27},{4,2},{5,29},{6,0},{7,31},{8,14},{9,17},... | collective-permute-start | bytes 442376 | tf_op jit(solution)/shard_map/ppermute | solution.py:50
  36.6 5.1 %collective-permute-start.12 = (bf16[4,6,48,256]{3,2,1,0:T(8,128)(2,1)S(1)}, bf16[4,6,48,256]{3,2,1,0:T(8,128)(2,1)S(1)}, u32[]{:S(2)}, u32[]{:S(2)}) collective-permute-start(bf16[4,6,48,256]{3,2,1,0:T(8,128)(2,1)S(1)} %constant_dynamic-update-slice_fusion.2.refs_0_), channel_id=1, source_target_pairs={{0,1},{1,0},{2,3},{3,2},{4,5},{5,4},{6,7},{7,6},{8,9},{9,8},{10,11... | collective-permute-start | bytes 1769480 | tf_op jit(solution)/shard_map/ppermute | solution.py:50
  38.2 3.5 %collective-permute-start.9 = (bf16[1,6,48,256]{3,2,1,0:T(8,128)(2,1)S(1)}, bf16[1,6,48,256]{3,2,1,0:T(8,128)(2,1)S(1)}, u32[]{:S(2)}, u32[]{:S(2)}) collective-permute-start(bf16[1,6,48,256]{3,2,1,0:T(8,128)(2,1)S(1)} %collective-permute-done.7.refs_2_), channel_id=1, source_target_pairs={{0,1},{1,0},{2,3},{3,2},{4,5},{5,4},{6,7},{7,6},{8,9},{9,8},{10,11... | collective-permute-start | bytes 442376 | tf_op jit(solution)/shard_map/ppermute | solution.py:50
  46.9 1.2 %collective-permute-start.13 = (f32[8,8]{1,0:T(8,128)S(1)}, f32[8,8]{1,0:T(8,128)S(1)}, u32[]{:S(2)}, u32[]{:S(2)}) collective-permute-start(f32[8,8]{1,0:T(8,128)S(1)} %get-tuple-element.168), channel_id=1, source_target_pairs={{0,1},{1,0},{2,3},{3,2},{4,5},{5,4},{6,7},{7,6},{8,9},{9,8},{10,11... | collective-permute-start | bytes 776 | tf_op jit(solution)/shard_map/ppermute | solution.py:50
  48.1 3.6 %collective-permute-start.14 = (f32[8,8]{1,0:T(8,128)S(1)}, f32[8,8]{1,0:T(8,128)S(1)}, u32[]{:S(2)}, u32[]{:S(2)}) collective-permute-start(f32[8,8]{1,0:T(8,128)S(1)} %max.12), channel_id=1, source_target_pairs={{0,2},{1,3},{2,0},{3,1},{4,6},{5,7},{6,4},{7,5},{8,10},{9,11},{10,... | collective-permute-start | bytes 776 | tf_op jit(solution)/shard_map/ppermute | solution.py:50
  51.7 4.8 %collective-permute-start.15 = (f32[8,8]{1,0:T(8,128)S(1)}, f32[8,8]{1,0:T(8,128)S(1)}, u32[]{:S(2)}, u32[]{:S(2)}) collective-permute-start(f32[8,8]{1,0:T(8,128)S(1)} %max.13), channel_id=1, source_target_pairs={{0,6},{1,7},{2,4},{3,5},{4,2},{5,3},{6,0},{7,1},{8,14},{9,15},{10,... | collective-permute-start | bytes 776 | tf_op jit(solution)/shard_map/ppermute | solution.py:50
  56.5 5.1 %collective-permute-start.16 = (f32[8,8]{1,0:T(8,128)S(1)}, f32[8,8]{1,0:T(8,128)S(1)}, u32[]{:S(2)}, u32[]{:S(2)}) collective-permute-start(f32[8,8]{1,0:T(8,128)S(1)} %max.14), channel_id=1, source_target_pairs={{0,8},{1,9},{2,10},{3,11},{4,12},{5,13},{6,14},{7,15},{8,0},{9,1},... | collective-permute-start | bytes 776 | tf_op jit(solution)/shard_map/ppermute | solution.py:50

commit v12 on v10

--- a/solution.py
+++ b/solution.py
@@ -368,11 +368,11 @@
     p2 = swap_with(p0, step_move(1))
     binned = add_bins((p0, q0), ((0, 1, 0), (0, 1, 1)), shared, binned)
     (p1, p2), binned = after((p1, p2), binned)
-    q1, q2 = to_core(p1), to_core(p2)
+    p12 = jnp.concatenate([p1, p2], axis=0)
+    q12 = to_core(p12)
     p3 = swap_with(p1, step_move(1))
     p45 = swap_with(jnp.concatenate([p0, p1], axis=0), step_move(2))
-    binned = add_bins((p1, q1), ((1, 1, 0), (1, 1, 1)), shared, binned)
-    binned = add_bins((p2, q2), ((2, 1, 0), (2, 1, 1)), shared, binned)
+    binned = add_bins((p12, q12), ((1, 2, 0), (1, 2, 1)), shared, binned)
     (p3, p45), binned = after((p3, p45), binned)
     p67 = swap_with(jnp.concatenate([p2, p3], axis=0), step_move(2))
     q3, q45 = to_core(p3), to_core(p45)

time: 61.8 us -> 62.8 us (1.016)
  starting transfers between devices: 21.9 us -> 23.6 us
  waiting for transfers between devices: 17.6 us -> 16.9 us
    ppermute x19 -> x18, starting transfers between devices: 21.9 us -> 23.6 us  [swap_with(): return lax.ppermute(value, AXES, pairs)]
    ppermute x19 -> x18, waiting for transfers between devices: 17.6 us -> 16.9 us  [swap_with(): return lax.ppermute(value, AXES, pairs)]
    pallas_call x7 -> x6, Pallas kernels: 13.9 us -> 13.9 us  [add_bins(): pl.pallas_call(functools.partial(bins_kernel, parts, last), out_shape=out...]
    unnamed x3 -> x4, local copies, waits for them, and re-layouts: 2 us -> 2.01 us
  transfers between devices with their start and end apart: 19 -> 18, of which waited for: 9 -> 9; matrix products, arithmetic and copies ran while one was open for 1% -> 1% of each run, Pallas kernels for 24% -> 24%
where the time goes in v12:
time: 62.8 us; the launch traced here: 62.6 us
  starting transfers between devices  23.6 us (38%)
  Pallas kernels  17.6 us (28%)
  waiting for transfers between devices  16.9 us (27%)
  local copies, waits for them, and re-layouts  2.14 us (3%)
  other arithmetic  1.54 us (2%)
  between operations  0.78 us (1%)
    ppermute x18, starting transfers between devices, swap_with(): return lax.ppermute(value, AXES, pairs)  23.6 us
    ppermute x18, waiting for transfers between devices, swap_with(): return lax.ppermute(value, AXES, pairs)  16.9 us
    pallas_call x6, Pallas kernels, add_bins(): pl.pallas_call(functools.partial(bins_kernel, parts, last), out_shape=out...  13.9 us
    pallas_call x1, Pallas kernels, prepare_tables(): pl.pallas_call(tables_kernel, out_shape=[jax.ShapeDtypeStruct((SLOTS, LAN...  2.03 us
    unnamed x4, local copies, waits for them, and re-layouts  2.01 us
    pallas_call x1, Pallas kernels, prepare_templates(): pl.pallas_call(templates_kernel, out_shape=[jax.ShapeDtypeStruct((SLOTS,...  1.66 us
  transfers between devices with their start and end apart: 18, of which 9 were waited for; matrix products, arithmetic and copies ran while one was open for 1% of the time, Pallas kernels for 24%

profile of v12, /device:TPU:0, one launch (start us, length us, event | category | flops | bytes accessed | tf_op | source)
XLA Modules:
  0.0 62.6 jit_solution(12618585589579862671)
XLA Ops:
  0.0 0.7 %copy.85 = bf16[1,3,2,6,256]{4,3,1,2,0:T(8,128)(2,1)S(1)} copy(bf16[1,3,2,6,256]{4,2,3,1,0:T(2,128)(2,1)} %param.5) | data formatting | bytes 36864 | tf_op args[0]
  0.7 1.6 %collective-permute-start = (bf16[6,6,1,256]{3,0,1,2:T(8,128)(2,1)S(1)}, bf16[6,6,1,256]{3,0,1,2:T(8,128)(2,1)S(1)}, u32[]{:S(2)}, u32[]{:S(2)}) collective-permute-start(bf16[6,6,1,256]{3,0,1,2:T(8,128)(2,1)S(1)} %bitcast.22), channel_id=1, source_target_pairs={{0,32},{1,33},{2,34},{3,35},{4,36},{5,37},{6,38},{7,39},{8,40},{9,... | collective-permute-start | bytes 55304 | tf_op jit(solution)/shard_map/ppermute | solution.py:50
  2.3 2.7 %collective-permute-start.1 = (bf16[6,6,1,256]{3,0,1,2:T(8,128)(2,1)S(1)}, bf16[6,6,1,256]{3,0,1,2:T(8,128)(2,1)S(1)}, u32[]{:S(2)}, u32[]{:S(2)}) collective-permute-start(bf16[6,6,1,256]{3,0,1,2:T(8,128)(2,1)S(1)} %bitcast.23), channel_id=1, source_target_pairs={{0,64},{1,65},{2,66},{3,67},{4,68},{5,69},{6,70},{7,71},{8,72},{9,... | collective-permute-start | bytes 55304 | tf_op jit(solution)/shard_map/ppermute | solution.py:50
  5.0 0.4 collective-permute-start.2
  6.1 0.1 pad.18.clone
  6.2 0.8 %fusion.small_ref = s32[16,128]{1,0:T(8,128)S(1)} fusion(s32[3,8]{1,0:T(4,128)} %bitcast.26, s32[12,15]{1,0:T(8,128)} %param.8, s32[16]{0:T(128)S(1)} %pad.18.clone), kind=kLoop, calls=%fused_computation.9 | loop fusion | flops 8192 | bytes 9072 | tf_op jit(solution)/shard_map/concatenate | solution.py:182
  6.9 2.0 %prepare_tables.1 = (f32[12,128]{1,0:T(8,128)S(1)}, f32[96,2,24,256]{3,2,1,0:T(8,128)S(1)}, bf16[512,256]{1,0:T(8,128)(2,1)S(1)}, f32[2,16,8,128]{3,2,1,0:T(8,12...) custom-call(s32[16,128]{1,0:T(8,128)S(1)} %fusion.small_ref), custom_call_target="tpu_custom_call" | custom-call | flops 1000000 | bytes 1000000 | tf_op jit(solution)/shard_map/prepare_tables/pallas_call | solution.py:190
  9.0 0.0 collective-permute-done
  9.0 0.0 collective-permute-done.1
  9.0 1.1 %collective-permute-done.2 = bf16[6,6,1,256]{3,0,1,2:T(8,128)(2,1)S(1)} collective-permute-done((bf16[6,6,1,256]{3,0,1,2:T(8,128)(2,1)S(1)}, bf16[6,6,1,256]{3,0,1,2:T(8,128)(2,1)S(1)}, u32[]{:S(2)}, u32[]{:S(2)}) %collective-permute-start.2) | collective-permute-done | bytes 18464 | tf_op jit(solution)/shard_map/ppermute | solution.py:50
  10.1 1.7 %collective-permute-start.3 = (bf16[6,6,4,256]{3,0,1,2:T(8,128)(2,1)S(1)}, bf16[6,6,4,256]{3,0,1,2:T(8,128)(2,1)S(1)}, u32[]{:S(2)}, u32[]{:S(2)}) collective-permute-start(bf16[6,6,4,256]{3,0,1,2:T(8,128)(2,1)S(1)} %pad_maximum_fusion.3), channel_id=1, source_target_pairs={{0,16},{1,17},{2,18},{3,19},{4,20},{5,21},{6,22},{7,23},{8,24},{9,... | collective-permute-start | bytes 221192 | tf_op jit(solution)/shard_map/ppermute | solution.py:50
  11.8 1.3 %copy-done = bf16[12,2,96,256]{3,2,1,0:T(8,128)(2,1)S(1)} copy-done((bf16[12,2,96,256]{3,2,1,0:T(8,128)(2,1)S(1)}, bf16[12,2,96,256]{3,2,1,0:T(8,128)(2,1)}, u32[]{:S(2)}) %copy-start) | copy-done | bytes 1179672
  13.0 1.7 %prepare_templates.1 = (f32[12,3,96,256]{3,2,1,0:T(8,128)S(1)}, f32[12,40,128]{2,1,0:T(8,128)S(1)}) custom-call(bf16[12,2,96,256]{3,2,1,0:T(8,128)(2,1)S(1)} %copy-done, s32[16,128]{1,0:T(8,128)S(1)} %fusion.small_ref), custom_call_target="tpu_custom_call" | custom-call | flops 1000000 | bytes 1000000 | tf_op jit(solution)/shard_map/prepare_templates/pallas_call | solution.py:209
  14.7 0.1 collective-permute-done.3
  14.9 0.1 collective-permute-start.6
  15.0 3.1 %collective-permute-start.4 = (bf16[1,6,48,256]{3,2,1,0:T(8,128)(2,1)S(1)}, bf16[1,6,48,256]{3,2,1,0:T(8,128)(2,1)S(1)}, u32[]{:S(2)}, u32[]{:S(2)}) collective-permute-start(bf16[1,6,48,256]{3,2,1,0:T(8,128)(2,1)S(1)} %bitcast.18), channel_id=1, source_target_pairs={{0,24},{1,3},{2,26},{3,1},{4,28},{5,7},{6,30},{7,5},{8,16},{9,11},... | collective-permute-start | bytes 442376 | tf_op jit(solution)/shard_map/ppermute | solution.py:50
  18.1 1.9 %collective-permute-start.5 = (bf16[1,6,48,256]{3,2,1,0:T(8,128)(2,1)S(1)}, bf16[1,6,48,256]{3,2,1,0:T(8,128)(2,1)S(1)}, u32[]{:S(2)}, u32[]{:S(2)}) collective-permute-start(bf16[1,6,48,256]{3,2,1,0:T(8,128)(2,1)S(1)} %bitcast.19), channel_id=1, source_target_pairs={{0,2},{1,7},{2,0},{3,5},{4,6},{5,3},{6,4},{7,1},{8,10},{9,15},{10,... | collective-permute-start | bytes 442376 | tf_op jit(solution)/shard_map/ppermute | solution.py:50
  20.0 0.0 collective-permute-done.6.refs_1_
  20.0 1.6 %add_bins.5 = (f32[16,24,256]{2,1,0:T(8,128)S(1)}, f32[16,24,256]{2,1,0:T(8,128)S(1)}, f32[16,24,256]{2,1,0:T(8,128)S(1)}, f32[16,24,256]{2,1,0:T(8,128)S(1)}, f...) custom-call(bf16[1,6,48,256]{3,2,1,0:T(8,128)(2,1)S(1)} %bitcast.20,, ...), custom_call_target="tpu_custom_call", output_to_operand_aliasing={{0}: (7, {}), {1}: (8, {}), {2}: (9, {}), {3}: (10, {}), {4... | custom-call | flops 1811939328 | bytes 1000000 | tf_op jit(solution)/shard_map/add_bins/pallas_call | solution.py:328
  21.6 0.0 collective-permute-done.4
  21.7 1.6 %collective-permute-done.5 = bf16[1,6,48,256]{3,2,1,0:T(8,128)(2,1)S(1)} collective-permute-done((bf16[1,6,48,256]{3,2,1,0:T(8,128)(2,1)S(1)}, bf16[1,6,48,256]{3,2,1,0:T(8,128)(2,1)S(1)}, u32[]{:S(2)}, u32[]{:S(2)}) %collective-permute-start.5) | collective-permute-done | bytes 147488 | tf_op jit(solution)/shard_map/ppermute | solution.py:50
  23.3 0.1 collective-permute-start.9
  23.4 2.0 %collective-permute-start.7 = (bf16[1,6,48,256]{3,2,1,0:T(8,128)(2,1)S(1)}, bf16[1,6,48,256]{3,2,1,0:T(8,128)(2,1)S(1)}, u32[]{:S(2)}, u32[]{:S(2)}) collective-permute-start(bf16[1,6,48,256]{3,2,1,0:T(8,128)(2,1)S(1)} %collective-permute-done.4), channel_id=1, source_target_pairs={{0,2},{1,7},{2,0},{3,5},{4,6},{5,3},{6,4},{7,1},{8,10},{9,15},{10,... | collective-permute-start | bytes 442376 | tf_op jit(solution)/shard_map/ppermute | solution.py:50
  25.4 2.6 %collective-permute-start.8 = (bf16[2,6,48,256]{3,2,1,0:T(8,128)(2,1)S(1)}, bf16[2,6,48,256]{3,2,1,0:T(8,128)(2,1)S(1)}, u32[]{:S(2)}, u32[]{:S(2)}) collective-permute-start(bf16[2,6,48,256]{3,2,1,0:T(8,128)(2,1)S(1)} %pad_maximum_fusion), channel_id=1, source_target_pairs={{0,6},{1,25},{2,4},{3,27},{4,2},{5,29},{6,0},{7,31},{8,14},{9,17},... | collective-permute-start | bytes 884744 | tf_op jit(solution)/shard_map/ppermute | solution.py:50
  28.0 0.0 collective-permute-done.9.refs_1_
  28.0 3.2 %add_bins.6 = (f32[16,24,256]{2,1,0:T(8,128)S(1)}, f32[16,24,256]{2,1,0:T(8,128)S(1)}, f32[16,24,256]{2,1,0:T(8,128)S(1)}, f32[16,24,256]{2,1,0:T(8,128)S(1)}, f...) custom-call(bf16[2,6,48,256]{3,2,1,0:T(8,128)(2,1)S(1)} %constant_dy, ...), custom_call_target="tpu_custom_call", output_to_operand_aliasing={{0}: (7, {}), {1}: (8, {}), {2}: (9, {}), {3}: (10, {}), {4... | custom-call | flops 3623878656 | bytes 1000000 | tf_op jit(solution)/shard_map/add_bins/pallas_call | solution.py:328
  31.3 0.0 collective-permute-done.7.refs_0_
  31.3 2.2 %collective-permute-done.8.refs_0_ = bf16[2,6,48,256]{3,2,1,0:T(8,128)(2,1)S(1)} collective-permute-done((bf16[2,6,48,256]{3,2,1,0:T(8,128)(2,1)S(1)}, bf16[2,6,48,256]{3,2,1,0:T(8,128)(2,1)S(1)}, u32[]{:S(2)}, u32[]{:S(2)}) %collective-permute-start.8) | collective-permute-done | bytes 294944 | tf_op jit(solution)/shard_map/ppermute | solution.py:50
  33.5 1.0 %collective-permute-start.12 = (bf16[1,6,48,256]{3,2,1,0:T(8,128)(2,1)S(1)}, bf16[1,6,48,256]{3,2,1,0:T(8,128)(2,1)S(1)}, u32[]{:S(2)}, u32[]{:S(2)}) collective-permute-start(bf16[1,6,48,256]{3,2,1,0:T(8,128)(2,1)S(1)} %collective-permute-done.7.refs_0_), channel_id=1, source_target_pairs={{0,1},{1,0},{2,3},{3,2},{4,5},{5,4},{6,7},{7,6},{8,9},{9,8},{10,11... | collective-permute-start | bytes 442376 | tf_op jit(solution)/shard_map/ppermute | solution.py:50
  34.5 0.0 collective-permute-start.11
  34.6 2.7 %collective-permute-start.10 = (bf16[2,6,48,256]{3,2,1,0:T(8,128)(2,1)S(1)}, bf16[2,6,48,256]{3,2,1,0:T(8,128)(2,1)S(1)}, u32[]{:S(2)}, u32[]{:S(2)}) collective-permute-start(bf16[2,6,48,256]{3,2,1,0:T(8,128)(2,1)S(1)} %pad_maximum_fusion.1), channel_id=1, source_target_pairs={{0,6},{1,25},{2,4},{3,27},{4,2},{5,29},{6,0},{7,31},{8,14},{9,17},... | collective-permute-start | bytes 884744 | tf_op jit(solution)/shard_map/ppermute | solution.py:50
  37.3 0.0 collective-permute-done.12.refs_1_
  37.3 1.6 %add_bins.7 = (f32[16,24,256]{2,1,0:T(8,128)S(1)}, f32[16,24,256]{2,1,0:T(8,128)S(1)}, f32[16,24,256]{2,1,0:T(8,128)S(1)}, f32[16,24,256]{2,1,0:T(8,128)S(1)}, f...) custom-call(bf16[1,6,48,256]{3,2,1,0:T(8,128)(2,1)S(1)} %collective-, ...), custom_call_target="tpu_custom_call", output_to_operand_aliasing={{0}: (7, {}), {1}: (8, {}), {2}: (9, {}), {3}: (10, {}), {4... | custom-call | flops 1811939328 | bytes 1000000 | tf_op jit(solution)/shard_map/add_bins/pallas_call | solution.py:328
  38.9 0.0 collective-permute-done.11.refs_1_
  38.9 3.3 %add_bins.8 = (f32[16,24,256]{2,1,0:T(8,128)S(1)}, f32[16,24,256]{2,1,0:T(8,128)S(1)}, f32[16,24,256]{2,1,0:T(8,128)S(1)}, f32[16,24,256]{2,1,0:T(8,128)S(1)}, f...) custom-call(bf16[2,6,48,256]{3,2,1,0:T(8,128)(2,1)S(1)} %collective-, ...), custom_call_target="tpu_custom_call", output_to_operand_aliasing={{0}: (7, {}), {1}: (8, {}), {2}: (9, {}), {3}: (10, {}), {4... | custom-call | flops 3623878656 | bytes 1000000 | tf_op jit(solution)/shard_map/add_bins/pallas_call | solution.py:328
  42.2 0.6 collective-permute-done.10.refs_0_
  42.8 0.0 collective-permute-start.13
  42.8 1.6 %add_bins.9 = (f32[16,24,256]{2,1,0:T(8,128)S(1)}, f32[16,24,256]{2,1,0:T(8,128)S(1)}, f32[16,24,256]{2,1,0:T(8,128)S(1)}, f32[16,24,256]{2,1,0:T(8,128)S(1)}, f...) custom-call(bf16[2,6,48,256]{3,2,1,0:T(8,128)(2,1)S(1)} %collective-, ...), custom_call_target="tpu_custom_call", output_to_operand_aliasing={{0}: (6, {}), {1}: (7, {}), {2}: (8, {}), {3}: (9, {}), {4}... | custom-call | flops 1811939328 | bytes 1000000 | tf_op jit(solution)/shard_map/add_bins/pallas_call | solution.py:328
  44.3 0.0 collective-permute-done.13.refs_0_
  44.4 2.7 %last_bins.1 = (f32[16,24,256]{2,1,0:T(8,128)S(1)}, f32[16,24,256]{2,1,0:T(8,128)S(1)}, f32[16,24,256]{2,1,0:T(8,128)S(1)}, f32[16,24,256]{2,1,0:T(8,128)S(1)}, ...) custom-call(bf16[2,6,48,256]{3,2,1,0:T(8,128)(2,1)S(1)} %collective-, ...), custom_call_target="tpu_custom_call", output_to_operand_aliasing={{0}: (7, {}), {1}: (8, {}), {2}: (9, {}), {3}: (10, {}), {4... | custom-call | flops 1811939328 | bytes 1000000 | tf_op jit(solution)/shard_map/last_bins/pallas_call | solution.py:328
  47.0 0.6 collective-permute-start.14
  47.6 0.8 %collective-permute-done.14 = f32[8,8]{1,0:T(8,128)S(1)} collective-permute-done((f32[8,8]{1,0:T(8,128)S(1)}, f32[8,8]{1,0:T(8,128)S(1)}, u32[]{:S(2)}, u32[]{:S(2)}) %collective-permute-start.14) | collective-permute-done | bytes 288 | tf_op jit(solution)/shard_map/ppermute | solution.py:50
  48.5 3.6 %collective-permute-done.15 = f32[8,8]{1,0:T(8,128)S(1)} collective-permute-done((f32[8,8]{1,0:T(8,128)S(1)}, f32[8,8]{1,0:T(8,128)S(1)}, u32[]{:S(2)}, u32[]{:S(2)}) %collective-permute-start.15) | collective-permute-done | bytes 288 | tf_op jit(solution)/shard_map/ppermute | solution.py:50
  52.1 2.5 %collective-permute-start.16 = (f32[8,8]{1,0:T(8,128)S(1)}, f32[8,8]{1,0:T(8,128)S(1)}, u32[]{:S(2)}, u32[]{:S(2)}) collective-permute-start(f32[8,8]{1,0:T(8,128)S(1)} %max.13), channel_id=1, source_target_pairs={{0,6},{1,7},{2,4},{3,5},{4,2},{5,3},{6,0},{7,1},{8,14},{9,15},{10,... | collective-permute-start | bytes 776 | tf_op jit(solution)/shard_map/ppermute | solution.py:50
  54.5 2.3 %collective-permute-done.16 = f32[8,8]{1,0:T(8,128)S(1)} collective-permute-done((f32[8,8]{1,0:T(8,128)S(1)}, f32[8,8]{1,0:T(8,128)S(1)}, u32[]{:S(2)}, u32[]{:S(2)}) %collective-permute-start.16) | collective-permute-done | bytes 288 | tf_op jit(solution)/shard_map/ppermute | solution.py:50
  56.9 0.7 %collective-permute-start.17 = (f32[8,8]{1,0:T(8,128)S(1)}, f32[8,8]{1,0:T(8,128)S(1)}, u32[]{:S(2)}, u32[]{:S(2)}) collective-permute-start(f32[8,8]{1,0:T(8,128)S(1)} %max.14), channel_id=1, source_target_pairs={{0,8},{1,9},{2,10},{3,11},{4,12},{5,13},{6,14},{7,15},{8,0},{9,1},... | collective-permute-start | bytes 776 | tf_op jit(solution)/shard_map/ppermute | solution.py:50
  57.6 4.4 %collective-permute-done.17 = f32[8,8]{1,0:T(8,128)S(1)} collective-permute-done((f32[8,8]{1,0:T(8,128)S(1)}, f32[8,8]{1,0:T(8,128)S(1)}, u32[]{:S(2)}, u32[]{:S(2)}) %collective-permute-start.17) | collective-permute-done | bytes 288 | tf_op jit(solution)/shard_map/ppermute | solution.py:50
  62.0 0.6 max.15
  (13 shorter events, 0.2 us)
Async XLA Ops:
  0.7 8.2 %collective-permute-start = (bf16[6,6,1,256]{3,0,1,2:T(8,128)(2,1)S(1)}, bf16[6,6,1,256]{3,0,1,2:T(8,128)(2,1)S(1)}, u32[]{:S(2)}, u32[]{:S(2)}) collective-permute-start(bf16[6,6,1,256]{3,0,1,2:T(8,128)(2,1)S(1)} %bitcast.22), channel_id=1, source_target_pairs={{0,32},{1,33},{2,34},{3,35},{4,36},{5,37},{6,38},{7,39},{8,40},{9,... | collective-permute-start | bytes 55304 | tf_op jit(solution)/shard_map/ppermute | solution.py:50
  2.3 6.7 %collective-permute-start.1 = (bf16[6,6,1,256]{3,0,1,2:T(8,128)(2,1)S(1)}, bf16[6,6,1,256]{3,0,1,2:T(8,128)(2,1)S(1)}, u32[]{:S(2)}, u32[]{:S(2)}) collective-permute-start(bf16[6,6,1,256]{3,0,1,2:T(8,128)(2,1)S(1)} %bitcast.23), channel_id=1, source_target_pairs={{0,64},{1,65},{2,66},{3,67},{4,68},{5,69},{6,70},{7,71},{8,72},{9,... | collective-permute-start | bytes 55304 | tf_op jit(solution)/shard_map/ppermute | solution.py:50
  5.0 5.0 %collective-permute-start.2 = (bf16[6,6,1,256]{3,0,1,2:T(8,128)(2,1)S(1)}, bf16[6,6,1,256]{3,0,1,2:T(8,128)(2,1)S(1)}, u32[]{:S(2)}, u32[]{:S(2)}) collective-permute-start(bf16[6,6,1,256]{3,0,1,2:T(8,128)(2,1)S(1)} %bitcast.24), channel_id=1, source_target_pairs={{0,96},{1,97},{2,98},{3,99},{4,100},{5,101},{6,102},{7,103},{8,104... | collective-permute-start | bytes 55304 | tf_op jit(solution)/shard_map/ppermute | solution.py:50
  10.1 4.7 %collective-permute-start.3 = (bf16[6,6,4,256]{3,0,1,2:T(8,128)(2,1)S(1)}, bf16[6,6,4,256]{3,0,1,2:T(8,128)(2,1)S(1)}, u32[]{:S(2)}, u32[]{:S(2)}) collective-permute-start(bf16[6,6,4,256]{3,0,1,2:T(8,128)(2,1)S(1)} %pad_maximum_fusion.3), channel_id=1, source_target_pairs={{0,16},{1,17},{2,18},{3,19},{4,20},{5,21},{6,22},{7,23},{8,24},{9,... | collective-permute-start | bytes 221192 | tf_op jit(solution)/shard_map/ppermute | solution.py:50
  11.8 1.3 %copy-start = (bf16[12,2,96,256]{3,2,1,0:T(8,128)(2,1)S(1)}, bf16[12,2,96,256]{3,2,1,0:T(8,128)(2,1)}, u32[]{:S(2)}) copy-start(bf16[12,2,96,256]{3,2,1,0:T(8,128)(2,1)} %templ_ref.1) | copy-start | bytes 3538948
  14.9 5.1 %collective-permute-start.6 = (bf16[1,6,48,256]{3,2,1,0:T(8,128)(2,1)S(1)}, bf16[1,6,48,256]{3,2,1,0:T(8,128)(2,1)S(1)}, u32[]{:S(2)}, u32[]{:S(2)}) collective-permute-start(bf16[1,6,48,256]{3,2,1,0:T(8,128)(2,1)S(1)} %bitcast.17), channel_id=1, source_target_pairs={{0,1},{1,0},{2,3},{3,2},{4,5},{5,4},{6,7},{7,6},{8,9},{9,8},{10,11... | collective-permute-start | bytes 442376 | tf_op jit(solution)/shard_map/ppermute | solution.py:50
  15.0 6.6 %collective-permute-start.4 = (bf16[1,6,48,256]{3,2,1,0:T(8,128)(2,1)S(1)}, bf16[1,6,48,256]{3,2,1,0:T(8,128)(2,1)S(1)}, u32[]{:S(2)}, u32[]{:S(2)}) collective-permute-start(bf16[1,6,48,256]{3,2,1,0:T(8,128)(2,1)S(1)} %bitcast.18), channel_id=1, source_target_pairs={{0,24},{1,3},{2,26},{3,1},{4,28},{5,7},{6,30},{7,5},{8,16},{9,11},... | collective-permute-start | bytes 442376 | tf_op jit(solution)/shard_map/ppermute | solution.py:50
  18.1 5.1 %collective-permute-start.5 = (bf16[1,6,48,256]{3,2,1,0:T(8,128)(2,1)S(1)}, bf16[1,6,48,256]{3,2,1,0:T(8,128)(2,1)S(1)}, u32[]{:S(2)}, u32[]{:S(2)}) collective-permute-start(bf16[1,6,48,256]{3,2,1,0:T(8,128)(2,1)S(1)} %bitcast.19), channel_id=1, source_target_pairs={{0,2},{1,7},{2,0},{3,5},{4,6},{5,3},{6,4},{7,1},{8,10},{9,15},{10,... | collective-permute-start | bytes 442376 | tf_op jit(solution)/shard_map/ppermute | solution.py:50
  23.3 4.7 %collective-permute-start.9 = (bf16[2,6,48,256]{3,2,1,0:T(8,128)(2,1)S(1)}, bf16[2,6,48,256]{3,2,1,0:T(8,128)(2,1)S(1)}, u32[]{:S(2)}, u32[]{:S(2)}) collective-permute-start(bf16[2,6,48,256]{3,2,1,0:T(8,128)(2,1)S(1)} %constant_dynamic-update-slice_fusion.refs_0_), channel_id=1, source_target_pairs={{0,1},{1,0},{2,3},{3,2},{4,5},{5,4},{6,7},{7,6},{8,9},{9,8},{10,11... | collective-permute-start | bytes 884744 | tf_op jit(solution)/shard_map/ppermute | solution.py:50
  23.4 7.9 %collective-permute-start.7 = (bf16[1,6,48,256]{3,2,1,0:T(8,128)(2,1)S(1)}, bf16[1,6,48,256]{3,2,1,0:T(8,128)(2,1)S(1)}, u32[]{:S(2)}, u32[]{:S(2)}) collective-permute-start(bf16[1,6,48,256]{3,2,1,0:T(8,128)(2,1)S(1)} %collective-permute-done.4), channel_id=1, source_target_pairs={{0,2},{1,7},{2,0},{3,5},{4,6},{5,3},{6,4},{7,1},{8,10},{9,15},{10,... | collective-permute-start | bytes 442376 | tf_op jit(solution)/shard_map/ppermute | solution.py:50
  25.4 8.1 %collective-permute-start.8 = (bf16[2,6,48,256]{3,2,1,0:T(8,128)(2,1)S(1)}, bf16[2,6,48,256]{3,2,1,0:T(8,128)(2,1)S(1)}, u32[]{:S(2)}, u32[]{:S(2)}) collective-permute-start(bf16[2,6,48,256]{3,2,1,0:T(8,128)(2,1)S(1)} %pad_maximum_fusion), channel_id=1, source_target_pairs={{0,6},{1,25},{2,4},{3,27},{4,2},{5,29},{6,0},{7,31},{8,14},{9,17},... | collective-permute-start | bytes 884744 | tf_op jit(solution)/shard_map/ppermute | solution.py:50
  33.5 3.8 %collective-permute-start.12 = (bf16[1,6,48,256]{3,2,1,0:T(8,128)(2,1)S(1)}, bf16[1,6,48,256]{3,2,1,0:T(8,128)(2,1)S(1)}, u32[]{:S(2)}, u32[]{:S(2)}) collective-permute-start(bf16[1,6,48,256]{3,2,1,0:T(8,128)(2,1)S(1)} %collective-permute-done.7.refs_0_), channel_id=1, source_target_pairs={{0,1},{1,0},{2,3},{3,2},{4,5},{5,4},{6,7},{7,6},{8,9},{9,8},{10,11... | collective-permute-start | bytes 442376 | tf_op jit(solution)/shard_map/ppermute | solution.py:50
  34.5 4.3 %collective-permute-start.11 = (bf16[2,6,48,256]{3,2,1,0:T(8,128)(2,1)S(1)}, bf16[2,6,48,256]{3,2,1,0:T(8,128)(2,1)S(1)}, u32[]{:S(2)}, u32[]{:S(2)}) collective-permute-start(bf16[2,6,48,256]{3,2,1,0:T(8,128)(2,1)S(1)} %collective-permute-done.8.refs_0_), channel_id=1, source_target_pairs={{0,1},{1,0},{2,3},{3,2},{4,5},{5,4},{6,7},{7,6},{8,9},{9,8},{10,11... | collective-permute-start | bytes 884744 | tf_op jit(solution)/shard_map/ppermute | solution.py:50
  34.6 8.2 %collective-permute-start.10 = (bf16[2,6,48,256]{3,2,1,0:T(8,128)(2,1)S(1)}, bf16[2,6,48,256]{3,2,1,0:T(8,128)(2,1)S(1)}, u32[]{:S(2)}, u32[]{:S(2)}) collective-permute-start(bf16[2,6,48,256]{3,2,1,0:T(8,128)(2,1)S(1)} %pad_maximum_fusion.1), channel_id=1, source_target_pairs={{0,6},{1,25},{2,4},{3,27},{4,2},{5,29},{6,0},{7,31},{8,14},{9,17},... | collective-permute-start | bytes 884744 | tf_op jit(solution)/shard_map/ppermute | solution.py:50
  42.8 1.6 %collective-permute-start.13 = (bf16[2,6,48,256]{3,2,1,0:T(8,128)(2,1)S(1)}, bf16[2,6,48,256]{3,2,1,0:T(8,128)(2,1)S(1)}, u32[]{:S(2)}, u32[]{:S(2)}) collective-permute-start(bf16[2,6,48,256]{3,2,1,0:T(8,128)(2,1)S(1)} %collective-permute-done.10.refs_0_), channel_id=1, source_target_pairs={{0,1},{1,0},{2,3},{3,2},{4,5},{5,4},{6,7},{7,6},{8,9},{9,8},{10,11... | collective-permute-start | bytes 884744 | tf_op jit(solution)/shard_map/ppermute | solution.py:50
  47.0 1.4 %collective-permute-start.14 = (f32[8,8]{1,0:T(8,128)S(1)}, f32[8,8]{1,0:T(8,128)S(1)}, u32[]{:S(2)}, u32[]{:S(2)}) collective-permute-start(f32[8,8]{1,0:T(8,128)S(1)} %get-tuple-element.192), channel_id=1, source_target_pairs={{0,1},{1,0},{2,3},{3,2},{4,5},{5,4},{6,7},{7,6},{8,9},{9,8},{10,11... | collective-permute-start | bytes 776 | tf_op jit(solution)/shard_map/ppermute | solution.py:50
  48.5 3.6 %collective-permute-start.15 = (f32[8,8]{1,0:T(8,128)S(1)}, f32[8,8]{1,0:T(8,128)S(1)}, u32[]{:S(2)}, u32[]{:S(2)}) collective-permute-start(f32[8,8]{1,0:T(8,128)S(1)} %max.12), channel_id=1, source_target_pairs={{0,2},{1,3},{2,0},{3,1},{4,6},{5,7},{6,4},{7,5},{8,10},{9,11},{10,... | collective-permute-start | bytes 776 | tf_op jit(solution)/shard_map/ppermute | solution.py:50
  52.1 4.8 %collective-permute-start.16 = (f32[8,8]{1,0:T(8,128)S(1)}, f32[8,8]{1,0:T(8,128)S(1)}, u32[]{:S(2)}, u32[]{:S(2)}) collective-permute-start(f32[8,8]{1,0:T(8,128)S(1)} %max.13), channel_id=1, source_target_pairs={{0,6},{1,7},{2,4},{3,5},{4,2},{5,3},{6,0},{7,1},{8,14},{9,15},{10,... | collective-permute-start | bytes 776 | tf_op jit(solution)/shard_map/ppermute | solution.py:50
  56.9 5.1 %collective-permute-start.17 = (f32[8,8]{1,0:T(8,128)S(1)}, f32[8,8]{1,0:T(8,128)S(1)}, u32[]{:S(2)}, u32[]{:S(2)}) collective-permute-start(f32[8,8]{1,0:T(8,128)S(1)} %max.14), channel_id=1, source_target_pairs={{0,8},{1,9},{2,10},{3,11},{4,12},{5,13},{6,14},{7,15},{8,0},{9,1},... | collective-permute-start | bytes 776 | tf_op jit(solution)/shard_map/ppermute | solution.py:50

commit v13 on v10

--- a/solution.py
+++ b/solution.py
@@ -51,8 +51,8 @@
 
 
 STEPS = (
-    ({"dy": 3}, {"dz": 1}),
-    ({"dz": 1}, {"dz": 3}),
+    ({"dy": 3}, {"dz": 3}),
+    ({"dz": 1}, {"dz": 1}),
     ({"dz": 3}, {"dy": 3}),
 )
 

time: 61.8 us -> 60.5 us (0.979)
  waiting for transfers between devices: 17.6 us -> 13.1 us
  starting transfers between devices: 21.9 us -> 25 us
    ppermute x19, waiting for transfers between devices: 17.6 us -> 13.1 us  [swap_with(): return lax.ppermute(value, AXES, pairs)]
    ppermute x19, starting transfers between devices: 21.9 us -> 25 us  [swap_with(): return lax.ppermute(value, AXES, pairs)]
  transfers between devices with their start and end apart: 19 -> 19, of which waited for: 9 -> 8; matrix products, arithmetic and copies ran while one was open for 1% -> 2% of each run, Pallas kernels for 24% -> 25%
where the time goes in v13:
time: 60.5 us; the launch traced here: 60.2 us
  starting transfers between devices  25 us (41%)
  Pallas kernels  17.6 us (29%)
  waiting for transfers between devices  13.1 us (22%)
  local copies, waits for them, and re-layouts  2.12 us (4%)
  other arithmetic  1.54 us (3%)
  between operations  0.79 us (1%)
    ppermute x19, starting transfers between devices, swap_with(): return lax.ppermute(value, AXES, pairs)  25 us
    pallas_call x7, Pallas kernels, add_bins(): pl.pallas_call(functools.partial(bins_kernel, parts, last), out_shape=out...  14 us
    ppermute x19, waiting for transfers between devices, swap_with(): return lax.ppermute(value, AXES, pairs)  13.1 us
    pallas_call x1, Pallas kernels, prepare_tables(): pl.pallas_call(tables_kernel, out_shape=[jax.ShapeDtypeStruct((SLOTS, LAN...  2.03 us
    unnamed x3, local copies, waits for them, and re-layouts  2 us
    pallas_call x1, Pallas kernels, prepare_templates(): pl.pallas_call(templates_kernel, out_shape=[jax.ShapeDtypeStruct((SLOTS,...  1.66 us
  transfers between devices with their start and end apart: 19, of which 8 were waited for; matrix products, arithmetic and copies ran while one was open for 2% of the time, Pallas kernels for 25%

profile of v13, /device:TPU:0, one launch (start us, length us, event | category | flops | bytes accessed | tf_op | source)
XLA Modules:
  0.0 60.2 jit_solution(6488718543068114482)
XLA Ops:
  0.0 0.7 %copy.97 = bf16[1,3,2,6,256]{4,3,1,2,0:T(8,128)(2,1)S(1)} copy(bf16[1,3,2,6,256]{4,2,3,1,0:T(2,128)(2,1)} %param.5) | data formatting | bytes 36864 | tf_op args[0]
  0.7 2.8 %collective-permute-start.2 = (bf16[6,6,1,256]{3,0,1,2:T(8,128)(2,1)S(1)}, bf16[6,6,1,256]{3,0,1,2:T(8,128)(2,1)S(1)}, u32[]{:S(2)}, u32[]{:S(2)}) collective-permute-start(bf16[6,6,1,256]{3,0,1,2:T(8,128)(2,1)S(1)} %bitcast.22), channel_id=1, source_target_pairs={{0,96},{1,97},{2,98},{3,99},{4,100},{5,101},{6,102},{7,103},{8,104... | collective-permute-start | bytes 55304 | tf_op jit(solution)/shard_map/ppermute | solution.py:50
  3.6 0.8 %collective-permute-start.1 = (bf16[6,6,1,256]{3,0,1,2:T(8,128)(2,1)S(1)}, bf16[6,6,1,256]{3,0,1,2:T(8,128)(2,1)S(1)}, u32[]{:S(2)}, u32[]{:S(2)}) collective-permute-start(bf16[6,6,1,256]{3,0,1,2:T(8,128)(2,1)S(1)} %bitcast.23), channel_id=1, source_target_pairs={{0,64},{1,65},{2,66},{3,67},{4,68},{5,69},{6,70},{7,71},{8,72},{9,... | collective-permute-start | bytes 55304 | tf_op jit(solution)/shard_map/ppermute | solution.py:50
  4.4 0.5 collective-permute-start
  5.5 0.1 pad.18.clone
  5.5 0.8 %fusion.small_ref = s32[16,128]{1,0:T(8,128)S(1)} fusion(s32[3,8]{1,0:T(4,128)} %bitcast.26, s32[12,15]{1,0:T(8,128)} %param.8, s32[16]{0:T(128)S(1)} %pad.18.clone), kind=kLoop, calls=%fused_computation.9 | loop fusion | flops 8192 | bytes 9072 | tf_op jit(solution)/shard_map/concatenate | solution.py:182
  6.3 2.0 %prepare_tables.1 = (f32[12,128]{1,0:T(8,128)S(1)}, f32[96,2,24,256]{3,2,1,0:T(8,128)S(1)}, bf16[512,256]{1,0:T(8,128)(2,1)S(1)}, f32[2,16,8,128]{3,2,1,0:T(8,12...) custom-call(s32[16,128]{1,0:T(8,128)S(1)} %fusion.small_ref), custom_call_target="tpu_custom_call" | custom-call | flops 1000000 | bytes 1000000 | tf_op jit(solution)/shard_map/prepare_tables/pallas_call | solution.py:190
  8.4 0.0 collective-permute-done.2
  8.4 0.5 collective-permute-done.1
  8.9 0.0 collective-permute-done
  8.9 1.7 %collective-permute-start.3 = (bf16[6,6,4,256]{3,0,1,2:T(8,128)(2,1)S(1)}, bf16[6,6,4,256]{3,0,1,2:T(8,128)(2,1)S(1)}, u32[]{:S(2)}, u32[]{:S(2)}) collective-permute-start(bf16[6,6,4,256]{3,0,1,2:T(8,128)(2,1)S(1)} %pad_maximum_fusion.3), channel_id=1, source_target_pairs={{0,16},{1,17},{2,18},{3,19},{4,20},{5,21},{6,22},{7,23},{8,24},{9,... | collective-permute-start | bytes 221192 | tf_op jit(solution)/shard_map/ppermute | solution.py:50
  10.6 1.3 %copy-done = bf16[12,2,96,256]{3,2,1,0:T(8,128)(2,1)S(1)} copy-done((bf16[12,2,96,256]{3,2,1,0:T(8,128)(2,1)S(1)}, bf16[12,2,96,256]{3,2,1,0:T(8,128)(2,1)}, u32[]{:S(2)}) %copy-start) | copy-done | bytes 1179672
  11.9 1.7 %prepare_templates.1 = (f32[12,3,96,256]{3,2,1,0:T(8,128)S(1)}, f32[12,40,128]{2,1,0:T(8,128)S(1)}) custom-call(bf16[12,2,96,256]{3,2,1,0:T(8,128)(2,1)S(1)} %copy-done, s32[16,128]{1,0:T(8,128)S(1)} %fusion.small_ref), custom_call_target="tpu_custom_call" | custom-call | flops 1000000 | bytes 1000000 | tf_op jit(solution)/shard_map/prepare_templates/pallas_call | solution.py:209
  13.5 0.1 collective-permute-done.3
  13.8 0.1 collective-permute-start.6
  13.9 2.0 %collective-permute-start.5 = (bf16[1,6,48,256]{3,2,1,0:T(8,128)(2,1)S(1)}, bf16[1,6,48,256]{3,2,1,0:T(8,128)(2,1)S(1)}, u32[]{:S(2)}, u32[]{:S(2)}) collective-permute-start(bf16[1,6,48,256]{3,2,1,0:T(8,128)(2,1)S(1)} %bitcast.18), channel_id=1, source_target_pairs={{0,2},{1,3},{2,0},{3,1},{4,6},{5,7},{6,4},{7,5},{8,10},{9,11},{10,... | collective-permute-start | bytes 442376 | tf_op jit(solution)/shard_map/ppermute | solution.py:50
  15.9 3.0 %collective-permute-start.4 = (bf16[1,6,48,256]{3,2,1,0:T(8,128)(2,1)S(1)}, bf16[1,6,48,256]{3,2,1,0:T(8,128)(2,1)S(1)}, u32[]{:S(2)}, u32[]{:S(2)}) collective-permute-start(bf16[1,6,48,256]{3,2,1,0:T(8,128)(2,1)S(1)} %bitcast.19), channel_id=1, source_target_pairs={{0,24},{1,7},{2,26},{3,5},{4,28},{5,3},{6,30},{7,1},{8,16},{9,15},... | collective-permute-start | bytes 442376 | tf_op jit(solution)/shard_map/ppermute | solution.py:50
  18.9 0.0 collective-permute-done.6.refs_1_
  18.9 1.6 %add_bins.6 = (f32[16,24,256]{2,1,0:T(8,128)S(1)}, f32[16,24,256]{2,1,0:T(8,128)S(1)}, f32[16,24,256]{2,1,0:T(8,128)S(1)}, f32[16,24,256]{2,1,0:T(8,128)S(1)}, f...) custom-call(bf16[1,6,48,256]{3,2,1,0:T(8,128)(2,1)S(1)} %bitcast.20,, ...), custom_call_target="tpu_custom_call", output_to_operand_aliasing={{0}: (7, {}), {1}: (8, {}), {2}: (9, {}), {3}: (10, {}), {4... | custom-call | flops 1811939328 | bytes 1000000 | tf_op jit(solution)/shard_map/add_bins/pallas_call | solution.py:328
  20.5 0.0 collective-permute-done.5.refs_0_
  20.5 1.7 %collective-permute-done.4.refs_0_ = bf16[1,6,48,256]{3,2,1,0:T(8,128)(2,1)S(1)} collective-permute-done((bf16[1,6,48,256]{3,2,1,0:T(8,128)(2,1)S(1)}, bf16[1,6,48,256]{3,2,1,0:T(8,128)(2,1)S(1)}, u32[]{:S(2)}, u32[]{:S(2)}) %collective-permute-start.4) | collective-permute-done | bytes 147488 | tf_op jit(solution)/shard_map/ppermute | solution.py:50
  22.2 0.0 collective-permute-start.10
  22.2 0.1 collective-permute-start.7
  22.3 0.4 collective-permute-start.9
  22.8 3.9 %collective-permute-start.8 = (bf16[2,6,48,256]{3,2,1,0:T(8,128)(2,1)S(1)}, bf16[2,6,48,256]{3,2,1,0:T(8,128)(2,1)S(1)}, u32[]{:S(2)}, u32[]{:S(2)}) collective-permute-start(bf16[2,6,48,256]{3,2,1,0:T(8,128)(2,1)S(1)} %pad_maximum_fusion), channel_id=1, source_target_pairs={{0,6},{1,25},{2,4},{3,27},{4,2},{5,29},{6,0},{7,31},{8,14},{9,17},... | collective-permute-start | bytes 884744 | tf_op jit(solution)/shard_map/ppermute | solution.py:50
  26.7 0.0 collective-permute-done.10.refs_1_
  26.7 1.6 %add_bins.7 = (f32[16,24,256]{2,1,0:T(8,128)S(1)}, f32[16,24,256]{2,1,0:T(8,128)S(1)}, f32[16,24,256]{2,1,0:T(8,128)S(1)}, f32[16,24,256]{2,1,0:T(8,128)S(1)}, f...) custom-call(bf16[1,6,48,256]{3,2,1,0:T(8,128)(2,1)S(1)} %collective-, ...), custom_call_target="tpu_custom_call", output_to_operand_aliasing={{0}: (7, {}), {1}: (8, {}), {2}: (9, {}), {3}: (10, {}), {4... | custom-call | flops 1811939328 | bytes 1000000 | tf_op jit(solution)/shard_map/add_bins/pallas_call | solution.py:328
  28.3 0.0 collective-permute-done.9.refs_1_
  28.3 1.6 %add_bins.8 = (f32[16,24,256]{2,1,0:T(8,128)S(1)}, f32[16,24,256]{2,1,0:T(8,128)S(1)}, f32[16,24,256]{2,1,0:T(8,128)S(1)}, f32[16,24,256]{2,1,0:T(8,128)S(1)}, f...) custom-call(bf16[1,6,48,256]{3,2,1,0:T(8,128)(2,1)S(1)} %collective-, ...), custom_call_target="tpu_custom_call", output_to_operand_aliasing={{0}: (7, {}), {1}: (8, {}), {2}: (9, {}), {3}: (10, {}), {4... | custom-call | flops 1811939328 | bytes 1000000 | tf_op jit(solution)/shard_map/add_bins/pallas_call | solution.py:328
  30.0 1.4 %collective-permute-done.8.refs_0_ = bf16[2,6,48,256]{3,2,1,0:T(8,128)(2,1)S(1)} collective-permute-done((bf16[2,6,48,256]{3,2,1,0:T(8,128)(2,1)S(1)}, bf16[2,6,48,256]{3,2,1,0:T(8,128)(2,1)S(1)}, u32[]{:S(2)}, u32[]{:S(2)}) %collective-permute-start.8) | collective-permute-done | bytes 294944 | tf_op jit(solution)/shard_map/ppermute | solution.py:50
  31.4 0.0 collective-permute-start.13
  31.4 0.5 collective-permute-start.12
  31.9 3.5 %collective-permute-start.11 = (bf16[2,6,48,256]{3,2,1,0:T(8,128)(2,1)S(1)}, bf16[2,6,48,256]{3,2,1,0:T(8,128)(2,1)S(1)}, u32[]{:S(2)}, u32[]{:S(2)}) collective-permute-start(bf16[2,6,48,256]{3,2,1,0:T(8,128)(2,1)S(1)} %pad_maximum_fusion.1), channel_id=1, source_target_pairs={{0,6},{1,25},{2,4},{3,27},{4,2},{5,29},{6,0},{7,31},{8,14},{9,17},... | collective-permute-start | bytes 884744 | tf_op jit(solution)/shard_map/ppermute | solution.py:50
  35.4 1.6 %add_bins.9 = (f32[16,24,256]{2,1,0:T(8,128)S(1)}, f32[16,24,256]{2,1,0:T(8,128)S(1)}, f32[16,24,256]{2,1,0:T(8,128)S(1)}, f32[16,24,256]{2,1,0:T(8,128)S(1)}, f...) custom-call(bf16[1,6,48,256]{3,2,1,0:T(8,128)(2,1)S(1)} %collective-, ...), custom_call_target="tpu_custom_call", output_to_operand_aliasing={{0}: (7, {}), {1}: (8, {}), {2}: (9, {}), {3}: (10, {}), {4... | custom-call | flops 1811939328 | bytes 1000000 | tf_op jit(solution)/shard_map/add_bins/pallas_call | solution.py:328
  37.1 3.2 %add_bins.10 = (f32[16,24,256]{2,1,0:T(8,128)S(1)}, f32[16,24,256]{2,1,0:T(8,128)S(1)}, f32[16,24,256]{2,1,0:T(8,128)S(1)}, f32[16,24,256]{2,1,0:T(8,128)S(1)}, ...) custom-call(bf16[2,6,48,256]{3,2,1,0:T(8,128)(2,1)S(1)} %collective-, ...), custom_call_target="tpu_custom_call", output_to_operand_aliasing={{0}: (7, {}), {1}: (8, {}), {2}: (9, {}), {3}: (10, {}), {4... | custom-call | flops 3623878656 | bytes 1000000 | tf_op jit(solution)/shard_map/add_bins/pallas_call | solution.py:328
  40.3 0.0 collective-permute-done.11.refs_0_
  40.3 0.1 collective-permute-start.14
  40.4 1.6 %add_bins.11 = (f32[16,24,256]{2,1,0:T(8,128)S(1)}, f32[16,24,256]{2,1,0:T(8,128)S(1)}, f32[16,24,256]{2,1,0:T(8,128)S(1)}, f32[16,24,256]{2,1,0:T(8,128)S(1)}, ...) custom-call(bf16[2,6,48,256]{3,2,1,0:T(8,128)(2,1)S(1)} %collective-, ...), custom_call_target="tpu_custom_call", output_to_operand_aliasing={{0}: (6, {}), {1}: (7, {}), {2}: (8, {}), {3}: (9, {}), {4}... | custom-call | flops 1811939328 | bytes 1000000 | tf_op jit(solution)/shard_map/add_bins/pallas_call | solution.py:328
  42.0 2.7 %last_bins.1 = (f32[16,24,256]{2,1,0:T(8,128)S(1)}, f32[16,24,256]{2,1,0:T(8,128)S(1)}, f32[16,24,256]{2,1,0:T(8,128)S(1)}, f32[16,24,256]{2,1,0:T(8,128)S(1)}, ...) custom-call(bf16[2,6,48,256]{3,2,1,0:T(8,128)(2,1)S(1)} %collective-, ...), custom_call_target="tpu_custom_call", output_to_operand_aliasing={{0}: (7, {}), {1}: (8, {}), {2}: (9, {}), {3}: (10, {}), {4... | custom-call | flops 1811939328 | bytes 1000000 | tf_op jit(solution)/shard_map/last_bins/pallas_call | solution.py:328
  44.7 0.6 collective-permute-start.15
  45.2 0.8 %collective-permute-done.15 = f32[8,8]{1,0:T(8,128)S(1)} collective-permute-done((f32[8,8]{1,0:T(8,128)S(1)}, f32[8,8]{1,0:T(8,128)S(1)}, u32[]{:S(2)}, u32[]{:S(2)}) %collective-permute-start.15) | collective-permute-done | bytes 288 | tf_op jit(solution)/shard_map/ppermute | solution.py:50
  46.1 0.0 collective-permute-start.16
  46.1 3.6 %collective-permute-done.16 = f32[8,8]{1,0:T(8,128)S(1)} collective-permute-done((f32[8,8]{1,0:T(8,128)S(1)}, f32[8,8]{1,0:T(8,128)S(1)}, u32[]{:S(2)}, u32[]{:S(2)}) %collective-permute-start.16) | collective-permute-done | bytes 288 | tf_op jit(solution)/shard_map/ppermute | solution.py:50
  49.7 3.0 %collective-permute-start.17 = (f32[8,8]{1,0:T(8,128)S(1)}, f32[8,8]{1,0:T(8,128)S(1)}, u32[]{:S(2)}, u32[]{:S(2)}) collective-permute-start(f32[8,8]{1,0:T(8,128)S(1)} %max.13), channel_id=1, source_target_pairs={{0,6},{1,7},{2,4},{3,5},{4,2},{5,3},{6,0},{7,1},{8,14},{9,15},{10,... | collective-permute-start | bytes 776 | tf_op jit(solution)/shard_map/ppermute | solution.py:50
  52.7 1.8 %collective-permute-done.17 = f32[8,8]{1,0:T(8,128)S(1)} collective-permute-done((f32[8,8]{1,0:T(8,128)S(1)}, f32[8,8]{1,0:T(8,128)S(1)}, u32[]{:S(2)}, u32[]{:S(2)}) %collective-permute-start.17) | collective-permute-done | bytes 288 | tf_op jit(solution)/shard_map/ppermute | solution.py:50
  54.5 2.0 %collective-permute-start.18 = (f32[8,8]{1,0:T(8,128)S(1)}, f32[8,8]{1,0:T(8,128)S(1)}, u32[]{:S(2)}, u32[]{:S(2)}) collective-permute-start(f32[8,8]{1,0:T(8,128)S(1)} %max.14), channel_id=1, source_target_pairs={{0,8},{1,9},{2,10},{3,11},{4,12},{5,13},{6,14},{7,15},{8,0},{9,1},... | collective-permute-start | bytes 776 | tf_op jit(solution)/shard_map/ppermute | solution.py:50
  56.5 3.1 %collective-permute-done.18 = f32[8,8]{1,0:T(8,128)S(1)} collective-permute-done((f32[8,8]{1,0:T(8,128)S(1)}, f32[8,8]{1,0:T(8,128)S(1)}, u32[]{:S(2)}, u32[]{:S(2)}) %collective-permute-start.18) | collective-permute-done | bytes 288 | tf_op jit(solution)/shard_map/ppermute | solution.py:50
  59.6 0.6 max.15
  (14 shorter events, 0.2 us)
Async XLA Ops:
  0.7 7.6 %collective-permute-start.2 = (bf16[6,6,1,256]{3,0,1,2:T(8,128)(2,1)S(1)}, bf16[6,6,1,256]{3,0,1,2:T(8,128)(2,1)S(1)}, u32[]{:S(2)}, u32[]{:S(2)}) collective-permute-start(bf16[6,6,1,256]{3,0,1,2:T(8,128)(2,1)S(1)} %bitcast.22), channel_id=1, source_target_pairs={{0,96},{1,97},{2,98},{3,99},{4,100},{5,101},{6,102},{7,103},{8,104... | collective-permute-start | bytes 55304 | tf_op jit(solution)/shard_map/ppermute | solution.py:50
  3.6 5.3 %collective-permute-start.1 = (bf16[6,6,1,256]{3,0,1,2:T(8,128)(2,1)S(1)}, bf16[6,6,1,256]{3,0,1,2:T(8,128)(2,1)S(1)}, u32[]{:S(2)}, u32[]{:S(2)}) collective-permute-start(bf16[6,6,1,256]{3,0,1,2:T(8,128)(2,1)S(1)} %bitcast.23), channel_id=1, source_target_pairs={{0,64},{1,65},{2,66},{3,67},{4,68},{5,69},{6,70},{7,71},{8,72},{9,... | collective-permute-start | bytes 55304 | tf_op jit(solution)/shard_map/ppermute | solution.py:50
  4.4 4.5 %collective-permute-start = (bf16[6,6,1,256]{3,0,1,2:T(8,128)(2,1)S(1)}, bf16[6,6,1,256]{3,0,1,2:T(8,128)(2,1)S(1)}, u32[]{:S(2)}, u32[]{:S(2)}) collective-permute-start(bf16[6,6,1,256]{3,0,1,2:T(8,128)(2,1)S(1)} %bitcast.24), channel_id=1, source_target_pairs={{0,32},{1,33},{2,34},{3,35},{4,36},{5,37},{6,38},{7,39},{8,40},{9,... | collective-permute-start | bytes 55304 | tf_op jit(solution)/shard_map/ppermute | solution.py:50
  8.9 4.7 %collective-permute-start.3 = (bf16[6,6,4,256]{3,0,1,2:T(8,128)(2,1)S(1)}, bf16[6,6,4,256]{3,0,1,2:T(8,128)(2,1)S(1)}, u32[]{:S(2)}, u32[]{:S(2)}) collective-permute-start(bf16[6,6,4,256]{3,0,1,2:T(8,128)(2,1)S(1)} %pad_maximum_fusion.3), channel_id=1, source_target_pairs={{0,16},{1,17},{2,18},{3,19},{4,20},{5,21},{6,22},{7,23},{8,24},{9,... | collective-permute-start | bytes 221192 | tf_op jit(solution)/shard_map/ppermute | solution.py:50
  10.6 1.3 %copy-start = (bf16[12,2,96,256]{3,2,1,0:T(8,128)(2,1)S(1)}, bf16[12,2,96,256]{3,2,1,0:T(8,128)(2,1)}, u32[]{:S(2)}) copy-start(bf16[12,2,96,256]{3,2,1,0:T(8,128)(2,1)} %templ_ref.1) | copy-start | bytes 3538948
  13.8 5.1 %collective-permute-start.6 = (bf16[1,6,48,256]{3,2,1,0:T(8,128)(2,1)S(1)}, bf16[1,6,48,256]{3,2,1,0:T(8,128)(2,1)S(1)}, u32[]{:S(2)}, u32[]{:S(2)}) collective-permute-start(bf16[1,6,48,256]{3,2,1,0:T(8,128)(2,1)S(1)} %bitcast.17), channel_id=1, source_target_pairs={{0,1},{1,0},{2,3},{3,2},{4,5},{5,4},{6,7},{7,6},{8,9},{9,8},{10,11... | collective-permute-start | bytes 442376 | tf_op jit(solution)/shard_map/ppermute | solution.py:50
  13.9 6.6 %collective-permute-start.5 = (bf16[1,6,48,256]{3,2,1,0:T(8,128)(2,1)S(1)}, bf16[1,6,48,256]{3,2,1,0:T(8,128)(2,1)S(1)}, u32[]{:S(2)}, u32[]{:S(2)}) collective-permute-start(bf16[1,6,48,256]{3,2,1,0:T(8,128)(2,1)S(1)} %bitcast.18), channel_id=1, source_target_pairs={{0,2},{1,3},{2,0},{3,1},{4,6},{5,7},{6,4},{7,5},{8,10},{9,11},{10,... | collective-permute-start | bytes 442376 | tf_op jit(solution)/shard_map/ppermute | solution.py:50
  15.9 6.4 %collective-permute-start.4 = (bf16[1,6,48,256]{3,2,1,0:T(8,128)(2,1)S(1)}, bf16[1,6,48,256]{3,2,1,0:T(8,128)(2,1)S(1)}, u32[]{:S(2)}, u32[]{:S(2)}) collective-permute-start(bf16[1,6,48,256]{3,2,1,0:T(8,128)(2,1)S(1)} %bitcast.19), channel_id=1, source_target_pairs={{0,24},{1,7},{2,26},{3,5},{4,28},{5,3},{6,30},{7,1},{8,16},{9,15},... | collective-permute-start | bytes 442376 | tf_op jit(solution)/shard_map/ppermute | solution.py:50
  22.2 4.5 %collective-permute-start.10 = (bf16[1,6,48,256]{3,2,1,0:T(8,128)(2,1)S(1)}, bf16[1,6,48,256]{3,2,1,0:T(8,128)(2,1)S(1)}, u32[]{:S(2)}, u32[]{:S(2)}) collective-permute-start(bf16[1,6,48,256]{3,2,1,0:T(8,128)(2,1)S(1)} %collective-permute-done.4.refs_0_), channel_id=1, source_target_pairs={{0,1},{1,0},{2,3},{3,2},{4,5},{5,4},{6,7},{7,6},{8,9},{9,8},{10,11... | collective-permute-start | bytes 442376 | tf_op jit(solution)/shard_map/ppermute | solution.py:50
  22.2 7.7 %collective-permute-start.7 = (bf16[1,6,48,256]{3,2,1,0:T(8,128)(2,1)S(1)}, bf16[1,6,48,256]{3,2,1,0:T(8,128)(2,1)S(1)}, u32[]{:S(2)}, u32[]{:S(2)}) collective-permute-start(bf16[1,6,48,256]{3,2,1,0:T(8,128)(2,1)S(1)} %collective-permute-done.4.refs_0_), channel_id=1, source_target_pairs={{0,2},{1,3},{2,0},{3,1},{4,6},{5,7},{6,4},{7,5},{8,10},{9,11},{10,... | collective-permute-start | bytes 442376 | tf_op jit(solution)/shard_map/ppermute | solution.py:50
  22.3 6.0 %collective-permute-start.9 = (bf16[1,6,48,256]{3,2,1,0:T(8,128)(2,1)S(1)}, bf16[1,6,48,256]{3,2,1,0:T(8,128)(2,1)S(1)}, u32[]{:S(2)}, u32[]{:S(2)}) collective-permute-start(bf16[1,6,48,256]{3,2,1,0:T(8,128)(2,1)S(1)} %collective-permute-done.5.refs_0_), channel_id=1, source_target_pairs={{0,1},{1,0},{2,3},{3,2},{4,5},{5,4},{6,7},{7,6},{8,9},{9,8},{10,11... | collective-permute-start | bytes 442376 | tf_op jit(solution)/shard_map/ppermute | solution.py:50
  22.8 8.6 %collective-permute-start.8 = (bf16[2,6,48,256]{3,2,1,0:T(8,128)(2,1)S(1)}, bf16[2,6,48,256]{3,2,1,0:T(8,128)(2,1)S(1)}, u32[]{:S(2)}, u32[]{:S(2)}) collective-permute-start(bf16[2,6,48,256]{3,2,1,0:T(8,128)(2,1)S(1)} %pad_maximum_fusion), channel_id=1, source_target_pairs={{0,6},{1,25},{2,4},{3,27},{4,2},{5,29},{6,0},{7,31},{8,14},{9,17},... | collective-permute-start | bytes 884744 | tf_op jit(solution)/shard_map/ppermute | solution.py:50
  31.4 4.0 %collective-permute-start.13 = (bf16[1,6,48,256]{3,2,1,0:T(8,128)(2,1)S(1)}, bf16[1,6,48,256]{3,2,1,0:T(8,128)(2,1)S(1)}, u32[]{:S(2)}, u32[]{:S(2)}) collective-permute-start(bf16[1,6,48,256]{3,2,1,0:T(8,128)(2,1)S(1)} %collective-permute-done.7.refs_0_), channel_id=1, source_target_pairs={{0,1},{1,0},{2,3},{3,2},{4,5},{5,4},{6,7},{7,6},{8,9},{9,8},{10,11... | collective-permute-start | bytes 442376 | tf_op jit(solution)/shard_map/ppermute | solution.py:50
  31.4 5.6 %collective-permute-start.12 = (bf16[2,6,48,256]{3,2,1,0:T(8,128)(2,1)S(1)}, bf16[2,6,48,256]{3,2,1,0:T(8,128)(2,1)S(1)}, u32[]{:S(2)}, u32[]{:S(2)}) collective-permute-start(bf16[2,6,48,256]{3,2,1,0:T(8,128)(2,1)S(1)} %collective-permute-done.8.refs_0_), channel_id=1, source_target_pairs={{0,1},{1,0},{2,3},{3,2},{4,5},{5,4},{6,7},{7,6},{8,9},{9,8},{10,11... | collective-permute-start | bytes 884744 | tf_op jit(solution)/shard_map/ppermute | solution.py:50
  31.9 8.3 %collective-permute-start.11 = (bf16[2,6,48,256]{3,2,1,0:T(8,128)(2,1)S(1)}, bf16[2,6,48,256]{3,2,1,0:T(8,128)(2,1)S(1)}, u32[]{:S(2)}, u32[]{:S(2)}) collective-permute-start(bf16[2,6,48,256]{3,2,1,0:T(8,128)(2,1)S(1)} %pad_maximum_fusion.1), channel_id=1, source_target_pairs={{0,6},{1,25},{2,4},{3,27},{4,2},{5,29},{6,0},{7,31},{8,14},{9,17},... | collective-permute-start | bytes 884744 | tf_op jit(solution)/shard_map/ppermute | solution.py:50
  40.3 1.7 %collective-permute-start.14 = (bf16[2,6,48,256]{3,2,1,0:T(8,128)(2,1)S(1)}, bf16[2,6,48,256]{3,2,1,0:T(8,128)(2,1)S(1)}, u32[]{:S(2)}, u32[]{:S(2)}) collective-permute-start(bf16[2,6,48,256]{3,2,1,0:T(8,128)(2,1)S(1)} %collective-permute-done.11.refs_0_), channel_id=1, source_target_pairs={{0,1},{1,0},{2,3},{3,2},{4,5},{5,4},{6,7},{7,6},{8,9},{9,8},{10,11... | collective-permute-start | bytes 884744 | tf_op jit(solution)/shard_map/ppermute | solution.py:50
  44.7 1.4 %collective-permute-start.15 = (f32[8,8]{1,0:T(8,128)S(1)}, f32[8,8]{1,0:T(8,128)S(1)}, u32[]{:S(2)}, u32[]{:S(2)}) collective-permute-start(f32[8,8]{1,0:T(8,128)S(1)} %get-tuple-element.216), channel_id=1, source_target_pairs={{0,1},{1,0},{2,3},{3,2},{4,5},{5,4},{6,7},{7,6},{8,9},{9,8},{10,11... | collective-permute-start | bytes 776 | tf_op jit(solution)/shard_map/ppermute | solution.py:50
  46.1 3.6 %collective-permute-start.16 = (f32[8,8]{1,0:T(8,128)S(1)}, f32[8,8]{1,0:T(8,128)S(1)}, u32[]{:S(2)}, u32[]{:S(2)}) collective-permute-start(f32[8,8]{1,0:T(8,128)S(1)} %max.12), channel_id=1, source_target_pairs={{0,2},{1,3},{2,0},{3,1},{4,6},{5,7},{6,4},{7,5},{8,10},{9,11},{10,... | collective-permute-start | bytes 776 | tf_op jit(solution)/shard_map/ppermute | solution.py:50
  49.7 4.8 %collective-permute-start.17 = (f32[8,8]{1,0:T(8,128)S(1)}, f32[8,8]{1,0:T(8,128)S(1)}, u32[]{:S(2)}, u32[]{:S(2)}) collective-permute-start(f32[8,8]{1,0:T(8,128)S(1)} %max.13), channel_id=1, source_target_pairs={{0,6},{1,7},{2,4},{3,5},{4,2},{5,3},{6,0},{7,1},{8,14},{9,15},{10,... | collective-permute-start | bytes 776 | tf_op jit(solution)/shard_map/ppermute | solution.py:50
  54.5 5.1 %collective-permute-start.18 = (f32[8,8]{1,0:T(8,128)S(1)}, f32[8,8]{1,0:T(8,128)S(1)}, u32[]{:S(2)}, u32[]{:S(2)}) collective-permute-start(f32[8,8]{1,0:T(8,128)S(1)} %max.14), channel_id=1, source_target_pairs={{0,8},{1,9},{2,10},{3,11},{4,12},{5,13},{6,14},{7,15},{8,0},{9,1},... | collective-permute-start | bytes 776 | tf_op jit(solution)/shard_map/ppermute | solution.py:50

commit v14 on v13

--- a/solution.py
+++ b/solution.py
@@ -344,11 +344,11 @@
     wide, stat = prepare_templates(templates, small)
 
     shard, even = lax.optimization_barrier((strain[0], lax.axis_index("dt") % 2 == 0))
-    x = jnp.transpose(shard, (2, 1, 0, 3)).reshape(JS, 2 * NDET, 1, FB)
-    got = {0: x}
+    got = {0: shard}
     for dx in (2, 3, 1):
-        got[dx] = swap_with(x, across(dx=dx))
-    x = jnp.concatenate([got[dx] for dx in range(4)], axis=2)
+        got[dx] = swap_with(shard, across(dx=dx))
+    pieces = [jnp.transpose(got[dx], (2, 1, 0, 3)).reshape(JS, 2 * NDET, 1, FB) for dx in range(4)]
+    x = jnp.concatenate(pieces, axis=2)
     x, turned = lax.optimization_barrier((x, turned))
     got = swap_with(x, across(dy=1))
     x, got, wide = lax.optimization_barrier((x, got, wide))

time: 60.5 us -> 60.5 us (level)
  no operation moved by 1% of the time
where the time goes in v14:
time: 60.5 us; the launch traced here: 60.2 us
  starting transfers between devices  24.9 us (41%)
  Pallas kernels  17.6 us (29%)
  waiting for transfers between devices  13.2 us (22%)
  local copies, waits for them, and re-layouts  2.12 us (4%)
  other arithmetic  1.54 us (3%)
  between operations  0.79 us (1%)
    ppermute x19, starting transfers between devices, swap_with(): return lax.ppermute(value, AXES, pairs)  24.9 us
    pallas_call x7, Pallas kernels, add_bins(): pl.pallas_call(functools.partial(bins_kernel, parts, last), out_shape=out...  14 us
    ppermute x19, waiting for transfers between devices, swap_with(): return lax.ppermute(value, AXES, pairs)  13.2 us
    pallas_call x1, Pallas kernels, prepare_tables(): pl.pallas_call(tables_kernel, out_shape=[jax.ShapeDtypeStruct((SLOTS, LAN...  2.03 us
    unnamed x3, local copies, waits for them, and re-layouts  2 us
    pallas_call x1, Pallas kernels, prepare_templates(): pl.pallas_call(templates_kernel, out_shape=[jax.ShapeDtypeStruct((SLOTS,...  1.66 us
  transfers between devices with their start and end apart: 19, of which 8 were waited for; matrix products, arithmetic and copies ran while one was open for 2% of the time, Pallas kernels for 25%

profile of v14, /device:TPU:0, one launch (start us, length us, event | category | flops | bytes accessed | tf_op | source)
XLA Modules:
  0.0 60.2 jit_solution(6488718543068114482)
XLA Ops:
  0.0 0.7 %copy.97 = bf16[1,3,2,6,256]{4,3,1,2,0:T(8,128)(2,1)S(1)} copy(bf16[1,3,2,6,256]{4,2,3,1,0:T(2,128)(2,1)} %param.5) | data formatting | bytes 36864 | tf_op args[0]
  0.7 2.8 %collective-permute-start.2 = (bf16[3,2,6,256]{3,2,0,1:T(8,128)(2,1)S(1)}, bf16[3,2,6,256]{3,2,0,1:T(8,128)(2,1)S(1)}, u32[]{:S(2)}, u32[]{:S(2)}) collective-permute-start(bf16[3,2,6,256]{3,2,0,1:T(8,128)(2,1)S(1)} %bitcast.31), channel_id=1, source_target_pairs={{0,96},{1,97},{2,98},{3,99},{4,100},{5,101},{6,102},{7,103},{8,104... | collective-permute-start | bytes 55304 | tf_op jit(solution)/shard_map/ppermute | solution.py:50
  3.6 0.8 %collective-permute-start.1 = (bf16[3,2,6,256]{3,2,0,1:T(8,128)(2,1)S(1)}, bf16[3,2,6,256]{3,2,0,1:T(8,128)(2,1)S(1)}, u32[]{:S(2)}, u32[]{:S(2)}) collective-permute-start(bf16[3,2,6,256]{3,2,0,1:T(8,128)(2,1)S(1)} %bitcast.32), channel_id=1, source_target_pairs={{0,64},{1,65},{2,66},{3,67},{4,68},{5,69},{6,70},{7,71},{8,72},{9,... | collective-permute-start | bytes 55304 | tf_op jit(solution)/shard_map/ppermute | solution.py:50
  4.4 0.5 collective-permute-start
  5.5 0.1 pad.18.clone
  5.5 0.8 %fusion.small_ref = s32[16,128]{1,0:T(8,128)S(1)} fusion(s32[3,8]{1,0:T(4,128)} %bitcast.38, s32[12,15]{1,0:T(8,128)} %param.8, s32[16]{0:T(128)S(1)} %pad.18.clone), kind=kLoop, calls=%fused_computation.9 | loop fusion | flops 8192 | bytes 9072 | tf_op jit(solution)/shard_map/concatenate | solution.py:182
  6.3 2.0 %prepare_tables.1 = (f32[12,128]{1,0:T(8,128)S(1)}, f32[96,2,24,256]{3,2,1,0:T(8,128)S(1)}, bf16[512,256]{1,0:T(8,128)(2,1)S(1)}, f32[2,16,8,128]{3,2,1,0:T(8,12...) custom-call(s32[16,128]{1,0:T(8,128)S(1)} %fusion.small_ref), custom_call_target="tpu_custom_call" | custom-call | flops 1000000 | bytes 1000000 | tf_op jit(solution)/shard_map/prepare_tables/pallas_call | solution.py:190
  8.4 0.5 collective-permute-done.1
  8.9 0.0 collective-permute-done
  8.9 1.7 %collective-permute-start.3 = (bf16[6,6,4,256]{3,0,1,2:T(8,128)(2,1)S(1)}, bf16[6,6,4,256]{3,0,1,2:T(8,128)(2,1)S(1)}, u32[]{:S(2)}, u32[]{:S(2)}) collective-permute-start(bf16[6,6,4,256]{3,0,1,2:T(8,128)(2,1)S(1)} %pad_maximum_fusion.3), channel_id=1, source_target_pairs={{0,16},{1,17},{2,18},{3,19},{4,20},{5,21},{6,22},{7,23},{8,24},{9,... | collective-permute-start | bytes 221192 | tf_op jit(solution)/shard_map/ppermute | solution.py:50
  10.6 1.3 %copy-done = bf16[12,2,96,256]{3,2,1,0:T(8,128)(2,1)S(1)} copy-done((bf16[12,2,96,256]{3,2,1,0:T(8,128)(2,1)S(1)}, bf16[12,2,96,256]{3,2,1,0:T(8,128)(2,1)}, u32[]{:S(2)}) %copy-start) | copy-done | bytes 1179672
  11.9 1.7 %prepare_templates.1 = (f32[12,3,96,256]{3,2,1,0:T(8,128)S(1)}, f32[12,40,128]{2,1,0:T(8,128)S(1)}) custom-call(bf16[12,2,96,256]{3,2,1,0:T(8,128)(2,1)S(1)} %copy-done, s32[16,128]{1,0:T(8,128)S(1)} %fusion.small_ref), custom_call_target="tpu_custom_call" | custom-call | flops 1000000 | bytes 1000000 | tf_op jit(solution)/shard_map/prepare_templates/pallas_call | solution.py:209
  13.5 0.1 collective-permute-done.3
  13.8 0.1 collective-permute-start.6
  13.9 2.0 %collective-permute-start.5 = (bf16[1,6,48,256]{3,2,1,0:T(8,128)(2,1)S(1)}, bf16[1,6,48,256]{3,2,1,0:T(8,128)(2,1)S(1)}, u32[]{:S(2)}, u32[]{:S(2)}) collective-permute-start(bf16[1,6,48,256]{3,2,1,0:T(8,128)(2,1)S(1)} %bitcast.27), channel_id=1, source_target_pairs={{0,2},{1,3},{2,0},{3,1},{4,6},{5,7},{6,4},{7,5},{8,10},{9,11},{10,... | collective-permute-start | bytes 442376 | tf_op jit(solution)/shard_map/ppermute | solution.py:50
  15.9 3.0 %collective-permute-start.4 = (bf16[1,6,48,256]{3,2,1,0:T(8,128)(2,1)S(1)}, bf16[1,6,48,256]{3,2,1,0:T(8,128)(2,1)S(1)}, u32[]{:S(2)}, u32[]{:S(2)}) collective-permute-start(bf16[1,6,48,256]{3,2,1,0:T(8,128)(2,1)S(1)} %bitcast.28), channel_id=1, source_target_pairs={{0,24},{1,7},{2,26},{3,5},{4,28},{5,3},{6,30},{7,1},{8,16},{9,15},... | collective-permute-start | bytes 442376 | tf_op jit(solution)/shard_map/ppermute | solution.py:50
  18.9 1.6 %add_bins.6 = (f32[16,24,256]{2,1,0:T(8,128)S(1)}, f32[16,24,256]{2,1,0:T(8,128)S(1)}, f32[16,24,256]{2,1,0:T(8,128)S(1)}, f32[16,24,256]{2,1,0:T(8,128)S(1)}, f...) custom-call(bf16[1,6,48,256]{3,2,1,0:T(8,128)(2,1)S(1)} %bitcast.29,, ...), custom_call_target="tpu_custom_call", output_to_operand_aliasing={{0}: (7, {}), {1}: (8, {}), {2}: (9, {}), {3}: (10, {}), {4... | custom-call | flops 1811939328 | bytes 1000000 | tf_op jit(solution)/shard_map/add_bins/pallas_call | solution.py:328
  20.5 0.0 collective-permute-done.5.refs_0_
  20.5 1.7 %collective-permute-done.4.refs_0_ = bf16[1,6,48,256]{3,2,1,0:T(8,128)(2,1)S(1)} collective-permute-done((bf16[1,6,48,256]{3,2,1,0:T(8,128)(2,1)S(1)}, bf16[1,6,48,256]{3,2,1,0:T(8,128)(2,1)S(1)}, u32[]{:S(2)}, u32[]{:S(2)}) %collective-permute-start.4) | collective-permute-done | bytes 147488 | tf_op jit(solution)/shard_map/ppermute | solution.py:50
  22.2 0.0 collective-permute-start.10
  22.2 0.1 collective-permute-start.7
  22.3 0.4 collective-permute-start.9
  22.8 3.9 %collective-permute-start.8 = (bf16[2,6,48,256]{3,2,1,0:T(8,128)(2,1)S(1)}, bf16[2,6,48,256]{3,2,1,0:T(8,128)(2,1)S(1)}, u32[]{:S(2)}, u32[]{:S(2)}) collective-permute-start(bf16[2,6,48,256]{3,2,1,0:T(8,128)(2,1)S(1)} %pad_maximum_fusion), channel_id=1, source_target_pairs={{0,6},{1,25},{2,4},{3,27},{4,2},{5,29},{6,0},{7,31},{8,14},{9,17},... | collective-permute-start | bytes 884744 | tf_op jit(solution)/shard_map/ppermute | solution.py:50
  26.7 0.0 collective-permute-done.10.refs_1_
  26.7 1.6 %add_bins.7 = (f32[16,24,256]{2,1,0:T(8,128)S(1)}, f32[16,24,256]{2,1,0:T(8,128)S(1)}, f32[16,24,256]{2,1,0:T(8,128)S(1)}, f32[16,24,256]{2,1,0:T(8,128)S(1)}, f...) custom-call(bf16[1,6,48,256]{3,2,1,0:T(8,128)(2,1)S(1)} %collective-, ...), custom_call_target="tpu_custom_call", output_to_operand_aliasing={{0}: (7, {}), {1}: (8, {}), {2}: (9, {}), {3}: (10, {}), {4... | custom-call | flops 1811939328 | bytes 1000000 | tf_op jit(solution)/shard_map/add_bins/pallas_call | solution.py:328
  28.3 1.6 %add_bins.8 = (f32[16,24,256]{2,1,0:T(8,128)S(1)}, f32[16,24,256]{2,1,0:T(8,128)S(1)}, f32[16,24,256]{2,1,0:T(8,128)S(1)}, f32[16,24,256]{2,1,0:T(8,128)S(1)}, f...) custom-call(bf16[1,6,48,256]{3,2,1,0:T(8,128)(2,1)S(1)} %collective-, ...), custom_call_target="tpu_custom_call", output_to_operand_aliasing={{0}: (7, {}), {1}: (8, {}), {2}: (9, {}), {3}: (10, {}), {4... | custom-call | flops 1811939328 | bytes 1000000 | tf_op jit(solution)/shard_map/add_bins/pallas_call | solution.py:328
  29.9 0.0 collective-permute-done.7.refs_0_
  30.0 1.4 %collective-permute-done.8.refs_0_ = bf16[2,6,48,256]{3,2,1,0:T(8,128)(2,1)S(1)} collective-permute-done((bf16[2,6,48,256]{3,2,1,0:T(8,128)(2,1)S(1)}, bf16[2,6,48,256]{3,2,1,0:T(8,128)(2,1)S(1)}, u32[]{:S(2)}, u32[]{:S(2)}) %collective-permute-start.8) | collective-permute-done | bytes 294944 | tf_op jit(solution)/shard_map/ppermute | solution.py:50
  31.4 0.0 collective-permute-start.13
  31.4 0.5 collective-permute-start.12
  31.9 3.5 %collective-permute-start.11 = (bf16[2,6,48,256]{3,2,1,0:T(8,128)(2,1)S(1)}, bf16[2,6,48,256]{3,2,1,0:T(8,128)(2,1)S(1)}, u32[]{:S(2)}, u32[]{:S(2)}) collective-permute-start(bf16[2,6,48,256]{3,2,1,0:T(8,128)(2,1)S(1)} %pad_maximum_fusion.1), channel_id=1, source_target_pairs={{0,6},{1,25},{2,4},{3,27},{4,2},{5,29},{6,0},{7,31},{8,14},{9,17},... | collective-permute-start | bytes 884744 | tf_op jit(solution)/shard_map/ppermute | solution.py:50
  35.4 0.0 collective-permute-done.13.refs_1_
  35.4 1.6 %add_bins.9 = (f32[16,24,256]{2,1,0:T(8,128)S(1)}, f32[16,24,256]{2,1,0:T(8,128)S(1)}, f32[16,24,256]{2,1,0:T(8,128)S(1)}, f32[16,24,256]{2,1,0:T(8,128)S(1)}, f...) custom-call(bf16[1,6,48,256]{3,2,1,0:T(8,128)(2,1)S(1)} %collective-, ...), custom_call_target="tpu_custom_call", output_to_operand_aliasing={{0}: (7, {}), {1}: (8, {}), {2}: (9, {}), {3}: (10, {}), {4... | custom-call | flops 1811939328 | bytes 1000000 | tf_op jit(solution)/shard_map/add_bins/pallas_call | solution.py:328
  37.0 0.0 collective-permute-done.12.refs_1_
  37.1 3.2 %add_bins.10 = (f32[16,24,256]{2,1,0:T(8,128)S(1)}, f32[16,24,256]{2,1,0:T(8,128)S(1)}, f32[16,24,256]{2,1,0:T(8,128)S(1)}, f32[16,24,256]{2,1,0:T(8,128)S(1)}, ...) custom-call(bf16[2,6,48,256]{3,2,1,0:T(8,128)(2,1)S(1)} %collective-, ...), custom_call_target="tpu_custom_call", output_to_operand_aliasing={{0}: (7, {}), {1}: (8, {}), {2}: (9, {}), {3}: (10, {}), {4... | custom-call | flops 3623878656 | bytes 1000000 | tf_op jit(solution)/shard_map/add_bins/pallas_call | solution.py:328
  40.3 0.1 collective-permute-start.14
  40.4 1.6 %add_bins.11 = (f32[16,24,256]{2,1,0:T(8,128)S(1)}, f32[16,24,256]{2,1,0:T(8,128)S(1)}, f32[16,24,256]{2,1,0:T(8,128)S(1)}, f32[16,24,256]{2,1,0:T(8,128)S(1)}, ...) custom-call(bf16[2,6,48,256]{3,2,1,0:T(8,128)(2,1)S(1)} %collective-, ...), custom_call_target="tpu_custom_call", output_to_operand_aliasing={{0}: (6, {}), {1}: (7, {}), {2}: (8, {}), {3}: (9, {}), {4}... | custom-call | flops 1811939328 | bytes 1000000 | tf_op jit(solution)/shard_map/add_bins/pallas_call | solution.py:328
  42.0 0.0 collective-permute-done.14.refs_0_
  42.0 2.7 %last_bins.1 = (f32[16,24,256]{2,1,0:T(8,128)S(1)}, f32[16,24,256]{2,1,0:T(8,128)S(1)}, f32[16,24,256]{2,1,0:T(8,128)S(1)}, f32[16,24,256]{2,1,0:T(8,128)S(1)}, ...) custom-call(bf16[2,6,48,256]{3,2,1,0:T(8,128)(2,1)S(1)} %collective-, ...), custom_call_target="tpu_custom_call", output_to_operand_aliasing={{0}: (7, {}), {1}: (8, {}), {2}: (9, {}), {3}: (10, {}), {4... | custom-call | flops 1811939328 | bytes 1000000 | tf_op jit(solution)/shard_map/last_bins/pallas_call | solution.py:328
  44.7 0.6 collective-permute-start.15
  45.3 0.8 %collective-permute-done.15 = f32[8,8]{1,0:T(8,128)S(1)} collective-permute-done((f32[8,8]{1,0:T(8,128)S(1)}, f32[8,8]{1,0:T(8,128)S(1)}, u32[]{:S(2)}, u32[]{:S(2)}) %collective-permute-start.15) | collective-permute-done | bytes 288 | tf_op jit(solution)/shard_map/ppermute | solution.py:50
  46.1 0.0 collective-permute-start.16
  46.1 3.6 %collective-permute-done.16 = f32[8,8]{1,0:T(8,128)S(1)} collective-permute-done((f32[8,8]{1,0:T(8,128)S(1)}, f32[8,8]{1,0:T(8,128)S(1)}, u32[]{:S(2)}, u32[]{:S(2)}) %collective-permute-start.16) | collective-permute-done | bytes 288 | tf_op jit(solution)/shard_map/ppermute | solution.py:50
  49.7 3.0 %collective-permute-start.17 = (f32[8,8]{1,0:T(8,128)S(1)}, f32[8,8]{1,0:T(8,128)S(1)}, u32[]{:S(2)}, u32[]{:S(2)}) collective-permute-start(f32[8,8]{1,0:T(8,128)S(1)} %max.13), channel_id=1, source_target_pairs={{0,6},{1,7},{2,4},{3,5},{4,2},{5,3},{6,0},{7,1},{8,14},{9,15},{10,... | collective-permute-start | bytes 776 | tf_op jit(solution)/shard_map/ppermute | solution.py:50
  52.7 1.8 %collective-permute-done.17 = f32[8,8]{1,0:T(8,128)S(1)} collective-permute-done((f32[8,8]{1,0:T(8,128)S(1)}, f32[8,8]{1,0:T(8,128)S(1)}, u32[]{:S(2)}, u32[]{:S(2)}) %collective-permute-start.17) | collective-permute-done | bytes 288 | tf_op jit(solution)/shard_map/ppermute | solution.py:50
  54.5 2.0 %collective-permute-start.18 = (f32[8,8]{1,0:T(8,128)S(1)}, f32[8,8]{1,0:T(8,128)S(1)}, u32[]{:S(2)}, u32[]{:S(2)}) collective-permute-start(f32[8,8]{1,0:T(8,128)S(1)} %max.14), channel_id=1, source_target_pairs={{0,8},{1,9},{2,10},{3,11},{4,12},{5,13},{6,14},{7,15},{8,0},{9,1},... | collective-permute-start | bytes 776 | tf_op jit(solution)/shard_map/ppermute | solution.py:50
  56.5 3.1 %collective-permute-done.18 = f32[8,8]{1,0:T(8,128)S(1)} collective-permute-done((f32[8,8]{1,0:T(8,128)S(1)}, f32[8,8]{1,0:T(8,128)S(1)}, u32[]{:S(2)}, u32[]{:S(2)}) %collective-permute-start.18) | collective-permute-done | bytes 288 | tf_op jit(solution)/shard_map/ppermute | solution.py:50
  59.6 0.6 max.15
  (14 shorter events, 0.2 us)
Async XLA Ops:
  0.7 7.6 %collective-permute-start.2 = (bf16[3,2,6,256]{3,2,0,1:T(8,128)(2,1)S(1)}, bf16[3,2,6,256]{3,2,0,1:T(8,128)(2,1)S(1)}, u32[]{:S(2)}, u32[]{:S(2)}) collective-permute-start(bf16[3,2,6,256]{3,2,0,1:T(8,128)(2,1)S(1)} %bitcast.31), channel_id=1, source_target_pairs={{0,96},{1,97},{2,98},{3,99},{4,100},{5,101},{6,102},{7,103},{8,104... | collective-permute-start | bytes 55304 | tf_op jit(solution)/shard_map/ppermute | solution.py:50
  3.6 5.3 %collective-permute-start.1 = (bf16[3,2,6,256]{3,2,0,1:T(8,128)(2,1)S(1)}, bf16[3,2,6,256]{3,2,0,1:T(8,128)(2,1)S(1)}, u32[]{:S(2)}, u32[]{:S(2)}) collective-permute-start(bf16[3,2,6,256]{3,2,0,1:T(8,128)(2,1)S(1)} %bitcast.32), channel_id=1, source_target_pairs={{0,64},{1,65},{2,66},{3,67},{4,68},{5,69},{6,70},{7,71},{8,72},{9,... | collective-permute-start | bytes 55304 | tf_op jit(solution)/shard_map/ppermute | solution.py:50
  4.4 4.5 %collective-permute-start = (bf16[3,2,6,256]{3,2,0,1:T(8,128)(2,1)S(1)}, bf16[3,2,6,256]{3,2,0,1:T(8,128)(2,1)S(1)}, u32[]{:S(2)}, u32[]{:S(2)}) collective-permute-start(bf16[3,2,6,256]{3,2,0,1:T(8,128)(2,1)S(1)} %bitcast.33), channel_id=1, source_target_pairs={{0,32},{1,33},{2,34},{3,35},{4,36},{5,37},{6,38},{7,39},{8,40},{9,... | collective-permute-start | bytes 55304 | tf_op jit(solution)/shard_map/ppermute | solution.py:50
  8.9 4.7 %collective-permute-start.3 = (bf16[6,6,4,256]{3,0,1,2:T(8,128)(2,1)S(1)}, bf16[6,6,4,256]{3,0,1,2:T(8,128)(2,1)S(1)}, u32[]{:S(2)}, u32[]{:S(2)}) collective-permute-start(bf16[6,6,4,256]{3,0,1,2:T(8,128)(2,1)S(1)} %pad_maximum_fusion.3), channel_id=1, source_target_pairs={{0,16},{1,17},{2,18},{3,19},{4,20},{5,21},{6,22},{7,23},{8,24},{9,... | collective-permute-start | bytes 221192 | tf_op jit(solution)/shard_map/ppermute | solution.py:50
  10.6 1.3 %copy-start = (bf16[12,2,96,256]{3,2,1,0:T(8,128)(2,1)S(1)}, bf16[12,2,96,256]{3,2,1,0:T(8,128)(2,1)}, u32[]{:S(2)}) copy-start(bf16[12,2,96,256]{3,2,1,0:T(8,128)(2,1)} %templ_ref.1) | copy-start | bytes 3538948
  13.8 5.1 %collective-permute-start.6 = (bf16[1,6,48,256]{3,2,1,0:T(8,128)(2,1)S(1)}, bf16[1,6,48,256]{3,2,1,0:T(8,128)(2,1)S(1)}, u32[]{:S(2)}, u32[]{:S(2)}) collective-permute-start(bf16[1,6,48,256]{3,2,1,0:T(8,128)(2,1)S(1)} %bitcast.26), channel_id=1, source_target_pairs={{0,1},{1,0},{2,3},{3,2},{4,5},{5,4},{6,7},{7,6},{8,9},{9,8},{10,11... | collective-permute-start | bytes 442376 | tf_op jit(solution)/shard_map/ppermute | solution.py:50
  13.9 6.6 %collective-permute-start.5 = (bf16[1,6,48,256]{3,2,1,0:T(8,128)(2,1)S(1)}, bf16[1,6,48,256]{3,2,1,0:T(8,128)(2,1)S(1)}, u32[]{:S(2)}, u32[]{:S(2)}) collective-permute-start(bf16[1,6,48,256]{3,2,1,0:T(8,128)(2,1)S(1)} %bitcast.27), channel_id=1, source_target_pairs={{0,2},{1,3},{2,0},{3,1},{4,6},{5,7},{6,4},{7,5},{8,10},{9,11},{10,... | collective-permute-start | bytes 442376 | tf_op jit(solution)/shard_map/ppermute | solution.py:50
  15.9 6.4 %collective-permute-start.4 = (bf16[1,6,48,256]{3,2,1,0:T(8,128)(2,1)S(1)}, bf16[1,6,48,256]{3,2,1,0:T(8,128)(2,1)S(1)}, u32[]{:S(2)}, u32[]{:S(2)}) collective-permute-start(bf16[1,6,48,256]{3,2,1,0:T(8,128)(2,1)S(1)} %bitcast.28), channel_id=1, source_target_pairs={{0,24},{1,7},{2,26},{3,5},{4,28},{5,3},{6,30},{7,1},{8,16},{9,15},... | collective-permute-start | bytes 442376 | tf_op jit(solution)/shard_map/ppermute | solution.py:50
  22.2 4.5 %collective-permute-start.10 = (bf16[1,6,48,256]{3,2,1,0:T(8,128)(2,1)S(1)}, bf16[1,6,48,256]{3,2,1,0:T(8,128)(2,1)S(1)}, u32[]{:S(2)}, u32[]{:S(2)}) collective-permute-start(bf16[1,6,48,256]{3,2,1,0:T(8,128)(2,1)S(1)} %collective-permute-done.4.refs_0_), channel_id=1, source_target_pairs={{0,1},{1,0},{2,3},{3,2},{4,5},{5,4},{6,7},{7,6},{8,9},{9,8},{10,11... | collective-permute-start | bytes 442376 | tf_op jit(solution)/shard_map/ppermute | solution.py:50
  22.2 7.7 %collective-permute-start.7 = (bf16[1,6,48,256]{3,2,1,0:T(8,128)(2,1)S(1)}, bf16[1,6,48,256]{3,2,1,0:T(8,128)(2,1)S(1)}, u32[]{:S(2)}, u32[]{:S(2)}) collective-permute-start(bf16[1,6,48,256]{3,2,1,0:T(8,128)(2,1)S(1)} %collective-permute-done.4.refs_0_), channel_id=1, source_target_pairs={{0,2},{1,3},{2,0},{3,1},{4,6},{5,7},{6,4},{7,5},{8,10},{9,11},{10,... | collective-permute-start | bytes 442376 | tf_op jit(solution)/shard_map/ppermute | solution.py:50
  22.3 6.0 %collective-permute-start.9 = (bf16[1,6,48,256]{3,2,1,0:T(8,128)(2,1)S(1)}, bf16[1,6,48,256]{3,2,1,0:T(8,128)(2,1)S(1)}, u32[]{:S(2)}, u32[]{:S(2)}) collective-permute-start(bf16[1,6,48,256]{3,2,1,0:T(8,128)(2,1)S(1)} %collective-permute-done.5.refs_0_), channel_id=1, source_target_pairs={{0,1},{1,0},{2,3},{3,2},{4,5},{5,4},{6,7},{7,6},{8,9},{9,8},{10,11... | collective-permute-start | bytes 442376 | tf_op jit(solution)/shard_map/ppermute | solution.py:50
  22.8 8.6 %collective-permute-start.8 = (bf16[2,6,48,256]{3,2,1,0:T(8,128)(2,1)S(1)}, bf16[2,6,48,256]{3,2,1,0:T(8,128)(2,1)S(1)}, u32[]{:S(2)}, u32[]{:S(2)}) collective-permute-start(bf16[2,6,48,256]{3,2,1,0:T(8,128)(2,1)S(1)} %pad_maximum_fusion), channel_id=1, source_target_pairs={{0,6},{1,25},{2,4},{3,27},{4,2},{5,29},{6,0},{7,31},{8,14},{9,17},... | collective-permute-start | bytes 884744 | tf_op jit(solution)/shard_map/ppermute | solution.py:50
  31.4 4.0 %collective-permute-start.13 = (bf16[1,6,48,256]{3,2,1,0:T(8,128)(2,1)S(1)}, bf16[1,6,48,256]{3,2,1,0:T(8,128)(2,1)S(1)}, u32[]{:S(2)}, u32[]{:S(2)}) collective-permute-start(bf16[1,6,48,256]{3,2,1,0:T(8,128)(2,1)S(1)} %collective-permute-done.7.refs_0_), channel_id=1, source_target_pairs={{0,1},{1,0},{2,3},{3,2},{4,5},{5,4},{6,7},{7,6},{8,9},{9,8},{10,11... | collective-permute-start | bytes 442376 | tf_op jit(solution)/shard_map/ppermute | solution.py:50
  31.4 5.6 %collective-permute-start.12 = (bf16[2,6,48,256]{3,2,1,0:T(8,128)(2,1)S(1)}, bf16[2,6,48,256]{3,2,1,0:T(8,128)(2,1)S(1)}, u32[]{:S(2)}, u32[]{:S(2)}) collective-permute-start(bf16[2,6,48,256]{3,2,1,0:T(8,128)(2,1)S(1)} %collective-permute-done.8.refs_0_), channel_id=1, source_target_pairs={{0,1},{1,0},{2,3},{3,2},{4,5},{5,4},{6,7},{7,6},{8,9},{9,8},{10,11... | collective-permute-start | bytes 884744 | tf_op jit(solution)/shard_map/ppermute | solution.py:50
  31.9 8.3 %collective-permute-start.11 = (bf16[2,6,48,256]{3,2,1,0:T(8,128)(2,1)S(1)}, bf16[2,6,48,256]{3,2,1,0:T(8,128)(2,1)S(1)}, u32[]{:S(2)}, u32[]{:S(2)}) collective-permute-start(bf16[2,6,48,256]{3,2,1,0:T(8,128)(2,1)S(1)} %pad_maximum_fusion.1), channel_id=1, source_target_pairs={{0,6},{1,25},{2,4},{3,27},{4,2},{5,29},{6,0},{7,31},{8,14},{9,17},... | collective-permute-start | bytes 884744 | tf_op jit(solution)/shard_map/ppermute | solution.py:50
  40.3 1.7 %collective-permute-start.14 = (bf16[2,6,48,256]{3,2,1,0:T(8,128)(2,1)S(1)}, bf16[2,6,48,256]{3,2,1,0:T(8,128)(2,1)S(1)}, u32[]{:S(2)}, u32[]{:S(2)}) collective-permute-start(bf16[2,6,48,256]{3,2,1,0:T(8,128)(2,1)S(1)} %collective-permute-done.11.refs_0_), channel_id=1, source_target_pairs={{0,1},{1,0},{2,3},{3,2},{4,5},{5,4},{6,7},{7,6},{8,9},{9,8},{10,11... | collective-permute-start | bytes 884744 | tf_op jit(solution)/shard_map/ppermute | solution.py:50
  44.7 1.4 %collective-permute-start.15 = (f32[8,8]{1,0:T(8,128)S(1)}, f32[8,8]{1,0:T(8,128)S(1)}, u32[]{:S(2)}, u32[]{:S(2)}) collective-permute-start(f32[8,8]{1,0:T(8,128)S(1)} %get-tuple-element.216), channel_id=1, source_target_pairs={{0,1},{1,0},{2,3},{3,2},{4,5},{5,4},{6,7},{7,6},{8,9},{9,8},{10,11... | collective-permute-start | bytes 776 | tf_op jit(solution)/shard_map/ppermute | solution.py:50
  46.1 3.6 %collective-permute-start.16 = (f32[8,8]{1,0:T(8,128)S(1)}, f32[8,8]{1,0:T(8,128)S(1)}, u32[]{:S(2)}, u32[]{:S(2)}) collective-permute-start(f32[8,8]{1,0:T(8,128)S(1)} %max.12), channel_id=1, source_target_pairs={{0,2},{1,3},{2,0},{3,1},{4,6},{5,7},{6,4},{7,5},{8,10},{9,11},{10,... | collective-permute-start | bytes 776 | tf_op jit(solution)/shard_map/ppermute | solution.py:50
  49.7 4.8 %collective-permute-start.17 = (f32[8,8]{1,0:T(8,128)S(1)}, f32[8,8]{1,0:T(8,128)S(1)}, u32[]{:S(2)}, u32[]{:S(2)}) collective-permute-start(f32[8,8]{1,0:T(8,128)S(1)} %max.13), channel_id=1, source_target_pairs={{0,6},{1,7},{2,4},{3,5},{4,2},{5,3},{6,0},{7,1},{8,14},{9,15},{10,... | collective-permute-start | bytes 776 | tf_op jit(solution)/shard_map/ppermute | solution.py:50
  54.5 5.1 %collective-permute-start.18 = (f32[8,8]{1,0:T(8,128)S(1)}, f32[8,8]{1,0:T(8,128)S(1)}, u32[]{:S(2)}, u32[]{:S(2)}) collective-permute-start(f32[8,8]{1,0:T(8,128)S(1)} %max.14), channel_id=1, source_target_pairs={{0,8},{1,9},{2,10},{3,11},{4,12},{5,13},{6,14},{7,15},{8,0},{9,1},... | collective-permute-start | bytes 776 | tf_op jit(solution)/shard_map/ppermute | solution.py:50

commit v15 on v13

--- a/solution.py
+++ b/solution.py
@@ -376,8 +376,7 @@
     (p3, p45), binned = after((p3, p45), binned)
     p67 = swap_with(jnp.concatenate([p2, p3], axis=0), step_move(2))
     q3, q45 = to_core(p3), to_core(p45)
-    binned = add_bins((p3, q3), ((3, 1, 0), (3, 1, 1)), shared, binned)
-    binned = add_bins((p45, q45), ((4, 2, 0), (4, 2, 1)), shared, binned)
+    binned = add_bins((p3, p45, q3, q45), ((3, 1, 0), (4, 2, 0), (3, 1, 1), (4, 2, 1)), shared, binned)
     p67, binned = after(p67, binned)
     q67 = to_core(p67)
     binned = add_bins((p67,), ((6, 2, 0),), shared, binned)

time: 60.5 us -> 62.5 us (1.033)
  waiting for transfers between devices: 13.1 us -> 17.5 us
  starting transfers between devices: 25 us -> 22.6 us
    ppermute x19, waiting for transfers between devices: 13.1 us -> 17.5 us  [swap_with(): return lax.ppermute(value, AXES, pairs)]
    ppermute x19, starting transfers between devices: 25 us -> 22.6 us  [swap_with(): return lax.ppermute(value, AXES, pairs)]
    pallas_call x7 -> x6, Pallas kernels: 14 us -> 14 us  [add_bins(): pl.pallas_call(functools.partial(bins_kernel, parts, last), out_shape=out...]
  transfers between devices with their start and end apart: 19 -> 19, of which waited for: 8 -> 9; matrix products, arithmetic and copies ran while one was open for 2% -> 1% of each run, Pallas kernels for 25% -> 24%
where the time goes in v15:
time: 62.5 us; the launch traced here: 62.2 us
  starting transfers between devices  22.6 us (36%)
  Pallas kernels  17.7 us (28%)
  waiting for transfers between devices  17.5 us (28%)
  local copies, waits for them, and re-layouts  2.12 us (3%)
  other arithmetic  1.54 us (2%)
  between operations  0.76 us (1%)
    ppermute x19, starting transfers between devices, swap_with(): return lax.ppermute(value, AXES, pairs)  22.6 us
    ppermute x19, waiting for transfers between devices, swap_with(): return lax.ppermute(value, AXES, pairs)  17.5 us
    pallas_call x6, Pallas kernels, add_bins(): pl.pallas_call(functools.partial(bins_kernel, parts, last), out_shape=out...  14 us
    pallas_call x1, Pallas kernels, prepare_tables(): pl.pallas_call(tables_kernel, out_shape=[jax.ShapeDtypeStruct((SLOTS, LAN...  2.03 us
    unnamed x3, local copies, waits for them, and re-layouts  2 us
    pallas_call x1, Pallas kernels, prepare_templates(): pl.pallas_call(templates_kernel, out_shape=[jax.ShapeDtypeStruct((SLOTS,...  1.66 us
  transfers between devices with their start and end apart: 19, of which 9 were waited for; matrix products, arithmetic and copies ran while one was open for 1% of the time, Pallas kernels for 24%

profile of v15, /device:TPU:0, one launch (start us, length us, event | category | flops | bytes accessed | tf_op | source)
XLA Modules:
  0.0 62.2 jit_solution(10980577135183280236)
XLA Ops:
  0.0 0.7 %copy.85 = bf16[1,3,2,6,256]{4,3,1,2,0:T(8,128)(2,1)S(1)} copy(bf16[1,3,2,6,256]{4,2,3,1,0:T(2,128)(2,1)} %param.5) | data formatting | bytes 36864 | tf_op args[0]
  0.7 1.6 %collective-permute-start = (bf16[6,6,1,256]{3,0,1,2:T(8,128)(2,1)S(1)}, bf16[6,6,1,256]{3,0,1,2:T(8,128)(2,1)S(1)}, u32[]{:S(2)}, u32[]{:S(2)}) collective-permute-start(bf16[6,6,1,256]{3,0,1,2:T(8,128)(2,1)S(1)} %bitcast.22), channel_id=1, source_target_pairs={{0,32},{1,33},{2,34},{3,35},{4,36},{5,37},{6,38},{7,39},{8,40},{9,... | collective-permute-start | bytes 55304 | tf_op jit(solution)/shard_map/ppermute | solution.py:50
  2.3 2.7 %collective-permute-start.1 = (bf16[6,6,1,256]{3,0,1,2:T(8,128)(2,1)S(1)}, bf16[6,6,1,256]{3,0,1,2:T(8,128)(2,1)S(1)}, u32[]{:S(2)}, u32[]{:S(2)}) collective-permute-start(bf16[6,6,1,256]{3,0,1,2:T(8,128)(2,1)S(1)} %bitcast.23), channel_id=1, source_target_pairs={{0,64},{1,65},{2,66},{3,67},{4,68},{5,69},{6,70},{7,71},{8,72},{9,... | collective-permute-start | bytes 55304 | tf_op jit(solution)/shard_map/ppermute | solution.py:50
  5.0 0.4 collective-permute-start.2
  6.1 0.1 pad.18.clone
  6.2 0.8 %fusion.small_ref = s32[16,128]{1,0:T(8,128)S(1)} fusion(s32[3,8]{1,0:T(4,128)} %bitcast.26, s32[12,15]{1,0:T(8,128)} %param.8, s32[16]{0:T(128)S(1)} %pad.18.clone), kind=kLoop, calls=%fused_computation.9 | loop fusion | flops 8192 | bytes 9072 | tf_op jit(solution)/shard_map/concatenate | solution.py:182
  6.9 2.0 %prepare_tables.1 = (f32[12,128]{1,0:T(8,128)S(1)}, f32[96,2,24,256]{3,2,1,0:T(8,128)S(1)}, bf16[512,256]{1,0:T(8,128)(2,1)S(1)}, f32[2,16,8,128]{3,2,1,0:T(8,12...) custom-call(s32[16,128]{1,0:T(8,128)S(1)} %fusion.small_ref), custom_call_target="tpu_custom_call" | custom-call | flops 1000000 | bytes 1000000 | tf_op jit(solution)/shard_map/prepare_tables/pallas_call | solution.py:190
  9.0 0.0 collective-permute-done
  9.0 0.0 collective-permute-done.1
  9.0 1.1 %collective-permute-done.2 = bf16[6,6,1,256]{3,0,1,2:T(8,128)(2,1)S(1)} collective-permute-done((bf16[6,6,1,256]{3,0,1,2:T(8,128)(2,1)S(1)}, bf16[6,6,1,256]{3,0,1,2:T(8,128)(2,1)S(1)}, u32[]{:S(2)}, u32[]{:S(2)}) %collective-permute-start.2) | collective-permute-done | bytes 18464 | tf_op jit(solution)/shard_map/ppermute | solution.py:50
  10.1 1.7 %collective-permute-start.3 = (bf16[6,6,4,256]{3,0,1,2:T(8,128)(2,1)S(1)}, bf16[6,6,4,256]{3,0,1,2:T(8,128)(2,1)S(1)}, u32[]{:S(2)}, u32[]{:S(2)}) collective-permute-start(bf16[6,6,4,256]{3,0,1,2:T(8,128)(2,1)S(1)} %pad_maximum_fusion.3), channel_id=1, source_target_pairs={{0,16},{1,17},{2,18},{3,19},{4,20},{5,21},{6,22},{7,23},{8,24},{9,... | collective-permute-start | bytes 221192 | tf_op jit(solution)/shard_map/ppermute | solution.py:50
  11.8 1.3 %copy-done = bf16[12,2,96,256]{3,2,1,0:T(8,128)(2,1)S(1)} copy-done((bf16[12,2,96,256]{3,2,1,0:T(8,128)(2,1)S(1)}, bf16[12,2,96,256]{3,2,1,0:T(8,128)(2,1)}, u32[]{:S(2)}) %copy-start) | copy-done | bytes 1179672
  13.0 1.7 %prepare_templates.1 = (f32[12,3,96,256]{3,2,1,0:T(8,128)S(1)}, f32[12,40,128]{2,1,0:T(8,128)S(1)}) custom-call(bf16[12,2,96,256]{3,2,1,0:T(8,128)(2,1)S(1)} %copy-done, s32[16,128]{1,0:T(8,128)S(1)} %fusion.small_ref), custom_call_target="tpu_custom_call" | custom-call | flops 1000000 | bytes 1000000 | tf_op jit(solution)/shard_map/prepare_templates/pallas_call | solution.py:209
  14.7 0.1 collective-permute-done.3
  14.9 0.1 collective-permute-start.6
  15.0 3.1 %collective-permute-start.4 = (bf16[1,6,48,256]{3,2,1,0:T(8,128)(2,1)S(1)}, bf16[1,6,48,256]{3,2,1,0:T(8,128)(2,1)S(1)}, u32[]{:S(2)}, u32[]{:S(2)}) collective-permute-start(bf16[1,6,48,256]{3,2,1,0:T(8,128)(2,1)S(1)} %bitcast.18), channel_id=1, source_target_pairs={{0,24},{1,7},{2,26},{3,5},{4,28},{5,3},{6,30},{7,1},{8,16},{9,15},... | collective-permute-start | bytes 442376 | tf_op jit(solution)/shard_map/ppermute | solution.py:50
  18.1 1.9 %collective-permute-start.5 = (bf16[1,6,48,256]{3,2,1,0:T(8,128)(2,1)S(1)}, bf16[1,6,48,256]{3,2,1,0:T(8,128)(2,1)S(1)}, u32[]{:S(2)}, u32[]{:S(2)}) collective-permute-start(bf16[1,6,48,256]{3,2,1,0:T(8,128)(2,1)S(1)} %bitcast.19), channel_id=1, source_target_pairs={{0,2},{1,3},{2,0},{3,1},{4,6},{5,7},{6,4},{7,5},{8,10},{9,11},{10,... | collective-permute-start | bytes 442376 | tf_op jit(solution)/shard_map/ppermute | solution.py:50
  20.0 0.0 collective-permute-done.6.refs_1_
  20.0 1.6 %add_bins.5 = (f32[16,24,256]{2,1,0:T(8,128)S(1)}, f32[16,24,256]{2,1,0:T(8,128)S(1)}, f32[16,24,256]{2,1,0:T(8,128)S(1)}, f32[16,24,256]{2,1,0:T(8,128)S(1)}, f...) custom-call(bf16[1,6,48,256]{3,2,1,0:T(8,128)(2,1)S(1)} %bitcast.20,, ...), custom_call_target="tpu_custom_call", output_to_operand_aliasing={{0}: (7, {}), {1}: (8, {}), {2}: (9, {}), {3}: (10, {}), {4... | custom-call | flops 1811939328 | bytes 1000000 | tf_op jit(solution)/shard_map/add_bins/pallas_call | solution.py:328
  21.6 0.0 collective-permute-done.4.refs_0_
  21.6 3.0 %collective-permute-done.5.refs_0_ = bf16[1,6,48,256]{3,2,1,0:T(8,128)(2,1)S(1)} collective-permute-done((bf16[1,6,48,256]{3,2,1,0:T(8,128)(2,1)S(1)}, bf16[1,6,48,256]{3,2,1,0:T(8,128)(2,1)S(1)}, u32[]{:S(2)}, u32[]{:S(2)}) %collective-permute-start.5) | collective-permute-done | bytes 147488 | tf_op jit(solution)/shard_map/ppermute | solution.py:50
  24.6 0.1 collective-permute-start.10
  24.8 0.6 collective-permute-start.7
  25.3 0.2 collective-permute-start.9
  25.6 2.5 %collective-permute-start.8 = (bf16[2,6,48,256]{3,2,1,0:T(8,128)(2,1)S(1)}, bf16[2,6,48,256]{3,2,1,0:T(8,128)(2,1)S(1)}, u32[]{:S(2)}, u32[]{:S(2)}) collective-permute-start(bf16[2,6,48,256]{3,2,1,0:T(8,128)(2,1)S(1)} %pad_maximum_fusion), channel_id=1, source_target_pairs={{0,6},{1,25},{2,4},{3,27},{4,2},{5,29},{6,0},{7,31},{8,14},{9,17},... | collective-permute-start | bytes 884744 | tf_op jit(solution)/shard_map/ppermute | solution.py:50
  28.0 0.0 collective-permute-done.10.refs_1_
  28.0 1.6 %add_bins.6 = (f32[16,24,256]{2,1,0:T(8,128)S(1)}, f32[16,24,256]{2,1,0:T(8,128)S(1)}, f32[16,24,256]{2,1,0:T(8,128)S(1)}, f32[16,24,256]{2,1,0:T(8,128)S(1)}, f...) custom-call(bf16[1,6,48,256]{3,2,1,0:T(8,128)(2,1)S(1)} %collective-, ...), custom_call_target="tpu_custom_call", output_to_operand_aliasing={{0}: (7, {}), {1}: (8, {}), {2}: (9, {}), {3}: (10, {}), {4... | custom-call | flops 1811939328 | bytes 1000000 | tf_op jit(solution)/shard_map/add_bins/pallas_call | solution.py:328
  29.7 1.6 %add_bins.7 = (f32[16,24,256]{2,1,0:T(8,128)S(1)}, f32[16,24,256]{2,1,0:T(8,128)S(1)}, f32[16,24,256]{2,1,0:T(8,128)S(1)}, f32[16,24,256]{2,1,0:T(8,128)S(1)}, f...) custom-call(bf16[1,6,48,256]{3,2,1,0:T(8,128)(2,1)S(1)} %collective-, ...), custom_call_target="tpu_custom_call", output_to_operand_aliasing={{0}: (7, {}), {1}: (8, {}), {2}: (9, {}), {3}: (10, {}), {4... | custom-call | flops 1811939328 | bytes 1000000 | tf_op jit(solution)/shard_map/add_bins/pallas_call | solution.py:328
  31.3 0.0 collective-permute-done.7.refs_0_
  31.3 2.3 %collective-permute-done.8.refs_1_ = bf16[2,6,48,256]{3,2,1,0:T(8,128)(2,1)S(1)} collective-permute-done((bf16[2,6,48,256]{3,2,1,0:T(8,128)(2,1)S(1)}, bf16[2,6,48,256]{3,2,1,0:T(8,128)(2,1)S(1)}, u32[]{:S(2)}, u32[]{:S(2)}) %collective-permute-start.8) | collective-permute-done | bytes 294944 | tf_op jit(solution)/shard_map/ppermute | solution.py:50
  33.6 0.0 collective-permute-start.13
  33.6 0.5 collective-permute-start.12
  34.1 2.6 %collective-permute-start.11 = (bf16[2,6,48,256]{3,2,1,0:T(8,128)(2,1)S(1)}, bf16[2,6,48,256]{3,2,1,0:T(8,128)(2,1)S(1)}, u32[]{:S(2)}, u32[]{:S(2)}) collective-permute-start(bf16[2,6,48,256]{3,2,1,0:T(8,128)(2,1)S(1)} %pad_maximum_fusion.1), channel_id=1, source_target_pairs={{0,6},{1,25},{2,4},{3,27},{4,2},{5,29},{6,0},{7,31},{8,14},{9,17},... | collective-permute-start | bytes 884744 | tf_op jit(solution)/shard_map/ppermute | solution.py:50
  36.8 0.0 collective-permute-done.13.refs_3_
  36.8 4.8 %add_bins.8 = (f32[16,24,256]{2,1,0:T(8,128)S(1)}, f32[16,24,256]{2,1,0:T(8,128)S(1)}, f32[16,24,256]{2,1,0:T(8,128)S(1)}, f32[16,24,256]{2,1,0:T(8,128)S(1)}, f...) custom-call(bf16[1,6,48,256]{3,2,1,0:T(8,128)(2,1)S(1)} %collective-, ...), custom_call_target="tpu_custom_call", output_to_operand_aliasing={{0}: (9, {}), {1}: (10, {}), {2}: (11, {}), {3}: (12, {}), ... | custom-call | flops 5435817984 | bytes 1000000 | tf_op jit(solution)/shard_map/add_bins/pallas_call | solution.py:328
  41.6 0.7 %collective-permute-done.11.refs_0_ = bf16[2,6,48,256]{3,2,1,0:T(8,128)(2,1)S(1)} collective-permute-done((bf16[2,6,48,256]{3,2,1,0:T(8,128)(2,1)S(1)}, bf16[2,6,48,256]{3,2,1,0:T(8,128)(2,1)S(1)}, u32[]{:S(2)}, u32[]{:S(2)}) %collective-permute-start.11) | collective-permute-done | bytes 294944 | tf_op jit(solution)/shard_map/ppermute | solution.py:50
  42.3 1.6 %add_bins.9 = (f32[16,24,256]{2,1,0:T(8,128)S(1)}, f32[16,24,256]{2,1,0:T(8,128)S(1)}, f32[16,24,256]{2,1,0:T(8,128)S(1)}, f32[16,24,256]{2,1,0:T(8,128)S(1)}, f...) custom-call(bf16[2,6,48,256]{3,2,1,0:T(8,128)(2,1)S(1)} %collective-, ...), custom_call_target="tpu_custom_call", output_to_operand_aliasing={{0}: (6, {}), {1}: (7, {}), {2}: (8, {}), {3}: (9, {}), {4}... | custom-call | flops 1811939328 | bytes 1000000 | tf_op jit(solution)/shard_map/add_bins/pallas_call | solution.py:328
  43.9 0.0 collective-permute-done.14.refs_0_
  43.9 2.7 %last_bins.1 = (f32[16,24,256]{2,1,0:T(8,128)S(1)}, f32[16,24,256]{2,1,0:T(8,128)S(1)}, f32[16,24,256]{2,1,0:T(8,128)S(1)}, f32[16,24,256]{2,1,0:T(8,128)S(1)}, ...) custom-call(bf16[2,6,48,256]{3,2,1,0:T(8,128)(2,1)S(1)} %collective-, ...), custom_call_target="tpu_custom_call", output_to_operand_aliasing={{0}: (7, {}), {1}: (8, {}), {2}: (9, {}), {3}: (10, {}), {4... | custom-call | flops 1811939328 | bytes 1000000 | tf_op jit(solution)/shard_map/last_bins/pallas_call | solution.py:328
  46.7 0.6 collective-permute-start.15
  47.3 0.8 %collective-permute-done.15 = f32[8,8]{1,0:T(8,128)S(1)} collective-permute-done((f32[8,8]{1,0:T(8,128)S(1)}, f32[8,8]{1,0:T(8,128)S(1)}, u32[]{:S(2)}, u32[]{:S(2)}) %collective-permute-start.15) | collective-permute-done | bytes 288 | tf_op jit(solution)/shard_map/ppermute | solution.py:50
  48.1 0.0 collective-permute-start.16
  48.1 3.6 %collective-permute-done.16 = f32[8,8]{1,0:T(8,128)S(1)} collective-permute-done((f32[8,8]{1,0:T(8,128)S(1)}, f32[8,8]{1,0:T(8,128)S(1)}, u32[]{:S(2)}, u32[]{:S(2)}) %collective-permute-start.16) | collective-permute-done | bytes 288 | tf_op jit(solution)/shard_map/ppermute | solution.py:50
  51.7 2.4 %collective-permute-start.17 = (f32[8,8]{1,0:T(8,128)S(1)}, f32[8,8]{1,0:T(8,128)S(1)}, u32[]{:S(2)}, u32[]{:S(2)}) collective-permute-start(f32[8,8]{1,0:T(8,128)S(1)} %max.13), channel_id=1, source_target_pairs={{0,6},{1,7},{2,4},{3,5},{4,2},{5,3},{6,0},{7,1},{8,14},{9,15},{10,... | collective-permute-start | bytes 776 | tf_op jit(solution)/shard_map/ppermute | solution.py:50
  54.1 2.4 %collective-permute-done.17 = f32[8,8]{1,0:T(8,128)S(1)} collective-permute-done((f32[8,8]{1,0:T(8,128)S(1)}, f32[8,8]{1,0:T(8,128)S(1)}, u32[]{:S(2)}, u32[]{:S(2)}) %collective-permute-start.17) | collective-permute-done | bytes 288 | tf_op jit(solution)/shard_map/ppermute | solution.py:50
  56.5 1.7 %collective-permute-start.18 = (f32[8,8]{1,0:T(8,128)S(1)}, f32[8,8]{1,0:T(8,128)S(1)}, u32[]{:S(2)}, u32[]{:S(2)}) collective-permute-start(f32[8,8]{1,0:T(8,128)S(1)} %max.14), channel_id=1, source_target_pairs={{0,8},{1,9},{2,10},{3,11},{4,12},{5,13},{6,14},{7,15},{8,0},{9,1},... | collective-permute-start | bytes 776 | tf_op jit(solution)/shard_map/ppermute | solution.py:50
  58.2 3.4 %collective-permute-done.18 = f32[8,8]{1,0:T(8,128)S(1)} collective-permute-done((f32[8,8]{1,0:T(8,128)S(1)}, f32[8,8]{1,0:T(8,128)S(1)}, u32[]{:S(2)}, u32[]{:S(2)}) %collective-permute-start.18) | collective-permute-done | bytes 288 | tf_op jit(solution)/shard_map/ppermute | solution.py:50
  61.6 0.6 max.15
  (13 shorter events, 0.2 us)
Async XLA Ops:
  0.7 8.2 %collective-permute-start = (bf16[6,6,1,256]{3,0,1,2:T(8,128)(2,1)S(1)}, bf16[6,6,1,256]{3,0,1,2:T(8,128)(2,1)S(1)}, u32[]{:S(2)}, u32[]{:S(2)}) collective-permute-start(bf16[6,6,1,256]{3,0,1,2:T(8,128)(2,1)S(1)} %bitcast.22), channel_id=1, source_target_pairs={{0,32},{1,33},{2,34},{3,35},{4,36},{5,37},{6,38},{7,39},{8,40},{9,... | collective-permute-start | bytes 55304 | tf_op jit(solution)/shard_map/ppermute | solution.py:50
  2.3 6.7 %collective-permute-start.1 = (bf16[6,6,1,256]{3,0,1,2:T(8,128)(2,1)S(1)}, bf16[6,6,1,256]{3,0,1,2:T(8,128)(2,1)S(1)}, u32[]{:S(2)}, u32[]{:S(2)}) collective-permute-start(bf16[6,6,1,256]{3,0,1,2:T(8,128)(2,1)S(1)} %bitcast.23), channel_id=1, source_target_pairs={{0,64},{1,65},{2,66},{3,67},{4,68},{5,69},{6,70},{7,71},{8,72},{9,... | collective-permute-start | bytes 55304 | tf_op jit(solution)/shard_map/ppermute | solution.py:50
  5.0 5.0 %collective-permute-start.2 = (bf16[6,6,1,256]{3,0,1,2:T(8,128)(2,1)S(1)}, bf16[6,6,1,256]{3,0,1,2:T(8,128)(2,1)S(1)}, u32[]{:S(2)}, u32[]{:S(2)}) collective-permute-start(bf16[6,6,1,256]{3,0,1,2:T(8,128)(2,1)S(1)} %bitcast.24), channel_id=1, source_target_pairs={{0,96},{1,97},{2,98},{3,99},{4,100},{5,101},{6,102},{7,103},{8,104... | collective-permute-start | bytes 55304 | tf_op jit(solution)/shard_map/ppermute | solution.py:50
  10.1 4.7 %collective-permute-start.3 = (bf16[6,6,4,256]{3,0,1,2:T(8,128)(2,1)S(1)}, bf16[6,6,4,256]{3,0,1,2:T(8,128)(2,1)S(1)}, u32[]{:S(2)}, u32[]{:S(2)}) collective-permute-start(bf16[6,6,4,256]{3,0,1,2:T(8,128)(2,1)S(1)} %pad_maximum_fusion.3), channel_id=1, source_target_pairs={{0,16},{1,17},{2,18},{3,19},{4,20},{5,21},{6,22},{7,23},{8,24},{9,... | collective-permute-start | bytes 221192 | tf_op jit(solution)/shard_map/ppermute | solution.py:50
  11.8 1.3 %copy-start = (bf16[12,2,96,256]{3,2,1,0:T(8,128)(2,1)S(1)}, bf16[12,2,96,256]{3,2,1,0:T(8,128)(2,1)}, u32[]{:S(2)}) copy-start(bf16[12,2,96,256]{3,2,1,0:T(8,128)(2,1)} %templ_ref.1) | copy-start | bytes 3538948
  14.9 5.1 %collective-permute-start.6 = (bf16[1,6,48,256]{3,2,1,0:T(8,128)(2,1)S(1)}, bf16[1,6,48,256]{3,2,1,0:T(8,128)(2,1)S(1)}, u32[]{:S(2)}, u32[]{:S(2)}) collective-permute-start(bf16[1,6,48,256]{3,2,1,0:T(8,128)(2,1)S(1)} %bitcast.17), channel_id=1, source_target_pairs={{0,1},{1,0},{2,3},{3,2},{4,5},{5,4},{6,7},{7,6},{8,9},{9,8},{10,11... | collective-permute-start | bytes 442376 | tf_op jit(solution)/shard_map/ppermute | solution.py:50
  15.0 6.6 %collective-permute-start.4 = (bf16[1,6,48,256]{3,2,1,0:T(8,128)(2,1)S(1)}, bf16[1,6,48,256]{3,2,1,0:T(8,128)(2,1)S(1)}, u32[]{:S(2)}, u32[]{:S(2)}) collective-permute-start(bf16[1,6,48,256]{3,2,1,0:T(8,128)(2,1)S(1)} %bitcast.18), channel_id=1, source_target_pairs={{0,24},{1,7},{2,26},{3,5},{4,28},{5,3},{6,30},{7,1},{8,16},{9,15},... | collective-permute-start | bytes 442376 | tf_op jit(solution)/shard_map/ppermute | solution.py:50
  18.1 6.5 %collective-permute-start.5 = (bf16[1,6,48,256]{3,2,1,0:T(8,128)(2,1)S(1)}, bf16[1,6,48,256]{3,2,1,0:T(8,128)(2,1)S(1)}, u32[]{:S(2)}, u32[]{:S(2)}) collective-permute-start(bf16[1,6,48,256]{3,2,1,0:T(8,128)(2,1)S(1)} %bitcast.19), channel_id=1, source_target_pairs={{0,2},{1,3},{2,0},{3,1},{4,6},{5,7},{6,4},{7,5},{8,10},{9,11},{10,... | collective-permute-start | bytes 442376 | tf_op jit(solution)/shard_map/ppermute | solution.py:50
  24.6 3.4 %collective-permute-start.10 = (bf16[1,6,48,256]{3,2,1,0:T(8,128)(2,1)S(1)}, bf16[1,6,48,256]{3,2,1,0:T(8,128)(2,1)S(1)}, u32[]{:S(2)}, u32[]{:S(2)}) collective-permute-start(bf16[1,6,48,256]{3,2,1,0:T(8,128)(2,1)S(1)} %collective-permute-done.4.refs_0_), channel_id=1, source_target_pairs={{0,1},{1,0},{2,3},{3,2},{4,5},{5,4},{6,7},{7,6},{8,9},{9,8},{10,11... | collective-permute-start | bytes 442376 | tf_op jit(solution)/shard_map/ppermute | solution.py:50
  24.8 6.5 %collective-permute-start.7 = (bf16[1,6,48,256]{3,2,1,0:T(8,128)(2,1)S(1)}, bf16[1,6,48,256]{3,2,1,0:T(8,128)(2,1)S(1)}, u32[]{:S(2)}, u32[]{:S(2)}) collective-permute-start(bf16[1,6,48,256]{3,2,1,0:T(8,128)(2,1)S(1)} %collective-permute-done.4.refs_0_), channel_id=1, source_target_pairs={{0,2},{1,3},{2,0},{3,1},{4,6},{5,7},{6,4},{7,5},{8,10},{9,11},{10,... | collective-permute-start | bytes 442376 | tf_op jit(solution)/shard_map/ppermute | solution.py:50
  25.3 4.3 %collective-permute-start.9 = (bf16[1,6,48,256]{3,2,1,0:T(8,128)(2,1)S(1)}, bf16[1,6,48,256]{3,2,1,0:T(8,128)(2,1)S(1)}, u32[]{:S(2)}, u32[]{:S(2)}) collective-permute-start(bf16[1,6,48,256]{3,2,1,0:T(8,128)(2,1)S(1)} %collective-permute-done.5.refs_0_), channel_id=1, source_target_pairs={{0,1},{1,0},{2,3},{3,2},{4,5},{5,4},{6,7},{7,6},{8,9},{9,8},{10,11... | collective-permute-start | bytes 442376 | tf_op jit(solution)/shard_map/ppermute | solution.py:50
  25.6 8.0 %collective-permute-start.8 = (bf16[2,6,48,256]{3,2,1,0:T(8,128)(2,1)S(1)}, bf16[2,6,48,256]{3,2,1,0:T(8,128)(2,1)S(1)}, u32[]{:S(2)}, u32[]{:S(2)}) collective-permute-start(bf16[2,6,48,256]{3,2,1,0:T(8,128)(2,1)S(1)} %pad_maximum_fusion), channel_id=1, source_target_pairs={{0,6},{1,25},{2,4},{3,27},{4,2},{5,29},{6,0},{7,31},{8,14},{9,17},... | collective-permute-start | bytes 884744 | tf_op jit(solution)/shard_map/ppermute | solution.py:50
  33.6 3.2 %collective-permute-start.13 = (bf16[2,6,48,256]{3,2,1,0:T(8,128)(2,1)S(1)}, bf16[2,6,48,256]{3,2,1,0:T(8,128)(2,1)S(1)}, u32[]{:S(2)}, u32[]{:S(2)}) collective-permute-start(bf16[2,6,48,256]{3,2,1,0:T(8,128)(2,1)S(1)} %collective-permute-done.8.refs_1_), channel_id=1, source_target_pairs={{0,1},{1,0},{2,3},{3,2},{4,5},{5,4},{6,7},{7,6},{8,9},{9,8},{10,11... | collective-permute-start | bytes 884744 | tf_op jit(solution)/shard_map/ppermute | solution.py:50
  33.6 3.2 %collective-permute-start.12 = (bf16[1,6,48,256]{3,2,1,0:T(8,128)(2,1)S(1)}, bf16[1,6,48,256]{3,2,1,0:T(8,128)(2,1)S(1)}, u32[]{:S(2)}, u32[]{:S(2)}) collective-permute-start(bf16[1,6,48,256]{3,2,1,0:T(8,128)(2,1)S(1)} %collective-permute-done.7.refs_0_), channel_id=1, source_target_pairs={{0,1},{1,0},{2,3},{3,2},{4,5},{5,4},{6,7},{7,6},{8,9},{9,8},{10,11... | collective-permute-start | bytes 442376 | tf_op jit(solution)/shard_map/ppermute | solution.py:50
  34.1 8.2 %collective-permute-start.11 = (bf16[2,6,48,256]{3,2,1,0:T(8,128)(2,1)S(1)}, bf16[2,6,48,256]{3,2,1,0:T(8,128)(2,1)S(1)}, u32[]{:S(2)}, u32[]{:S(2)}) collective-permute-start(bf16[2,6,48,256]{3,2,1,0:T(8,128)(2,1)S(1)} %pad_maximum_fusion.1), channel_id=1, source_target_pairs={{0,6},{1,25},{2,4},{3,27},{4,2},{5,29},{6,0},{7,31},{8,14},{9,17},... | collective-permute-start | bytes 884744 | tf_op jit(solution)/shard_map/ppermute | solution.py:50
  42.3 1.6 %collective-permute-start.14 = (bf16[2,6,48,256]{3,2,1,0:T(8,128)(2,1)S(1)}, bf16[2,6,48,256]{3,2,1,0:T(8,128)(2,1)S(1)}, u32[]{:S(2)}, u32[]{:S(2)}) collective-permute-start(bf16[2,6,48,256]{3,2,1,0:T(8,128)(2,1)S(1)} %collective-permute-done.11.refs_0_), channel_id=1, source_target_pairs={{0,1},{1,0},{2,3},{3,2},{4,5},{5,4},{6,7},{7,6},{8,9},{9,8},{10,11... | collective-permute-start | bytes 884744 | tf_op jit(solution)/shard_map/ppermute | solution.py:50
  46.7 1.4 %collective-permute-start.15 = (f32[8,8]{1,0:T(8,128)S(1)}, f32[8,8]{1,0:T(8,128)S(1)}, u32[]{:S(2)}, u32[]{:S(2)}) collective-permute-start(f32[8,8]{1,0:T(8,128)S(1)} %get-tuple-element.192), channel_id=1, source_target_pairs={{0,1},{1,0},{2,3},{3,2},{4,5},{5,4},{6,7},{7,6},{8,9},{9,8},{10,11... | collective-permute-start | bytes 776 | tf_op jit(solution)/shard_map/ppermute | solution.py:50
  48.1 3.6 %collective-permute-start.16 = (f32[8,8]{1,0:T(8,128)S(1)}, f32[8,8]{1,0:T(8,128)S(1)}, u32[]{:S(2)}, u32[]{:S(2)}) collective-permute-start(f32[8,8]{1,0:T(8,128)S(1)} %max.12), channel_id=1, source_target_pairs={{0,2},{1,3},{2,0},{3,1},{4,6},{5,7},{6,4},{7,5},{8,10},{9,11},{10,... | collective-permute-start | bytes 776 | tf_op jit(solution)/shard_map/ppermute | solution.py:50
  51.7 4.8 %collective-permute-start.17 = (f32[8,8]{1,0:T(8,128)S(1)}, f32[8,8]{1,0:T(8,128)S(1)}, u32[]{:S(2)}, u32[]{:S(2)}) collective-permute-start(f32[8,8]{1,0:T(8,128)S(1)} %max.13), channel_id=1, source_target_pairs={{0,6},{1,7},{2,4},{3,5},{4,2},{5,3},{6,0},{7,1},{8,14},{9,15},{10,... | collective-permute-start | bytes 776 | tf_op jit(solution)/shard_map/ppermute | solution.py:50
  56.5 5.1 %collective-permute-start.18 = (f32[8,8]{1,0:T(8,128)S(1)}, f32[8,8]{1,0:T(8,128)S(1)}, u32[]{:S(2)}, u32[]{:S(2)}) collective-permute-start(f32[8,8]{1,0:T(8,128)S(1)} %max.14), channel_id=1, source_target_pairs={{0,8},{1,9},{2,10},{3,11},{4,12},{5,13},{6,14},{7,15},{8,0},{9,1},... | collective-permute-start | bytes 776 | tf_op jit(solution)/shard_map/ppermute | solution.py:50
